TPU v7x, 32 devices: a whole 2x2x4 slice. The times are simulated.
32 devices in a mesh: ens: 2 (over y), dom: 4 (over z), feat: 2 (over x), rep: 2 (over core).
Axes of the slice: x: 2, y: 2, z: 4, core: 2. Of those that a mesh axis runs over, the one named last changes fastest.
Arguments:
- grid_state: bfloat16 [8192, 512], P(('ens', 'dom', 'feat', 'rep')), parts along dimension 0, may hold values from -6 to 6
- mesh_base: bfloat16 [2048, 512], P('dom'), may hold values from -6 to 6
- edge_state: bfloat16 [16384, 512], P(('dom', 'feat', 'rep')), may hold values from -6 to 6
- enc_weight: bfloat16 [512, 512], P(('feat', 'rep')), may hold values from -0.25 to 0.25
- edge_in_weight: bfloat16 [1536, 512], P(('feat', 'rep')), may hold values from -0.15625 to 0.15625
- edge_out_weight: bfloat16 [512, 512], P(('feat', 'rep')), may hold values from -0.25 to 0.25
- node_in_weight: bfloat16 [1024, 512], P(('feat', 'rep')), may hold values from -0.1875 to 0.1875
- node_out_weight: bfloat16 [512, 512], P(('feat', 'rep')), may hold values from -0.25 to 0.25
- node_grad: bfloat16 [4096, 512], P(('ens', 'dom')), parts along dimension 0, may hold values from -6 to 6
- edge_grad: bfloat16 [32768, 512], P(('ens', 'dom', 'feat', 'rep')), parts along dimension 0, may hold values from -6 to 6
- halo_rows: int32 [4, 4, 128], P('dom'), may hold values from 0 to 511
- edge_send: int32 [16384], P(('dom', 'feat', 'rep')), may hold values from 0 to 1023
- edge_recv: int32 [16384], P(('dom', 'feat', 'rep')), may hold values from 0 to 511
- grid_send: int32 [16, 4, 128], P(('dom', 'feat', 'rep')), may hold values from 0 to 256, as said below
- grid_recv: int32 [16, 4, 128], P(('dom', 'feat', 'rep')), may hold values from 0 to 512, as said below
Outputs:
- grid_adjoint: float32 [8192, 512], P(('ens', 'dom', 'feat', 'rep')), parts along dimension 0
There are 2 independent parts, one for each index of `ens`. A program takes and returns all parts, laid end to end along the dimension named above; an argument that names none is the same for every part. Nothing has to cross between parts.
Inputs may be any that keep to these rules, and one draw needn't show every extreme that they name: `edge_send`: values below 512 name local nodes; the others name halo rows. `grid_send`: 256 marks an empty slot; each of a device's 256 rows fills exactly one slot; every device fills all 128 slots to its own partition and to one partition that is the same for all devices (when these are the same partition, the device's other rows may go to any partitions). `grid_recv`: 512 stands exactly where the matching grid_send slot is empty.
All inputs are finite; a program needn't handle non-finite values.
Results may differ from a plain program's by a relative error of at most 0.02.
Values may be sent and summed in bfloat16 or wider, within the bound.
No kernel may reach another device: no remote copies, remote signals or barrier semaphores. Data moves between devices by JAX's collectives and lax.ppermute only.
A program may use at most 64 MiB of HBM per device.

v0:
```python
import jax
import jax.numpy as jnp
from jax import lax
from jax.sharding import PartitionSpec as P


def silu_slope(values):
    logistic = jax.nn.sigmoid(values)
    return logistic * (1.0 + values * (1.0 - logistic))


def matmul(first_op, second_op):
    return jnp.dot(first_op, second_op, preferred_element_type=jnp.float32)


def against(first_op, second_op):
    return lax.dot_general(
        first_op, second_op, (((1,), (1,)), ((), ())), preferred_element_type=jnp.float32
    )


def trade_rows(block_rows):
    return lax.all_to_all(block_rows, "dom", split_axis=0, concat_axis=0, tiled=True)


def trade_grads(block_rows):
    return lax.all_to_all(block_rows, "dom", split_axis=0, concat_axis=0, tiled=True)


def node_backward(state_rows, aggregate_rows, grad_rows, node_in, node_out, model_width):
    node_pre = matmul(state_rows, node_in[:model_width]) + matmul(
        aggregate_rows, node_in[model_width:]
    )
    node_dpre = (against(grad_rows, node_out) * silu_slope(node_pre)).astype(jnp.bfloat16)
    return against(node_dpre, node_in)


def per_device(
    grid_state,
    mesh_base,
    edge_state,
    enc_weight,
    edge_in_weight,
    edge_out_weight,
    node_in_weight,
    node_out_weight,
    node_grad,
    edge_grad,
    halo_rows,
    edge_send,
    edge_recv,
    grid_send,
    grid_recv,
):
    model_width = mesh_base.shape[1]
    node_count = mesh_base.shape[0]
    grid_count = grid_state.shape[0]
    enc_full, in_full, out_full, node_in, node_out = (
        lax.all_gather(enc_weight, ("feat", "rep"), axis=0, tiled=True),
        lax.all_gather(edge_in_weight, ("feat", "rep"), axis=0, tiled=True),
        lax.all_gather(edge_out_weight, ("feat", "rep"), axis=0, tiled=True),
        lax.all_gather(node_in_weight, ("feat", "rep"), axis=0, tiled=True),
        lax.all_gather(node_out_weight, ("feat", "rep"), axis=0, tiled=True),
    )
    grid_pre = matmul(grid_state, enc_full)
    grid_message = jax.nn.silu(grid_pre).astype(jnp.bfloat16)
    send_rows = grid_send[0]
    recv_nodes = grid_recv[0]
    outgoing = jnp.take(grid_message, send_rows, axis=0, mode="fill", fill_value=0)
    incoming = trade_rows(outgoing)
    encoded = (
        jnp.zeros((node_count, model_width), jnp.float32)
        .at[recv_nodes.reshape(-1)]
        .add(incoming.reshape(-1, model_width).astype(jnp.float32), mode="drop")
    )
    encoded = lax.psum(encoded.astype(jnp.bfloat16), ("feat", "rep")).astype(jnp.float32)
    mesh_state = (mesh_base.astype(jnp.float32) + encoded).astype(jnp.bfloat16)
    halo_list = halo_rows[0]
    peers, per_peer = halo_list.shape
    halo_block = trade_rows(jnp.take(mesh_state, halo_list, axis=0))
    node_table = jnp.concatenate(
        [mesh_state, halo_block.reshape(peers * per_peer, model_width)], axis=0
    )
    sender_rows = jnp.take(node_table, edge_send, axis=0)
    receiver_rows = jnp.take(mesh_state, edge_recv, axis=0)
    edge_pre = (
        matmul(edge_state, in_full[:model_width])
        + matmul(sender_rows, in_full[model_width : 2 * model_width])
        + matmul(receiver_rows, in_full[2 * model_width :])
    )
    edge_hidden = jax.nn.silu(edge_pre).astype(jnp.bfloat16)
    edge_new = (edge_state.astype(jnp.float32) + matmul(edge_hidden, out_full)).astype(jnp.bfloat16)
    edge_sums = (
        jnp.zeros((node_count, model_width), jnp.float32)
        .at[edge_recv]
        .add(edge_new.astype(jnp.float32))
    )
    aggregate = lax.psum(edge_sums.astype(jnp.bfloat16), ("feat", "rep"))
    node_dinput = node_backward(mesh_state, aggregate, node_grad, node_in, node_out, model_width)
    edge_cot = (
        edge_grad.astype(jnp.float32) + jnp.take(node_dinput[:, model_width:], edge_recv, axis=0)
    ).astype(jnp.bfloat16)
    edge_dpre = (against(edge_cot, out_full) * silu_slope(edge_pre)).astype(jnp.bfloat16)
    edge_dnodes = against(edge_dpre, in_full[model_width:])
    table_grad = (
        jnp.zeros((node_table.shape[0], model_width), jnp.float32)
        .at[edge_send]
        .add(edge_dnodes[:, :model_width])
    )
    local_grad = table_grad[:node_count].at[edge_recv].add(edge_dnodes[:, model_width:])
    halo_grad = table_grad[node_count:].reshape(peers, per_peer, model_width)
    returned = trade_grads(halo_grad)
    local_grad = local_grad.at[halo_list.reshape(-1)].add(returned.reshape(-1, model_width))
    mesh_cot = (
        lax.psum(local_grad.astype(jnp.bfloat16), ("feat", "rep")).astype(jnp.float32)
        + node_grad.astype(jnp.float32)
        + node_dinput[:, :model_width]
    )
    owed_rows = jnp.take(mesh_cot, recv_nodes, axis=0, mode="fill", fill_value=0.0)
    returned_rows = trade_grads(owed_rows)
    grid_cot = (
        jnp.zeros((grid_count, model_width), jnp.float32)
        .at[send_rows.reshape(-1)]
        .add(returned_rows.reshape(-1, model_width), mode="drop")
    )
    grid_dpre = (grid_cot * silu_slope(grid_pre)).astype(jnp.bfloat16)
    return against(grid_dpre, enc_full)


def solution(mesh):
    return jax.shard_map(
        per_device,
        mesh=mesh,
        in_specs=(
            P(("ens", "dom", "feat", "rep"), None),
            P("dom", None),
            P(("dom", "feat", "rep"), None),
            P(("feat", "rep"), None),
            P(("feat", "rep"), None),
            P(("feat", "rep"), None),
            P(("feat", "rep"), None),
            P(("feat", "rep"), None),
            P(("ens", "dom"), None),
            P(("ens", "dom", "feat", "rep"), None),
            P("dom", None, None),
            P(("dom", "feat", "rep")),
            P(("dom", "feat", "rep")),
            P(("dom", "feat", "rep"), None, None),
            P(("dom", "feat", "rep"), None, None),
        ),
        out_specs=P(("ens", "dom", "feat", "rep"), None),
        check_vma=False,
    )
```

profile of v0, /device:TPU:0, one launch (start us, length us, event | category | flops | bytes accessed | tf_op | source)
XLA Modules:
  0.0 291.5 jit_solution(1933452939408861185)
XLA Ops:
  6.5 0.7 fusion.46
  7.3 0.7 compare_and_fusion.3
  8.0 8.8 %all_gather.16 = bf16[512,512]{1,0:T(8,128)(2,1)S(1)} all-gather(bf16[128,512]{1,0:T(8,128)(2,1)} %param.18), channel_id=1, replica_groups=mesh['ens'=2,'dom'=4,'feat'=2,'rep'=2] {'feat','rep'}, dimensions={0}, use_global_device_ids=true | all-gather | bytes 655360 | tf_op jit(solution)/shard_map/all_gather | solution.py:59
  16.8 1.1 multiply_convert_fusion.4
  17.9 2.0 gather_fusion
  19.9 0.9 broadcast_select_fusion.2
  20.8 4.9 %all-to-all-start = ((bf16[4,128,512]{2,1,0:T(8,128)(2,1)}), bf16[4,128,512]{2,1,0:T(8,128)(2,1)S(1)}, u32[]{:S(2)}, u32[]{:S(2)}) async-start(bf16[4,128,512]{2,1,0:T(8,128)(2,1)} %broadcast_select_fusion.2), calls=%async_computation | async-start | bytes 1048576 | tf_op jit(solution)/shard_map/all_to_all | solution.py:23
  25.7 15.0 %all-to-all-done = bf16[4,128,512]{2,1,0:T(8,128)(2,1)S(1)} async-done(((bf16[4,128,512]{2,1,0:T(8,128)(2,1)}), bf16[4,128,512]{2,1,0:T(8,128)(2,1)S(1)}, u32[]{:S(2)}, u32[]{:S(2)}) %all-to-all-start) | async-done | bytes 524320 | tf_op jit(solution)/shard_map/all_to_all | solution.py:23
  40.7 3.9 %scatter_custom_fusion = f32[512,512]{1,0:T(8,128)S(1)} fusion(s32[512]{0:T(512)S(1)} %bitcast.63, bf16[512,512]{1,0:T(8,128)(2,1)S(1)} %bitcast.55, f32[]{:T(128)} %constant.64.clone.1), kind=kCustom, calls=%fused_computation.32 | custom fusion | flops 524288 | bytes 1572868 | tf_op jit(solution)/shard_map/scatter-add | solution.py:74
  44.6 0.9 convert_element_type.65
  45.6 0.7 all-gather.5.cloned.1.call-update
  47.1 8.9 %all_gather.19 = bf16[512,512]{1,0:T(8,128)(2,1)} all-gather(bf16[128,512]{1,0:T(8,128)(2,1)S(1)} %copy-done.11), channel_id=1, replica_groups=mesh['ens'=2,'dom'=4,'feat'=2,'rep'=2] {'feat','rep'}, dimensions={0}, use_global_device_ids=true | all-gather | bytes 655360 | tf_op jit(solution)/shard_map/all_gather | solution.py:61
  56.0 21.6 %all-reduce.4.cloned.1.call-done = bf16[512,512]{1,0:T(8,128)(2,1)} async-done(((bf16[512,512]{1,0:T(8,128)(2,1)}), bf16[512,512]{1,0:T(8,128)(2,1)}) %all-reduce.4.cloned.1.call-update) | async-done | bytes 524304 | tf_op jit(solution)/shard_map/psum | solution.py:76
  77.6 1.2 add_convert_fusion.4
  78.8 2.0 gather_fusion.1
  80.8 1.0 broadcast_select_fusion.1
  81.7 4.6 %all-to-all-start.1 = ((bf16[4,128,512]{2,1,0:T(8,128)(2,1)}), bf16[4,128,512]{2,1,0:T(8,128)(2,1)S(1)}, u32[]{:S(2)}, u32[]{:S(2)}) async-start(bf16[4,128,512]{2,1,0:T(8,128)(2,1)} %broadcast_select_fusion.1), calls=%async_computation.1 | async-start | bytes 1048576 | tf_op jit(solution)/shard_map/all_to_all | solution.py:23
  86.3 10.6 %all_gather.15 = bf16[512,512]{1,0:T(8,128)(2,1)} all-gather(bf16[128,512]{1,0:T(8,128)(2,1)S(1)} %copy-done.12), channel_id=1, replica_groups=mesh['ens'=2,'dom'=4,'feat'=2,'rep'=2] {'feat','rep'}, dimensions={0}, use_global_device_ids=true | all-gather | bytes 655360 | tf_op jit(solution)/shard_map/all_gather | solution.py:63
  97.0 4.0 %gather_fusion.3 = bf16[1024,512]{1,0:T(8,128)(2,1)S(1)} fusion(bf16[512,512]{1,0:T(8,128)(2,1)S(1)} %add_convert_fusion.4, s32[1024]{0:T(1024)S(1)} %get-tuple-element.9), kind=kCustom, calls=%fused_computation.3 | custom fusion | bytes 2101248 | tf_op jit(solution)/shard_map/jit(_take)/gather | solution.py:85
  101.1 5.1 %gather_fusion.2 = bf16[1024,512]{1,0:T(8,128)(2,1)} fusion(bf16[1024,512]{1,0:T(8,128)(2,1)S(1)} %pad_maximum_fusion, s32[1024]{0:T(1024)S(1)} %get-tuple-element.8), kind=kCustom, calls=%fused_computation.2 | custom fusion | bytes 2101248 | tf_op jit(solution)/shard_map/jit(_take)/gather | solution.py:84
  106.2 2.2 fusion.34
  108.4 0.8 fusion.24
  109.2 0.8 add_add_fusion
  110.6 0.8 add_convert_fusion.1
  111.9 7.0 %scatter_custom_fusion.1 = f32[512,512]{1,0:T(8,128)S(1)} fusion(s32[1024]{0:T(1024)S(1)} %get-tuple-element.10, bf16[1024,512]{1,0:T(8,128)(2,1)S(1)} %add_convert_fusion.1, f32[]{:T(128)} %constant.64.clone.1), kind=kCustom, calls=%fused_computation.18 | custom fusion | flops 1048576 | bytes 2097156 | tf_op jit(solution)/shard_map/scatter-add | solution.py:96
  118.9 0.9 convert_element_type.72
  120.0 1.5 fusion.36
  121.5 33.9 %all-reduce.6.cloned.1.call-done = bf16[512,512]{1,0:T(8,128)(2,1)} async-done(((bf16[512,512]{1,0:T(8,128)(2,1)}), bf16[512,512]{1,0:T(8,128)(2,1)}) %all-reduce.6.cloned.1.call-update) | async-done | bytes 524304 | tf_op jit(solution)/shard_map/psum | solution.py:98
  155.4 1.6 convolution_add_fusion
  157.0 2.8 fusion.8
  159.8 1.4 copy-done.1
  161.3 3.5 %gather_fusion.4 = f32[1024,512]{1,0:T(8,128)S(1)} fusion(f32[512,512]{1,0:T(8,128)S(1)} %slice.65, s32[1024]{0:T(1024)S(1)} %get-tuple-element.9), kind=kCustom, calls=%fused_computation.4 | custom fusion | bytes 4198400 | tf_op jit(solution)/shard_map/jit(_take)/gather | solution.py:101
  164.8 6.5 %fusion.6 = f32[1024,1024]{1,0:T(8,128)} fusion(f32[1024,512]{1,0:T(8,128)} %copy-done.2, bf16[512,512]{1,0:T(8,128)(2,1)} %all_gather.19, f32[1024,512]{1,0:T(8,128)S(1)} %gather_fusion.4, bf16[1024,512]{1,0:T(8,128)(2,1)} %param.24, bf16[1536,512]{1,0:T(8,128)(2,1)} %all-gather.5.cloned.1.call-done, pred[1024]{0:T(1024)(128)(4,1)S(1)} %compare_and_fusion.1), kind=kOutput, calls=%fused_computation.24 | convolution fusion | flops 1617428480 | bytes 11011072 | tf_op jit(solution)/shard_map/dot_general | solution.py:17
  171.3 8.1 %scatter_custom_fusion.2 = f32[1024,512]{1,0:T(8,128)S(1)} fusion(s32[1024]{0:T(1024)S(1)} %get-tuple-element.7, f32[1024,1024]{1,0:T(8,128)} %fusion.6, f32[]{:T(128)} %constant.64.clone.1), kind=kCustom, calls=%fused_computation.14 | custom fusion | flops 524288 | bytes 4194816 | tf_op jit(solution)/shard_map/scatter-add | solution.py:108
  179.4 1.1 fusion.57
  180.6 4.6 %all-to-all-start.2 = ((f32[4,128,512]{2,1,0:T(8,128)}), f32[4,128,512]{2,1,0:T(8,128)S(1)}, u32[]{:S(2)}, u32[]{:S(2)}) async-start(f32[4,128,512]{2,1,0:T(8,128)} %bitcast.52), calls=%async_computation.2 | async-start | bytes 2097152 | tf_op jit(solution)/shard_map/all_to_all | solution.py:27
  185.2 7.8 %scatter_custom_fusion.3 = f32[512,512]{1,0:T(8,128)S(1)} fusion(f32[512,512]{1,0:T(8,128)S(1)} %get-tuple-element.6, s32[1024]{0:T(1024)S(1)} %get-tuple-element.10, f32[1024,1024]{1,0:T(8,128)} %fusion.6), kind=kCustom, calls=%fused_computation.12 | custom fusion | flops 524288 | bytes 3145728 | tf_op jit(solution)/shard_map/scatter-add | solution.py:110
  193.0 17.0 %all-to-all-done.2 = f32[4,128,512]{2,1,0:T(8,128)S(1)} async-done(((f32[4,128,512]{2,1,0:T(8,128)}), f32[4,128,512]{2,1,0:T(8,128)S(1)}, u32[]{:S(2)}, u32[]{:S(2)}) %all-to-all-start.2) | async-done | bytes 1048608 | tf_op jit(solution)/shard_map/all_to_all | solution.py:27
  210.0 4.0 %scatter_fusion = f32[512,512]{1,0:T(8,128)S(1)} fusion(f32[512,512]{1,0:T(8,128)S(1)} %scatter_custom_fusion.3, s32[512]{0:T(512)S(1)} %bitcast.61, f32[512,512]{1,0:T(8,128)S(1)} %bitcast.51), kind=kCustom, calls=%fused_computation.10 | custom fusion | flops 262144 | bytes 3147776 | tf_op jit(solution)/shard_map/scatter-add | solution.py:113
  214.0 0.9 convert_element_type.76
  214.9 31.4 %all-reduce.8.cloned.1.call-done = bf16[512,512]{1,0:T(8,128)(2,1)} async-done(((bf16[512,512]{1,0:T(8,128)(2,1)}), bf16[512,512]{1,0:T(8,128)(2,1)}) %all-reduce.8.cloned.1.call-update) | async-done | bytes 524304 | tf_op jit(solution)/shard_map/psum | solution.py:115
  246.3 1.6 slice_add_fusion
  247.9 1.6 gather_fusion.5
  249.5 1.1 broadcast_select_fusion
  250.7 4.6 %all-to-all-start.3 = ((f32[4,128,512]{2,1,0:T(8,128)}), f32[4,128,512]{2,1,0:T(8,128)S(1)}, u32[]{:S(2)}, u32[]{:S(2)}) async-start(f32[4,128,512]{2,1,0:T(8,128)} %broadcast_select_fusion), calls=%async_computation.3 | async-start | bytes 2097152 | tf_op jit(solution)/shard_map/all_to_all | solution.py:27
  255.3 24.8 %all-to-all-done.3 = f32[4,128,512]{2,1,0:T(8,128)S(1)} async-done(((f32[4,128,512]{2,1,0:T(8,128)}), f32[4,128,512]{2,1,0:T(8,128)S(1)}, u32[]{:S(2)}, u32[]{:S(2)}) %all-to-all-start.3) | async-done | bytes 1048608 | tf_op jit(solution)/shard_map/all_to_all | solution.py:27
  280.0 3.7 %scatter_custom_fusion.5 = f32[256,512]{1,0:T(8,128)S(1)} fusion(s32[512]{0:T(512)S(1)} %bitcast.62, f32[512,512]{1,0:T(8,128)S(1)} %bitcast.57, f32[]{:T(128)} %constant.64.clone.1), kind=kCustom, calls=%fused_computation.70 | custom fusion | flops 262144 | bytes 524292 | tf_op jit(solution)/shard_map/scatter-add | solution.py:124
  283.8 1.2 fusion.45
  (65 shorter events, 2.5 us)
Async XLA Ops:
  6.5 10.2 %copy-start = (bf16[256,512]{1,0:T(8,128)(2,1)S(1)}, bf16[256,512]{1,0:T(8,128)(2,1)}, u32[]{:S(2)}) copy-start(bf16[256,512]{1,0:T(8,128)(2,1)} %param.15) | copy-start | bytes 786436
  16.8 1.1 copy-start.7
  19.9 5.8 %copy-start.14 = (s32[1,4,128]{2,1,0:T(4,128)S(1)}, s32[1,4,128]{2,1,0:T(4,128)}, u32[]{:S(2)}) copy-start(s32[1,4,128]{2,1,0:T(4,128)} %param.29) | copy-start | bytes 6148
  20.8 19.9 %all-to-all-start = ((bf16[4,128,512]{2,1,0:T(8,128)(2,1)}), bf16[4,128,512]{2,1,0:T(8,128)(2,1)S(1)}, u32[]{:S(2)}, u32[]{:S(2)}) async-start(bf16[4,128,512]{2,1,0:T(8,128)(2,1)} %broadcast_select_fusion.2), calls=%async_computation | async-start | bytes 1048576 | tf_op jit(solution)/shard_map/all_to_all | solution.py:23
  25.7 51.9 %all-reduce.4.cloned.1.call-start = ((), (), s32[]{:S(2)}) async-start(), calls=%async_computation.4 | async-start | bytes 1048576 | tf_op jit(solution)/shard_map/psum | solution.py:76
  40.7 6.3 %copy-start.13 = (s32[1,4,128]{2,1,0:T(4,128)S(1)}, s32[1,4,128]{2,1,0:T(4,128)}, u32[]{:S(2)}) copy-start(s32[1,4,128]{2,1,0:T(4,128)} %param.25) | copy-start | bytes 6148
  40.7 6.4 %copy-start.16 = (s32[1024]{0:T(1024)S(1)}, s32[1024]{0:T(1024)}, u32[]{:S(2)}) copy-start(s32[1024]{0:T(1024)} %param.26) | copy-start | bytes 12292
  40.7 6.4 %copy-start.11 = (bf16[128,512]{1,0:T(8,128)(2,1)S(1)}, bf16[128,512]{1,0:T(8,128)(2,1)}, u32[]{:S(2)}) copy-start(bf16[128,512]{1,0:T(8,128)(2,1)} %param.20) | copy-start | bytes 393220
  44.6 33.0 %copy-start.6 = (bf16[512,512]{1,0:T(8,128)(2,1)S(1)}, bf16[512,512]{1,0:T(8,128)(2,1)}, u32[]{:S(2)}) copy-start(bf16[512,512]{1,0:T(8,128)(2,1)} %param.16) | copy-start | bytes 1572868
  45.6 60.6 %all-gather.5.cloned.1.call-start = ((), (), s32[]{:S(2)}) async-start(), calls=%async_computation.6 | async-start | bytes 1966080 | tf_op jit(solution)/shard_map/all_gather | solution.py:60
  46.3 73.7 %all-gather.3.cloned.1.call-start = ((), (), s32[]{:S(2)}) async-start(), calls=%async_computation.5 | async-start | bytes 1310720 | tf_op jit(solution)/shard_map/all_gather | solution.py:62
  80.8 5.6 %copy-start.12 = (bf16[128,512]{1,0:T(8,128)(2,1)S(1)}, bf16[128,512]{1,0:T(8,128)(2,1)}, u32[]{:S(2)}) copy-start(bf16[128,512]{1,0:T(8,128)(2,1)} %param.22) | copy-start | bytes 393220
  80.8 16.2 %copy-start.17 = (s32[1024]{0:T(1024)S(1)}, s32[1024]{0:T(1024)}, u32[]{:S(2)}) copy-start(s32[1024]{0:T(1024)} %param.27) | copy-start | bytes 12292
  81.7 19.3 %all-to-all-start.1 = ((bf16[4,128,512]{2,1,0:T(8,128)(2,1)}), bf16[4,128,512]{2,1,0:T(8,128)(2,1)S(1)}, u32[]{:S(2)}, u32[]{:S(2)}) async-start(bf16[4,128,512]{2,1,0:T(8,128)(2,1)} %broadcast_select_fusion.1), calls=%async_computation.1 | async-start | bytes 1048576 | tf_op jit(solution)/shard_map/all_to_all | solution.py:23
  86.3 69.1 %all-reduce.6.cloned.1.call-start = ((), (), s32[]{:S(2)}) async-start(), calls=%async_computation.7 | async-start | bytes 1048576 | tf_op jit(solution)/shard_map/psum | solution.py:98
  106.2 2.2 copy-start.4
  106.2 2.2 copy-start.5
  109.2 1.3 copy-start.3
  109.2 1.4 copy-start.9
  110.6 1.4 copy-start.2
  159.8 1.4 copy-start.1
  180.6 29.4 %all-to-all-start.2 = ((f32[4,128,512]{2,1,0:T(8,128)}), f32[4,128,512]{2,1,0:T(8,128)S(1)}, u32[]{:S(2)}, u32[]{:S(2)}) async-start(f32[4,128,512]{2,1,0:T(8,128)} %bitcast.52), calls=%async_computation.2 | async-start | bytes 2097152 | tf_op jit(solution)/shard_map/all_to_all | solution.py:27
  185.2 61.1 %all-reduce.8.cloned.1.call-start = ((), (), s32[]{:S(2)}) async-start(), calls=%async_computation.8 | async-start | bytes 1048576 | tf_op jit(solution)/shard_map/psum | solution.py:115
  213.9 32.4 %copy-start.10 = (bf16[512,512]{1,0:T(8,128)(2,1)S(1)}, bf16[512,512]{1,0:T(8,128)(2,1)}, u32[]{:S(2)}) copy-start(bf16[512,512]{1,0:T(8,128)(2,1)} %param.23) | copy-start | bytes 1572868
  249.5 5.8 %copy-start.15 = (s32[1,4,128]{2,1,0:T(4,128)S(1)}, s32[1,4,128]{2,1,0:T(4,128)}, u32[]{:S(2)}) copy-start(s32[1,4,128]{2,1,0:T(4,128)} %param.28) | copy-start | bytes 6148
  249.5 34.3 %copy-start.8 = (bf16[512,512]{1,0:T(8,128)(2,1)S(1)}, bf16[512,512]{1,0:T(8,128)(2,1)}, u32[]{:S(2)}) copy-start(bf16[512,512]{1,0:T(8,128)(2,1)} %copy-done.7) | copy-start | bytes 1572868
  249.5 34.3 %copy-start.18 = (f32[256,512]{1,0:T(8,128)S(1)}, f32[256,512]{1,0:T(8,128)}, u32[]{:S(2)}) copy-start(f32[256,512]{1,0:T(8,128)} %get-tuple-element.12) | copy-start | bytes 1572868
  250.7 29.4 %all-to-all-start.3 = ((f32[4,128,512]{2,1,0:T(8,128)}), f32[4,128,512]{2,1,0:T(8,128)S(1)}, u32[]{:S(2)}, u32[]{:S(2)}) async-start(f32[4,128,512]{2,1,0:T(8,128)} %broadcast_select_fusion), calls=%async_computation.3 | async-start | bytes 2097152 | tf_op jit(solution)/shard_map/all_to_all | solution.py:27
Sparse Core Ops, SparseCore 0:
  45.7 31.8 all-reduce.3
  79.2 22.4 all-gather.4
  103.2 16.7 all-gather.2
  122.2 33.1 all-reduce.5
  215.0 31.2 all-reduce.7
where the time goes:
time: 292 us; the launch traced here: 291 us
  waiting for transfers between devices  145 us (50%)
  other arithmetic  44.4 us (15%)
  blocking collectives  28.3 us (10%)
  local copies, waits for them, and re-layouts  22 us (8%)
  matrix products  19.2 us (7%)
  starting transfers between devices  18.8 us (6%)
  between operations  13.5 us (5%)
    all_to_all x2, waiting for transfers between devices, trade_grads(): lax.all_to_all(block_rows, 'dom', split_axis=0, concat_axis=0, tiled=True)  41.8 us
    psum x1, waiting for transfers between devices, per_device(): aggregate = lax.psum(edge_sums.astype(jnp.bfloat16), ('feat', 'rep'))  33.9 us
    psum x1, waiting for transfers between devices, per_device(): lax.psum(local_grad.astype(jnp.bfloat16), ('feat', 'rep'))  31.4 us
    psum x1, waiting for transfers between devices, per_device(): lax.psum(encoded.astype(jnp.bfloat16), ('feat', 'rep')).astype(jnp.float32)  21.6 us
    all_to_all x2, waiting for transfers between devices, trade_rows(): lax.all_to_all(block_rows, 'dom', split_axis=0, concat_axis=0, tiled=True)  15 us
    all_gather x1, blocking collectives, per_device(): lax.all_gather(node_out_weight, ('feat', 'rep'), axis=0, tiled=True)  10.6 us
    dot_general x3, matrix products, against(): lax.dot_general(first_op, second_op, (((1,), (1,)), ((), ())), preferred_...  10.4 us
    all_to_all x2, starting transfers between devices, trade_rows(): lax.all_to_all(block_rows, 'dom', split_axis=0, concat_axis=0, tiled=True)  9.47 us
  transfers between devices with their start and end apart: 9, of which 7 were waited for; matrix products, arithmetic and copies ran while one was open for 12% of the time, Pallas kernels for 0%

commit v1 on v0

v1 whole, which is shorter than its diff:
```python
import jax
import jax.numpy as jnp
from jax import lax
from jax.experimental import pallas as pl
from jax.experimental.pallas import tpu as pltpu
from jax.sharding import PartitionSpec as P

BF = jnp.bfloat16
F32 = jnp.float32
SMEM = pl.BlockSpec(memory_space=pltpu.SMEM)
VMEM = pl.BlockSpec(memory_space=pltpu.VMEM)


def dot(a, b):
    return jnp.dot(a, b, preferred_element_type=F32)


def dot_t(a, b):
    return lax.dot_general(a, b, (((1,), (1,)), ((), ())), preferred_element_type=F32)


def silu_slope(values):
    logistic = jax.nn.sigmoid(values)
    return logistic * (1.0 + values * (1.0 - logistic))


def to_column(row):
    return jnp.transpose(jnp.broadcast_to(row, (8, row.shape[1])))[:, :1]


def hot_rows(row, depth):
    length = row.shape[1]
    return (to_column(row) == lax.broadcasted_iota(jnp.int32, (length, depth), 1)).astype(BF)


def hot_columns(row, depth):
    length = row.shape[1]
    return (row == lax.broadcasted_iota(jnp.int32, (depth, length), 0)).astype(BF)


def column_pick(me, depth, cols):
    at = lax.broadcasted_iota(jnp.int32, (depth, cols), 0) - me * cols
    return (at == lax.broadcasted_iota(jnp.int32, (depth, cols), 1)).astype(BF)


def rows_at(index, count):
    return pl.ds(pl.multiple_of(index * count, count), count)


def lanes(parts):
    return parts[0] if len(parts) == 1 else jnp.concatenate(parts, axis=1)


def stack(parts):
    return parts[0] if len(parts) == 1 else jnp.concatenate(parts, axis=0)


def call(body, name, me, ins, outs, scratch=(), flops=0):
    size = lambda s: s.size * s.dtype.itemsize
    moved = sum(size(x) for x in ins) + sum(size(x) for x in outs)
    return pl.pallas_call(
        body,
        out_shape=list(outs),
        in_specs=[SMEM] + [VMEM] * len(ins),
        out_specs=[VMEM] * len(outs),
        scratch_shapes=list(scratch),
        compiler_params=pltpu.CompilerParams(vmem_limit_bytes=48 * 2**20),
        cost_estimate=pl.CostEstimate(flops=flops, bytes_accessed=moved, transcendentals=0),
        name=name,
    )(me, *ins)


def shape(dims, dtype=BF):
    return jax.ShapeDtypeStruct(tuple(dims), dtype)


def make_per_device(mesh):
    n_dom, n_feat, n_rep = mesh.shape["dom"], mesh.shape["feat"], mesh.shape["rep"]
    M = n_feat * n_rep

    def member_swap(x, k):
        return lax.ppermute(x, ("feat", "rep"), [(i, i ^ k) for i in range(M)])

    def dom_swap(x, k):
        return lax.ppermute(x, "dom", [(i, i ^ k) for i in range(n_dom)])

    def member_gather(x):
        return [x] + [member_swap(x, k) for k in range(1, M)]

    def member_gather_chips(x):
        parts = [None] * M
        for kf in range(n_feat):
            parts[kf * n_rep] = member_swap(x, kf * n_rep) if kf else x
        for kf in range(n_feat):
            for kr in range(1, n_rep):
                parts[kf * n_rep + kr] = member_swap(parts[kf * n_rep], kr)
        return parts

    def member_trade(parts):
        return [parts[0]] + [member_swap(parts[k], k) for k in range(1, M)]

    def dom_trade(parts):
        return [parts[0]] + [dom_swap(parts[k], k) for k in range(1, n_dom)]

    def dom_order(table, dom):
        bit = 1
        while bit < n_dom:
            pairs = table.reshape((n_dom // (2 * bit), 2, bit) + table.shape[1:])
            swapped = pairs[:, ::-1].reshape(table.shape)
            table = jnp.where((dom & bit) != 0, swapped, table)
            bit *= 2
        return table

    def per_device(
        grid_state,
        mesh_base,
        edge_state,
        enc_weight,
        edge_in_weight,
        edge_out_weight,
        node_in_weight,
        node_out_weight,
        node_grad,
        edge_grad,
        halo_rows,
        edge_send,
        edge_recv,
        grid_send,
        grid_recv,
    ):
        D = mesh_base.shape[1]
        N = mesh_base.shape[0]
        E = edge_state.shape[0]
        G = grid_state.shape[0]
        H = halo_rows.shape[2]
        S = grid_send.shape[2]
        NH = n_dom * H
        NS = n_dom * S
        C = D // M
        R = N // M
        T = 256
        rows_enc, rows_in, rows_out, rows_node = (
            enc_weight.shape[0],
            edge_in_weight.shape[0],
            edge_out_weight.shape[0],
            node_in_weight.shape[0],
        )
        me = lax.axis_index(("feat", "rep")).astype(jnp.int32)
        dom = lax.axis_index("dom").astype(jnp.int32)
        me1 = me.reshape(1)

        slots = jnp.stack(
            [dom_order(grid_send[0], dom).reshape(-1), dom_order(grid_recv[0], dom).reshape(-1)]
        )
        halo_row = dom_order(halo_rows[0], dom).reshape(1, NH)
        recv_row = edge_recv.reshape(1, E)
        away = edge_send - N
        send_row = jnp.where(away < 0, edge_send, N + ((away // H) ^ dom) * H + away % H).reshape(1, E)

        state_parts = member_gather_chips(grid_state)
        enc_parts = member_gather_chips(enc_weight)
        slot_parts = member_gather(slots)
        in_parts = member_gather_chips(edge_in_weight)
        rest = jnp.concatenate([edge_out_weight, node_in_weight, node_out_weight], axis=0)
        rest_parts = member_gather_chips(rest)

        def grid_kernel(me_ref, *refs):
            states, encs, tables = refs[:M], refs[M : 2 * M], refs[2 * M : 3 * M]
            enc_out, slope_out = refs[3 * M], refs[3 * M + 1]
            outs = refs[3 * M + 2 :]
            me = me_ref[0]
            for k in range(M):
                enc_out[rows_at(me ^ k, rows_enc), :] = encs[k][...]
            enc_cols = dot(enc_out[...], column_pick(me, D, C)).astype(BF)
            for k in range(M):
                pre = dot(states[k][...], enc_cols)
                logistic = jax.nn.sigmoid(pre)
                slope_out[k] = logistic * (1.0 + pre * (1.0 - logistic))
                message = (pre * logistic).astype(BF)
                rows = dot(hot_rows(tables[k][0:1, :], G), message).astype(BF)
                for j in range(n_dom):
                    outs[j][k * S : (k + 1) * S, :] = rows[j * S : (j + 1) * S]

        enc_full, grid_slope, *outgoing = call(
            grid_kernel,
            "grid_messages",
            me1,
            state_parts + enc_parts + slot_parts,
            [shape((D, D)), shape((M, G, C), F32)] + [shape((M * S, C))] * n_dom,
            flops=2 * M * G * D * C + 2 * M * NS * G * C,
        )
        incoming = dom_trade(outgoing)

        def encode_kernel(me_ref, base_ref, halo_ref, *refs):
            tables, arrived = refs[:M], refs[M : M + n_dom]
            state_out, outs = refs[M + n_dom], refs[M + n_dom + 1 :]
            total = dot(base_ref[...], column_pick(me_ref[0], D, C))
            for k in range(M):
                rows = stack([arrived[j][k * S : (k + 1) * S, :] for j in range(n_dom)])
                total += dot(hot_columns(tables[k][1:2, :], N), rows)
            state = total.astype(BF)
            state_out[...] = state
            rows = dot(hot_rows(halo_ref[...], N), state).astype(BF)
            for j in range(n_dom):
                outs[j][...] = rows[j * H : (j + 1) * H]

        state_cols, *halo_out = call(
            encode_kernel,
            "encode",
            me1,
            [mesh_base, halo_row] + slot_parts + incoming,
            [shape((N, C))] + [shape((H, C))] * n_dom,
            flops=2 * M * N * NS * C,
        )
        halo_in = dom_trade(halo_out)
        state_parts2 = member_gather(state_cols)
        halo_cols = jnp.concatenate(halo_in, axis=0)
        halo_parts = member_gather(halo_cols)

        def local_kernel(me_ref, es_ref, send_ref, recv_ref, *refs):
            cols, weights = refs[:M], refs[M : 2 * M]
            pre_out, state_out, w_out, parts = refs[2 * M :]
            me = me_ref[0]
            for k in range(M):
                parts[me ^ k] = cols[k][...]
                w_out[rows_at(me ^ k, rows_in), :] = weights[k][...]
            state_out[...] = lanes([parts[j] for j in range(M)])

            def step(i, _):
                at = rows_at(i, T)
                sent = dot(hot_rows(send_ref[:, at], N), state_out[...]).astype(BF)
                got = dot(hot_rows(recv_ref[:, at], N), state_out[...]).astype(BF)
                pre_out[at, :] = (
                    dot(es_ref[at, :], w_out[:D, :])
                    + dot(sent, w_out[D : 2 * D, :])
                    + dot(got, w_out[2 * D :, :])
                )
                return 0

            lax.fori_loop(0, E // T, step, 0)

        local_pre, mesh_state, in_full = call(
            local_kernel,
            "edge_local",
            me1,
            [edge_state, send_row, recv_row] + state_parts2 + in_parts,
            [shape((E, D), F32), shape((N, D)), shape((3 * D, D))],
            scratch=[pltpu.VMEM((M, N, C), BF)],
            flops=2 * E * D * (3 * D + 2 * N),
        )

        def node_ahead_kernel(me_ref, state_ref, grad_ref, *refs):
            weights = refs[:M]
            out_full, node_in_full, pre_out, cot_out, node_out_full = refs[M:]
            me = me_ref[0]
            for k in range(M):
                first, second = rows_out, rows_out + rows_node
                out_full[rows_at(me ^ k, rows_out), :] = weights[k][:first, :]
                node_in_full[rows_at(me ^ k, rows_node), :] = weights[k][first:second, :]
                node_out_full[rows_at(me ^ k, rows_out), :] = weights[k][second:, :]
            mine = rows_at(me, R)
            pre_out[...] = dot(state_ref[mine, :], node_in_full[:D, :])
            cot_out[...] = dot_t(grad_ref[mine, :], node_out_full[...])

        out_full, node_in_full, node_pre, node_cot = call(
            node_ahead_kernel,
            "node_ahead",
            me1,
            [mesh_state, node_grad] + rest_parts,
            [shape((D, D)), shape((2 * D, D)), shape((R, D), F32), shape((R, D), F32)],
            scratch=[pltpu.VMEM((D, D), BF)],
            flops=4 * R * D * D,
        )

        def edge_kernel(me_ref, local_ref, es_ref, send_ref, recv_ref, w_ref, out_ref, *refs):
            cols = refs[:M]
            pre_out, outs = refs[M], refs[M + 1 : 2 * M + 1]
            parts, halo, total = refs[2 * M + 1 :]
            me = me_ref[0]
            for k in range(M):
                parts[me ^ k] = cols[k][...]
            halo[...] = lanes([parts[j] for j in range(M)])
            total[...] = jnp.zeros_like(total)

            def step(i, _):
                at = rows_at(i, T)
                sent = dot(hot_rows(send_ref[:, at] - N, NH), halo[...]).astype(BF)
                pre = local_ref[at, :] + dot(sent, w_ref[D : 2 * D, :])
                pre_out[at, :] = pre
                hidden = (pre * jax.nn.sigmoid(pre)).astype(BF)
                new = (es_ref[at, :].astype(F32) + dot(hidden, out_ref[...])).astype(BF)
                total[...] += dot(hot_columns(recv_ref[:, at], N), new)
                return 0

            lax.fori_loop(0, E // T, step, 0)
            for k in range(M):
                outs[k][...] = total[rows_at(me ^ k, R), :].astype(BF)

        edge_pre, *sums = call(
            edge_kernel,
            "edge_update",
            me1,
            [local_pre, edge_state, send_row, recv_row, in_full, out_full] + halo_parts,
            [shape((E, D), F32)] + [shape((R, D))] * M,
            scratch=[pltpu.VMEM((M, NH, C), BF), pltpu.VMEM((NH, D), BF), pltpu.VMEM((N, D), F32)],
            flops=2 * E * D * (NH + D + D + N),
        )
        sums = member_trade(sums)

        def node_kernel(me_ref, pre_ref, cot_ref, w_ref, grad_ref, *refs):
            first_out, second_out = refs[M:]
            total = refs[0][...].astype(F32)
            for k in range(1, M):
                total += refs[k][...].astype(F32)
            pre = pre_ref[...] + dot(total.astype(BF), w_ref[D:, :])
            dpre = (cot_ref[...] * silu_slope(pre)).astype(BF)
            second_out[...] = dot_t(dpre, w_ref[D:, :]).astype(BF)
            mine = grad_ref[rows_at(me_ref[0], R), :].astype(F32)
            first_out[...] = mine + dot_t(dpre, w_ref[:D, :])

        node_first, node_second = call(
            node_kernel,
            "node_backward",
            me1,
            [node_pre, node_cot, node_in_full, node_grad] + sums,
            [shape((R, D), F32), shape((R, D))],
            flops=6 * R * D * D,
        )
        second_parts = member_gather(node_second)

        def edge_back_kernel(me_ref, grad_ref, pre_ref, send_ref, recv_ref, w_ref, out_ref, *refs):
            nodes = refs[:M]
            dpre_out, outs = refs[M], refs[M + 1 : 2 * M + 1]
            second, total, parts = refs[2 * M + 1 :]
            me = me_ref[0]
            for k in range(M):
                second[rows_at(me ^ k, R), :] = nodes[k][...]
            total[...] = jnp.zeros_like(total)

            def step(i, _):
                at = rows_at(i, T)
                got = dot(hot_rows(recv_ref[:, at], N), second[...])
                cot = (grad_ref[at, :].astype(F32) + got).astype(BF)
                dpre = (dot_t(cot, out_ref[...]) * silu_slope(pre_ref[at, :])).astype(BF)
                dpre_out[at, :] = dpre
                total[...] += dot(hot_columns(send_ref[:, at] - N, NH), dpre)
                return 0

            lax.fori_loop(0, E // T, step, 0)
            halo = dot_t(total[...].astype(BF), w_ref[D : 2 * D, :]).astype(BF)
            for j in range(M):
                parts[j] = halo[:, j * C : (j + 1) * C]
            for k in range(M):
                outs[k][...] = parts[me ^ k]

        edge_dpre, *halo_grads = call(
            edge_back_kernel,
            "edge_backward",
            me1,
            [edge_grad, edge_pre, send_row, recv_row, in_full, out_full] + second_parts,
            [shape((E, D))] + [shape((NH, C))] * M,
            scratch=[pltpu.VMEM((N, D), BF), pltpu.VMEM((NH, D), F32), pltpu.VMEM((M, NH, C), BF)],
            flops=2 * E * D * (N + D + NH) + 2 * NH * D * D,
        )
        halo_grads = member_trade(halo_grads)

        def local_back_kernel(me_ref, dpre_ref, send_ref, recv_ref, w_ref, first_ref, *refs):
            outs, (sent, got, parts) = refs[:M], refs[M:]
            me = me_ref[0]
            sent[...] = jnp.zeros_like(sent)
            got[...] = jnp.zeros_like(got)

            def step(i, _):
                at = rows_at(i, T)
                sent[...] += dot(hot_columns(send_ref[:, at], N), dpre_ref[at, :])
                got[...] += dot(hot_columns(recv_ref[:, at], N), dpre_ref[at, :])
                return 0

            lax.fori_loop(0, E // T, step, 0)
            sent[...] = dot_t(sent[...].astype(BF), w_ref[D : 2 * D, :]) + dot_t(
                got[...].astype(BF), w_ref[2 * D :, :]
            )
            sent[rows_at(me, R), :] += first_ref[...]
            for j in range(M):
                parts[j] = sent[:, j * C : (j + 1) * C].astype(BF)
            for k in range(M):
                outs[k][...] = parts[me ^ k]

        local_grads = call(
            local_back_kernel,
            "local_backward",
            me1,
            [edge_dpre, send_row, recv_row, in_full, node_first],
            [shape((N, C))] * M,
            scratch=[pltpu.VMEM((N, D), F32), pltpu.VMEM((N, D), F32), pltpu.VMEM((M, N, C), BF)],
            flops=4 * E * D * N + 4 * N * D * D,
        )
        local_grads = member_trade(local_grads)

        def halo_sum_kernel(me_ref, *refs):
            total = refs[0][...].astype(F32)
            for k in range(1, M):
                total += refs[k][...].astype(F32)
            for j in range(n_dom):
                refs[M + j][...] = total[j * H : (j + 1) * H].astype(BF)

        halo_back = call(halo_sum_kernel, "halo_sums", me1, halo_grads, [shape((H, C))] * n_dom)
        halo_back = dom_trade(halo_back)

        def owed_kernel(me_ref, halo_ref, *refs):
            tables, local, back = refs[:M], refs[M : 2 * M], refs[2 * M : 2 * M + n_dom]
            outs = refs[2 * M + n_dom :]
            total = local[0][...].astype(F32)
            for k in range(1, M):
                total += local[k][...].astype(F32)
            rows = stack([back[j][...] for j in range(n_dom)])
            cot = (total + dot(hot_columns(halo_ref[...], N), rows)).astype(BF)
            for k in range(M):
                owed = dot(hot_rows(tables[k][1:2, :], N), cot).astype(BF)
                for j in range(n_dom):
                    outs[j][k * S : (k + 1) * S, :] = owed[j * S : (j + 1) * S]

        owed = call(
            owed_kernel,
            "owed_rows",
            me1,
            [halo_row] + slot_parts + local_grads + halo_back,
            [shape((M * S, C))] * n_dom,
            flops=2 * M * NS * N * C,
        )
        owed = dom_trade(owed)

        def grid_back_kernel(me_ref, slope_ref, *refs):
            tables, back, outs = refs[:M], refs[M : M + n_dom], refs[M + n_dom :]
            for k in range(M):
                rows = stack([back[j][k * S : (k + 1) * S, :] for j in range(n_dom)])
                cot = dot(hot_columns(tables[k][0:1, :], G), rows)
                outs[k][...] = (cot * slope_ref[k]).astype(BF)

        grid_dpre = call(
            grid_back_kernel,
            "grid_backward",
            me1,
            [grid_slope] + slot_parts + owed,
            [shape((G, C))] * M,
            flops=2 * M * G * NS * C,
        )
        grid_dpre = member_trade(grid_dpre)

        def adjoint_kernel(me_ref, enc_ref, *refs):
            cols, out, parts = refs[:M], refs[M], refs[M + 1]
            for k in range(M):
                parts[me_ref[0] ^ k] = cols[k][...]
            out[...] = dot_t(lanes([parts[j] for j in range(M)]), enc_ref[...])

        return call(
            adjoint_kernel,
            "adjoint",
            me1,
            [enc_full] + grid_dpre,
            [shape((G, D), F32)],
            scratch=[pltpu.VMEM((M, G, C), BF)],
            flops=2 * G * D * D,
        )[0]

    return per_device


def solution(mesh):
    return jax.shard_map(
        make_per_device(mesh),
        mesh=mesh,
        in_specs=(
            P(("ens", "dom", "feat", "rep"), None),
            P("dom", None),
            P(("dom", "feat", "rep"), None),
            P(("feat", "rep"), None),
            P(("feat", "rep"), None),
            P(("feat", "rep"), None),
            P(("feat", "rep"), None),
            P(("feat", "rep"), None),
            P(("ens", "dom"), None),
            P(("ens", "dom", "feat", "rep"), None),
            P("dom", None, None),
            P(("dom", "feat", "rep")),
            P(("dom", "feat", "rep")),
            P(("dom", "feat", "rep"), None, None),
            P(("dom", "feat", "rep"), None, None),
        ),
        out_specs=P(("ens", "dom", "feat", "rep"), None),
        check_vma=False,
    )
```

time: 292 us -> 138 us (0.47)
  waiting for transfers between devices: 145 us -> 53.4 us
  other arithmetic: 44.4 us -> 3.48 us
  Pallas kernels: 0 us -> 29.5 us
  blocking collectives: 28.3 us -> 0 us
  starting transfers between devices: 18.8 us -> 44 us
  matrix products: 19.2 us -> 0 us
  local copies, waits for them, and re-layouts: 22 us -> 6.9 us
  between operations: 13.5 us -> 0.29 us
    psum x3 -> x0, waiting for transfers between devices: 87 us -> none  [the longest x1 33.9 us: per_device(): aggregate = lax.psum(edge_sums.astype(jnp.bfloat16), ('feat', 'rep'))]
    all_to_all x4 -> x0, waiting for transfers between devices: 56.7 us -> none  [the longest x2 41.8 us: trade_grads(): lax.all_to_all(block_rows, 'dom', split_axis=0, concat_axis=0, tiled=True)]
    ppermute x0 -> x48, waiting for transfers between devices: none -> 53.4 us  [the longest x36 28.2 us: member_swap(): return lax.ppermute(x, ('feat', 'rep'), [(i, i ^ k) for i in range(M)])]
    ppermute x0 -> x48, starting transfers between devices: none -> 44 us  [the longest x36 22.8 us: member_swap(): return lax.ppermute(x, ('feat', 'rep'), [(i, i ^ k) for i in range(M)])]
    scatter-add x6 -> x0, other arithmetic: 34.5 us -> none  [the longest x1 8.11 us: per_device(): table_grad = jnp.zeros((node_table.shape[0], model_width), jnp.float32).a...]
    pallas_call x0 -> x12, Pallas kernels: none -> 29.5 us  [call(): pl.pallas_call(body, out_shape=list(outs), in_specs=[SMEM] + [VMEM] * len...]
    all_gather x3 -> x0, blocking collectives: 28.3 us -> none  [the longest x1 10.6 us: per_device(): lax.all_gather(node_out_weight, ('feat', 'rep'), axis=0, tiled=True)]
    dot_general x10 -> x0, matrix products: 19.2 us -> none  [the longest x3 10.4 us: against(): lax.dot_general(first_op, second_op, (((1,), (1,)), ((), ())), preferred_...]
  transfers between devices with their start and end apart: 9 -> 48, of which waited for: 7 -> 19; matrix products, arithmetic and copies ran while one was open for 12% -> 4% of each run, Pallas kernels for 0% -> 9%
where the time goes in v1:
time: 138 us
  waiting for transfers between devices  53.4 us (39%)
  starting transfers between devices  44 us (32%)
  Pallas kernels  29.5 us (21%)
  local copies, waits for them, and re-layouts  6.9 us (5%)
  other arithmetic  3.48 us (3%)
    pallas_call x12, Pallas kernels, call(): pl.pallas_call(body, out_shape=list(outs), in_specs=[SMEM] + [VMEM] * len...  29.5 us
    ppermute x36, waiting for transfers between devices, member_swap(): return lax.ppermute(x, ('feat', 'rep'), [(i, i ^ k) for i in range(M)])  28.2 us
    ppermute x12, waiting for transfers between devices, dom_swap(): return lax.ppermute(x, 'dom', [(i, i ^ k) for i in range(n_dom)])  25.2 us
    ppermute x36, starting transfers between devices, member_swap(): return lax.ppermute(x, ('feat', 'rep'), [(i, i ^ k) for i in range(M)])  22.8 us
    ppermute x12, starting transfers between devices, dom_swap(): return lax.ppermute(x, 'dom', [(i, i ^ k) for i in range(n_dom)])  21.2 us
    unnamed x23, local copies, waits for them, and re-layouts  3.78 us
    select_n x5, other arithmetic, dom_order(): table = jnp.where(dom & bit != 0, swapped, table)  2.77 us
  transfers between devices with their start and end apart: 48, of which 19 were waited for; matrix products, arithmetic and copies ran while one was open for 4% of the time, Pallas kernels for 9%

profile of v1, /device:TPU:0, one launch (start us, length us, event | category | flops | bytes accessed | tf_op | source)
XLA Modules:
  0.0 137.7 jit_solution(12655015141470511867)
XLA Ops:
  3.6 2.5 %collective-permute-start.8 = (s32[2,512]{1,0:T(2,128)S(1)}, s32[2,512]{1,0:T(2,128)S(1)}, u32[]{:S(2)}, u32[]{:S(2)}) collective-permute-start(s32[2,512]{1,0:T(2,128)S(1)} %pad_add_fusion.refs_8_.refs_0_), channel_id=1, source_target_pairs={{0,3},{1,2},{2,1},{3,0},{4,7},{5,6},{6,5},{7,4},{8,11},{9,10},{10,... | collective-permute-start | bytes 12296 | tf_op jit(solution)/shard_map/ppermute | solution.py:82
  6.7 1.7 %collective-permute-start.4 = (bf16[128,512]{1,0:T(8,128)(2,1)}, bf16[128,512]{1,0:T(8,128)(2,1)S(1)}, u32[]{:S(2)}, u32[]{:S(2)}) collective-permute-start(bf16[128,512]{1,0:T(8,128)(2,1)} %refs_4_.2), channel_id=1, source_target_pairs={{0,2},{1,3},{2,0},{3,1},{4,6},{5,7},{6,4},{7,5},{8,10},{9,11},{10,... | collective-permute-start | bytes 393224 | tf_op jit(solution)/shard_map/ppermute | solution.py:82
  10.2 0.9 constant_dynamic-update-slice_fusion.2
  11.2 1.8 %collective-permute-start.16 = (bf16[384,512]{1,0:T(8,128)(2,1)}, bf16[384,512]{1,0:T(8,128)(2,1)S(1)}, u32[]{:S(2)}, u32[]{:S(2)}) collective-permute-start(bf16[384,512]{1,0:T(8,128)(2,1)} %refs_4_.3), channel_id=1, source_target_pairs={{0,2},{1,3},{2,0},{3,1},{4,6},{5,7},{6,4},{7,5},{8,10},{9,11},{10,... | collective-permute-start | bytes 1179656 | tf_op jit(solution)/shard_map/ppermute | solution.py:82
  13.3 1.0 constant_dynamic-update-slice_fusion.1
  14.8 4.1 %collective-permute-done.1.refs_2_ = bf16[256,512]{1,0:T(8,128)(2,1)S(1)} collective-permute-done((bf16[256,512]{1,0:T(8,128)(2,1)}, bf16[256,512]{1,0:T(8,128)(2,1)S(1)}, u32[]{:S(2)}, u32[]{:S(2)}) %collective-permute-start.1) | collective-permute-done | bytes 262176 | tf_op jit(solution)/shard_map/ppermute | solution.py:82
  18.9 0.9 constant_dynamic-update-slice_fusion.refs_0_
  20.4 1.8 %collective-permute-start.19 = (bf16[512,512]{1,0:T(8,128)(2,1)S(1)}, bf16[512,512]{1,0:T(8,128)(2,1)S(1)}, u32[]{:S(2)}, u32[]{:S(2)}) collective-permute-start(bf16[512,512]{1,0:T(8,128)(2,1)S(1)} %constant_dynamic-update-slice_fusion.refs_0_), channel_id=1, source_target_pairs={{0,2},{1,3},{2,0},{3,1},{4,6},{5,7},{6,4},{7,5},{8,10},{9,11},{10,... | collective-permute-start | bytes 1572872 | tf_op jit(solution)/shard_map/ppermute | solution.py:82
  22.9 0.9 copy-done.2
  23.9 0.9 copy-done.3
  24.8 1.5 %grid_messages.1 = (bf16[512,512]{1,0:T(8,128)(2,1)S(1)}, f32[4,256,128]{2,1,0:T(8,128)S(1)}, bf16[512,128]{1,0:T(8,128)(2,1)S(1)}, bf16[512,128]{1,0:T(8,128)(2...) custom-call(s32[1]{0:T(128)} %bitcast.me_ref, bf16[256,512]{1,0:T(8,128)(2,1)S(1)} %copy-done.2, ...), custom_call_target="tpu_custom_call" | custom-call | flops 268435456 | bytes 3162112 | tf_op jit(solution)/shard_map/grid_messages/pallas_call | solution.py:61
  26.4 2.7 %collective-permute-start.10 = (bf16[512,128]{1,0:T(8,128)(2,1)S(1)}, bf16[512,128]{1,0:T(8,128)(2,1)S(1)}, u32[]{:S(2)}, u32[]{:S(2)}) collective-permute-start(bf16[512,128]{1,0:T(8,128)(2,1)S(1)} %get-tuple-element.55), channel_id=1, source_target_pairs={{0,8},{4,12},{8,0},{12,4},{1,9},{5,13},{9,1},{13,5},{2,10},{6,14},... | collective-permute-start | bytes 393224 | tf_op jit(solution)/shard_map/ppermute | solution.py:85
  29.0 1.7 %collective-permute-start.11 = (bf16[512,128]{1,0:T(8,128)(2,1)S(1)}, bf16[512,128]{1,0:T(8,128)(2,1)S(1)}, u32[]{:S(2)}, u32[]{:S(2)}) collective-permute-start(bf16[512,128]{1,0:T(8,128)(2,1)S(1)} %get-tuple-element.56), channel_id=1, source_target_pairs={{0,12},{4,8},{8,4},{12,0},{1,13},{5,9},{9,5},{13,1},{2,14},{6,10},... | collective-permute-start | bytes 393224 | tf_op jit(solution)/shard_map/ppermute | solution.py:85
  30.7 3.6 %collective-permute-done.9.refs_5_ = bf16[512,128]{1,0:T(8,128)(2,1)S(1)} collective-permute-done((bf16[512,128]{1,0:T(8,128)(2,1)S(1)}, bf16[512,128]{1,0:T(8,128)(2,1)S(1)}, u32[]{:S(2)}, u32[]{:S(2)}) %collective-permute-start.9) | collective-permute-done | bytes 131104 | tf_op jit(solution)/shard_map/ppermute | solution.py:85
  34.4 4.9 %collective-permute-done.11.refs_7_ = bf16[512,128]{1,0:T(8,128)(2,1)S(1)} collective-permute-done((bf16[512,128]{1,0:T(8,128)(2,1)S(1)}, bf16[512,128]{1,0:T(8,128)(2,1)S(1)}, u32[]{:S(2)}, u32[]{:S(2)}) %collective-permute-start.11) | collective-permute-done | bytes 131104 | tf_op jit(solution)/shard_map/ppermute | solution.py:85
  39.3 1.4 encode.1
  40.7 2.5 %collective-permute-start.21 = (bf16[128,128]{1,0:T(8,128)(2,1)S(1)}, bf16[128,128]{1,0:T(8,128)(2,1)S(1)}, u32[]{:S(2)}, u32[]{:S(2)}) collective-permute-start(bf16[128,128]{1,0:T(8,128)(2,1)S(1)} %get-tuple-element.63), channel_id=1, source_target_pairs={{0,4},{4,0},{8,12},{12,8},{1,5},{5,1},{9,13},{13,9},{2,6},{6,2},{1... | collective-permute-start | bytes 98312 | tf_op jit(solution)/shard_map/ppermute | solution.py:85
  43.2 2.0 %collective-permute-start.22 = (bf16[128,128]{1,0:T(8,128)(2,1)S(1)}, bf16[128,128]{1,0:T(8,128)(2,1)S(1)}, u32[]{:S(2)}, u32[]{:S(2)}) collective-permute-start(bf16[128,128]{1,0:T(8,128)(2,1)S(1)} %get-tuple-element.64), channel_id=1, source_target_pairs={{0,8},{4,12},{8,0},{12,4},{1,9},{5,13},{9,1},{13,5},{2,10},{6,14},... | collective-permute-start | bytes 98312 | tf_op jit(solution)/shard_map/ppermute | solution.py:85
  45.9 2.1 %collective-permute-done.22 = bf16[128,128]{1,0:T(8,128)(2,1)S(1)} collective-permute-done((bf16[128,128]{1,0:T(8,128)(2,1)S(1)}, bf16[128,128]{1,0:T(8,128)(2,1)S(1)}, u32[]{:S(2)}, u32[]{:S(2)}) %collective-permute-start.22) | collective-permute-done | bytes 32800 | tf_op jit(solution)/shard_map/ppermute | solution.py:85
  48.0 3.4 %collective-permute-start.23 = (bf16[128,128]{1,0:T(8,128)(2,1)S(1)}, bf16[128,128]{1,0:T(8,128)(2,1)S(1)}, u32[]{:S(2)}, u32[]{:S(2)}) collective-permute-start(bf16[128,128]{1,0:T(8,128)(2,1)S(1)} %get-tuple-element.65), channel_id=1, source_target_pairs={{0,12},{4,8},{8,4},{12,0},{1,13},{5,9},{9,5},{13,1},{2,14},{6,10},... | collective-permute-start | bytes 98312 | tf_op jit(solution)/shard_map/ppermute | solution.py:85
  51.4 2.3 %collective-permute-done.23 = bf16[128,128]{1,0:T(8,128)(2,1)S(1)} collective-permute-done((bf16[128,128]{1,0:T(8,128)(2,1)S(1)}, bf16[128,128]{1,0:T(8,128)(2,1)S(1)}, u32[]{:S(2)}, u32[]{:S(2)}) %collective-permute-start.23) | collective-permute-done | bytes 32800 | tf_op jit(solution)/shard_map/ppermute | solution.py:85
  54.4 4.3 %collective-permute-done.13.refs_2_ = bf16[512,128]{1,0:T(8,128)(2,1)S(1)} collective-permute-done((bf16[512,128]{1,0:T(8,128)(2,1)S(1)}, bf16[512,128]{1,0:T(8,128)(2,1)S(1)}, u32[]{:S(2)}, u32[]{:S(2)}) %collective-permute-start.13) | collective-permute-done | bytes 131104 | tf_op jit(solution)/shard_map/ppermute | solution.py:82
  59.4 1.2 collective-permute-start.24
  60.6 6.3 %edge_local.1 = (f32[1024,512]{1,0:T(8,128)}, bf16[512,512]{1,0:T(8,128)(2,1)S(1)}, bf16[1536,512]{1,0:T(8,128)(2,1)S(1)}) custom-call(s32[1]{0:T(128)} %bitcast.me_ref, bf16[1024,512]{1,0:T(8,128)(2,1)S(1)} %copy-done.4, s32[1,1024]{1,0:T(1,128)S(1)} %bitcast.24, s32[1,1024]{1,0:T(1,128)S(1)} %bitcast.28, bf16[512,128]{1,0:T(8,128)(2,1)S(1)} %get-tuple-element.57.refs_0_, ...), custom_call_target="tpu_custom_call" | custom-call | flops 2684354560 | bytes 7348224 | tf_op jit(solution)/shard_map/edge_local/pallas_call | solution.py:61
  67.5 7.5 %edge_update.1 = (f32[1024,512]{1,0:T(8,128)}, bf16[128,512]{1,0:T(8,128)(2,1)S(1)}, bf16[128,512]{1,0:T(8,128)(2,1)S(1)}, bf16[128,512]{1,0:T(8,128)(2,1)S(1)}, bf16[128,512]{1,0:T(8,128)(2,1)S(1)}) custom-call(s32[1]{0:T(128)} %bitcast.me_ref, f32[1024,512]{1,0:T(8,128)} %get-tuple-element.58.local_ref, bf16[1024,512]{1,0:T(8,128)(2,1)S(1)} %copy-done.4, ...), custom_call_target="tpu_custom_call" | custom-call | flops 2147483648 | bytes 8396800 | tf_op jit(solution)/shard_map/edge_update/pallas_call | solution.py:61
  75.6 1.1 collective-permute-start.29
  76.8 4.5 %collective-permute-done.28.refs_2_ = bf16[128,512]{1,0:T(8,128)(2,1)S(1)} collective-permute-done((bf16[128,512]{1,0:T(8,128)(2,1)S(1)}, bf16[128,512]{1,0:T(8,128)(2,1)S(1)}, u32[]{:S(2)}, u32[]{:S(2)}) %collective-permute-start.28) | collective-permute-done | bytes 131104 | tf_op jit(solution)/shard_map/ppermute | solution.py:82
  81.3 2.0 %collective-permute-done.29.refs_3_ = bf16[128,512]{1,0:T(8,128)(2,1)S(1)} collective-permute-done((bf16[128,512]{1,0:T(8,128)(2,1)S(1)}, bf16[128,512]{1,0:T(8,128)(2,1)S(1)}, u32[]{:S(2)}, u32[]{:S(2)}) %collective-permute-start.29) | collective-permute-done | bytes 131104 | tf_op jit(solution)/shard_map/ppermute | solution.py:82
  84.4 1.4 %collective-permute-start.31 = (bf16[128,512]{1,0:T(8,128)(2,1)S(1)}, bf16[128,512]{1,0:T(8,128)(2,1)S(1)}, u32[]{:S(2)}, u32[]{:S(2)}) collective-permute-start(bf16[128,512]{1,0:T(8,128)(2,1)S(1)} %get-tuple-element.74.refs_0_), channel_id=1, source_target_pairs={{0,2},{1,3},{2,0},{3,1},{4,6},{5,7},{6,4},{7,5},{8,10},{9,11},{10,... | collective-permute-start | bytes 393224 | tf_op jit(solution)/shard_map/ppermute | solution.py:82
  85.8 3.6 %collective-permute-done.32.refs_3_ = bf16[128,512]{1,0:T(8,128)(2,1)S(1)} collective-permute-done((bf16[128,512]{1,0:T(8,128)(2,1)S(1)}, bf16[128,512]{1,0:T(8,128)(2,1)S(1)}, u32[]{:S(2)}, u32[]{:S(2)}) %collective-permute-start.32) | collective-permute-done | bytes 131104 | tf_op jit(solution)/shard_map/ppermute | solution.py:82
  89.4 3.2 %collective-permute-done.31.refs_2_ = bf16[128,512]{1,0:T(8,128)(2,1)S(1)} collective-permute-done((bf16[128,512]{1,0:T(8,128)(2,1)S(1)}, bf16[128,512]{1,0:T(8,128)(2,1)S(1)}, u32[]{:S(2)}, u32[]{:S(2)}) %collective-permute-start.31) | collective-permute-done | bytes 131104 | tf_op jit(solution)/shard_map/ppermute | solution.py:82
  92.6 6.2 %edge_backward.1 = (bf16[1024,512]{1,0:T(8,128)(2,1)S(1)}, bf16[512,128]{1,0:T(8,128)(2,1)S(1)}, bf16[512,128]{1,0:T(8,128)(2,1)S(1)}, bf16[512,128]{1,0:T(8,128)(2,1)S(1)}, bf16[512,128]{1,0:T(8,128)(2,1)S(1)}) custom-call(s32[1]{0:T(128)} %bitcast.me_ref, bf16[1024,512]{1,0:T(8,128)(2,1)S(1)} %copy-done.5, f32[1024,512]{1,0:T(8,128)} %get-tuple-element.66.pre_ref, ...), custom_call_target="tpu_custom_call" | custom-call | flops 1879048192 | bytes 7348224 | tf_op jit(solution)/shard_map/edge_backward/pallas_call | solution.py:61
  99.5 1.2 collective-permute-start.38
  100.7 2.8 %local_backward.1 = (bf16[512,128]{1,0:T(8,128)(2,1)S(1)}, bf16[512,128]{1,0:T(8,128)(2,1)S(1)}, bf16[512,128]{1,0:T(8,128)(2,1)S(1)}, bf16[512,128]{1,0:T(8,128)(2,1)S(1)}) custom-call(s32[1]{0:T(128)} %bitcast.me_ref, bf16[1024,512]{1,0:T(8,128)(2,1)S(1)} %get-tuple-element.75.dpre_ref, s32[1,1024]{1,0:T(1,128)S(1)} %bitcast.27, s32[1,1024]{1,0:T(1,128)S(1)} %bitcast.31, ...), custom_call_target="tpu_custom_call" | custom-call | flops 1610612736 | bytes 3416064 | tf_op jit(solution)/shard_map/local_backward/pallas_call | solution.py:61
  104.5 0.9 collective-permute-start.35
  105.4 1.7 %collective-permute-done.38.refs_3_ = bf16[512,128]{1,0:T(8,128)(2,1)S(1)} collective-permute-done((bf16[512,128]{1,0:T(8,128)(2,1)S(1)}, bf16[512,128]{1,0:T(8,128)(2,1)S(1)}, u32[]{:S(2)}, u32[]{:S(2)}) %collective-permute-start.38) | collective-permute-done | bytes 131104 | tf_op jit(solution)/shard_map/ppermute | solution.py:82
  107.2 3.9 %collective-permute-start.40 = (bf16[128,128]{1,0:T(8,128)(2,1)S(1)}, bf16[128,128]{1,0:T(8,128)(2,1)S(1)}, u32[]{:S(2)}, u32[]{:S(2)}) collective-permute-start(bf16[128,128]{1,0:T(8,128)(2,1)S(1)} %get-tuple-element.87), channel_id=1, source_target_pairs={{0,8},{4,12},{8,0},{12,4},{1,9},{5,13},{9,1},{13,5},{2,10},{6,14},... | collective-permute-start | bytes 98312 | tf_op jit(solution)/shard_map/ppermute | solution.py:85
  111.6 1.1 collective-permute-done.35.refs_7_
  112.7 1.3 collective-permute-done.40.refs_10_
  114.0 2.9 %collective-permute-done.41.refs_11_ = bf16[128,128]{1,0:T(8,128)(2,1)S(1)} collective-permute-done((bf16[128,128]{1,0:T(8,128)(2,1)S(1)}, bf16[128,128]{1,0:T(8,128)(2,1)S(1)}, u32[]{:S(2)}, u32[]{:S(2)}) %collective-permute-start.41) | collective-permute-done | bytes 32800 | tf_op jit(solution)/shard_map/ppermute | solution.py:85
  116.9 1.2 owed_rows.1
  118.1 1.2 collective-permute-start.43
  119.3 3.2 %collective-permute-start.44 = (bf16[512,128]{1,0:T(8,128)(2,1)S(1)}, bf16[512,128]{1,0:T(8,128)(2,1)S(1)}, u32[]{:S(2)}, u32[]{:S(2)}) collective-permute-start(bf16[512,128]{1,0:T(8,128)(2,1)S(1)} %get-tuple-element.92), channel_id=1, source_target_pairs={{0,12},{4,8},{8,4},{12,0},{1,13},{5,9},{9,5},{13,1},{2,14},{6,10},... | collective-permute-start | bytes 393224 | tf_op jit(solution)/shard_map/ppermute | solution.py:85
  122.5 1.9 %collective-permute-done.42.refs_5_ = bf16[512,128]{1,0:T(8,128)(2,1)S(1)} collective-permute-done((bf16[512,128]{1,0:T(8,128)(2,1)S(1)}, bf16[512,128]{1,0:T(8,128)(2,1)S(1)}, u32[]{:S(2)}, u32[]{:S(2)}) %collective-permute-start.42) | collective-permute-done | bytes 131104 | tf_op jit(solution)/shard_map/ppermute | solution.py:85
  124.5 6.1 %collective-permute-done.43.refs_6_ = bf16[512,128]{1,0:T(8,128)(2,1)S(1)} collective-permute-done((bf16[512,128]{1,0:T(8,128)(2,1)S(1)}, bf16[512,128]{1,0:T(8,128)(2,1)S(1)}, u32[]{:S(2)}, u32[]{:S(2)}) %collective-permute-start.43) | collective-permute-done | bytes 131104 | tf_op jit(solution)/shard_map/ppermute | solution.py:85
  131.5 1.5 %collective-permute-start.47 = (bf16[256,128]{1,0:T(8,128)(2,1)S(1)}, bf16[256,128]{1,0:T(8,128)(2,1)S(1)}, u32[]{:S(2)}, u32[]{:S(2)}) collective-permute-start(bf16[256,128]{1,0:T(8,128)(2,1)S(1)} %get-tuple-element.96), channel_id=1, source_target_pairs={{0,3},{1,2},{2,1},{3,0},{4,7},{5,6},{6,5},{7,4},{8,11},{9,10},{10,... | collective-permute-start | bytes 196616 | tf_op jit(solution)/shard_map/ppermute | solution.py:82
  133.0 3.1 %collective-permute-done.46.refs_2_ = bf16[256,128]{1,0:T(8,128)(2,1)S(1)} collective-permute-done((bf16[256,128]{1,0:T(8,128)(2,1)S(1)}, bf16[256,128]{1,0:T(8,128)(2,1)S(1)}, u32[]{:S(2)}, u32[]{:S(2)}) %collective-permute-start.46) | collective-permute-done | bytes 65568 | tf_op jit(solution)/shard_map/ppermute | solution.py:82
  136.6 1.1 adjoint.1
  (98 shorter events, 16.6 us)
Async XLA Ops:
  3.6 7.5 %collective-permute-start.8 = (s32[2,512]{1,0:T(2,128)S(1)}, s32[2,512]{1,0:T(2,128)S(1)}, u32[]{:S(2)}, u32[]{:S(2)}) collective-permute-start(s32[2,512]{1,0:T(2,128)S(1)} %pad_add_fusion.refs_8_.refs_0_), channel_id=1, source_target_pairs={{0,3},{1,2},{2,1},{3,0},{4,7},{5,6},{6,5},{7,4},{8,11},{9,10},{10,... | collective-permute-start | bytes 12296 | tf_op jit(solution)/shard_map/ppermute | solution.py:82
  6.1 5.1 %collective-permute-start.7 = (s32[2,512]{1,0:T(2,128)S(1)}, s32[2,512]{1,0:T(2,128)S(1)}, u32[]{:S(2)}, u32[]{:S(2)}) collective-permute-start(s32[2,512]{1,0:T(2,128)S(1)} %pad_add_fusion.refs_8_.refs_0_), channel_id=1, source_target_pairs={{0,2},{1,3},{2,0},{3,1},{4,6},{5,7},{6,4},{7,5},{8,10},{9,11},{10,... | collective-permute-start | bytes 12296 | tf_op jit(solution)/shard_map/ppermute | solution.py:82
  6.7 7.5 %collective-permute-start.6 = (s32[2,512]{1,0:T(2,128)S(1)}, s32[2,512]{1,0:T(2,128)S(1)}, u32[]{:S(2)}, u32[]{:S(2)}) collective-permute-start(s32[2,512]{1,0:T(2,128)S(1)} %pad_add_fusion.refs_8_.refs_0_), channel_id=1, source_target_pairs={{0,1},{1,0},{2,3},{3,2},{4,5},{5,4},{6,7},{7,6},{8,9},{9,8},{10,11... | collective-permute-start | bytes 12296 | tf_op jit(solution)/shard_map/ppermute | solution.py:82
  6.7 6.5 %collective-permute-start.4 = (bf16[128,512]{1,0:T(8,128)(2,1)}, bf16[128,512]{1,0:T(8,128)(2,1)S(1)}, u32[]{:S(2)}, u32[]{:S(2)}) collective-permute-start(bf16[128,512]{1,0:T(8,128)(2,1)} %refs_4_.2), channel_id=1, source_target_pairs={{0,2},{1,3},{2,0},{3,1},{4,6},{5,7},{6,4},{7,5},{8,10},{9,11},{10,... | collective-permute-start | bytes 393224 | tf_op jit(solution)/shard_map/ppermute | solution.py:82
  8.5 10.4 %collective-permute-start.1 = (bf16[256,512]{1,0:T(8,128)(2,1)}, bf16[256,512]{1,0:T(8,128)(2,1)S(1)}, u32[]{:S(2)}, u32[]{:S(2)}) collective-permute-start(bf16[256,512]{1,0:T(8,128)(2,1)} %refs_0_.1), channel_id=1, source_target_pairs={{0,2},{1,3},{2,0},{3,1},{4,6},{5,7},{6,4},{7,5},{8,10},{9,11},{10,... | collective-permute-start | bytes 786440 | tf_op jit(solution)/shard_map/ppermute | solution.py:82
  11.1 8.7 %collective-permute-start.3 = (bf16[128,512]{1,0:T(8,128)(2,1)}, bf16[128,512]{1,0:T(8,128)(2,1)S(1)}, u32[]{:S(2)}, u32[]{:S(2)}) collective-permute-start(bf16[128,512]{1,0:T(8,128)(2,1)} %refs_4_.2), channel_id=1, source_target_pairs={{0,1},{1,0},{2,3},{3,2},{4,5},{5,4},{6,7},{7,6},{8,9},{9,8},{10,11... | collective-permute-start | bytes 393224 | tf_op jit(solution)/shard_map/ppermute | solution.py:82
  11.2 17.8 %collective-permute-start.16 = (bf16[384,512]{1,0:T(8,128)(2,1)}, bf16[384,512]{1,0:T(8,128)(2,1)S(1)}, u32[]{:S(2)}, u32[]{:S(2)}) collective-permute-start(bf16[384,512]{1,0:T(8,128)(2,1)} %refs_4_.3), channel_id=1, source_target_pairs={{0,2},{1,3},{2,0},{3,1},{4,6},{5,7},{6,4},{7,5},{8,10},{9,11},{10,... | collective-permute-start | bytes 1179656 | tf_op jit(solution)/shard_map/ppermute | solution.py:82
  13.3 7.1 %collective-permute-start.5 = (bf16[128,512]{1,0:T(8,128)(2,1)S(1)}, bf16[128,512]{1,0:T(8,128)(2,1)S(1)}, u32[]{:S(2)}, u32[]{:S(2)}) collective-permute-start(bf16[128,512]{1,0:T(8,128)(2,1)S(1)} %collective-permute-done.4.refs_6_), channel_id=1, source_target_pairs={{0,1},{1,0},{2,3},{3,2},{4,5},{5,4},{6,7},{7,6},{8,9},{9,8},{10,11... | collective-permute-start | bytes 393224 | tf_op jit(solution)/shard_map/ppermute | solution.py:82
  14.2 8.7 %collective-permute-start = (bf16[256,512]{1,0:T(8,128)(2,1)}, bf16[256,512]{1,0:T(8,128)(2,1)S(1)}, u32[]{:S(2)}, u32[]{:S(2)}) collective-permute-start(bf16[256,512]{1,0:T(8,128)(2,1)} %refs_0_.1), channel_id=1, source_target_pairs={{0,1},{1,0},{2,3},{3,2},{4,5},{5,4},{6,7},{7,6},{8,9},{9,8},{10,11... | collective-permute-start | bytes 786440 | tf_op jit(solution)/shard_map/ppermute | solution.py:82
  18.9 4.0 %collective-permute-start.2 = (bf16[256,512]{1,0:T(8,128)(2,1)S(1)}, bf16[256,512]{1,0:T(8,128)(2,1)S(1)}, u32[]{:S(2)}, u32[]{:S(2)}) collective-permute-start(bf16[256,512]{1,0:T(8,128)(2,1)S(1)} %collective-permute-done.1.refs_2_), channel_id=1, source_target_pairs={{0,1},{1,0},{2,3},{3,2},{4,5},{5,4},{6,7},{7,6},{8,9},{9,8},{10,11... | collective-permute-start | bytes 786440 | tf_op jit(solution)/shard_map/ppermute | solution.py:82
  19.8 25.4 %collective-permute-start.15 = (bf16[384,512]{1,0:T(8,128)(2,1)}, bf16[384,512]{1,0:T(8,128)(2,1)S(1)}, u32[]{:S(2)}, u32[]{:S(2)}) collective-permute-start(bf16[384,512]{1,0:T(8,128)(2,1)} %refs_4_.3), channel_id=1, source_target_pairs={{0,1},{1,0},{2,3},{3,2},{4,5},{5,4},{6,7},{7,6},{8,9},{9,8},{10,11... | collective-permute-start | bytes 1179656 | tf_op jit(solution)/shard_map/ppermute | solution.py:82
  20.4 24.8 %collective-permute-start.19 = (bf16[512,512]{1,0:T(8,128)(2,1)S(1)}, bf16[512,512]{1,0:T(8,128)(2,1)S(1)}, u32[]{:S(2)}, u32[]{:S(2)}) collective-permute-start(bf16[512,512]{1,0:T(8,128)(2,1)S(1)} %constant_dynamic-update-slice_fusion.refs_0_), channel_id=1, source_target_pairs={{0,2},{1,3},{2,0},{3,1},{4,6},{5,7},{6,4},{7,5},{8,10},{9,11},{10,... | collective-permute-start | bytes 1572872 | tf_op jit(solution)/shard_map/ppermute | solution.py:82
  26.3 8.1 %collective-permute-start.9 = (bf16[512,128]{1,0:T(8,128)(2,1)S(1)}, bf16[512,128]{1,0:T(8,128)(2,1)S(1)}, u32[]{:S(2)}, u32[]{:S(2)}) collective-permute-start(bf16[512,128]{1,0:T(8,128)(2,1)S(1)} %get-tuple-element.54), channel_id=1, source_target_pairs={{0,4},{4,0},{8,12},{12,8},{1,5},{5,1},{9,13},{13,9},{2,6},{6,2},{1... | collective-permute-start | bytes 393224 | tf_op jit(solution)/shard_map/ppermute | solution.py:85
  26.4 8.0 %collective-permute-start.10 = (bf16[512,128]{1,0:T(8,128)(2,1)S(1)}, bf16[512,128]{1,0:T(8,128)(2,1)S(1)}, u32[]{:S(2)}, u32[]{:S(2)}) collective-permute-start(bf16[512,128]{1,0:T(8,128)(2,1)S(1)} %get-tuple-element.55), channel_id=1, source_target_pairs={{0,8},{4,12},{8,0},{12,4},{1,9},{5,13},{9,1},{13,5},{2,10},{6,14},... | collective-permute-start | bytes 393224 | tf_op jit(solution)/shard_map/ppermute | solution.py:85
  29.0 10.3 %collective-permute-start.11 = (bf16[512,128]{1,0:T(8,128)(2,1)S(1)}, bf16[512,128]{1,0:T(8,128)(2,1)S(1)}, u32[]{:S(2)}, u32[]{:S(2)}) collective-permute-start(bf16[512,128]{1,0:T(8,128)(2,1)S(1)} %get-tuple-element.56), channel_id=1, source_target_pairs={{0,12},{4,8},{8,4},{12,0},{1,13},{5,9},{9,5},{13,1},{2,14},{6,10},... | collective-permute-start | bytes 393224 | tf_op jit(solution)/shard_map/ppermute | solution.py:85
  34.4 25.0 %collective-permute-start.17 = (bf16[384,512]{1,0:T(8,128)(2,1)S(1)}, bf16[384,512]{1,0:T(8,128)(2,1)S(1)}, u32[]{:S(2)}, u32[]{:S(2)}) collective-permute-start(bf16[384,512]{1,0:T(8,128)(2,1)S(1)} %collective-permute-done.16.refs_6_), channel_id=1, source_target_pairs={{0,1},{1,0},{2,3},{3,2},{4,5},{5,4},{6,7},{7,6},{8,9},{9,8},{10,11... | collective-permute-start | bytes 1179656 | tf_op jit(solution)/shard_map/ppermute | solution.py:82
  40.7 5.2 %collective-permute-start.21 = (bf16[128,128]{1,0:T(8,128)(2,1)S(1)}, bf16[128,128]{1,0:T(8,128)(2,1)S(1)}, u32[]{:S(2)}, u32[]{:S(2)}) collective-permute-start(bf16[128,128]{1,0:T(8,128)(2,1)S(1)} %get-tuple-element.63), channel_id=1, source_target_pairs={{0,4},{4,0},{8,12},{12,8},{1,5},{5,1},{9,13},{13,9},{2,6},{6,2},{1... | collective-permute-start | bytes 98312 | tf_op jit(solution)/shard_map/ppermute | solution.py:85
  43.2 4.8 %collective-permute-start.22 = (bf16[128,128]{1,0:T(8,128)(2,1)S(1)}, bf16[128,128]{1,0:T(8,128)(2,1)S(1)}, u32[]{:S(2)}, u32[]{:S(2)}) collective-permute-start(bf16[128,128]{1,0:T(8,128)(2,1)S(1)} %get-tuple-element.64), channel_id=1, source_target_pairs={{0,8},{4,12},{8,0},{12,4},{1,9},{5,13},{9,1},{13,5},{2,10},{6,14},... | collective-permute-start | bytes 98312 | tf_op jit(solution)/shard_map/ppermute | solution.py:85
  45.2 9.2 %collective-permute-start.14 = (bf16[512,128]{1,0:T(8,128)(2,1)S(1)}, bf16[512,128]{1,0:T(8,128)(2,1)S(1)}, u32[]{:S(2)}, u32[]{:S(2)}) collective-permute-start(bf16[512,128]{1,0:T(8,128)(2,1)S(1)} %get-tuple-element.57.refs_0_), channel_id=1, source_target_pairs={{0,3},{1,2},{2,1},{3,0},{4,7},{5,6},{6,5},{7,4},{8,11},{9,10},{10,... | collective-permute-start | bytes 393224 | tf_op jit(solution)/shard_map/ppermute | solution.py:82
  45.2 21.7 %collective-permute-start.18 = (bf16[512,512]{1,0:T(8,128)(2,1)S(1)}, bf16[512,512]{1,0:T(8,128)(2,1)S(1)}, u32[]{:S(2)}, u32[]{:S(2)}) collective-permute-start(bf16[512,512]{1,0:T(8,128)(2,1)S(1)} %constant_dynamic-update-slice_fusion.refs_0_), channel_id=1, source_target_pairs={{0,1},{1,0},{2,3},{3,2},{4,5},{5,4},{6,7},{7,6},{8,9},{9,8},{10,11... | collective-permute-start | bytes 1572872 | tf_op jit(solution)/shard_map/ppermute | solution.py:82
  45.8 21.1 %collective-permute-start.20 = (bf16[512,512]{1,0:T(8,128)(2,1)S(1)}, bf16[512,512]{1,0:T(8,128)(2,1)S(1)}, u32[]{:S(2)}, u32[]{:S(2)}) collective-permute-start(bf16[512,512]{1,0:T(8,128)(2,1)S(1)} %collective-permute-done.19.refs_2_), channel_id=1, source_target_pairs={{0,1},{1,0},{2,3},{3,2},{4,5},{5,4},{6,7},{7,6},{8,9},{9,8},{10,11... | collective-permute-start | bytes 1572872 | tf_op jit(solution)/shard_map/ppermute | solution.py:82
  48.0 5.7 %collective-permute-start.23 = (bf16[128,128]{1,0:T(8,128)(2,1)S(1)}, bf16[128,128]{1,0:T(8,128)(2,1)S(1)}, u32[]{:S(2)}, u32[]{:S(2)}) collective-permute-start(bf16[128,128]{1,0:T(8,128)(2,1)S(1)} %get-tuple-element.65), channel_id=1, source_target_pairs={{0,12},{4,8},{8,4},{12,0},{1,13},{5,9},{9,5},{13,1},{2,14},{6,10},... | collective-permute-start | bytes 98312 | tf_op jit(solution)/shard_map/ppermute | solution.py:85
  53.7 5.0 %collective-permute-start.13 = (bf16[512,128]{1,0:T(8,128)(2,1)S(1)}, bf16[512,128]{1,0:T(8,128)(2,1)S(1)}, u32[]{:S(2)}, u32[]{:S(2)}) collective-permute-start(bf16[512,128]{1,0:T(8,128)(2,1)S(1)} %get-tuple-element.57.refs_0_), channel_id=1, source_target_pairs={{0,2},{1,3},{2,0},{3,1},{4,6},{5,7},{6,4},{7,5},{8,10},{9,11},{10,... | collective-permute-start | bytes 393224 | tf_op jit(solution)/shard_map/ppermute | solution.py:82
  54.4 4.3 %collective-permute-start.12 = (bf16[512,128]{1,0:T(8,128)(2,1)S(1)}, bf16[512,128]{1,0:T(8,128)(2,1)S(1)}, u32[]{:S(2)}, u32[]{:S(2)}) collective-permute-start(bf16[512,128]{1,0:T(8,128)(2,1)S(1)} %get-tuple-element.57.refs_0_), channel_id=1, source_target_pairs={{0,1},{1,0},{2,3},{3,2},{4,5},{5,4},{6,7},{7,6},{8,9},{9,8},{10,11... | collective-permute-start | bytes 393224 | tf_op jit(solution)/shard_map/ppermute | solution.py:82
  58.7 8.7 %collective-permute-start.26 = (bf16[512,128]{1,0:T(8,128)(2,1)S(1)}, bf16[512,128]{1,0:T(8,128)(2,1)S(1)}, u32[]{:S(2)}, u32[]{:S(2)}) collective-permute-start(bf16[512,128]{1,0:T(8,128)(2,1)S(1)} %constant_dynamic-update-slice_fusion.3.refs_0_), channel_id=1, source_target_pairs={{0,3},{1,2},{2,1},{3,0},{4,7},{5,6},{6,5},{7,4},{8,11},{9,10},{10,... | collective-permute-start | bytes 393224 | tf_op jit(solution)/shard_map/ppermute | solution.py:82
  58.7 8.8 %collective-permute-start.25 = (bf16[512,128]{1,0:T(8,128)(2,1)S(1)}, bf16[512,128]{1,0:T(8,128)(2,1)S(1)}, u32[]{:S(2)}, u32[]{:S(2)}) collective-permute-start(bf16[512,128]{1,0:T(8,128)(2,1)S(1)} %constant_dynamic-update-slice_fusion.3.refs_0_), channel_id=1, source_target_pairs={{0,2},{1,3},{2,0},{3,1},{4,6},{5,7},{6,4},{7,5},{8,10},{9,11},{10,... | collective-permute-start | bytes 393224 | tf_op jit(solution)/shard_map/ppermute | solution.py:82
  59.4 8.1 %collective-permute-start.24 = (bf16[512,128]{1,0:T(8,128)(2,1)S(1)}, bf16[512,128]{1,0:T(8,128)(2,1)S(1)}, u32[]{:S(2)}, u32[]{:S(2)}) collective-permute-start(bf16[512,128]{1,0:T(8,128)(2,1)S(1)} %constant_dynamic-update-slice_fusion.3.refs_0_), channel_id=1, source_target_pairs={{0,1},{1,0},{2,3},{3,2},{4,5},{5,4},{6,7},{7,6},{8,9},{9,8},{10,11... | collective-permute-start | bytes 393224 | tf_op jit(solution)/shard_map/ppermute | solution.py:82
  74.9 1.9 %collective-permute-start.27 = (bf16[128,512]{1,0:T(8,128)(2,1)S(1)}, bf16[128,512]{1,0:T(8,128)(2,1)S(1)}, u32[]{:S(2)}, u32[]{:S(2)}) collective-permute-start(bf16[128,512]{1,0:T(8,128)(2,1)S(1)} %get-tuple-element.71), channel_id=1, source_target_pairs={{0,1},{1,0},{2,3},{3,2},{4,5},{5,4},{6,7},{7,6},{8,9},{9,8},{10,11... | collective-permute-start | bytes 393224 | tf_op jit(solution)/shard_map/ppermute | solution.py:82
  75.0 6.3 %collective-permute-start.28 = (bf16[128,512]{1,0:T(8,128)(2,1)S(1)}, bf16[128,512]{1,0:T(8,128)(2,1)S(1)}, u32[]{:S(2)}, u32[]{:S(2)}) collective-permute-start(bf16[128,512]{1,0:T(8,128)(2,1)S(1)} %get-tuple-element.72), channel_id=1, source_target_pairs={{0,2},{1,3},{2,0},{3,1},{4,6},{5,7},{6,4},{7,5},{8,10},{9,11},{10,... | collective-permute-start | bytes 393224 | tf_op jit(solution)/shard_map/ppermute | solution.py:82
  75.6 7.6 %collective-permute-start.29 = (bf16[128,512]{1,0:T(8,128)(2,1)S(1)}, bf16[128,512]{1,0:T(8,128)(2,1)S(1)}, u32[]{:S(2)}, u32[]{:S(2)}) collective-permute-start(bf16[128,512]{1,0:T(8,128)(2,1)S(1)} %get-tuple-element.73), channel_id=1, source_target_pairs={{0,3},{1,2},{2,1},{3,0},{4,7},{5,6},{6,5},{7,4},{8,11},{9,10},{10,... | collective-permute-start | bytes 393224 | tf_op jit(solution)/shard_map/ppermute | solution.py:82
  83.9 5.5 %collective-permute-start.32 = (bf16[128,512]{1,0:T(8,128)(2,1)S(1)}, bf16[128,512]{1,0:T(8,128)(2,1)S(1)}, u32[]{:S(2)}, u32[]{:S(2)}) collective-permute-start(bf16[128,512]{1,0:T(8,128)(2,1)S(1)} %get-tuple-element.74.refs_0_), channel_id=1, source_target_pairs={{0,3},{1,2},{2,1},{3,0},{4,7},{5,6},{6,5},{7,4},{8,11},{9,10},{10,... | collective-permute-start | bytes 393224 | tf_op jit(solution)/shard_map/ppermute | solution.py:82
  84.4 8.1 %collective-permute-start.31 = (bf16[128,512]{1,0:T(8,128)(2,1)S(1)}, bf16[128,512]{1,0:T(8,128)(2,1)S(1)}, u32[]{:S(2)}, u32[]{:S(2)}) collective-permute-start(bf16[128,512]{1,0:T(8,128)(2,1)S(1)} %get-tuple-element.74.refs_0_), channel_id=1, source_target_pairs={{0,2},{1,3},{2,0},{3,1},{4,6},{5,7},{6,4},{7,5},{8,10},{9,11},{10,... | collective-permute-start | bytes 393224 | tf_op jit(solution)/shard_map/ppermute | solution.py:82
  85.8 6.7 %collective-permute-start.30 = (bf16[128,512]{1,0:T(8,128)(2,1)S(1)}, bf16[128,512]{1,0:T(8,128)(2,1)S(1)}, u32[]{:S(2)}, u32[]{:S(2)}) collective-permute-start(bf16[128,512]{1,0:T(8,128)(2,1)S(1)} %get-tuple-element.74.refs_0_), channel_id=1, source_target_pairs={{0,1},{1,0},{2,3},{3,2},{4,5},{5,4},{6,7},{7,6},{8,9},{9,8},{10,11... | collective-permute-start | bytes 393224 | tf_op jit(solution)/shard_map/ppermute | solution.py:82
  98.7 5.8 %collective-permute-start.36 = (bf16[512,128]{1,0:T(8,128)(2,1)S(1)}, bf16[512,128]{1,0:T(8,128)(2,1)S(1)}, u32[]{:S(2)}, u32[]{:S(2)}) collective-permute-start(bf16[512,128]{1,0:T(8,128)(2,1)S(1)} %get-tuple-element.82), channel_id=1, source_target_pairs={{0,1},{1,0},{2,3},{3,2},{4,5},{5,4},{6,7},{7,6},{8,9},{9,8},{10,11... | collective-permute-start | bytes 393224 | tf_op jit(solution)/shard_map/ppermute | solution.py:82
  98.8 6.6 %collective-permute-start.37 = (bf16[512,128]{1,0:T(8,128)(2,1)S(1)}, bf16[512,128]{1,0:T(8,128)(2,1)S(1)}, u32[]{:S(2)}, u32[]{:S(2)}) collective-permute-start(bf16[512,128]{1,0:T(8,128)(2,1)S(1)} %get-tuple-element.83), channel_id=1, source_target_pairs={{0,2},{1,3},{2,0},{3,1},{4,6},{5,7},{6,4},{7,5},{8,10},{9,11},{10,... | collective-permute-start | bytes 393224 | tf_op jit(solution)/shard_map/ppermute | solution.py:82
  99.5 7.6 %collective-permute-start.38 = (bf16[512,128]{1,0:T(8,128)(2,1)S(1)}, bf16[512,128]{1,0:T(8,128)(2,1)S(1)}, u32[]{:S(2)}, u32[]{:S(2)}) collective-permute-start(bf16[512,128]{1,0:T(8,128)(2,1)S(1)} %get-tuple-element.84), channel_id=1, source_target_pairs={{0,3},{1,2},{2,1},{3,0},{4,7},{5,6},{6,5},{7,4},{8,11},{9,10},{10,... | collective-permute-start | bytes 393224 | tf_op jit(solution)/shard_map/ppermute | solution.py:82
  103.4 7.7 %collective-permute-start.33 = (bf16[512,128]{1,0:T(8,128)(2,1)S(1)}, bf16[512,128]{1,0:T(8,128)(2,1)S(1)}, u32[]{:S(2)}, u32[]{:S(2)}) collective-permute-start(bf16[512,128]{1,0:T(8,128)(2,1)S(1)} %get-tuple-element.78), channel_id=1, source_target_pairs={{0,1},{1,0},{2,3},{3,2},{4,5},{5,4},{6,7},{7,6},{8,9},{9,8},{10,11... | collective-permute-start | bytes 393224 | tf_op jit(solution)/shard_map/ppermute | solution.py:82
  103.9 7.7 %collective-permute-start.34 = (bf16[512,128]{1,0:T(8,128)(2,1)S(1)}, bf16[512,128]{1,0:T(8,128)(2,1)S(1)}, u32[]{:S(2)}, u32[]{:S(2)}) collective-permute-start(bf16[512,128]{1,0:T(8,128)(2,1)S(1)} %get-tuple-element.79), channel_id=1, source_target_pairs={{0,2},{1,3},{2,0},{3,1},{4,6},{5,7},{6,4},{7,5},{8,10},{9,11},{10,... | collective-permute-start | bytes 393224 | tf_op jit(solution)/shard_map/ppermute | solution.py:82
  104.5 8.2 %collective-permute-start.35 = (bf16[512,128]{1,0:T(8,128)(2,1)S(1)}, bf16[512,128]{1,0:T(8,128)(2,1)S(1)}, u32[]{:S(2)}, u32[]{:S(2)}) collective-permute-start(bf16[512,128]{1,0:T(8,128)(2,1)S(1)} %get-tuple-element.80), channel_id=1, source_target_pairs={{0,3},{1,2},{2,1},{3,0},{4,7},{5,6},{6,5},{7,4},{8,11},{9,10},{10,... | collective-permute-start | bytes 393224 | tf_op jit(solution)/shard_map/ppermute | solution.py:82
  107.1 5.5 %collective-permute-start.39 = (bf16[128,128]{1,0:T(8,128)(2,1)S(1)}, bf16[128,128]{1,0:T(8,128)(2,1)S(1)}, u32[]{:S(2)}, u32[]{:S(2)}) collective-permute-start(bf16[128,128]{1,0:T(8,128)(2,1)S(1)} %get-tuple-element.86), channel_id=1, source_target_pairs={{0,4},{4,0},{8,12},{12,8},{1,5},{5,1},{9,13},{13,9},{2,6},{6,2},{1... | collective-permute-start | bytes 98312 | tf_op jit(solution)/shard_map/ppermute | solution.py:85
  107.2 6.8 %collective-permute-start.40 = (bf16[128,128]{1,0:T(8,128)(2,1)S(1)}, bf16[128,128]{1,0:T(8,128)(2,1)S(1)}, u32[]{:S(2)}, u32[]{:S(2)}) collective-permute-start(bf16[128,128]{1,0:T(8,128)(2,1)S(1)} %get-tuple-element.87), channel_id=1, source_target_pairs={{0,8},{4,12},{8,0},{12,4},{1,9},{5,13},{9,1},{13,5},{2,10},{6,14},... | collective-permute-start | bytes 98312 | tf_op jit(solution)/shard_map/ppermute | solution.py:85
  111.2 5.7 %collective-permute-start.41 = (bf16[128,128]{1,0:T(8,128)(2,1)S(1)}, bf16[128,128]{1,0:T(8,128)(2,1)S(1)}, u32[]{:S(2)}, u32[]{:S(2)}) collective-permute-start(bf16[128,128]{1,0:T(8,128)(2,1)S(1)} %get-tuple-element.88), channel_id=1, source_target_pairs={{0,12},{4,8},{8,4},{12,0},{1,13},{5,9},{9,5},{13,1},{2,14},{6,10},... | collective-permute-start | bytes 98312 | tf_op jit(solution)/shard_map/ppermute | solution.py:85
  118.1 6.4 %collective-permute-start.42 = (bf16[512,128]{1,0:T(8,128)(2,1)S(1)}, bf16[512,128]{1,0:T(8,128)(2,1)S(1)}, u32[]{:S(2)}, u32[]{:S(2)}) collective-permute-start(bf16[512,128]{1,0:T(8,128)(2,1)S(1)} %get-tuple-element.90), channel_id=1, source_target_pairs={{0,4},{4,0},{8,12},{12,8},{1,5},{5,1},{9,13},{13,9},{2,6},{6,2},{1... | collective-permute-start | bytes 393224 | tf_op jit(solution)/shard_map/ppermute | solution.py:85
  118.1 12.5 %collective-permute-start.43 = (bf16[512,128]{1,0:T(8,128)(2,1)S(1)}, bf16[512,128]{1,0:T(8,128)(2,1)S(1)}, u32[]{:S(2)}, u32[]{:S(2)}) collective-permute-start(bf16[512,128]{1,0:T(8,128)(2,1)S(1)} %get-tuple-element.91), channel_id=1, source_target_pairs={{0,8},{4,12},{8,0},{12,4},{1,9},{5,13},{9,1},{13,5},{2,10},{6,14},... | collective-permute-start | bytes 393224 | tf_op jit(solution)/shard_map/ppermute | solution.py:85
  119.3 11.3 %collective-permute-start.44 = (bf16[512,128]{1,0:T(8,128)(2,1)S(1)}, bf16[512,128]{1,0:T(8,128)(2,1)S(1)}, u32[]{:S(2)}, u32[]{:S(2)}) collective-permute-start(bf16[512,128]{1,0:T(8,128)(2,1)S(1)} %get-tuple-element.92), channel_id=1, source_target_pairs={{0,12},{4,8},{8,4},{12,0},{1,13},{5,9},{9,5},{13,1},{2,14},{6,10},... | collective-permute-start | bytes 393224 | tf_op jit(solution)/shard_map/ppermute | solution.py:85
  131.0 1.9 %collective-permute-start.45 = (bf16[256,128]{1,0:T(8,128)(2,1)S(1)}, bf16[256,128]{1,0:T(8,128)(2,1)S(1)}, u32[]{:S(2)}, u32[]{:S(2)}) collective-permute-start(bf16[256,128]{1,0:T(8,128)(2,1)S(1)} %get-tuple-element.94), channel_id=1, source_target_pairs={{0,1},{1,0},{2,3},{3,2},{4,5},{5,4},{6,7},{7,6},{8,9},{9,8},{10,11... | collective-permute-start | bytes 196616 | tf_op jit(solution)/shard_map/ppermute | solution.py:82
  131.1 5.0 %collective-permute-start.46 = (bf16[256,128]{1,0:T(8,128)(2,1)S(1)}, bf16[256,128]{1,0:T(8,128)(2,1)S(1)}, u32[]{:S(2)}, u32[]{:S(2)}) collective-permute-start(bf16[256,128]{1,0:T(8,128)(2,1)S(1)} %get-tuple-element.95), channel_id=1, source_target_pairs={{0,2},{1,3},{2,0},{3,1},{4,6},{5,7},{6,4},{7,5},{8,10},{9,11},{10,... | collective-permute-start | bytes 196616 | tf_op jit(solution)/shard_map/ppermute | solution.py:82
  131.5 5.1 %collective-permute-start.47 = (bf16[256,128]{1,0:T(8,128)(2,1)S(1)}, bf16[256,128]{1,0:T(8,128)(2,1)S(1)}, u32[]{:S(2)}, u32[]{:S(2)}) collective-permute-start(bf16[256,128]{1,0:T(8,128)(2,1)S(1)} %get-tuple-element.96), channel_id=1, source_target_pairs={{0,3},{1,2},{2,1},{3,0},{4,7},{5,6},{6,5},{7,4},{8,11},{9,10},{10,... | collective-permute-start | bytes 196616 | tf_op jit(solution)/shard_map/ppermute | solution.py:82
  (9 other events, 252.8 us)

commit v2 on v1

--- a/solution.py
+++ b/solution.py
@@ -9,6 +9,7 @@
 F32 = jnp.float32
 SMEM = pl.BlockSpec(memory_space=pltpu.SMEM)
 VMEM = pl.BlockSpec(memory_space=pltpu.VMEM)
+ANY = pl.BlockSpec(memory_space=pl.ANY)
 
 
 def dot(a, b):
@@ -55,16 +56,16 @@
     return parts[0] if len(parts) == 1 else jnp.concatenate(parts, axis=0)
 
 
-def call(body, name, me, ins, outs, scratch=(), flops=0):
+def call(body, name, me, ins, outs, scratch=(), flops=0, unread=0):
     size = lambda s: s.size * s.dtype.itemsize
     moved = sum(size(x) for x in ins) + sum(size(x) for x in outs)
     return pl.pallas_call(
         body,
         out_shape=list(outs),
-        in_specs=[SMEM] + [VMEM] * len(ins),
+        in_specs=[SMEM] + [VMEM] * (len(ins) - unread) + [ANY] * unread,
         out_specs=[VMEM] * len(outs),
         scratch_shapes=list(scratch),
-        compiler_params=pltpu.CompilerParams(vmem_limit_bytes=48 * 2**20),
+        compiler_params=pltpu.CompilerParams(vmem_limit_bytes=24 * 2**20),
         cost_estimate=pl.CostEstimate(flops=flops, bytes_accessed=moved, transcendentals=0),
         name=name,
     )(me, *ins)
@@ -99,17 +100,21 @@
     def member_trade(parts):
         return [parts[0]] + [member_swap(parts[k], k) for k in range(1, M)]
 
+    def member_sums(parts, me1, name):
+        arrived = [parts[0]] + [member_swap(parts[kr], kr) for kr in range(1, n_rep)]
+
+        def add_kernel(me_ref, *refs):
+            for kf in range(n_feat):
+                total = refs[0][kf].astype(F32)
+                for kr in range(1, n_rep):
+                    total += refs[kr][kf].astype(F32)
+                refs[n_rep + kf][...] = total.astype(BF)
+
+        halves = call(add_kernel, name, me1, arrived, [shape(parts[0].shape[1:])] * n_feat)
+        return [halves[0]] + [member_swap(halves[kf], kf * n_rep) for kf in range(1, n_feat)]
+
     def dom_trade(parts):
         return [parts[0]] + [dom_swap(parts[k], k) for k in range(1, n_dom)]
-
-    def dom_order(table, dom):
-        bit = 1
-        while bit < n_dom:
-            pairs = table.reshape((n_dom // (2 * bit), 2, bit) + table.shape[1:])
-            swapped = pairs[:, ::-1].reshape(table.shape)
-            table = jnp.where((dom & bit) != 0, swapped, table)
-            bit *= 2
-        return table
 
     def per_device(
         grid_state,
@@ -149,25 +154,69 @@
         dom = lax.axis_index("dom").astype(jnp.int32)
         me1 = me.reshape(1)
 
-        slots = jnp.stack(
-            [dom_order(grid_send[0], dom).reshape(-1), dom_order(grid_recv[0], dom).reshape(-1)]
-        )
-        halo_row = dom_order(halo_rows[0], dom).reshape(1, NH)
+        where = jnp.stack([me, dom])
         recv_row = edge_recv.reshape(1, E)
-        away = edge_send - N
-        send_row = jnp.where(away < 0, edge_send, N + ((away // H) ^ dom) * H + away % H).reshape(1, E)
+
+        def tables_kernel(where_ref, gs_ref, gr_ref, halo_ref, send_ref, slot_out, halo_out, send_out):
+            dom = where_ref[1]
+            for j in range(n_dom):
+                at, to = pl.ds(dom ^ j, 1), slice(j * S, (j + 1) * S)
+                slot_out[0:1, to] = gs_ref[0, at, :]
+                slot_out[1:2, to] = gr_ref[0, at, :]
+                halo_out[:, j * H : (j + 1) * H] = halo_ref[0, at, :]
+            sent = send_ref[...]
+            away = jnp.maximum(sent - N, 0)
+            peer = away // H
+            send_out[...] = jnp.where(sent < N, sent, N + (peer ^ dom) * H + (away - peer * H))
+
+        slots, halo_row, send_row = call(
+            tables_kernel,
+            "tables",
+            where,
+            [grid_send, grid_recv, halo_rows, edge_send.reshape(1, E)],
+            [shape((2, NS), jnp.int32), shape((1, NH), jnp.int32), shape((1, E), jnp.int32)],
+        )
 
         state_parts = member_gather_chips(grid_state)
         enc_parts = member_gather_chips(enc_weight)
         slot_parts = member_gather(slots)
-        in_parts = member_gather_chips(edge_in_weight)
-        rest = jnp.concatenate([edge_out_weight, node_in_weight, node_out_weight], axis=0)
-        rest_parts = member_gather_chips(rest)
-
-        def grid_kernel(me_ref, *refs):
+
+        def relay_kernel(me_ref, weight_ref, arrived_ref, out_ref):
+            out_ref[...] = weight_ref[...]
+
+        edge_in_own = call(
+            relay_kernel,
+            "relay",
+            me1,
+            [edge_in_weight, state_parts[n_rep]],
+            [shape((rows_in, D))],
+            unread=1,
+        )[0]
+        in_parts = member_gather_chips(edge_in_own)
+
+        def hots_kernel(me_ref, send_ref, recv_ref, sl_out, sh_out, r_out, slt_out, sht_out, rt_out):
+            for i in range(E // T):
+                at = slice(i * T, (i + 1) * T)
+                sent, got = send_ref[:, at], recv_ref[:, at]
+                sl_out[at, :] = hot_rows(sent, N)
+                sh_out[at, :] = hot_rows(sent - N, NH)
+                r_out[at, :] = hot_rows(got, N)
+                slt_out[:, at] = hot_columns(sent, N)
+                sht_out[:, at] = hot_columns(sent - N, NH)
+                rt_out[:, at] = hot_columns(got, N)
+
+        sl_hot, sh_hot, r_hot, slt_hot, sht_hot, rt_hot = call(
+            hots_kernel,
+            "edge_hots",
+            me1,
+            [send_row, recv_row],
+            [shape((E, N)), shape((E, NH)), shape((E, N)), shape((N, E)), shape((NH, E)), shape((N, E))],
+        )
+
+        def grid_kernel(me_ref, out_ref, node_in_ref, node_out_ref, *refs):
             states, encs, tables = refs[:M], refs[M : 2 * M], refs[2 * M : 3 * M]
-            enc_out, slope_out = refs[3 * M], refs[3 * M + 1]
-            outs = refs[3 * M + 2 :]
+            enc_out, slope_out, rest_out = refs[3 * M : 3 * M + 3]
+            outs = refs[3 * M + 3 :]
             me = me_ref[0]
             for k in range(M):
                 enc_out[rows_at(me ^ k, rows_enc), :] = encs[k][...]
@@ -180,16 +229,21 @@
                 rows = dot(hot_rows(tables[k][0:1, :], G), message).astype(BF)
                 for j in range(n_dom):
                     outs[j][k * S : (k + 1) * S, :] = rows[j * S : (j + 1) * S]
-
-        enc_full, grid_slope, *outgoing = call(
+            rest_out[:rows_out, :] = out_ref[...]
+            rest_out[rows_out : rows_out + rows_node, :] = node_in_ref[...]
+            rest_out[rows_out + rows_node :, :] = node_out_ref[...]
+
+        enc_full, grid_slope, rest, *outgoing = call(
             grid_kernel,
             "grid_messages",
             me1,
-            state_parts + enc_parts + slot_parts,
-            [shape((D, D)), shape((M, G, C), F32)] + [shape((M * S, C))] * n_dom,
+            [edge_out_weight, node_in_weight, node_out_weight] + state_parts + enc_parts + slot_parts,
+            [shape((D, D)), shape((M, G, C), F32), shape((2 * rows_out + rows_node, D))]
+            + [shape((M * S, C))] * n_dom,
             flops=2 * M * G * D * C + 2 * M * NS * G * C,
         )
         incoming = dom_trade(outgoing)
+        rest_parts = member_gather_chips(rest)
 
         def encode_kernel(me_ref, base_ref, halo_ref, *refs):
             tables, arrived = refs[:M], refs[M : M + n_dom]
@@ -213,9 +267,9 @@
             flops=2 * M * N * NS * C,
         )
         halo_in = dom_trade(halo_out)
-        state_parts2 = member_gather(state_cols)
+        state_parts2 = member_gather_chips(state_cols)
         halo_cols = jnp.concatenate(halo_in, axis=0)
-        halo_parts = member_gather(halo_cols)
+        halo_parts = member_gather_chips(halo_cols)
 
         def local_kernel(me_ref, es_ref, send_ref, recv_ref, *refs):
             cols, weights = refs[:M], refs[M : 2 * M]
@@ -225,25 +279,21 @@
                 parts[me ^ k] = cols[k][...]
                 w_out[rows_at(me ^ k, rows_in), :] = weights[k][...]
             state_out[...] = lanes([parts[j] for j in range(M)])
-
-            def step(i, _):
-                at = rows_at(i, T)
-                sent = dot(hot_rows(send_ref[:, at], N), state_out[...]).astype(BF)
-                got = dot(hot_rows(recv_ref[:, at], N), state_out[...]).astype(BF)
+            for i in range(E // T):
+                at = slice(i * T, (i + 1) * T)
+                sent = dot(send_ref[at, :], state_out[...]).astype(BF)
+                got = dot(recv_ref[at, :], state_out[...]).astype(BF)
                 pre_out[at, :] = (
                     dot(es_ref[at, :], w_out[:D, :])
                     + dot(sent, w_out[D : 2 * D, :])
                     + dot(got, w_out[2 * D :, :])
                 )
-                return 0
-
-            lax.fori_loop(0, E // T, step, 0)
 
         local_pre, mesh_state, in_full = call(
             local_kernel,
             "edge_local",
             me1,
-            [edge_state, send_row, recv_row] + state_parts2 + in_parts,
+            [edge_state, sl_hot, r_hot] + state_parts2 + in_parts,
             [shape((E, D), F32), shape((N, D)), shape((3 * D, D))],
             scratch=[pltpu.VMEM((M, N, C), BF)],
             flops=2 * E * D * (3 * D + 2 * N),
@@ -274,43 +324,46 @@
 
         def edge_kernel(me_ref, local_ref, es_ref, send_ref, recv_ref, w_ref, out_ref, *refs):
             cols = refs[:M]
-            pre_out, outs = refs[M], refs[M + 1 : 2 * M + 1]
-            parts, halo, total = refs[2 * M + 1 :]
+            pre_out, outs = refs[M], refs[M + 1 : M + 1 + n_rep]
+            parts, halo, new, total = refs[M + 1 + n_rep :]
             me = me_ref[0]
             for k in range(M):
                 parts[me ^ k] = cols[k][...]
             halo[...] = lanes([parts[j] for j in range(M)])
-            total[...] = jnp.zeros_like(total)
-
-            def step(i, _):
-                at = rows_at(i, T)
-                sent = dot(hot_rows(send_ref[:, at] - N, NH), halo[...]).astype(BF)
+            for i in range(E // T):
+                at = slice(i * T, (i + 1) * T)
+                sent = dot(send_ref[at, :], halo[...]).astype(BF)
                 pre = local_ref[at, :] + dot(sent, w_ref[D : 2 * D, :])
                 pre_out[at, :] = pre
                 hidden = (pre * jax.nn.sigmoid(pre)).astype(BF)
-                new = (es_ref[at, :].astype(F32) + dot(hidden, out_ref[...])).astype(BF)
-                total[...] += dot(hot_columns(recv_ref[:, at], N), new)
-                return 0
-
-            lax.fori_loop(0, E // T, step, 0)
-            for k in range(M):
-                outs[k][...] = total[rows_at(me ^ k, R), :].astype(BF)
+                new[at, :] = (es_ref[at, :].astype(F32) + dot(hidden, out_ref[...])).astype(BF)
+            for i in range(N // T):
+                at = slice(i * T, (i + 1) * T)
+                total[at, :] = dot(recv_ref[at, :], new[...]).astype(BF)
+            for kr in range(n_rep):
+                for kf in range(n_feat):
+                    outs[kr][kf] = total[rows_at(me ^ (kf * n_rep + kr), R), :]
 
         edge_pre, *sums = call(
             edge_kernel,
             "edge_update",
             me1,
-            [local_pre, edge_state, send_row, recv_row, in_full, out_full] + halo_parts,
-            [shape((E, D), F32)] + [shape((R, D))] * M,
-            scratch=[pltpu.VMEM((M, NH, C), BF), pltpu.VMEM((NH, D), BF), pltpu.VMEM((N, D), F32)],
+            [local_pre, edge_state, sh_hot, rt_hot, in_full, out_full] + halo_parts,
+            [shape((E, D), F32)] + [shape((n_feat, R, D))] * n_rep,
+            scratch=[
+                pltpu.VMEM((M, NH, C), BF),
+                pltpu.VMEM((NH, D), BF),
+                pltpu.VMEM((E, D), BF),
+                pltpu.VMEM((N, D), BF),
+            ],
             flops=2 * E * D * (NH + D + D + N),
         )
-        sums = member_trade(sums)
+        sums = member_sums(sums, me1, "node_sums")
 
         def node_kernel(me_ref, pre_ref, cot_ref, w_ref, grad_ref, *refs):
-            first_out, second_out = refs[M:]
+            first_out, second_out = refs[n_feat:]
             total = refs[0][...].astype(F32)
-            for k in range(1, M):
+            for k in range(1, n_feat):
                 total += refs[k][...].astype(F32)
             pre = pre_ref[...] + dot(total.astype(BF), w_ref[D:, :])
             dpre = (cot_ref[...] * silu_slope(pre)).astype(BF)
@@ -326,92 +379,82 @@
             [shape((R, D), F32), shape((R, D))],
             flops=6 * R * D * D,
         )
-        second_parts = member_gather(node_second)
+        second_parts = member_gather_chips(node_second)
 
         def edge_back_kernel(me_ref, grad_ref, pre_ref, send_ref, recv_ref, w_ref, out_ref, *refs):
             nodes = refs[:M]
-            dpre_out, outs = refs[M], refs[M + 1 : 2 * M + 1]
-            second, total, parts = refs[2 * M + 1 :]
+            dpre_out, outs = refs[M], refs[M + 1 : M + 1 + n_rep]
+            second, parts = refs[M + 1 + n_rep :]
             me = me_ref[0]
             for k in range(M):
                 second[rows_at(me ^ k, R), :] = nodes[k][...]
-            total[...] = jnp.zeros_like(total)
-
-            def step(i, _):
-                at = rows_at(i, T)
-                got = dot(hot_rows(recv_ref[:, at], N), second[...])
+            for i in range(E // T):
+                at = slice(i * T, (i + 1) * T)
+                got = dot(recv_ref[at, :], second[...])
                 cot = (grad_ref[at, :].astype(F32) + got).astype(BF)
-                dpre = (dot_t(cot, out_ref[...]) * silu_slope(pre_ref[at, :])).astype(BF)
-                dpre_out[at, :] = dpre
-                total[...] += dot(hot_columns(send_ref[:, at] - N, NH), dpre)
-                return 0
-
-            lax.fori_loop(0, E // T, step, 0)
-            halo = dot_t(total[...].astype(BF), w_ref[D : 2 * D, :]).astype(BF)
-            for j in range(M):
-                parts[j] = halo[:, j * C : (j + 1) * C]
-            for k in range(M):
-                outs[k][...] = parts[me ^ k]
+                dpre_out[at, :] = (dot_t(cot, out_ref[...]) * silu_slope(pre_ref[at, :])).astype(BF)
+            for i in range(NH // T):
+                at = slice(i * T, (i + 1) * T)
+                sent = dot(send_ref[at, :], dpre_out[...]).astype(BF)
+                halo = dot_t(sent, w_ref[D : 2 * D, :]).astype(BF)
+                for j in range(M):
+                    parts[j, at, :] = halo[:, j * C : (j + 1) * C]
+            for kr in range(n_rep):
+                for kf in range(n_feat):
+                    outs[kr][kf] = parts[me ^ (kf * n_rep + kr)]
 
         edge_dpre, *halo_grads = call(
             edge_back_kernel,
             "edge_backward",
             me1,
-            [edge_grad, edge_pre, send_row, recv_row, in_full, out_full] + second_parts,
-            [shape((E, D))] + [shape((NH, C))] * M,
-            scratch=[pltpu.VMEM((N, D), BF), pltpu.VMEM((NH, D), F32), pltpu.VMEM((M, NH, C), BF)],
+            [edge_grad, edge_pre, sht_hot, r_hot, in_full, out_full] + second_parts,
+            [shape((E, D))] + [shape((n_feat, NH, C))] * n_rep,
+            scratch=[pltpu.VMEM((N, D), BF), pltpu.VMEM((M, NH, C), BF)],
             flops=2 * E * D * (N + D + NH) + 2 * NH * D * D,
         )
-        halo_grads = member_trade(halo_grads)
+        halo_grads = member_sums(halo_grads, me1, "halo_pairs")
 
         def local_back_kernel(me_ref, dpre_ref, send_ref, recv_ref, w_ref, first_ref, *refs):
-            outs, (sent, got, parts) = refs[:M], refs[M:]
+            outs, (total, parts) = refs[:n_rep], refs[n_rep:]
             me = me_ref[0]
-            sent[...] = jnp.zeros_like(sent)
-            got[...] = jnp.zeros_like(got)
-
-            def step(i, _):
-                at = rows_at(i, T)
-                sent[...] += dot(hot_columns(send_ref[:, at], N), dpre_ref[at, :])
-                got[...] += dot(hot_columns(recv_ref[:, at], N), dpre_ref[at, :])
-                return 0
-
-            lax.fori_loop(0, E // T, step, 0)
-            sent[...] = dot_t(sent[...].astype(BF), w_ref[D : 2 * D, :]) + dot_t(
-                got[...].astype(BF), w_ref[2 * D :, :]
-            )
-            sent[rows_at(me, R), :] += first_ref[...]
+            for i in range(N // T):
+                at = slice(i * T, (i + 1) * T)
+                sent = dot(send_ref[at, :], dpre_ref[...]).astype(BF)
+                got = dot(recv_ref[at, :], dpre_ref[...]).astype(BF)
+                total[at, :] = dot_t(sent, w_ref[D : 2 * D, :]) + dot_t(got, w_ref[2 * D :, :])
+            total[rows_at(me, R), :] += first_ref[...]
             for j in range(M):
-                parts[j] = sent[:, j * C : (j + 1) * C].astype(BF)
-            for k in range(M):
-                outs[k][...] = parts[me ^ k]
+                parts[j] = total[:, j * C : (j + 1) * C].astype(BF)
+            for kr in range(n_rep):
+                for kf in range(n_feat):
+                    outs[kr][kf] = parts[me ^ (kf * n_rep + kr)]
 
         local_grads = call(
             local_back_kernel,
             "local_backward",
             me1,
-            [edge_dpre, send_row, recv_row, in_full, node_first],
-            [shape((N, C))] * M,
-            scratch=[pltpu.VMEM((N, D), F32), pltpu.VMEM((N, D), F32), pltpu.VMEM((M, N, C), BF)],
+            [edge_dpre, slt_hot, rt_hot, in_full, node_first],
+            [shape((n_feat, N, C))] * n_rep,
+            scratch=[pltpu.VMEM((N, D), F32), pltpu.VMEM((M, N, C), BF)],
             flops=4 * E * D * N + 4 * N * D * D,
         )
-        local_grads = member_trade(local_grads)
+        local_grads = member_sums(local_grads, me1, "local_pairs")
 
         def halo_sum_kernel(me_ref, *refs):
             total = refs[0][...].astype(F32)
-            for k in range(1, M):
+            for k in range(1, n_feat):
                 total += refs[k][...].astype(F32)
             for j in range(n_dom):
-                refs[M + j][...] = total[j * H : (j + 1) * H].astype(BF)
+                refs[n_feat + j][...] = total[j * H : (j + 1) * H].astype(BF)
 
         halo_back = call(halo_sum_kernel, "halo_sums", me1, halo_grads, [shape((H, C))] * n_dom)
         halo_back = dom_trade(halo_back)
 
         def owed_kernel(me_ref, halo_ref, *refs):
-            tables, local, back = refs[:M], refs[M : 2 * M], refs[2 * M : 2 * M + n_dom]
-            outs = refs[2 * M + n_dom :]
+            tables, local = refs[:M], refs[M : M + n_feat]
+            back, outs = refs[M + n_feat : M + n_feat + n_dom], refs[M + n_feat + n_dom :]
             total = local[0][...].astype(F32)
-            for k in range(1, M):
+            for k in range(1, n_feat):
                 total += local[k][...].astype(F32)
             rows = stack([back[j][...] for j in range(n_dom)])
             cot = (total + dot(hot_columns(halo_ref[...], N), rows)).astype(BF)

time: 138 us -> 130 us (0.942)
  Pallas kernels: 29.5 us -> 20.7 us
  other arithmetic: 3.48 us -> 0.07 us
  starting transfers between devices: 44 us -> 46.9 us
    pallas_call x12 -> x18, Pallas kernels: 29.5 us -> 20.7 us  [call(): pl.pallas_call(body, out_shape=list(outs), in_specs=[SMEM] + [VMEM] * (le...]
    ppermute x36 -> x33, waiting for transfers between devices: 28.2 us -> 34.8 us  [member_swap(): return lax.ppermute(x, ('feat', 'rep'), [(i, i ^ k) for i in range(M)])]
    ppermute x12, waiting for transfers between devices: 25.2 us -> 19.2 us  [dom_swap(): return lax.ppermute(x, 'dom', [(i, i ^ k) for i in range(n_dom)])]
    ppermute x12, starting transfers between devices: 21.2 us -> 25.1 us  [dom_swap(): return lax.ppermute(x, 'dom', [(i, i ^ k) for i in range(n_dom)])]
    unnamed x23 -> x33, local copies, waits for them, and re-layouts: 3.78 us -> 7.38 us
    select_n x6 -> x0, other arithmetic: 3.47 us -> none  [the longest x5 2.77 us: dom_order(): table = jnp.where(dom & bit != 0, swapped, table)]
    rev x6 -> x0, local copies, waits for them, and re-layouts: 2.2 us -> none  [dom_order(): swapped = pairs[:, ::-1].reshape(table.shape)]
    ppermute x36 -> x33, starting transfers between devices: 22.8 us -> 21.7 us  [member_swap(): return lax.ppermute(x, ('feat', 'rep'), [(i, i ^ k) for i in range(M)])]
  transfers between devices with their start and end apart: 48 -> 45, of which waited for: 19 -> 23; matrix products, arithmetic and copies ran while one was open for 4% -> 0% of each run, Pallas kernels for 9% -> 8%
where the time goes in v2:
time: 130 us; the launch traced here: 129 us
  waiting for transfers between devices  54 us (42%)
  starting transfers between devices  46.9 us (36%)
  Pallas kernels  20.7 us (16%)
  local copies, waits for them, and re-layouts  7.39 us (6%)
    ppermute x33, waiting for transfers between devices, member_swap(): return lax.ppermute(x, ('feat', 'rep'), [(i, i ^ k) for i in range(M)])  34.8 us
    ppermute x12, starting transfers between devices, dom_swap(): return lax.ppermute(x, 'dom', [(i, i ^ k) for i in range(n_dom)])  25.1 us
    ppermute x33, starting transfers between devices, member_swap(): return lax.ppermute(x, ('feat', 'rep'), [(i, i ^ k) for i in range(M)])  21.7 us
    pallas_call x18, Pallas kernels, call(): pl.pallas_call(body, out_shape=list(outs), in_specs=[SMEM] + [VMEM] * (le...  20.7 us
    ppermute x12, waiting for transfers between devices, dom_swap(): return lax.ppermute(x, 'dom', [(i, i ^ k) for i in range(n_dom)])  19.2 us
    unnamed x33, local copies, waits for them, and re-layouts  7.38 us
  transfers between devices with their start and end apart: 45, of which 23 were waited for; matrix products, arithmetic and copies ran while one was open for 0% of the time, Pallas kernels for 8%

profile of v2, /device:TPU:0, one launch (start us, length us, event | category | flops | bytes accessed | tf_op | source)
XLA Modules:
  0.0 129.3 jit_solution(10155015963457953070)
XLA Ops:
  0.0 2.9 %collective-permute-start.1 = (bf16[256,512]{1,0:T(8,128)(2,1)}, bf16[256,512]{1,0:T(8,128)(2,1)S(1)}, u32[]{:S(2)}, u32[]{:S(2)}) collective-permute-start(bf16[256,512]{1,0:T(8,128)(2,1)} %refs_0_.1), channel_id=1, source_target_pairs={{0,2},{1,3},{2,0},{3,1},{4,6},{5,7},{6,4},{7,5},{8,10},{9,11},{10,... | collective-permute-start | bytes 786440 | tf_op jit(solution)/shard_map/ppermute | solution.py:83
  3.1 7.2 %collective-permute-done.1.refs_2_.arrived_ref = bf16[256,512]{1,0:T(8,128)(2,1)S(1)} collective-permute-done((bf16[256,512]{1,0:T(8,128)(2,1)}, bf16[256,512]{1,0:T(8,128)(2,1)S(1)}, u32[]{:S(2)}, u32[]{:S(2)}) %collective-permute-start.1) | collective-permute-done | bytes 262176 | tf_op jit(solution)/shard_map/ppermute | solution.py:83
  10.8 1.5 %collective-permute-done.4.refs_6_ = bf16[128,512]{1,0:T(8,128)(2,1)S(1)} collective-permute-done((bf16[128,512]{1,0:T(8,128)(2,1)}, bf16[128,512]{1,0:T(8,128)(2,1)S(1)}, u32[]{:S(2)}, u32[]{:S(2)}) %collective-permute-start.4) | collective-permute-done | bytes 131104 | tf_op jit(solution)/shard_map/ppermute | solution.py:83
  17.0 1.7 %collective-permute-start.7 = (s32[2,512]{1,0:T(2,128)S(1)}, s32[2,512]{1,0:T(2,128)S(1)}, u32[]{:S(2)}, u32[]{:S(2)}) collective-permute-start(s32[2,512]{1,0:T(2,128)S(1)} %get-tuple-element.61.refs_8_.refs_0_), channel_id=1, source_target_pairs={{0,2},{1,3},{2,0},{3,1},{4,6},{5,7},{6,4},{7,5},{8,10},{9,11},{10,... | collective-permute-start | bytes 12296 | tf_op jit(solution)/shard_map/ppermute | solution.py:83
  18.8 1.9 %collective-permute-done.7.refs_10_.refs_2_ = s32[2,512]{1,0:T(2,128)S(1)} collective-permute-done((s32[2,512]{1,0:T(2,128)S(1)}, s32[2,512]{1,0:T(2,128)S(1)}, u32[]{:S(2)}, u32[]{:S(2)}) %collective-permute-start.7) | collective-permute-done | bytes 4128 | tf_op jit(solution)/shard_map/ppermute | solution.py:83
  21.2 2.5 %collective-permute-done.8.refs_11_.refs_3_ = s32[2,512]{1,0:T(2,128)S(1)} collective-permute-done((s32[2,512]{1,0:T(2,128)S(1)}, s32[2,512]{1,0:T(2,128)S(1)}, u32[]{:S(2)}, u32[]{:S(2)}) %collective-permute-start.8) | collective-permute-done | bytes 4128 | tf_op jit(solution)/shard_map/ppermute | solution.py:83
  23.7 0.9 copy-done.4
  24.7 0.9 copy-done.5
  25.6 0.9 copy-done.6
  26.5 0.9 copy-done.7
  28.3 1.5 %grid_messages.1 = (bf16[512,512]{1,0:T(8,128)(2,1)S(1)}, f32[4,256,128]{2,1,0:T(8,128)S(1)}, bf16[512,512]{1,0:T(8,128)(2,1)S(1)}, bf16[512,128]{1,0:T(8,128)(2...) custom-call(s32[1]{0:T(128)} %bitcast.me_ref, ...), custom_call_target="tpu_custom_call" | custom-call | flops 268435456 | bytes 4210688 | tf_op jit(solution)/shard_map/grid_messages/pallas_call | solution.py:62
  29.8 1.8 %collective-permute-start.19 = (bf16[512,512]{1,0:T(8,128)(2,1)S(1)}, bf16[512,512]{1,0:T(8,128)(2,1)S(1)}, u32[]{:S(2)}, u32[]{:S(2)}) collective-permute-start(bf16[512,512]{1,0:T(8,128)(2,1)S(1)} %get-tuple-element.78.refs_0_), channel_id=1, source_target_pairs={{0,2},{1,3},{2,0},{3,1},{4,6},{5,7},{6,4},{7,5},{8,10},{9,11},{10,... | collective-permute-start | bytes 1572872 | tf_op jit(solution)/shard_map/ppermute | solution.py:83
  31.6 1.6 %collective-permute-start.9 = (bf16[512,128]{1,0:T(8,128)(2,1)S(1)}, bf16[512,128]{1,0:T(8,128)(2,1)S(1)}, u32[]{:S(2)}, u32[]{:S(2)}) collective-permute-start(bf16[512,128]{1,0:T(8,128)(2,1)S(1)} %get-tuple-element.69), channel_id=1, source_target_pairs={{0,4},{4,0},{8,12},{12,8},{1,5},{5,1},{9,13},{13,9},{2,6},{6,2},{1... | collective-permute-start | bytes 393224 | tf_op jit(solution)/shard_map/ppermute | solution.py:86
  33.9 2.6 %collective-permute-start.10 = (bf16[512,128]{1,0:T(8,128)(2,1)S(1)}, bf16[512,128]{1,0:T(8,128)(2,1)S(1)}, u32[]{:S(2)}, u32[]{:S(2)}) collective-permute-start(bf16[512,128]{1,0:T(8,128)(2,1)S(1)} %get-tuple-element.70), channel_id=1, source_target_pairs={{0,8},{4,12},{8,0},{12,4},{1,9},{5,13},{9,1},{13,5},{2,10},{6,14},... | collective-permute-start | bytes 393224 | tf_op jit(solution)/shard_map/ppermute | solution.py:86
  36.6 3.6 %collective-permute-start.11 = (bf16[512,128]{1,0:T(8,128)(2,1)S(1)}, bf16[512,128]{1,0:T(8,128)(2,1)S(1)}, u32[]{:S(2)}, u32[]{:S(2)}) collective-permute-start(bf16[512,128]{1,0:T(8,128)(2,1)S(1)} %get-tuple-element.71), channel_id=1, source_target_pairs={{0,12},{4,8},{8,4},{12,0},{1,13},{5,9},{9,5},{13,1},{2,14},{6,10},... | collective-permute-start | bytes 393224 | tf_op jit(solution)/shard_map/ppermute | solution.py:86
  40.2 6.2 %collective-permute-done.10.refs_6_ = bf16[512,128]{1,0:T(8,128)(2,1)S(1)} collective-permute-done((bf16[512,128]{1,0:T(8,128)(2,1)S(1)}, bf16[512,128]{1,0:T(8,128)(2,1)S(1)}, u32[]{:S(2)}, u32[]{:S(2)}) %collective-permute-start.10) | collective-permute-done | bytes 131104 | tf_op jit(solution)/shard_map/ppermute | solution.py:86
  46.4 1.4 %encode.1 = (bf16[512,128]{1,0:T(8,128)(2,1)S(1)}, bf16[128,128]{1,0:T(8,128)(2,1)S(1)}, bf16[128,128]{1,0:T(8,128)(2,1)S(1)}, bf16[128,128]{1,0:T(8,128)(2,1)S(1)}, bf16[128,128]{1,0:T(8,128)(2,1)S(1)}) custom-call(s32[1]{0:T(128)} %bitcast.me_ref, bf16[512,512]{1,0:T(8,128)(2,1)S(1)} %copy-done.2, s32[1,512]{1,0:T(1,128)S(1)} %get-tuple-element.64.halo_ref, ...), custom_call_target="tpu_custom_call" | custom-call | flops 268435456 | bytes 1329152 | tf_op jit(solution)/shard_map/encode/pallas_call | solution.py:62
  47.8 3.2 %collective-permute-start.21 = (bf16[128,128]{1,0:T(8,128)(2,1)S(1)}, bf16[128,128]{1,0:T(8,128)(2,1)S(1)}, u32[]{:S(2)}, u32[]{:S(2)}) collective-permute-start(bf16[128,128]{1,0:T(8,128)(2,1)S(1)} %get-tuple-element.81), channel_id=1, source_target_pairs={{0,4},{4,0},{8,12},{12,8},{1,5},{5,1},{9,13},{13,9},{2,6},{6,2},{1... | collective-permute-start | bytes 98312 | tf_op jit(solution)/shard_map/ppermute | solution.py:86
  51.0 1.2 collective-permute-start.22
  52.3 3.9 %collective-permute-start.23 = (bf16[128,128]{1,0:T(8,128)(2,1)S(1)}, bf16[128,128]{1,0:T(8,128)(2,1)S(1)}, u32[]{:S(2)}, u32[]{:S(2)}) collective-permute-start(bf16[128,128]{1,0:T(8,128)(2,1)S(1)} %get-tuple-element.83), channel_id=1, source_target_pairs={{0,12},{4,8},{8,4},{12,0},{1,13},{5,9},{9,5},{13,1},{2,14},{6,10},... | collective-permute-start | bytes 98312 | tf_op jit(solution)/shard_map/ppermute | solution.py:86
  56.8 1.2 collective-permute-done.23
  58.0 1.4 %collective-permute-start.13 = (bf16[512,128]{1,0:T(8,128)(2,1)S(1)}, bf16[512,128]{1,0:T(8,128)(2,1)S(1)}, u32[]{:S(2)}, u32[]{:S(2)}) collective-permute-start(bf16[512,128]{1,0:T(8,128)(2,1)S(1)} %get-tuple-element.72.refs_0_), channel_id=1, source_target_pairs={{0,2},{1,3},{2,0},{3,1},{4,6},{5,7},{6,4},{7,5},{8,10},{9,11},{10,... | collective-permute-start | bytes 393224 | tf_op jit(solution)/shard_map/ppermute | solution.py:83
  60.2 3.2 %collective-permute-done.13.refs_2_ = bf16[512,128]{1,0:T(8,128)(2,1)S(1)} collective-permute-done((bf16[512,128]{1,0:T(8,128)(2,1)S(1)}, bf16[512,128]{1,0:T(8,128)(2,1)S(1)}, u32[]{:S(2)}, u32[]{:S(2)}) %collective-permute-start.13) | collective-permute-done | bytes 131104 | tf_op jit(solution)/shard_map/ppermute | solution.py:83
  63.4 2.1 %edge_hots.1 = (bf16[1024,512]{1,0:T(8,128)(2,1)S(1)}, bf16[1024,512]{1,0:T(8,128)(2,1)S(1)}, bf16[1024,512]{1,0:T(8,128)(2,1)S(1)}, bf16[512,1024]{1,0:T(8,128)...) custom-call(s32[1]{0:T(128)} %bitcast.me_ref, s32[1,1024]{1,0:T(1,128)S(1)} %get-tuple-element.65.send_ref, ...), custom_call_target="tpu_custom_call" | custom-call | bytes 6299648 | tf_op jit(solution)/shard_map/edge_hots/pallas_call | solution.py:62
  66.3 3.0 %edge_local.1 = (f32[1024,512]{1,0:T(8,128)S(1)}, bf16[512,512]{1,0:T(8,128)(2,1)S(1)}, bf16[1536,512]{1,0:T(8,128)(2,1)S(1)}) custom-call(s32[1]{0:T(128)} %bitcast.me_ref, bf16[1024,512]{1,0:T(8,128)(2,1)S(1)} %copy-done.14, bf16[1024,512]{1,0:T(8,128)(2,1)S(1)} %get-tuple-element.66.send_ref, bf16[1024,512]{1,0:T(8,128)(2,1)S(1)} %get-tuple-element.67.recv_ref, ...), custom_call_target="tpu_custom_call" | custom-call | flops 2684354560 | bytes 9437184 | tf_op jit(solution)/shard_map/edge_local/pallas_call | solution.py:62
  69.9 3.2 %edge_update.1 = (f32[1024,512]{1,0:T(8,128)S(1)}, bf16[2,128,512]{2,1,0:T(8,128)(2,1)S(1)}, bf16[2,128,512]{2,1,0:T(8,128)(2,1)S(1)}) custom-call(s32[1]{0:T(128)} %bitcast.me_ref, f32[1024,512]{1,0:T(8,128)S(1)} %get-tuple-element.73.local_ref, bf16[1024,512]{1,0:T(8,128)(2,1)S(1)} %copy-done.14, bf16[1024,512]{1,0:T(8,128)(2,1)S(1)} %get-tuple-element.74.send_ref, ...), custom_call_target="tpu_custom_call" | custom-call | flops 2147483648 | bytes 10485760 | tf_op jit(solution)/shard_map/edge_update/pallas_call | solution.py:62
  73.4 1.3 collective-permute-done.27.refs_1_
  74.8 2.1 %collective-permute-start.28 = (bf16[128,512]{1,0:T(8,128)(2,1)S(1)}, bf16[128,512]{1,0:T(8,128)(2,1)S(1)}, u32[]{:S(2)}, u32[]{:S(2)}) collective-permute-start(bf16[128,512]{1,0:T(8,128)(2,1)S(1)} %get-tuple-element.92), channel_id=1, source_target_pairs={{0,2},{1,3},{2,0},{3,1},{4,6},{5,7},{6,4},{7,5},{8,10},{9,11},{10,... | collective-permute-start | bytes 393224 | tf_op jit(solution)/shard_map/ppermute | solution.py:83
  76.9 4.0 %collective-permute-done.28.refs_1_ = bf16[128,512]{1,0:T(8,128)(2,1)S(1)} collective-permute-done((bf16[128,512]{1,0:T(8,128)(2,1)S(1)}, bf16[128,512]{1,0:T(8,128)(2,1)S(1)}, u32[]{:S(2)}, u32[]{:S(2)}) %collective-permute-start.28) | collective-permute-done | bytes 131104 | tf_op jit(solution)/shard_map/ppermute | solution.py:83
  81.5 2.0 %collective-permute-start.30 = (bf16[128,512]{1,0:T(8,128)(2,1)S(1)}, bf16[128,512]{1,0:T(8,128)(2,1)S(1)}, u32[]{:S(2)}, u32[]{:S(2)}) collective-permute-start(bf16[128,512]{1,0:T(8,128)(2,1)S(1)} %get-tuple-element.93.refs_0_), channel_id=1, source_target_pairs={{0,2},{1,3},{2,0},{3,1},{4,6},{5,7},{6,4},{7,5},{8,10},{9,11},{10,... | collective-permute-start | bytes 393224 | tf_op jit(solution)/shard_map/ppermute | solution.py:83
  83.5 3.5 %collective-permute-done.30.refs_2_ = bf16[128,512]{1,0:T(8,128)(2,1)S(1)} collective-permute-done((bf16[128,512]{1,0:T(8,128)(2,1)S(1)}, bf16[128,512]{1,0:T(8,128)(2,1)S(1)}, u32[]{:S(2)}, u32[]{:S(2)}) %collective-permute-start.30) | collective-permute-done | bytes 131104 | tf_op jit(solution)/shard_map/ppermute | solution.py:83
  87.0 1.3 %collective-permute-done.31.refs_3_ = bf16[128,512]{1,0:T(8,128)(2,1)S(1)} collective-permute-done((bf16[128,512]{1,0:T(8,128)(2,1)S(1)}, bf16[128,512]{1,0:T(8,128)(2,1)S(1)}, u32[]{:S(2)}, u32[]{:S(2)}) %collective-permute-start.31) | collective-permute-done | bytes 131104 | tf_op jit(solution)/shard_map/ppermute | solution.py:83
  88.3 2.7 %edge_backward.1 = (bf16[1024,512]{1,0:T(8,128)(2,1)S(1)}, bf16[2,512,128]{2,1,0:T(8,128)(2,1)S(1)}, bf16[2,512,128]{2,1,0:T(8,128)(2,1)S(1)}) custom-call(s32[1]{0:T(128)} %bitcast.me_ref, bf16[1024,512]{1,0:T(8,128)(2,1)S(1)} %copy-done.1, f32[1024,512]{1,0:T(8,128)S(1)} %get-tuple-element.84.pre_ref, bf16[512,1024]{1,0:T(8,128)(2,1)S(1)} %get-tuple-element.85.send_ref, ...), custom_call_target="tpu_custom_call" | custom-call | flops 1879048192 | bytes 9437184 | tf_op jit(solution)/shard_map/edge_backward/pallas_call | solution.py:62
  91.3 2.1 %local_backward.1 = (bf16[2,512,128]{2,1,0:T(8,128)(2,1)S(1)}, bf16[2,512,128]{2,1,0:T(8,128)(2,1)S(1)}) custom-call(s32[1]{0:T(128)} %bitcast.me_ref, bf16[1024,512]{1,0:T(8,128)(2,1)S(1)} %get-tuple-element.94.dpre_ref, bf16[512,1024]{1,0:T(8,128)(2,1)S(1)} %get-tuple-element.95.send_ref, bf16[512,1024]{1,0:T(8,128)(2,1)S(1)} %get-tuple-element.75.recv_ref, ...), custom_call_target="tpu_custom_call" | custom-call | flops 1610612736 | bytes 5505024 | tf_op jit(solution)/shard_map/local_backward/pallas_call | solution.py:62
  93.9 1.6 %collective-permute-start.35 = (bf16[512,128]{1,0:T(8,128)(2,1)S(1)}, bf16[512,128]{1,0:T(8,128)(2,1)S(1)}, u32[]{:S(2)}, u32[]{:S(2)}) collective-permute-start(bf16[512,128]{1,0:T(8,128)(2,1)S(1)} %get-tuple-element.104), channel_id=1, source_target_pairs={{0,2},{1,3},{2,0},{3,1},{4,6},{5,7},{6,4},{7,5},{8,10},{9,11},{10,... | collective-permute-start | bytes 393224 | tf_op jit(solution)/shard_map/ppermute | solution.py:83
  95.6 1.1 collective-permute-start.33
  96.7 3.6 %collective-permute-done.35.refs_1_ = bf16[512,128]{1,0:T(8,128)(2,1)S(1)} collective-permute-done((bf16[512,128]{1,0:T(8,128)(2,1)S(1)}, bf16[512,128]{1,0:T(8,128)(2,1)S(1)}, u32[]{:S(2)}, u32[]{:S(2)}) %collective-permute-start.35) | collective-permute-done | bytes 131104 | tf_op jit(solution)/shard_map/ppermute | solution.py:83
  100.7 4.3 %collective-permute-start.37 = (bf16[128,128]{1,0:T(8,128)(2,1)S(1)}, bf16[128,128]{1,0:T(8,128)(2,1)S(1)}, u32[]{:S(2)}, u32[]{:S(2)}) collective-permute-start(bf16[128,128]{1,0:T(8,128)(2,1)S(1)} %get-tuple-element.107), channel_id=1, source_target_pairs={{0,8},{4,12},{8,0},{12,4},{1,9},{5,13},{9,1},{13,5},{2,10},{6,14},... | collective-permute-start | bytes 98312 | tf_op jit(solution)/shard_map/ppermute | solution.py:86
  105.0 2.0 %collective-permute-done.37.refs_8_ = bf16[128,128]{1,0:T(8,128)(2,1)S(1)} collective-permute-done((bf16[128,128]{1,0:T(8,128)(2,1)S(1)}, bf16[128,128]{1,0:T(8,128)(2,1)S(1)}, u32[]{:S(2)}, u32[]{:S(2)}) %collective-permute-start.37) | collective-permute-done | bytes 32800 | tf_op jit(solution)/shard_map/ppermute | solution.py:86
  107.0 4.0 %collective-permute-done.38.refs_9_ = bf16[128,128]{1,0:T(8,128)(2,1)S(1)} collective-permute-done((bf16[128,128]{1,0:T(8,128)(2,1)S(1)}, bf16[128,128]{1,0:T(8,128)(2,1)S(1)}, u32[]{:S(2)}, u32[]{:S(2)}) %collective-permute-start.38) | collective-permute-done | bytes 32800 | tf_op jit(solution)/shard_map/ppermute | solution.py:86
  111.0 1.2 owed_rows.1
  112.9 3.8 %collective-permute-start.41 = (bf16[512,128]{1,0:T(8,128)(2,1)S(1)}, bf16[512,128]{1,0:T(8,128)(2,1)S(1)}, u32[]{:S(2)}, u32[]{:S(2)}) collective-permute-start(bf16[512,128]{1,0:T(8,128)(2,1)S(1)} %get-tuple-element.112), channel_id=1, source_target_pairs={{0,12},{4,8},{8,4},{12,0},{1,13},{5,9},{9,5},{13,1},{2,14},{6,10},... | collective-permute-start | bytes 393224 | tf_op jit(solution)/shard_map/ppermute | solution.py:86
  116.7 2.2 %collective-permute-done.39.refs_5_ = bf16[512,128]{1,0:T(8,128)(2,1)S(1)} collective-permute-done((bf16[512,128]{1,0:T(8,128)(2,1)S(1)}, bf16[512,128]{1,0:T(8,128)(2,1)S(1)}, u32[]{:S(2)}, u32[]{:S(2)}) %collective-permute-start.39) | collective-permute-done | bytes 131104 | tf_op jit(solution)/shard_map/ppermute | solution.py:86
  118.9 3.3 %collective-permute-done.40.refs_6_ = bf16[512,128]{1,0:T(8,128)(2,1)S(1)} collective-permute-done((bf16[512,128]{1,0:T(8,128)(2,1)S(1)}, bf16[512,128]{1,0:T(8,128)(2,1)S(1)}, u32[]{:S(2)}, u32[]{:S(2)}) %collective-permute-start.40) | collective-permute-done | bytes 131104 | tf_op jit(solution)/shard_map/ppermute | solution.py:86
  122.7 0.9 collective-permute-start.43
  123.7 1.0 collective-permute-start.44
  124.6 3.1 %collective-permute-done.43.refs_2_ = bf16[256,128]{1,0:T(8,128)(2,1)S(1)} collective-permute-done((bf16[256,128]{1,0:T(8,128)(2,1)S(1)}, bf16[256,128]{1,0:T(8,128)(2,1)S(1)}, u32[]{:S(2)}, u32[]{:S(2)}) %collective-permute-start.43) | collective-permute-done | bytes 65568 | tf_op jit(solution)/shard_map/ppermute | solution.py:83
  128.2 1.1 adjoint.1
  (95 shorter events, 14.3 us)
Async XLA Ops:
  0.0 46.4 %copy-start.2 = (bf16[512,512]{1,0:T(8,128)(2,1)S(1)}, bf16[512,512]{1,0:T(8,128)(2,1)}, u32[]{:S(2)}) copy-start(bf16[512,512]{1,0:T(8,128)(2,1)} %base_ref.1) | copy-start | bytes 1572868
  0.0 10.3 %collective-permute-start.1 = (bf16[256,512]{1,0:T(8,128)(2,1)}, bf16[256,512]{1,0:T(8,128)(2,1)S(1)}, u32[]{:S(2)}, u32[]{:S(2)}) collective-permute-start(bf16[256,512]{1,0:T(8,128)(2,1)} %refs_0_.1), channel_id=1, source_target_pairs={{0,2},{1,3},{2,0},{3,1},{4,6},{5,7},{6,4},{7,5},{8,10},{9,11},{10,... | collective-permute-start | bytes 786440 | tf_op jit(solution)/shard_map/ppermute | solution.py:83
  2.9 20.7 %collective-permute-start = (bf16[256,512]{1,0:T(8,128)(2,1)}, bf16[256,512]{1,0:T(8,128)(2,1)S(1)}, u32[]{:S(2)}, u32[]{:S(2)}) collective-permute-start(bf16[256,512]{1,0:T(8,128)(2,1)} %refs_0_.1), channel_id=1, source_target_pairs={{0,1},{1,0},{2,3},{3,2},{4,5},{5,4},{6,7},{7,6},{8,9},{9,8},{10,11... | collective-permute-start | bytes 786440 | tf_op jit(solution)/shard_map/ppermute | solution.py:83
  2.9 9.3 %collective-permute-start.4 = (bf16[128,512]{1,0:T(8,128)(2,1)}, bf16[128,512]{1,0:T(8,128)(2,1)S(1)}, u32[]{:S(2)}, u32[]{:S(2)}) collective-permute-start(bf16[128,512]{1,0:T(8,128)(2,1)} %refs_4_.1), channel_id=1, source_target_pairs={{0,2},{1,3},{2,0},{3,1},{4,6},{5,7},{6,4},{7,5},{8,10},{9,11},{10,... | collective-permute-start | bytes 393224 | tf_op jit(solution)/shard_map/ppermute | solution.py:83
  10.3 13.4 %collective-permute-start.2 = (bf16[256,512]{1,0:T(8,128)(2,1)S(1)}, bf16[256,512]{1,0:T(8,128)(2,1)S(1)}, u32[]{:S(2)}, u32[]{:S(2)}) collective-permute-start(bf16[256,512]{1,0:T(8,128)(2,1)S(1)} %collective-permute-done.1.refs_2_.arrived_ref), channel_id=1, source_target_pairs={{0,1},{1,0},{2,3},{3,2},{4,5},{5,4},{6,7},{7,6},{8,9},{9,8},{10,11... | collective-permute-start | bytes 786440 | tf_op jit(solution)/shard_map/ppermute | solution.py:83
  10.3 13.4 %collective-permute-start.3 = (bf16[128,512]{1,0:T(8,128)(2,1)}, bf16[128,512]{1,0:T(8,128)(2,1)S(1)}, u32[]{:S(2)}, u32[]{:S(2)}) collective-permute-start(bf16[128,512]{1,0:T(8,128)(2,1)} %refs_4_.1), channel_id=1, source_target_pairs={{0,1},{1,0},{2,3},{3,2},{4,5},{5,4},{6,7},{7,6},{8,9},{9,8},{10,11... | collective-permute-start | bytes 393224 | tf_op jit(solution)/shard_map/ppermute | solution.py:83
  12.3 11.4 %collective-permute-start.5 = (bf16[128,512]{1,0:T(8,128)(2,1)S(1)}, bf16[128,512]{1,0:T(8,128)(2,1)S(1)}, u32[]{:S(2)}, u32[]{:S(2)}) collective-permute-start(bf16[128,512]{1,0:T(8,128)(2,1)S(1)} %collective-permute-done.4.refs_6_), channel_id=1, source_target_pairs={{0,1},{1,0},{2,3},{3,2},{4,5},{5,4},{6,7},{7,6},{8,9},{9,8},{10,11... | collective-permute-start | bytes 393224 | tf_op jit(solution)/shard_map/ppermute | solution.py:83
  15.6 1.4 %collective-permute-start.6 = (s32[2,512]{1,0:T(2,128)S(1)}, s32[2,512]{1,0:T(2,128)S(1)}, u32[]{:S(2)}, u32[]{:S(2)}) collective-permute-start(s32[2,512]{1,0:T(2,128)S(1)} %get-tuple-element.61.refs_8_.refs_0_), channel_id=1, source_target_pairs={{0,1},{1,0},{2,3},{3,2},{4,5},{5,4},{6,7},{7,6},{8,9},{9,8},{10,11... | collective-permute-start | bytes 12296 | tf_op jit(solution)/shard_map/ppermute | solution.py:83
  17.0 3.6 %collective-permute-start.7 = (s32[2,512]{1,0:T(2,128)S(1)}, s32[2,512]{1,0:T(2,128)S(1)}, u32[]{:S(2)}, u32[]{:S(2)}) collective-permute-start(s32[2,512]{1,0:T(2,128)S(1)} %get-tuple-element.61.refs_8_.refs_0_), channel_id=1, source_target_pairs={{0,2},{1,3},{2,0},{3,1},{4,6},{5,7},{6,4},{7,5},{8,10},{9,11},{10,... | collective-permute-start | bytes 12296 | tf_op jit(solution)/shard_map/ppermute | solution.py:83
  20.6 3.0 %collective-permute-start.8 = (s32[2,512]{1,0:T(2,128)S(1)}, s32[2,512]{1,0:T(2,128)S(1)}, u32[]{:S(2)}, u32[]{:S(2)}) collective-permute-start(s32[2,512]{1,0:T(2,128)S(1)} %get-tuple-element.61.refs_8_.refs_0_), channel_id=1, source_target_pairs={{0,3},{1,2},{2,1},{3,0},{4,7},{5,6},{6,5},{7,4},{8,11},{9,10},{10,... | collective-permute-start | bytes 12296 | tf_op jit(solution)/shard_map/ppermute | solution.py:83
  28.3 35.1 %copy-start.10 = (s32[1024]{0:T(1024)S(1)}, s32[1024]{0:T(1024)}, u32[]{:S(2)}) copy-start(s32[1024]{0:T(1024)} %param.27) | copy-start | bytes 12292
  28.3 38.0 %copy-start.14 = (bf16[1024,512]{1,0:T(8,128)(2,1)S(1)}, bf16[1024,512]{1,0:T(8,128)(2,1)}, u32[]{:S(2)}) copy-start(bf16[1024,512]{1,0:T(8,128)(2,1)} %es_ref.3) | copy-start | bytes 3145732
  29.8 29.6 %collective-permute-start.19 = (bf16[512,512]{1,0:T(8,128)(2,1)S(1)}, bf16[512,512]{1,0:T(8,128)(2,1)S(1)}, u32[]{:S(2)}, u32[]{:S(2)}) collective-permute-start(bf16[512,512]{1,0:T(8,128)(2,1)S(1)} %get-tuple-element.78.refs_0_), channel_id=1, source_target_pairs={{0,2},{1,3},{2,0},{3,1},{4,6},{5,7},{6,4},{7,5},{8,10},{9,11},{10,... | collective-permute-start | bytes 1572872 | tf_op jit(solution)/shard_map/ppermute | solution.py:83
  31.6 5.0 %collective-permute-start.9 = (bf16[512,128]{1,0:T(8,128)(2,1)S(1)}, bf16[512,128]{1,0:T(8,128)(2,1)S(1)}, u32[]{:S(2)}, u32[]{:S(2)}) collective-permute-start(bf16[512,128]{1,0:T(8,128)(2,1)S(1)} %get-tuple-element.69), channel_id=1, source_target_pairs={{0,4},{4,0},{8,12},{12,8},{1,5},{5,1},{9,13},{13,9},{2,6},{6,2},{1... | collective-permute-start | bytes 393224 | tf_op jit(solution)/shard_map/ppermute | solution.py:86
  33.3 19.0 %collective-permute-start.16 = (bf16[384,512]{1,0:T(8,128)(2,1)S(1)}, bf16[384,512]{1,0:T(8,128)(2,1)S(1)}, u32[]{:S(2)}, u32[]{:S(2)}) collective-permute-start(bf16[384,512]{1,0:T(8,128)(2,1)S(1)} %relay.1.refs_4_), channel_id=1, source_target_pairs={{0,2},{1,3},{2,0},{3,1},{4,6},{5,7},{6,4},{7,5},{8,10},{9,11},{10,... | collective-permute-start | bytes 1179656 | tf_op jit(solution)/shard_map/ppermute | solution.py:83
  33.9 22.3 %collective-permute-start.15 = (bf16[384,512]{1,0:T(8,128)(2,1)S(1)}, bf16[384,512]{1,0:T(8,128)(2,1)S(1)}, u32[]{:S(2)}, u32[]{:S(2)}) collective-permute-start(bf16[384,512]{1,0:T(8,128)(2,1)S(1)} %relay.1.refs_4_), channel_id=1, source_target_pairs={{0,1},{1,0},{2,3},{3,2},{4,5},{5,4},{6,7},{7,6},{8,9},{9,8},{10,11... | collective-permute-start | bytes 1179656 | tf_op jit(solution)/shard_map/ppermute | solution.py:83
  33.9 12.5 %collective-permute-start.10 = (bf16[512,128]{1,0:T(8,128)(2,1)S(1)}, bf16[512,128]{1,0:T(8,128)(2,1)S(1)}, u32[]{:S(2)}, u32[]{:S(2)}) collective-permute-start(bf16[512,128]{1,0:T(8,128)(2,1)S(1)} %get-tuple-element.70), channel_id=1, source_target_pairs={{0,8},{4,12},{8,0},{12,4},{1,9},{5,13},{9,1},{13,5},{2,10},{6,14},... | collective-permute-start | bytes 393224 | tf_op jit(solution)/shard_map/ppermute | solution.py:86
  36.6 9.8 %collective-permute-start.11 = (bf16[512,128]{1,0:T(8,128)(2,1)S(1)}, bf16[512,128]{1,0:T(8,128)(2,1)S(1)}, u32[]{:S(2)}, u32[]{:S(2)}) collective-permute-start(bf16[512,128]{1,0:T(8,128)(2,1)S(1)} %get-tuple-element.71), channel_id=1, source_target_pairs={{0,12},{4,8},{8,4},{12,0},{1,13},{5,9},{9,5},{13,1},{2,14},{6,10},... | collective-permute-start | bytes 393224 | tf_op jit(solution)/shard_map/ppermute | solution.py:86
  47.8 8.4 %collective-permute-start.21 = (bf16[128,128]{1,0:T(8,128)(2,1)S(1)}, bf16[128,128]{1,0:T(8,128)(2,1)S(1)}, u32[]{:S(2)}, u32[]{:S(2)}) collective-permute-start(bf16[128,128]{1,0:T(8,128)(2,1)S(1)} %get-tuple-element.81), channel_id=1, source_target_pairs={{0,4},{4,0},{8,12},{12,8},{1,5},{5,1},{9,13},{13,9},{2,6},{6,2},{1... | collective-permute-start | bytes 98312 | tf_op jit(solution)/shard_map/ppermute | solution.py:86
  51.0 5.8 %collective-permute-start.22 = (bf16[128,128]{1,0:T(8,128)(2,1)S(1)}, bf16[128,128]{1,0:T(8,128)(2,1)S(1)}, u32[]{:S(2)}, u32[]{:S(2)}) collective-permute-start(bf16[128,128]{1,0:T(8,128)(2,1)S(1)} %get-tuple-element.82), channel_id=1, source_target_pairs={{0,8},{4,12},{8,0},{12,4},{1,9},{5,13},{9,1},{13,5},{2,10},{6,14},... | collective-permute-start | bytes 98312 | tf_op jit(solution)/shard_map/ppermute | solution.py:86
  52.3 5.7 %collective-permute-start.23 = (bf16[128,128]{1,0:T(8,128)(2,1)S(1)}, bf16[128,128]{1,0:T(8,128)(2,1)S(1)}, u32[]{:S(2)}, u32[]{:S(2)}) collective-permute-start(bf16[128,128]{1,0:T(8,128)(2,1)S(1)} %get-tuple-element.83), channel_id=1, source_target_pairs={{0,12},{4,8},{8,4},{12,0},{1,13},{5,9},{9,5},{13,1},{2,14},{6,10},... | collective-permute-start | bytes 98312 | tf_op jit(solution)/shard_map/ppermute | solution.py:86
  56.1 10.2 %collective-permute-start.17 = (bf16[384,512]{1,0:T(8,128)(2,1)S(1)}, bf16[384,512]{1,0:T(8,128)(2,1)S(1)}, u32[]{:S(2)}, u32[]{:S(2)}) collective-permute-start(bf16[384,512]{1,0:T(8,128)(2,1)S(1)} %collective-permute-done.16.refs_6_), channel_id=1, source_target_pairs={{0,1},{1,0},{2,3},{3,2},{4,5},{5,4},{6,7},{7,6},{8,9},{9,8},{10,11... | collective-permute-start | bytes 1179656 | tf_op jit(solution)/shard_map/ppermute | solution.py:83
  56.2 13.2 %collective-permute-start.18 = (bf16[512,512]{1,0:T(8,128)(2,1)S(1)}, bf16[512,512]{1,0:T(8,128)(2,1)S(1)}, u32[]{:S(2)}, u32[]{:S(2)}) collective-permute-start(bf16[512,512]{1,0:T(8,128)(2,1)S(1)} %get-tuple-element.78.refs_0_), channel_id=1, source_target_pairs={{0,1},{1,0},{2,3},{3,2},{4,5},{5,4},{6,7},{7,6},{8,9},{9,8},{10,11... | collective-permute-start | bytes 1572872 | tf_op jit(solution)/shard_map/ppermute | solution.py:83
  56.8 2.6 %collective-permute-start.12 = (bf16[512,128]{1,0:T(8,128)(2,1)S(1)}, bf16[512,128]{1,0:T(8,128)(2,1)S(1)}, u32[]{:S(2)}, u32[]{:S(2)}) collective-permute-start(bf16[512,128]{1,0:T(8,128)(2,1)S(1)} %get-tuple-element.72.refs_0_), channel_id=1, source_target_pairs={{0,1},{1,0},{2,3},{3,2},{4,5},{5,4},{6,7},{7,6},{8,9},{9,8},{10,11... | collective-permute-start | bytes 393224 | tf_op jit(solution)/shard_map/ppermute | solution.py:83
  58.0 5.4 %collective-permute-start.13 = (bf16[512,128]{1,0:T(8,128)(2,1)S(1)}, bf16[512,128]{1,0:T(8,128)(2,1)S(1)}, u32[]{:S(2)}, u32[]{:S(2)}) collective-permute-start(bf16[512,128]{1,0:T(8,128)(2,1)S(1)} %get-tuple-element.72.refs_0_), channel_id=1, source_target_pairs={{0,2},{1,3},{2,0},{3,1},{4,6},{5,7},{6,4},{7,5},{8,10},{9,11},{10,... | collective-permute-start | bytes 393224 | tf_op jit(solution)/shard_map/ppermute | solution.py:83
  59.4 9.9 %collective-permute-start.20 = (bf16[512,512]{1,0:T(8,128)(2,1)S(1)}, bf16[512,512]{1,0:T(8,128)(2,1)S(1)}, u32[]{:S(2)}, u32[]{:S(2)}) collective-permute-start(bf16[512,512]{1,0:T(8,128)(2,1)S(1)} %collective-permute-done.19.refs_2_), channel_id=1, source_target_pairs={{0,1},{1,0},{2,3},{3,2},{4,5},{5,4},{6,7},{7,6},{8,9},{9,8},{10,11... | collective-permute-start | bytes 1572872 | tf_op jit(solution)/shard_map/ppermute | solution.py:83
  59.4 6.4 %collective-permute-start.25 = (bf16[512,128]{1,0:T(8,128)(2,1)S(1)}, bf16[512,128]{1,0:T(8,128)(2,1)S(1)}, u32[]{:S(2)}, u32[]{:S(2)}) collective-permute-start(bf16[512,128]{1,0:T(8,128)(2,1)S(1)} %constant_dynamic-update-slice_fusion.refs_0_), channel_id=1, source_target_pairs={{0,2},{1,3},{2,0},{3,1},{4,6},{5,7},{6,4},{7,5},{8,10},{9,11},{10,... | collective-permute-start | bytes 393224 | tf_op jit(solution)/shard_map/ppermute | solution.py:83
  63.4 2.7 %collective-permute-start.14 = (bf16[512,128]{1,0:T(8,128)(2,1)S(1)}, bf16[512,128]{1,0:T(8,128)(2,1)S(1)}, u32[]{:S(2)}, u32[]{:S(2)}) collective-permute-start(bf16[512,128]{1,0:T(8,128)(2,1)S(1)} %collective-permute-done.13.refs_2_), channel_id=1, source_target_pairs={{0,1},{1,0},{2,3},{3,2},{4,5},{5,4},{6,7},{7,6},{8,9},{9,8},{10,11... | collective-permute-start | bytes 393224 | tf_op jit(solution)/shard_map/ppermute | solution.py:83
  65.8 4.1 %collective-permute-start.24 = (bf16[512,128]{1,0:T(8,128)(2,1)S(1)}, bf16[512,128]{1,0:T(8,128)(2,1)S(1)}, u32[]{:S(2)}, u32[]{:S(2)}) collective-permute-start(bf16[512,128]{1,0:T(8,128)(2,1)S(1)} %constant_dynamic-update-slice_fusion.refs_0_), channel_id=1, source_target_pairs={{0,1},{1,0},{2,3},{3,2},{4,5},{5,4},{6,7},{7,6},{8,9},{9,8},{10,11... | collective-permute-start | bytes 393224 | tf_op jit(solution)/shard_map/ppermute | solution.py:83
  66.1 3.8 %collective-permute-start.26 = (bf16[512,128]{1,0:T(8,128)(2,1)S(1)}, bf16[512,128]{1,0:T(8,128)(2,1)S(1)}, u32[]{:S(2)}, u32[]{:S(2)}) collective-permute-start(bf16[512,128]{1,0:T(8,128)(2,1)S(1)} %collective-permute-done.25.refs_2_), channel_id=1, source_target_pairs={{0,1},{1,0},{2,3},{3,2},{4,5},{5,4},{6,7},{7,6},{8,9},{9,8},{10,11... | collective-permute-start | bytes 393224 | tf_op jit(solution)/shard_map/ppermute | solution.py:83
  73.1 1.6 %collective-permute-start.27 = (bf16[2,128,512]{2,1,0:T(8,128)(2,1)S(1)}, bf16[2,128,512]{2,1,0:T(8,128)(2,1)S(1)}, u32[]{:S(2)}, u32[]{:S(2)}) collective-permute-start(bf16[2,128,512]{2,1,0:T(8,128)(2,1)S(1)} %get-tuple-element.90), channel_id=1, source_target_pairs={{0,1},{1,0},{2,3},{3,2},{4,5},{5,4},{6,7},{7,6},{8,9},{9,8},{10,11... | collective-permute-start | bytes 786440 | tf_op jit(solution)/shard_map/ppermute | solution.py:83
  74.8 6.1 %collective-permute-start.28 = (bf16[128,512]{1,0:T(8,128)(2,1)S(1)}, bf16[128,512]{1,0:T(8,128)(2,1)S(1)}, u32[]{:S(2)}, u32[]{:S(2)}) collective-permute-start(bf16[128,512]{1,0:T(8,128)(2,1)S(1)} %get-tuple-element.92), channel_id=1, source_target_pairs={{0,2},{1,3},{2,0},{3,1},{4,6},{5,7},{6,4},{7,5},{8,10},{9,11},{10,... | collective-permute-start | bytes 393224 | tf_op jit(solution)/shard_map/ppermute | solution.py:83
  81.5 5.4 %collective-permute-start.30 = (bf16[128,512]{1,0:T(8,128)(2,1)S(1)}, bf16[128,512]{1,0:T(8,128)(2,1)S(1)}, u32[]{:S(2)}, u32[]{:S(2)}) collective-permute-start(bf16[128,512]{1,0:T(8,128)(2,1)S(1)} %get-tuple-element.93.refs_0_), channel_id=1, source_target_pairs={{0,2},{1,3},{2,0},{3,1},{4,6},{5,7},{6,4},{7,5},{8,10},{9,11},{10,... | collective-permute-start | bytes 393224 | tf_op jit(solution)/shard_map/ppermute | solution.py:83
  83.5 3.5 %collective-permute-start.29 = (bf16[128,512]{1,0:T(8,128)(2,1)S(1)}, bf16[128,512]{1,0:T(8,128)(2,1)S(1)}, u32[]{:S(2)}, u32[]{:S(2)}) collective-permute-start(bf16[128,512]{1,0:T(8,128)(2,1)S(1)} %get-tuple-element.93.refs_0_), channel_id=1, source_target_pairs={{0,1},{1,0},{2,3},{3,2},{4,5},{5,4},{6,7},{7,6},{8,9},{9,8},{10,11... | collective-permute-start | bytes 393224 | tf_op jit(solution)/shard_map/ppermute | solution.py:83
  87.0 1.3 %collective-permute-start.31 = (bf16[128,512]{1,0:T(8,128)(2,1)S(1)}, bf16[128,512]{1,0:T(8,128)(2,1)S(1)}, u32[]{:S(2)}, u32[]{:S(2)}) collective-permute-start(bf16[128,512]{1,0:T(8,128)(2,1)S(1)} %collective-permute-done.30.refs_2_), channel_id=1, source_target_pairs={{0,1},{1,0},{2,3},{3,2},{4,5},{5,4},{6,7},{7,6},{8,9},{9,8},{10,11... | collective-permute-start | bytes 393224 | tf_op jit(solution)/shard_map/ppermute | solution.py:83
  91.1 2.8 %collective-permute-start.34 = (bf16[2,512,128]{2,1,0:T(8,128)(2,1)S(1)}, bf16[2,512,128]{2,1,0:T(8,128)(2,1)S(1)}, u32[]{:S(2)}, u32[]{:S(2)}) collective-permute-start(bf16[2,512,128]{2,1,0:T(8,128)(2,1)S(1)} %get-tuple-element.102), channel_id=1, source_target_pairs={{0,1},{1,0},{2,3},{3,2},{4,5},{5,4},{6,7},{7,6},{8,9},{9,8},{10,11... | collective-permute-start | bytes 786440 | tf_op jit(solution)/shard_map/ppermute | solution.py:83
  93.4 2.1 %collective-permute-start.32 = (bf16[2,512,128]{2,1,0:T(8,128)(2,1)S(1)}, bf16[2,512,128]{2,1,0:T(8,128)(2,1)S(1)}, u32[]{:S(2)}, u32[]{:S(2)}) collective-permute-start(bf16[2,512,128]{2,1,0:T(8,128)(2,1)S(1)} %get-tuple-element.98), channel_id=1, source_target_pairs={{0,1},{1,0},{2,3},{3,2},{4,5},{5,4},{6,7},{7,6},{8,9},{9,8},{10,11... | collective-permute-start | bytes 786440 | tf_op jit(solution)/shard_map/ppermute | solution.py:83
  93.9 6.4 %collective-permute-start.35 = (bf16[512,128]{1,0:T(8,128)(2,1)S(1)}, bf16[512,128]{1,0:T(8,128)(2,1)S(1)}, u32[]{:S(2)}, u32[]{:S(2)}) collective-permute-start(bf16[512,128]{1,0:T(8,128)(2,1)S(1)} %get-tuple-element.104), channel_id=1, source_target_pairs={{0,2},{1,3},{2,0},{3,1},{4,6},{5,7},{6,4},{7,5},{8,10},{9,11},{10,... | collective-permute-start | bytes 393224 | tf_op jit(solution)/shard_map/ppermute | solution.py:83
  95.6 9.4 %collective-permute-start.33 = (bf16[512,128]{1,0:T(8,128)(2,1)S(1)}, bf16[512,128]{1,0:T(8,128)(2,1)S(1)}, u32[]{:S(2)}, u32[]{:S(2)}) collective-permute-start(bf16[512,128]{1,0:T(8,128)(2,1)S(1)} %get-tuple-element.100), channel_id=1, source_target_pairs={{0,2},{1,3},{2,0},{3,1},{4,6},{5,7},{6,4},{7,5},{8,10},{9,11},{10,... | collective-permute-start | bytes 393224 | tf_op jit(solution)/shard_map/ppermute | solution.py:83
  100.4 4.6 %collective-permute-start.36 = (bf16[128,128]{1,0:T(8,128)(2,1)S(1)}, bf16[128,128]{1,0:T(8,128)(2,1)S(1)}, u32[]{:S(2)}, u32[]{:S(2)}) collective-permute-start(bf16[128,128]{1,0:T(8,128)(2,1)S(1)} %get-tuple-element.106), channel_id=1, source_target_pairs={{0,4},{4,0},{8,12},{12,8},{1,5},{5,1},{9,13},{13,9},{2,6},{6,2},{1... | collective-permute-start | bytes 98312 | tf_op jit(solution)/shard_map/ppermute | solution.py:86
  100.7 6.4 %collective-permute-start.37 = (bf16[128,128]{1,0:T(8,128)(2,1)S(1)}, bf16[128,128]{1,0:T(8,128)(2,1)S(1)}, u32[]{:S(2)}, u32[]{:S(2)}) collective-permute-start(bf16[128,128]{1,0:T(8,128)(2,1)S(1)} %get-tuple-element.107), channel_id=1, source_target_pairs={{0,8},{4,12},{8,0},{12,4},{1,9},{5,13},{9,1},{13,5},{2,10},{6,14},... | collective-permute-start | bytes 98312 | tf_op jit(solution)/shard_map/ppermute | solution.py:86
  105.0 6.0 %collective-permute-start.38 = (bf16[128,128]{1,0:T(8,128)(2,1)S(1)}, bf16[128,128]{1,0:T(8,128)(2,1)S(1)}, u32[]{:S(2)}, u32[]{:S(2)}) collective-permute-start(bf16[128,128]{1,0:T(8,128)(2,1)S(1)} %get-tuple-element.108), channel_id=1, source_target_pairs={{0,12},{4,8},{8,4},{12,0},{1,13},{5,9},{9,5},{13,1},{2,14},{6,10},... | collective-permute-start | bytes 98312 | tf_op jit(solution)/shard_map/ppermute | solution.py:86
  112.2 6.7 %collective-permute-start.39 = (bf16[512,128]{1,0:T(8,128)(2,1)S(1)}, bf16[512,128]{1,0:T(8,128)(2,1)S(1)}, u32[]{:S(2)}, u32[]{:S(2)}) collective-permute-start(bf16[512,128]{1,0:T(8,128)(2,1)S(1)} %get-tuple-element.110), channel_id=1, source_target_pairs={{0,4},{4,0},{8,12},{12,8},{1,5},{5,1},{9,13},{13,9},{2,6},{6,2},{1... | collective-permute-start | bytes 393224 | tf_op jit(solution)/shard_map/ppermute | solution.py:86
  112.3 9.9 %collective-permute-start.40 = (bf16[512,128]{1,0:T(8,128)(2,1)S(1)}, bf16[512,128]{1,0:T(8,128)(2,1)S(1)}, u32[]{:S(2)}, u32[]{:S(2)}) collective-permute-start(bf16[512,128]{1,0:T(8,128)(2,1)S(1)} %get-tuple-element.111), channel_id=1, source_target_pairs={{0,8},{4,12},{8,0},{12,4},{1,9},{5,13},{9,1},{13,5},{2,10},{6,14},... | collective-permute-start | bytes 393224 | tf_op jit(solution)/shard_map/ppermute | solution.py:86
  112.9 9.4 %collective-permute-start.41 = (bf16[512,128]{1,0:T(8,128)(2,1)S(1)}, bf16[512,128]{1,0:T(8,128)(2,1)S(1)}, u32[]{:S(2)}, u32[]{:S(2)}) collective-permute-start(bf16[512,128]{1,0:T(8,128)(2,1)S(1)} %get-tuple-element.112), channel_id=1, source_target_pairs={{0,12},{4,8},{8,4},{12,0},{1,13},{5,9},{9,5},{13,1},{2,14},{6,10},... | collective-permute-start | bytes 393224 | tf_op jit(solution)/shard_map/ppermute | solution.py:86
  122.7 1.9 %collective-permute-start.42 = (bf16[256,128]{1,0:T(8,128)(2,1)S(1)}, bf16[256,128]{1,0:T(8,128)(2,1)S(1)}, u32[]{:S(2)}, u32[]{:S(2)}) collective-permute-start(bf16[256,128]{1,0:T(8,128)(2,1)S(1)} %get-tuple-element.114), channel_id=1, source_target_pairs={{0,1},{1,0},{2,3},{3,2},{4,5},{5,4},{6,7},{7,6},{8,9},{9,8},{10,11... | collective-permute-start | bytes 196616 | tf_op jit(solution)/shard_map/ppermute | solution.py:83
  122.7 5.0 %collective-permute-start.43 = (bf16[256,128]{1,0:T(8,128)(2,1)S(1)}, bf16[256,128]{1,0:T(8,128)(2,1)S(1)}, u32[]{:S(2)}, u32[]{:S(2)}) collective-permute-start(bf16[256,128]{1,0:T(8,128)(2,1)S(1)} %get-tuple-element.115), channel_id=1, source_target_pairs={{0,2},{1,3},{2,0},{3,1},{4,6},{5,7},{6,4},{7,5},{8,10},{9,11},{10,... | collective-permute-start | bytes 196616 | tf_op jit(solution)/shard_map/ppermute | solution.py:83
  123.7 4.5 %collective-permute-start.44 = (bf16[256,128]{1,0:T(8,128)(2,1)S(1)}, bf16[256,128]{1,0:T(8,128)(2,1)S(1)}, u32[]{:S(2)}, u32[]{:S(2)}) collective-permute-start(bf16[256,128]{1,0:T(8,128)(2,1)S(1)} %get-tuple-element.116), channel_id=1, source_target_pairs={{0,3},{1,2},{2,1},{3,0},{4,7},{5,6},{6,5},{7,4},{8,11},{9,10},{10,... | collective-permute-start | bytes 196616 | tf_op jit(solution)/shard_map/ppermute | solution.py:83
  (12 other events, 58.8 us)

commit v3 on v2

--- a/solution.py
+++ b/solution.py
@@ -9,7 +9,7 @@
 F32 = jnp.float32
 SMEM = pl.BlockSpec(memory_space=pltpu.SMEM)
 VMEM = pl.BlockSpec(memory_space=pltpu.VMEM)
-ANY = pl.BlockSpec(memory_space=pl.ANY)
+HBM = pl.BlockSpec(memory_space=pltpu.HBM)
 
 
 def dot(a, b):
@@ -56,13 +56,13 @@
     return parts[0] if len(parts) == 1 else jnp.concatenate(parts, axis=0)
 
 
-def call(body, name, me, ins, outs, scratch=(), flops=0, unread=0):
+def call(body, name, me, ins, outs, scratch=(), flops=0, far=()):
     size = lambda s: s.size * s.dtype.itemsize
     moved = sum(size(x) for x in ins) + sum(size(x) for x in outs)
     return pl.pallas_call(
         body,
         out_shape=list(outs),
-        in_specs=[SMEM] + [VMEM] * (len(ins) - unread) + [ANY] * unread,
+        in_specs=[SMEM] + [HBM if i in far else VMEM for i in range(len(ins))],
         out_specs=[VMEM] * len(outs),
         scratch_shapes=list(scratch),
         compiler_params=pltpu.CompilerParams(vmem_limit_bytes=24 * 2**20),
@@ -144,6 +144,8 @@
         C = D // M
         R = N // M
         T = 256
+        PACK = 16
+        assert NS == D
         rows_enc, rows_in, rows_out, rows_node = (
             enc_weight.shape[0],
             edge_in_weight.shape[0],
@@ -157,42 +159,55 @@
         where = jnp.stack([me, dom])
         recv_row = edge_recv.reshape(1, E)
 
-        def tables_kernel(where_ref, gs_ref, gr_ref, halo_ref, send_ref, slot_out, halo_out, send_out):
+        def tables_kernel(where_ref, enc_ref, gs_ref, gr_ref, halo_ref, send_ref, *refs):
+            pack_out, halo_out, send_out, gs, gr, halo, sent, sems = refs
             dom = where_ref[1]
-            for j in range(n_dom):
-                at, to = pl.ds(dom ^ j, 1), slice(j * S, (j + 1) * S)
-                slot_out[0:1, to] = gs_ref[0, at, :]
-                slot_out[1:2, to] = gr_ref[0, at, :]
-                halo_out[:, j * H : (j + 1) * H] = halo_ref[0, at, :]
-            sent = send_ref[...]
-            away = jnp.maximum(sent - N, 0)
+            pairs = [
+                (enc_ref, pack_out.at[:rows_enc, :]),
+                (gs_ref.at[0], gs),
+                (gr_ref.at[0], gr),
+                (halo_ref.at[0], halo),
+                (send_ref, sent),
+            ]
+            copies = [pltpu.make_async_copy(a, b, sems.at[i]) for i, (a, b) in enumerate(pairs)]
+            for copy in copies:
+                copy.start()
+            for copy in copies:
+                copy.wait()
+            order = [pl.ds(dom ^ j, 1) for j in range(n_dom)]
+            sends, recvs = lanes([gs[at, :] for at in order]), lanes([gr[at, :] for at in order])
+            halo_out[...] = lanes([halo[at, :] for at in order])
+            fill = jnp.zeros((PACK - 3, NS), jnp.int32)
+            rows = stack([sends, recvs // 2, recvs % 2, fill])
+            pack_out[rows_enc:, :] = rows.astype(F32).astype(BF)
+            value = sent[...]
+            away = jnp.maximum(value - N, 0)
             peer = away // H
-            send_out[...] = jnp.where(sent < N, sent, N + (peer ^ dom) * H + (away - peer * H))
-
-        slots, halo_row, send_row = call(
+            send_out[...] = jnp.where(value < N, value, N + (peer ^ dom) * H + (away - peer * H))
+
+        pack, halo_row, send_row = call(
             tables_kernel,
             "tables",
             where,
-            [grid_send, grid_recv, halo_rows, edge_send.reshape(1, E)],
-            [shape((2, NS), jnp.int32), shape((1, NH), jnp.int32), shape((1, E), jnp.int32)],
+            [enc_weight, grid_send, grid_recv, halo_rows, edge_send.reshape(1, E)],
+            [shape((rows_enc + PACK, D)), shape((1, NH), jnp.int32), shape((1, E), jnp.int32)],
+            scratch=[
+                pltpu.VMEM((n_dom, S), jnp.int32),
+                pltpu.VMEM((n_dom, S), jnp.int32),
+                pltpu.VMEM((n_dom, H), jnp.int32),
+                pltpu.VMEM((1, E), jnp.int32),
+                pltpu.SemaphoreType.DMA((5,)),
+            ],
+            far=range(5),
         )
 
         state_parts = member_gather_chips(grid_state)
-        enc_parts = member_gather_chips(enc_weight)
-        slot_parts = member_gather(slots)
-
-        def relay_kernel(me_ref, weight_ref, arrived_ref, out_ref):
-            out_ref[...] = weight_ref[...]
-
-        edge_in_own = call(
-            relay_kernel,
-            "relay",
-            me1,
-            [edge_in_weight, state_parts[n_rep]],
-            [shape((rows_in, D))],
-            unread=1,
-        )[0]
-        in_parts = member_gather_chips(edge_in_own)
+        pack_parts = member_gather_chips(pack)
+        gather = lambda w: lax.all_gather(w, ("feat", "rep"), axis=0, tiled=True)
+        in_full = gather(edge_in_weight)
+        out_full = gather(edge_out_weight)
+        node_in_full = gather(node_in_weight)
+        node_out_full = gather(node_out_weight)
 
         def hots_kernel(me_ref, send_ref, recv_ref, sl_out, sh_out, r_out, slt_out, sht_out, rt_out):
             for i in range(E // T):
@@ -213,45 +228,49 @@
             [shape((E, N)), shape((E, NH)), shape((E, N)), shape((N, E)), shape((NH, E)), shape((N, E))],
         )
 
-        def grid_kernel(me_ref, out_ref, node_in_ref, node_out_ref, *refs):
-            states, encs, tables = refs[:M], refs[M : 2 * M], refs[2 * M : 3 * M]
-            enc_out, slope_out, rest_out = refs[3 * M : 3 * M + 3]
-            outs = refs[3 * M + 3 :]
+        def grid_kernel(me_ref, *refs):
+            states, packs = refs[:M], refs[M : 2 * M]
+            enc_out, slope_out, table_out = refs[2 * M : 2 * M + 3]
+            outs, (own, sem) = refs[2 * M + 3 : 2 * M + 3 + n_dom], refs[2 * M + 3 + n_dom :]
             me = me_ref[0]
-            for k in range(M):
-                enc_out[rows_at(me ^ k, rows_enc), :] = encs[k][...]
+            copy = pltpu.make_async_copy(states[0], own, sem)
+            copy.start()
+            for k in range(M):
+                enc_out[rows_at(me ^ k, rows_enc), :] = packs[k][:rows_enc, :]
+                rows = packs[k][rows_enc:, :].astype(F32).astype(jnp.int32)
+                table_out[k, 0:1, :] = rows[0:1]
+                table_out[k, 1:2, :] = 2 * rows[1:2] + rows[2:3]
             enc_cols = dot(enc_out[...], column_pick(me, D, C)).astype(BF)
-            for k in range(M):
-                pre = dot(states[k][...], enc_cols)
+            for k in list(range(1, M)) + [0]:
+                if k == 0:
+                    copy.wait()
+                pre = dot(states[k][...] if k else own[...], enc_cols)
                 logistic = jax.nn.sigmoid(pre)
                 slope_out[k] = logistic * (1.0 + pre * (1.0 - logistic))
                 message = (pre * logistic).astype(BF)
-                rows = dot(hot_rows(tables[k][0:1, :], G), message).astype(BF)
+                rows = dot(hot_rows(table_out[k, 0:1, :], G), message).astype(BF)
                 for j in range(n_dom):
                     outs[j][k * S : (k + 1) * S, :] = rows[j * S : (j + 1) * S]
-            rest_out[:rows_out, :] = out_ref[...]
-            rest_out[rows_out : rows_out + rows_node, :] = node_in_ref[...]
-            rest_out[rows_out + rows_node :, :] = node_out_ref[...]
-
-        enc_full, grid_slope, rest, *outgoing = call(
+
+        enc_full, grid_slope, slots, *outgoing = call(
             grid_kernel,
             "grid_messages",
             me1,
-            [edge_out_weight, node_in_weight, node_out_weight] + state_parts + enc_parts + slot_parts,
-            [shape((D, D)), shape((M, G, C), F32), shape((2 * rows_out + rows_node, D))]
+            state_parts + pack_parts,
+            [shape((D, D)), shape((M, G, C), F32), shape((M, 2, NS), jnp.int32)]
             + [shape((M * S, C))] * n_dom,
+            scratch=[pltpu.VMEM((G, D), BF), pltpu.SemaphoreType.DMA(())],
             flops=2 * M * G * D * C + 2 * M * NS * G * C,
+            far=(0,),
         )
         incoming = dom_trade(outgoing)
-        rest_parts = member_gather_chips(rest)
-
-        def encode_kernel(me_ref, base_ref, halo_ref, *refs):
-            tables, arrived = refs[:M], refs[M : M + n_dom]
-            state_out, outs = refs[M + n_dom], refs[M + n_dom + 1 :]
+
+        def encode_kernel(me_ref, base_ref, halo_ref, table_ref, *refs):
+            arrived, state_out, outs = refs[:n_dom], refs[n_dom], refs[n_dom + 1 :]
             total = dot(base_ref[...], column_pick(me_ref[0], D, C))
             for k in range(M):
                 rows = stack([arrived[j][k * S : (k + 1) * S, :] for j in range(n_dom)])
-                total += dot(hot_columns(tables[k][1:2, :], N), rows)
+                total += dot(hot_columns(table_ref[k, 1:2, :], N), rows)
             state = total.astype(BF)
             state_out[...] = state
             rows = dot(hot_rows(halo_ref[...], N), state).astype(BF)
@@ -262,7 +281,7 @@
             encode_kernel,
             "encode",
             me1,
-            [mesh_base, halo_row] + slot_parts + incoming,
+            [mesh_base, halo_row, slots] + incoming,
             [shape((N, C))] + [shape((H, C))] * n_dom,
             flops=2 * M * N * NS * C,
         )
@@ -271,54 +290,43 @@
         halo_cols = jnp.concatenate(halo_in, axis=0)
         halo_parts = member_gather_chips(halo_cols)
 
-        def local_kernel(me_ref, es_ref, send_ref, recv_ref, *refs):
-            cols, weights = refs[:M], refs[M : 2 * M]
-            pre_out, state_out, w_out, parts = refs[2 * M :]
+        def local_kernel(me_ref, es_ref, send_ref, recv_ref, w_ref, *refs):
+            cols, (pre_out, state_out, parts) = refs[:M], refs[M:]
             me = me_ref[0]
             for k in range(M):
                 parts[me ^ k] = cols[k][...]
-                w_out[rows_at(me ^ k, rows_in), :] = weights[k][...]
             state_out[...] = lanes([parts[j] for j in range(M)])
             for i in range(E // T):
                 at = slice(i * T, (i + 1) * T)
                 sent = dot(send_ref[at, :], state_out[...]).astype(BF)
                 got = dot(recv_ref[at, :], state_out[...]).astype(BF)
                 pre_out[at, :] = (
-                    dot(es_ref[at, :], w_out[:D, :])
-                    + dot(sent, w_out[D : 2 * D, :])
-                    + dot(got, w_out[2 * D :, :])
+                    dot(es_ref[at, :], w_ref[:D, :])
+                    + dot(sent, w_ref[D : 2 * D, :])
+                    + dot(got, w_ref[2 * D :, :])
                 )
 
-        local_pre, mesh_state, in_full = call(
+        local_pre, mesh_state = call(
             local_kernel,
             "edge_local",
             me1,
-            [edge_state, sl_hot, r_hot] + state_parts2 + in_parts,
-            [shape((E, D), F32), shape((N, D)), shape((3 * D, D))],
+            [edge_state, sl_hot, r_hot, in_full] + state_parts2,
+            [shape((E, D), F32), shape((N, D))],
             scratch=[pltpu.VMEM((M, N, C), BF)],
             flops=2 * E * D * (3 * D + 2 * N),
         )
 
-        def node_ahead_kernel(me_ref, state_ref, grad_ref, *refs):
-            weights = refs[:M]
-            out_full, node_in_full, pre_out, cot_out, node_out_full = refs[M:]
-            me = me_ref[0]
-            for k in range(M):
-                first, second = rows_out, rows_out + rows_node
-                out_full[rows_at(me ^ k, rows_out), :] = weights[k][:first, :]
-                node_in_full[rows_at(me ^ k, rows_node), :] = weights[k][first:second, :]
-                node_out_full[rows_at(me ^ k, rows_out), :] = weights[k][second:, :]
-            mine = rows_at(me, R)
-            pre_out[...] = dot(state_ref[mine, :], node_in_full[:D, :])
-            cot_out[...] = dot_t(grad_ref[mine, :], node_out_full[...])
-
-        out_full, node_in_full, node_pre, node_cot = call(
+        def node_ahead_kernel(me_ref, state_ref, grad_ref, in_ref, out_ref, pre_out, cot_out):
+            mine = rows_at(me_ref[0], R)
+            pre_out[...] = dot(state_ref[mine, :], in_ref[:D, :])
+            cot_out[...] = dot_t(grad_ref[mine, :], out_ref[...])
+
+        node_pre, node_cot = call(
             node_ahead_kernel,
             "node_ahead",
             me1,
-            [mesh_state, node_grad] + rest_parts,
-            [shape((D, D)), shape((2 * D, D)), shape((R, D), F32), shape((R, D), F32)],
-            scratch=[pltpu.VMEM((D, D), BF)],
+            [mesh_state, node_grad, node_in_full, node_out_full],
+            [shape((R, D), F32), shape((R, D), F32)],
             flops=4 * R * D * D,
         )
 
@@ -450,16 +458,16 @@
         halo_back = call(halo_sum_kernel, "halo_sums", me1, halo_grads, [shape((H, C))] * n_dom)
         halo_back = dom_trade(halo_back)
 
-        def owed_kernel(me_ref, halo_ref, *refs):
-            tables, local = refs[:M], refs[M : M + n_feat]
-            back, outs = refs[M + n_feat : M + n_feat + n_dom], refs[M + n_feat + n_dom :]
+        def owed_kernel(me_ref, halo_ref, table_ref, *refs):
+            local, back = refs[:n_feat], refs[n_feat : n_feat + n_dom]
+            outs = refs[n_feat + n_dom :]
             total = local[0][...].astype(F32)
             for k in range(1, n_feat):
                 total += local[k][...].astype(F32)
             rows = stack([back[j][...] for j in range(n_dom)])
             cot = (total + dot(hot_columns(halo_ref[...], N), rows)).astype(BF)
             for k in range(M):
-                owed = dot(hot_rows(tables[k][1:2, :], N), cot).astype(BF)
+                owed = dot(hot_rows(table_ref[k, 1:2, :], N), cot).astype(BF)
                 for j in range(n_dom):
                     outs[j][k * S : (k + 1) * S, :] = owed[j * S : (j + 1) * S]
 
@@ -467,24 +475,24 @@
             owed_kernel,
             "owed_rows",
             me1,
-            [halo_row] + slot_parts + local_grads + halo_back,
+            [halo_row, slots] + local_grads + halo_back,
             [shape((M * S, C))] * n_dom,
             flops=2 * M * NS * N * C,
         )
         owed = dom_trade(owed)
 
-        def grid_back_kernel(me_ref, slope_ref, *refs):
-            tables, back, outs = refs[:M], refs[M : M + n_dom], refs[M + n_dom :]
+        def grid_back_kernel(me_ref, slope_ref, table_ref, *refs):
+            back, outs = refs[:n_dom], refs[n_dom:]
             for k in range(M):
                 rows = stack([back[j][k * S : (k + 1) * S, :] for j in range(n_dom)])
-                cot = dot(hot_columns(tables[k][0:1, :], G), rows)
+                cot = dot(hot_columns(table_ref[k, 0:1, :], G), rows)
                 outs[k][...] = (cot * slope_ref[k]).astype(BF)
 
         grid_dpre = call(
             grid_back_kernel,
             "grid_backward",
             me1,
-            [grid_slope] + slot_parts + owed,
+            [grid_slope, slots] + owed,
             [shape((G, C))] * M,
             flops=2 * M * G * NS * C,
         )

time: 130 us -> 151 us (1.16)
  local copies, waits for them, and re-layouts: 7.39 us -> 27.4 us
  blocking collectives: 0 us -> 16.9 us
  starting transfers between devices: 46.9 us -> 31.1 us
  waiting for transfers between devices: 54 us -> 38.2 us
  between operations: 0.26 us -> 13.7 us
  Pallas kernels: 20.7 us -> 23.4 us
    unnamed x33 -> x91, local copies, waits for them, and re-layouts: 7.38 us -> 27.4 us
    all_gather x0 -> x2, blocking collectives: none -> 16.9 us  [per_device(): gather = lambda w: lax.all_gather(w, ('feat', 'rep'), axis=0, tiled=True)]
    ppermute x33 -> x24, waiting for transfers between devices: 34.8 us -> 21.4 us  [member_swap(): return lax.ppermute(x, ('feat', 'rep'), [(i, i ^ k) for i in range(M)])]
    ppermute x33 -> x24, starting transfers between devices: 21.7 us -> 13 us  [member_swap(): return lax.ppermute(x, ('feat', 'rep'), [(i, i ^ k) for i in range(M)])]
    ppermute x12, starting transfers between devices: 25.1 us -> 18.1 us  [dom_swap(): return lax.ppermute(x, 'dom', [(i, i ^ k) for i in range(n_dom)])]
    ppermute x12, waiting for transfers between devices: 19.2 us -> 16.1 us  [dom_swap(): return lax.ppermute(x, 'dom', [(i, i ^ k) for i in range(n_dom)])]
    pallas_call x18 -> x17, Pallas kernels: 20.7 us -> 23.4 us  [call(): pl.pallas_call(body, out_shape=list(outs), in_specs=[SMEM] + [HBM if i in...]
  transfers between devices with their start and end apart: 45 -> 38, of which waited for: 23 -> 17; matrix products, arithmetic and copies ran while one was open for 0% -> 0% of each run, Pallas kernels for 8% -> 11%
where the time goes in v3:
time: 151 us
  waiting for transfers between devices  38.2 us (25%)
  starting transfers between devices  31.1 us (21%)
  local copies, waits for them, and re-layouts  27.4 us (18%)
  Pallas kernels  23.4 us (15%)
  blocking collectives  16.9 us (11%)
  between operations  13.7 us (9%)
    unnamed x91, local copies, waits for them, and re-layouts  27.4 us
    pallas_call x17, Pallas kernels, call(): pl.pallas_call(body, out_shape=list(outs), in_specs=[SMEM] + [HBM if i in...  23.4 us
    ppermute x24, waiting for transfers between devices, member_swap(): return lax.ppermute(x, ('feat', 'rep'), [(i, i ^ k) for i in range(M)])  21.4 us
    ppermute x12, starting transfers between devices, dom_swap(): return lax.ppermute(x, 'dom', [(i, i ^ k) for i in range(n_dom)])  18.1 us
    all_gather x2, blocking collectives, per_device(): gather = lambda w: lax.all_gather(w, ('feat', 'rep'), axis=0, tiled=True)  16.9 us
    ppermute x12, waiting for transfers between devices, dom_swap(): return lax.ppermute(x, 'dom', [(i, i ^ k) for i in range(n_dom)])  16.1 us
    ppermute x24, starting transfers between devices, member_swap(): return lax.ppermute(x, ('feat', 'rep'), [(i, i ^ k) for i in range(M)])  13 us
  transfers between devices with their start and end apart: 38, of which 17 were waited for; matrix products, arithmetic and copies ran while one was open for 0% of the time, Pallas kernels for 11%

profile of v3, /device:TPU:0, one launch (start us, length us, event | category | flops | bytes accessed | tf_op | source)
XLA Modules:
  0.0 150.8 jit_solution(17805099141049760668)
XLA Ops:
  7.3 3.0 %collective-permute-start.1 = (bf16[256,512]{1,0:T(8,128)(2,1)}, bf16[256,512]{1,0:T(8,128)(2,1)S(1)}, u32[]{:S(2)}, u32[]{:S(2)}) collective-permute-start(bf16[256,512]{1,0:T(8,128)(2,1)} %refs_0_.1), channel_id=1, source_target_pairs={{0,2},{1,3},{2,0},{3,1},{4,6},{5,7},{6,4},{7,5},{8,10},{9,11},{10,... | collective-permute-start | bytes 786440 | tf_op jit(solution)/shard_map/ppermute | solution.py:83
  15.0 2.3 %collective-permute-done.1.refs_2_ = bf16[256,512]{1,0:T(8,128)(2,1)S(1)} collective-permute-done((bf16[256,512]{1,0:T(8,128)(2,1)}, bf16[256,512]{1,0:T(8,128)(2,1)S(1)}, u32[]{:S(2)}, u32[]{:S(2)}) %collective-permute-start.1) | collective-permute-done | bytes 262176 | tf_op jit(solution)/shard_map/ppermute | solution.py:83
  17.8 2.4 %collective-permute-done.4.refs_6_ = bf16[144,512]{1,0:T(8,128)(2,1)S(1)} collective-permute-done((bf16[144,512]{1,0:T(8,128)(2,1)S(1)}, bf16[144,512]{1,0:T(8,128)(2,1)S(1)}, u32[]{:S(2)}, u32[]{:S(2)}) %collective-permute-start.4) | collective-permute-done | bytes 147488 | tf_op jit(solution)/shard_map/ppermute | solution.py:83
  20.2 1.4 collective-permute-done.5.refs_7_
  22.5 2.6 %grid_messages.1 = (bf16[512,512]{1,0:T(8,128)(2,1)S(1)}, f32[4,256,128]{2,1,0:T(8,128)S(1)}, s32[4,2,512]{2,1,0:T(2,128)S(1)}, bf16[512,128]{1,0:T(8,128)(2,1)S...) custom-call(s32[1]{0:T(128)} %bitcast.me_ref, ...), custom_call_target="tpu_custom_call" | custom-call | flops 268435456 | bytes 3227648 | tf_op jit(solution)/shard_map/grid_messages/pallas_call | solution.py:62
  26.7 1.6 %collective-permute-start.6 = (bf16[512,128]{1,0:T(8,128)(2,1)}, bf16[512,128]{1,0:T(8,128)(2,1)S(1)}, u32[]{:S(2)}, u32[]{:S(2)}) collective-permute-start(bf16[512,128]{1,0:T(8,128)(2,1)} %get-tuple-element.67), channel_id=1, source_target_pairs={{0,4},{4,0},{8,12},{12,8},{1,5},{5,1},{9,13},{13,9},{2,6},{6,2},{1... | collective-permute-start | bytes 393224 | tf_op jit(solution)/shard_map/ppermute | solution.py:86
  28.3 2.6 %collective-permute-start.7 = (bf16[512,128]{1,0:T(8,128)(2,1)}, bf16[512,128]{1,0:T(8,128)(2,1)S(1)}, u32[]{:S(2)}, u32[]{:S(2)}) collective-permute-start(bf16[512,128]{1,0:T(8,128)(2,1)} %get-tuple-element.68), channel_id=1, source_target_pairs={{0,8},{4,12},{8,0},{12,4},{1,9},{5,13},{9,1},{13,5},{2,10},{6,14},... | collective-permute-start | bytes 393224 | tf_op jit(solution)/shard_map/ppermute | solution.py:86
  31.8 2.1 %edge_hots.1 = (bf16[1024,512]{1,0:T(8,128)(2,1)S(1)}, bf16[1024,512]{1,0:T(8,128)(2,1)S(1)}, bf16[1024,512]{1,0:T(8,128)(2,1)S(1)}, bf16[512,1024]{1,0:T(8,128)...) custom-call(s32[1]{0:T(128)} %bitcast.me_ref, s32[1,1024]{1,0:T(1,128)S(1)} %get-tuple-element.63.send_ref, ...), custom_call_target="tpu_custom_call" | custom-call | bytes 6299648 | tf_op jit(solution)/shard_map/edge_hots/pallas_call | solution.py:62
  34.0 1.0 copy-done.10
  35.0 1.0 copy-done.27
  37.0 1.0 copy-done.32
  38.0 1.0 copy-done.34
  39.0 2.5 %collective-permute-done.7.refs_2_ = bf16[512,128]{1,0:T(8,128)(2,1)S(1)} collective-permute-done((bf16[512,128]{1,0:T(8,128)(2,1)}, bf16[512,128]{1,0:T(8,128)(2,1)S(1)}, u32[]{:S(2)}, u32[]{:S(2)}) %collective-permute-start.7) | collective-permute-done | bytes 131104 | tf_op jit(solution)/shard_map/ppermute | solution.py:86
  41.4 1.4 encode.1
  42.9 1.6 %collective-permute-start.10 = (bf16[512,128]{1,0:T(8,128)(2,1)S(1)}, bf16[512,128]{1,0:T(8,128)(2,1)S(1)}, u32[]{:S(2)}, u32[]{:S(2)}) collective-permute-start(bf16[512,128]{1,0:T(8,128)(2,1)S(1)} %get-tuple-element.70.refs_0_), channel_id=1, source_target_pairs={{0,2},{1,3},{2,0},{3,1},{4,6},{5,7},{6,4},{7,5},{8,10},{9,11},{10,... | collective-permute-start | bytes 393224 | tf_op jit(solution)/shard_map/ppermute | solution.py:83
  44.4 2.3 %collective-permute-start.12 = (bf16[128,128]{1,0:T(8,128)(2,1)S(1)}, bf16[128,128]{1,0:T(8,128)(2,1)S(1)}, u32[]{:S(2)}, u32[]{:S(2)}) collective-permute-start(bf16[128,128]{1,0:T(8,128)(2,1)S(1)} %get-tuple-element.75), channel_id=1, source_target_pairs={{0,4},{4,0},{8,12},{12,8},{1,5},{5,1},{9,13},{13,9},{2,6},{6,2},{1... | collective-permute-start | bytes 98312 | tf_op jit(solution)/shard_map/ppermute | solution.py:86
  46.7 1.0 collective-permute-start.13
  47.8 1.5 collective-permute-start.14
  49.2 3.3 %collective-permute-done.13 = bf16[128,128]{1,0:T(8,128)(2,1)S(1)} collective-permute-done((bf16[128,128]{1,0:T(8,128)(2,1)S(1)}, bf16[128,128]{1,0:T(8,128)(2,1)S(1)}, u32[]{:S(2)}, u32[]{:S(2)}) %collective-permute-start.13) | collective-permute-done | bytes 32800 | tf_op jit(solution)/shard_map/ppermute | solution.py:86
  54.1 8.1 %all_gather.13.out_ref = bf16[512,512]{1,0:T(8,128)(2,1)S(1)} all-gather(bf16[128,512]{1,0:T(8,128)(2,1)S(1)} %copy-done.42), channel_id=1, replica_groups=mesh['ens'=2,'dom'=4,'feat'=2,'rep'=2] {'feat','rep'}, dimensions={0}, use_global_device_ids=true | all-gather | bytes 655360 | tf_op jit(solution)/shard_map/all_gather | solution.py:206
  63.9 1.4 copy-done.5
  65.4 1.2 copy-done.26
  66.6 1.2 copy-done.35
  70.5 2.9 %edge_local.1 = (f32[1024,512]{1,0:T(8,128)S(1)}, bf16[512,512]{1,0:T(8,128)(2,1)S(1)}) custom-call(s32[1]{0:T(128)} %bitcast.me_ref, bf16[1024,512]{1,0:T(8,128)(2,1)S(1)} %copy-done.26, bf16[1024,512]{1,0:T(8,128)(2,1)S(1)} %copy-done.35, bf16[1024,512]{1,0:T(8,128)(2,1)S(1)} %get-tuple-element.65.recv_ref, bf16[1536,512]{1,0:T(8,128)(2,1)S(1)} %copy-done.5, ...), custom_call_target="tpu_custom_call" | custom-call | flops 2684354560 | bytes 7864320 | tf_op jit(solution)/shard_map/edge_local/pallas_call | solution.py:62
  74.3 4.2 %edge_update.1 = (f32[1024,512]{1,0:T(8,128)S(1)}, bf16[2,128,512]{2,1,0:T(8,128)(2,1)S(1)}, bf16[2,128,512]{2,1,0:T(8,128)(2,1)S(1)}) custom-call(s32[1]{0:T(128)} %bitcast.me_ref, f32[1024,512]{1,0:T(8,128)S(1)} %get-tuple-element.71.local_ref, bf16[1024,512]{1,0:T(8,128)(2,1)S(1)} %copy-done.26, bf16[1024,512]{1,0:T(8,128)(2,1)S(1)} %copy-done.33, ...), custom_call_target="tpu_custom_call" | custom-call | flops 2147483648 | bytes 10485760 | tf_op jit(solution)/shard_map/edge_update/pallas_call | solution.py:62
  78.5 1.3 copy-done.3
  80.2 1.2 collective-permute-done.18.refs_1_
  82.9 8.8 %all_gather.15.out_ref = bf16[512,512]{1,0:T(8,128)(2,1)S(1)} all-gather(bf16[128,512]{1,0:T(8,128)(2,1)S(1)} %copy-done.43), channel_id=1, replica_groups=mesh['ens'=2,'dom'=4,'feat'=2,'rep'=2] {'feat','rep'}, dimensions={0}, use_global_device_ids=true | all-gather | bytes 655360 | tf_op jit(solution)/shard_map/all_gather | solution.py:206
  91.7 1.2 copy-done
  92.9 1.0 copy-done.18
  96.8 4.8 %collective-permute-done.21.refs_2_ = bf16[128,512]{1,0:T(8,128)(2,1)S(1)} collective-permute-done((bf16[128,512]{1,0:T(8,128)(2,1)S(1)}, bf16[128,512]{1,0:T(8,128)(2,1)S(1)}, u32[]{:S(2)}, u32[]{:S(2)}) %collective-permute-start.21) | collective-permute-done | bytes 131104 | tf_op jit(solution)/shard_map/ppermute | solution.py:83
  101.7 1.3 collective-permute-done.22.refs_3_
  103.0 1.2 copy-done.9
  104.2 1.2 copy-done.11
  105.5 2.7 %edge_backward.1 = (bf16[1024,512]{1,0:T(8,128)(2,1)S(1)}, bf16[2,512,128]{2,1,0:T(8,128)(2,1)S(1)}, bf16[2,512,128]{2,1,0:T(8,128)(2,1)S(1)}) custom-call(s32[1]{0:T(128)} %bitcast.me_ref, bf16[1024,512]{1,0:T(8,128)(2,1)S(1)} %copy-done.7, f32[1024,512]{1,0:T(8,128)S(1)} %copy-done.4, bf16[512,1024]{1,0:T(8,128)(2,1)S(1)} %copy-done.11, ...), custom_call_target="tpu_custom_call" | custom-call | flops 1879048192 | bytes 9437184 | tf_op jit(solution)/shard_map/edge_backward/pallas_call | solution.py:62
  108.4 2.1 %local_backward.1 = (bf16[2,512,128]{2,1,0:T(8,128)(2,1)S(1)}, bf16[2,512,128]{2,1,0:T(8,128)(2,1)S(1)}) custom-call(s32[1]{0:T(128)} %bitcast.me_ref, bf16[1024,512]{1,0:T(8,128)(2,1)S(1)} %get-tuple-element.88.dpre_ref, bf16[512,1024]{1,0:T(8,128)(2,1)S(1)} %copy-done.28, bf16[512,1024]{1,0:T(8,128)(2,1)S(1)} %copy-done.31, ...), custom_call_target="tpu_custom_call" | custom-call | flops 1610612736 | bytes 5505024 | tf_op jit(solution)/shard_map/local_backward/pallas_call | solution.py:62
  112.2 1.1 collective-permute-start.24
  113.2 4.2 %collective-permute-done.26.refs_1_ = bf16[512,128]{1,0:T(8,128)(2,1)S(1)} collective-permute-done((bf16[512,128]{1,0:T(8,128)(2,1)S(1)}, bf16[512,128]{1,0:T(8,128)(2,1)S(1)}, u32[]{:S(2)}, u32[]{:S(2)}) %collective-permute-start.26) | collective-permute-done | bytes 131104 | tf_op jit(solution)/shard_map/ppermute | solution.py:83
  117.8 1.9 %collective-permute-start.28 = (bf16[128,128]{1,0:T(8,128)(2,1)S(1)}, bf16[128,128]{1,0:T(8,128)(2,1)S(1)}, u32[]{:S(2)}, u32[]{:S(2)}) collective-permute-start(bf16[128,128]{1,0:T(8,128)(2,1)S(1)} %get-tuple-element.101), channel_id=1, source_target_pairs={{0,8},{4,12},{8,0},{12,4},{1,9},{5,13},{9,1},{13,5},{2,10},{6,14},... | collective-permute-start | bytes 98312 | tf_op jit(solution)/shard_map/ppermute | solution.py:86
  119.7 2.3 %collective-permute-start.29 = (bf16[128,128]{1,0:T(8,128)(2,1)S(1)}, bf16[128,128]{1,0:T(8,128)(2,1)S(1)}, u32[]{:S(2)}, u32[]{:S(2)}) collective-permute-start(bf16[128,128]{1,0:T(8,128)(2,1)S(1)} %get-tuple-element.102), channel_id=1, source_target_pairs={{0,12},{4,8},{8,4},{12,0},{1,13},{5,9},{9,5},{13,1},{2,14},{6,10},... | collective-permute-start | bytes 98312 | tf_op jit(solution)/shard_map/ppermute | solution.py:86
  122.7 2.6 %collective-permute-done.29.refs_5_ = bf16[128,128]{1,0:T(8,128)(2,1)S(1)} collective-permute-done((bf16[128,128]{1,0:T(8,128)(2,1)S(1)}, bf16[128,128]{1,0:T(8,128)(2,1)S(1)}, u32[]{:S(2)}, u32[]{:S(2)}) %collective-permute-start.29) | collective-permute-done | bytes 32800 | tf_op jit(solution)/shard_map/ppermute | solution.py:86
  125.4 1.2 owed_rows.1
  126.6 2.8 %collective-permute-start.31 = (bf16[512,128]{1,0:T(8,128)(2,1)S(1)}, bf16[512,128]{1,0:T(8,128)(2,1)S(1)}, u32[]{:S(2)}, u32[]{:S(2)}) collective-permute-start(bf16[512,128]{1,0:T(8,128)(2,1)S(1)} %get-tuple-element.105), channel_id=1, source_target_pairs={{0,8},{4,12},{8,0},{12,4},{1,9},{5,13},{9,1},{13,5},{2,10},{6,14},... | collective-permute-start | bytes 393224 | tf_op jit(solution)/shard_map/ppermute | solution.py:86
  129.4 1.6 %collective-permute-start.32 = (bf16[512,128]{1,0:T(8,128)(2,1)S(1)}, bf16[512,128]{1,0:T(8,128)(2,1)S(1)}, u32[]{:S(2)}, u32[]{:S(2)}) collective-permute-start(bf16[512,128]{1,0:T(8,128)(2,1)S(1)} %get-tuple-element.106), channel_id=1, source_target_pairs={{0,12},{4,8},{8,4},{12,0},{1,13},{5,9},{9,5},{13,1},{2,14},{6,10},... | collective-permute-start | bytes 393224 | tf_op jit(solution)/shard_map/ppermute | solution.py:86
  131.0 2.5 %collective-permute-done.30.refs_1_ = bf16[512,128]{1,0:T(8,128)(2,1)S(1)} collective-permute-done((bf16[512,128]{1,0:T(8,128)(2,1)S(1)}, bf16[512,128]{1,0:T(8,128)(2,1)S(1)}, u32[]{:S(2)}, u32[]{:S(2)}) %collective-permute-start.30) | collective-permute-done | bytes 131104 | tf_op jit(solution)/shard_map/ppermute | solution.py:86
  133.5 3.4 %collective-permute-done.31.refs_2_ = bf16[512,128]{1,0:T(8,128)(2,1)S(1)} collective-permute-done((bf16[512,128]{1,0:T(8,128)(2,1)S(1)}, bf16[512,128]{1,0:T(8,128)(2,1)S(1)}, u32[]{:S(2)}, u32[]{:S(2)}) %collective-permute-start.31) | collective-permute-done | bytes 131104 | tf_op jit(solution)/shard_map/ppermute | solution.py:86
  139.3 3.1 %collective-permute-done.34.refs_2_ = bf16[256,128]{1,0:T(8,128)(2,1)S(1)} collective-permute-done((bf16[256,128]{1,0:T(8,128)(2,1)S(1)}, bf16[256,128]{1,0:T(8,128)(2,1)S(1)}, u32[]{:S(2)}, u32[]{:S(2)}) %collective-permute-start.34) | collective-permute-done | bytes 65568 | tf_op jit(solution)/shard_map/ppermute | solution.py:83
  142.9 1.1 adjoint.1
  (142 shorter events, 27.9 us)
Async XLA Ops:
  6.5 34.9 %copy-start.14 = (bf16[512,512]{1,0:T(8,128)(2,1)S(1)}, bf16[512,512]{1,0:T(8,128)(2,1)}, u32[]{:S(2)}) copy-start(bf16[512,512]{1,0:T(8,128)(2,1)} %base_ref.1) | copy-start | bytes 1572868
  6.5 57.4 %all-gather.3.cloned.1.call-start = ((), (), s32[]{:S(2)}) async-start(), calls=%async_computation | async-start | bytes 1966080 | tf_op jit(solution)/shard_map/all_gather | solution.py:206
  7.3 84.5 %all-gather.5.cloned.1.call-start = ((), (), s32[]{:S(2)}) async-start(), calls=%async_computation.1 | async-start | bytes 1310720 | tf_op jit(solution)/shard_map/all_gather | solution.py:206
  7.3 10.0 %collective-permute-start.1 = (bf16[256,512]{1,0:T(8,128)(2,1)}, bf16[256,512]{1,0:T(8,128)(2,1)S(1)}, u32[]{:S(2)}, u32[]{:S(2)}) collective-permute-start(bf16[256,512]{1,0:T(8,128)(2,1)} %refs_0_.1), channel_id=1, source_target_pairs={{0,2},{1,3},{2,0},{3,1},{4,6},{5,7},{6,4},{7,5},{8,10},{9,11},{10,... | collective-permute-start | bytes 786440 | tf_op jit(solution)/shard_map/ppermute | solution.py:83
  14.8 5.4 %collective-permute-start.4 = (bf16[144,512]{1,0:T(8,128)(2,1)S(1)}, bf16[144,512]{1,0:T(8,128)(2,1)S(1)}, u32[]{:S(2)}, u32[]{:S(2)}) collective-permute-start(bf16[144,512]{1,0:T(8,128)(2,1)S(1)} %get-tuple-element.58.refs_4_), channel_id=1, source_target_pairs={{0,2},{1,3},{2,0},{3,1},{4,6},{5,7},{6,4},{7,5},{8,10},{9,11},{10,... | collective-permute-start | bytes 442376 | tf_op jit(solution)/shard_map/ppermute | solution.py:83
  14.9 5.3 %collective-permute-start = (bf16[256,512]{1,0:T(8,128)(2,1)}, bf16[256,512]{1,0:T(8,128)(2,1)S(1)}, u32[]{:S(2)}, u32[]{:S(2)}) collective-permute-start(bf16[256,512]{1,0:T(8,128)(2,1)} %refs_0_.1), channel_id=1, source_target_pairs={{0,1},{1,0},{2,3},{3,2},{4,5},{5,4},{6,7},{7,6},{8,9},{9,8},{10,11... | collective-permute-start | bytes 786440 | tf_op jit(solution)/shard_map/ppermute | solution.py:83
  17.3 4.2 %collective-permute-start.2 = (bf16[256,512]{1,0:T(8,128)(2,1)S(1)}, bf16[256,512]{1,0:T(8,128)(2,1)S(1)}, u32[]{:S(2)}, u32[]{:S(2)}) collective-permute-start(bf16[256,512]{1,0:T(8,128)(2,1)S(1)} %collective-permute-done.1.refs_2_), channel_id=1, source_target_pairs={{0,1},{1,0},{2,3},{3,2},{4,5},{5,4},{6,7},{7,6},{8,9},{9,8},{10,11... | collective-permute-start | bytes 786440 | tf_op jit(solution)/shard_map/ppermute | solution.py:83
  17.3 2.9 %collective-permute-start.3 = (bf16[144,512]{1,0:T(8,128)(2,1)S(1)}, bf16[144,512]{1,0:T(8,128)(2,1)S(1)}, u32[]{:S(2)}, u32[]{:S(2)}) collective-permute-start(bf16[144,512]{1,0:T(8,128)(2,1)S(1)} %get-tuple-element.58.refs_4_), channel_id=1, source_target_pairs={{0,1},{1,0},{2,3},{3,2},{4,5},{5,4},{6,7},{7,6},{8,9},{9,8},{10,11... | collective-permute-start | bytes 442376 | tf_op jit(solution)/shard_map/ppermute | solution.py:83
  20.2 1.4 collective-permute-start.5
  22.5 31.5 %copy-start.42 = (bf16[128,512]{1,0:T(8,128)(2,1)S(1)}, bf16[128,512]{1,0:T(8,128)(2,1)}, u32[]{:S(2)}) copy-start(bf16[128,512]{1,0:T(8,128)(2,1)} %param.20) | copy-start | bytes 393220
  26.7 12.2 %collective-permute-start.6 = (bf16[512,128]{1,0:T(8,128)(2,1)}, bf16[512,128]{1,0:T(8,128)(2,1)S(1)}, u32[]{:S(2)}, u32[]{:S(2)}) collective-permute-start(bf16[512,128]{1,0:T(8,128)(2,1)} %get-tuple-element.67), channel_id=1, source_target_pairs={{0,4},{4,0},{8,12},{12,8},{1,5},{5,1},{9,13},{13,9},{2,6},{6,2},{1... | collective-permute-start | bytes 393224 | tf_op jit(solution)/shard_map/ppermute | solution.py:86
  28.3 13.1 %collective-permute-start.7 = (bf16[512,128]{1,0:T(8,128)(2,1)}, bf16[512,128]{1,0:T(8,128)(2,1)S(1)}, u32[]{:S(2)}, u32[]{:S(2)}) collective-permute-start(bf16[512,128]{1,0:T(8,128)(2,1)} %get-tuple-element.68), channel_id=1, source_target_pairs={{0,8},{4,12},{8,0},{12,4},{1,9},{5,13},{9,1},{13,5},{2,10},{6,14},... | collective-permute-start | bytes 393224 | tf_op jit(solution)/shard_map/ppermute | solution.py:86
  30.9 10.5 %collective-permute-start.8 = (bf16[512,128]{1,0:T(8,128)(2,1)S(1)}, bf16[512,128]{1,0:T(8,128)(2,1)S(1)}, u32[]{:S(2)}, u32[]{:S(2)}) collective-permute-start(bf16[512,128]{1,0:T(8,128)(2,1)S(1)} %get-tuple-element.69), channel_id=1, source_target_pairs={{0,12},{4,8},{8,4},{12,0},{1,13},{5,9},{9,5},{13,1},{2,14},{6,10},... | collective-permute-start | bytes 393224 | tf_op jit(solution)/shard_map/ppermute | solution.py:86
  39.0 34.5 %copy-start.8 = (bf16[1024,512]{1,0:T(8,128)(2,1)}, bf16[1024,512]{1,0:T(8,128)(2,1)S(1)}, u32[]{:S(2)}) copy-start(bf16[1024,512]{1,0:T(8,128)(2,1)S(1)} %get-tuple-element.65.recv_ref) | copy-start | bytes 3145732
  42.8 19.8 %collective-permute-start.9 = (bf16[512,128]{1,0:T(8,128)(2,1)S(1)}, bf16[512,128]{1,0:T(8,128)(2,1)S(1)}, u32[]{:S(2)}, u32[]{:S(2)}) collective-permute-start(bf16[512,128]{1,0:T(8,128)(2,1)S(1)} %get-tuple-element.70.refs_0_), channel_id=1, source_target_pairs={{0,1},{1,0},{2,3},{3,2},{4,5},{5,4},{6,7},{7,6},{8,9},{9,8},{10,11... | collective-permute-start | bytes 393224 | tf_op jit(solution)/shard_map/ppermute | solution.py:83
  42.9 11.1 %collective-permute-start.10 = (bf16[512,128]{1,0:T(8,128)(2,1)S(1)}, bf16[512,128]{1,0:T(8,128)(2,1)S(1)}, u32[]{:S(2)}, u32[]{:S(2)}) collective-permute-start(bf16[512,128]{1,0:T(8,128)(2,1)S(1)} %get-tuple-element.70.refs_0_), channel_id=1, source_target_pairs={{0,2},{1,3},{2,0},{3,1},{4,6},{5,7},{6,4},{7,5},{8,10},{9,11},{10,... | collective-permute-start | bytes 393224 | tf_op jit(solution)/shard_map/ppermute | solution.py:83
  44.4 4.8 %collective-permute-start.12 = (bf16[128,128]{1,0:T(8,128)(2,1)S(1)}, bf16[128,128]{1,0:T(8,128)(2,1)S(1)}, u32[]{:S(2)}, u32[]{:S(2)}) collective-permute-start(bf16[128,128]{1,0:T(8,128)(2,1)S(1)} %get-tuple-element.75), channel_id=1, source_target_pairs={{0,4},{4,0},{8,12},{12,8},{1,5},{5,1},{9,13},{13,9},{2,6},{6,2},{1... | collective-permute-start | bytes 98312 | tf_op jit(solution)/shard_map/ppermute | solution.py:86
  46.7 5.8 %collective-permute-start.13 = (bf16[128,128]{1,0:T(8,128)(2,1)S(1)}, bf16[128,128]{1,0:T(8,128)(2,1)S(1)}, u32[]{:S(2)}, u32[]{:S(2)}) collective-permute-start(bf16[128,128]{1,0:T(8,128)(2,1)S(1)} %get-tuple-element.76), channel_id=1, source_target_pairs={{0,8},{4,12},{8,0},{12,4},{1,9},{5,13},{9,1},{13,5},{2,10},{6,14},... | collective-permute-start | bytes 98312 | tf_op jit(solution)/shard_map/ppermute | solution.py:86
  47.8 5.7 %collective-permute-start.14 = (bf16[128,128]{1,0:T(8,128)(2,1)S(1)}, bf16[128,128]{1,0:T(8,128)(2,1)S(1)}, u32[]{:S(2)}, u32[]{:S(2)}) collective-permute-start(bf16[128,128]{1,0:T(8,128)(2,1)S(1)} %get-tuple-element.77), channel_id=1, source_target_pairs={{0,12},{4,8},{8,4},{12,0},{1,13},{5,9},{9,5},{13,1},{2,14},{6,10},... | collective-permute-start | bytes 98312 | tf_op jit(solution)/shard_map/ppermute | solution.py:86
  53.5 9.0 %collective-permute-start.16 = (bf16[512,128]{1,0:T(8,128)(2,1)S(1)}, bf16[512,128]{1,0:T(8,128)(2,1)}, u32[]{:S(2)}, u32[]{:S(2)}) collective-permute-start(bf16[512,128]{1,0:T(8,128)(2,1)S(1)} %constant_dynamic-update-slice_fusion.refs_0_), channel_id=1, source_target_pairs={{0,2},{1,3},{2,0},{3,1},{4,6},{5,7},{6,4},{7,5},{8,10},{9,11},{10,... | collective-permute-start | bytes 393224 | tf_op jit(solution)/shard_map/ppermute | solution.py:83
  54.0 9.9 %copy-start.38 = (bf16[512,128]{1,0:T(8,128)(2,1)}, bf16[512,128]{1,0:T(8,128)(2,1)S(1)}, u32[]{:S(2)}) copy-start(bf16[512,128]{1,0:T(8,128)(2,1)S(1)} %collective-permute-done.10.refs_2_) | copy-start | bytes 393220
  54.0 9.3 %collective-permute-start.11 = (bf16[512,128]{1,0:T(8,128)(2,1)S(1)}, bf16[512,128]{1,0:T(8,128)(2,1)S(1)}, u32[]{:S(2)}, u32[]{:S(2)}) collective-permute-start(bf16[512,128]{1,0:T(8,128)(2,1)S(1)} %collective-permute-done.10.refs_2_), channel_id=1, source_target_pairs={{0,1},{1,0},{2,3},{3,2},{4,5},{5,4},{6,7},{7,6},{8,9},{9,8},{10,11... | collective-permute-start | bytes 393224 | tf_op jit(solution)/shard_map/ppermute | solution.py:83
  62.1 12.1 %collective-permute-start.15 = (bf16[512,128]{1,0:T(8,128)(2,1)S(1)}, bf16[512,128]{1,0:T(8,128)(2,1)}, u32[]{:S(2)}, u32[]{:S(2)}) collective-permute-start(bf16[512,128]{1,0:T(8,128)(2,1)S(1)} %constant_dynamic-update-slice_fusion.refs_0_), channel_id=1, source_target_pairs={{0,1},{1,0},{2,3},{3,2},{4,5},{5,4},{6,7},{7,6},{8,9},{9,8},{10,11... | collective-permute-start | bytes 393224 | tf_op jit(solution)/shard_map/ppermute | solution.py:83
  62.5 11.8 %collective-permute-start.17 = (bf16[512,128]{1,0:T(8,128)(2,1)}, bf16[512,128]{1,0:T(8,128)(2,1)}, u32[]{:S(2)}, u32[]{:S(2)}) collective-permute-start(bf16[512,128]{1,0:T(8,128)(2,1)} %collective-permute-done.16.refs_2_), channel_id=1, source_target_pairs={{0,1},{1,0},{2,3},{3,2},{4,5},{5,4},{6,7},{7,6},{8,9},{9,8},{10,11... | collective-permute-start | bytes 393224 | tf_op jit(solution)/shard_map/ppermute | solution.py:83
  74.3 8.6 %copy-start.43 = (bf16[128,512]{1,0:T(8,128)(2,1)S(1)}, bf16[128,512]{1,0:T(8,128)(2,1)}, u32[]{:S(2)}) copy-start(bf16[128,512]{1,0:T(8,128)(2,1)} %param.22) | copy-start | bytes 393220
  74.3 17.4 %copy-start.2 = (bf16[512,512]{1,0:T(8,128)(2,1)S(1)}, bf16[512,512]{1,0:T(8,128)(2,1)}, u32[]{:S(2)}) copy-start(bf16[512,512]{1,0:T(8,128)(2,1)} %grad_ref.4) | copy-start | bytes 1572868
  79.9 1.5 %collective-permute-start.18 = (bf16[2,128,512]{2,1,0:T(8,128)(2,1)S(1)}, bf16[2,128,512]{2,1,0:T(8,128)(2,1)S(1)}, u32[]{:S(2)}, u32[]{:S(2)}) collective-permute-start(bf16[2,128,512]{2,1,0:T(8,128)(2,1)S(1)} %get-tuple-element.84), channel_id=1, source_target_pairs={{0,1},{1,0},{2,3},{3,2},{4,5},{5,4},{6,7},{7,6},{8,9},{9,8},{10,11... | collective-permute-start | bytes 786440 | tf_op jit(solution)/shard_map/ppermute | solution.py:83
  82.1 12.3 %collective-permute-start.19 = (bf16[128,512]{1,0:T(8,128)(2,1)}, bf16[128,512]{1,0:T(8,128)(2,1)S(1)}, u32[]{:S(2)}, u32[]{:S(2)}) collective-permute-start(bf16[128,512]{1,0:T(8,128)(2,1)} %get-tuple-element.86), channel_id=1, source_target_pairs={{0,2},{1,3},{2,0},{3,1},{4,6},{5,7},{6,4},{7,5},{8,10},{9,11},{10,... | collective-permute-start | bytes 393224 | tf_op jit(solution)/shard_map/ppermute | solution.py:83
  94.0 9.0 %copy-start.4 = (f32[1024,512]{1,0:T(8,128)S(1)}, f32[1024,512]{1,0:T(8,128)}, u32[]{:S(2)}) copy-start(f32[1024,512]{1,0:T(8,128)} %copy-done.3) | copy-start | bytes 6291460
  94.0 9.0 %copy-start.7 = (bf16[1024,512]{1,0:T(8,128)(2,1)S(1)}, bf16[1024,512]{1,0:T(8,128)(2,1)}, u32[]{:S(2)}) copy-start(bf16[1024,512]{1,0:T(8,128)(2,1)} %grad_ref.5) | copy-start | bytes 3145732
  95.8 5.8 %collective-permute-start.21 = (bf16[128,512]{1,0:T(8,128)(2,1)S(1)}, bf16[128,512]{1,0:T(8,128)(2,1)S(1)}, u32[]{:S(2)}, u32[]{:S(2)}) collective-permute-start(bf16[128,512]{1,0:T(8,128)(2,1)S(1)} %get-tuple-element.87.refs_0_), channel_id=1, source_target_pairs={{0,2},{1,3},{2,0},{3,1},{4,6},{5,7},{6,4},{7,5},{8,10},{9,11},{10,... | collective-permute-start | bytes 393224 | tf_op jit(solution)/shard_map/ppermute | solution.py:83
  96.8 4.9 %collective-permute-start.20 = (bf16[128,512]{1,0:T(8,128)(2,1)S(1)}, bf16[128,512]{1,0:T(8,128)(2,1)S(1)}, u32[]{:S(2)}, u32[]{:S(2)}) collective-permute-start(bf16[128,512]{1,0:T(8,128)(2,1)S(1)} %get-tuple-element.87.refs_0_), channel_id=1, source_target_pairs={{0,1},{1,0},{2,3},{3,2},{4,5},{5,4},{6,7},{7,6},{8,9},{9,8},{10,11... | collective-permute-start | bytes 393224 | tf_op jit(solution)/shard_map/ppermute | solution.py:83
  101.7 1.3 collective-permute-start.22
  108.2 2.8 %collective-permute-start.25 = (bf16[2,512,128]{2,1,0:T(8,128)(2,1)S(1)}, bf16[2,512,128]{2,1,0:T(8,128)(2,1)S(1)}, u32[]{:S(2)}, u32[]{:S(2)}) collective-permute-start(bf16[2,512,128]{2,1,0:T(8,128)(2,1)S(1)} %get-tuple-element.96), channel_id=1, source_target_pairs={{0,1},{1,0},{2,3},{3,2},{4,5},{5,4},{6,7},{7,6},{8,9},{9,8},{10,11... | collective-permute-start | bytes 786440 | tf_op jit(solution)/shard_map/ppermute | solution.py:83
  110.5 26.4 %copy-start.16 = (f32[4,256,128]{2,1,0:T(8,128)S(1)}, f32[4,256,128]{2,1,0:T(8,128)}, u32[]{:S(2)}) copy-start(f32[4,256,128]{2,1,0:T(8,128)} %copy-done.15) | copy-start | bytes 1572868
  110.5 32.3 %copy-start.13 = (bf16[512,512]{1,0:T(8,128)(2,1)S(1)}, bf16[512,512]{1,0:T(8,128)(2,1)}, u32[]{:S(2)}) copy-start(bf16[512,512]{1,0:T(8,128)(2,1)} %copy-done.12) | copy-start | bytes 1572868
  110.5 1.6 %collective-permute-start.23 = (bf16[2,512,128]{2,1,0:T(8,128)(2,1)S(1)}, bf16[2,512,128]{2,1,0:T(8,128)(2,1)S(1)}, u32[]{:S(2)}, u32[]{:S(2)}) collective-permute-start(bf16[2,512,128]{2,1,0:T(8,128)(2,1)S(1)} %get-tuple-element.92), channel_id=1, source_target_pairs={{0,1},{1,0},{2,3},{3,2},{4,5},{5,4},{6,7},{7,6},{8,9},{9,8},{10,11... | collective-permute-start | bytes 786440 | tf_op jit(solution)/shard_map/ppermute | solution.py:83
  111.0 6.4 %collective-permute-start.26 = (bf16[512,128]{1,0:T(8,128)(2,1)S(1)}, bf16[512,128]{1,0:T(8,128)(2,1)S(1)}, u32[]{:S(2)}, u32[]{:S(2)}) collective-permute-start(bf16[512,128]{1,0:T(8,128)(2,1)S(1)} %get-tuple-element.98), channel_id=1, source_target_pairs={{0,2},{1,3},{2,0},{3,1},{4,6},{5,7},{6,4},{7,5},{8,10},{9,11},{10,... | collective-permute-start | bytes 393224 | tf_op jit(solution)/shard_map/ppermute | solution.py:83
  112.2 9.7 %collective-permute-start.24 = (bf16[512,128]{1,0:T(8,128)(2,1)S(1)}, bf16[512,128]{1,0:T(8,128)(2,1)S(1)}, u32[]{:S(2)}, u32[]{:S(2)}) collective-permute-start(bf16[512,128]{1,0:T(8,128)(2,1)S(1)} %get-tuple-element.94), channel_id=1, source_target_pairs={{0,2},{1,3},{2,0},{3,1},{4,6},{5,7},{6,4},{7,5},{8,10},{9,11},{10,... | collective-permute-start | bytes 393224 | tf_op jit(solution)/shard_map/ppermute | solution.py:83
  117.5 4.5 %collective-permute-start.27 = (bf16[128,128]{1,0:T(8,128)(2,1)S(1)}, bf16[128,128]{1,0:T(8,128)(2,1)S(1)}, u32[]{:S(2)}, u32[]{:S(2)}) collective-permute-start(bf16[128,128]{1,0:T(8,128)(2,1)S(1)} %get-tuple-element.100), channel_id=1, source_target_pairs={{0,4},{4,0},{8,12},{12,8},{1,5},{5,1},{9,13},{13,9},{2,6},{6,2},{1... | collective-permute-start | bytes 98312 | tf_op jit(solution)/shard_map/ppermute | solution.py:86
  117.8 5.0 %collective-permute-start.28 = (bf16[128,128]{1,0:T(8,128)(2,1)S(1)}, bf16[128,128]{1,0:T(8,128)(2,1)S(1)}, u32[]{:S(2)}, u32[]{:S(2)}) collective-permute-start(bf16[128,128]{1,0:T(8,128)(2,1)S(1)} %get-tuple-element.101), channel_id=1, source_target_pairs={{0,8},{4,12},{8,0},{12,4},{1,9},{5,13},{9,1},{13,5},{2,10},{6,14},... | collective-permute-start | bytes 98312 | tf_op jit(solution)/shard_map/ppermute | solution.py:86
  119.7 5.7 %collective-permute-start.29 = (bf16[128,128]{1,0:T(8,128)(2,1)S(1)}, bf16[128,128]{1,0:T(8,128)(2,1)S(1)}, u32[]{:S(2)}, u32[]{:S(2)}) collective-permute-start(bf16[128,128]{1,0:T(8,128)(2,1)S(1)} %get-tuple-element.102), channel_id=1, source_target_pairs={{0,12},{4,8},{8,4},{12,0},{1,13},{5,9},{9,5},{13,1},{2,14},{6,10},... | collective-permute-start | bytes 98312 | tf_op jit(solution)/shard_map/ppermute | solution.py:86
  126.5 6.9 %collective-permute-start.30 = (bf16[512,128]{1,0:T(8,128)(2,1)S(1)}, bf16[512,128]{1,0:T(8,128)(2,1)S(1)}, u32[]{:S(2)}, u32[]{:S(2)}) collective-permute-start(bf16[512,128]{1,0:T(8,128)(2,1)S(1)} %get-tuple-element.104), channel_id=1, source_target_pairs={{0,4},{4,0},{8,12},{12,8},{1,5},{5,1},{9,13},{13,9},{2,6},{6,2},{1... | collective-permute-start | bytes 393224 | tf_op jit(solution)/shard_map/ppermute | solution.py:86
  126.6 10.3 %collective-permute-start.31 = (bf16[512,128]{1,0:T(8,128)(2,1)S(1)}, bf16[512,128]{1,0:T(8,128)(2,1)S(1)}, u32[]{:S(2)}, u32[]{:S(2)}) collective-permute-start(bf16[512,128]{1,0:T(8,128)(2,1)S(1)} %get-tuple-element.105), channel_id=1, source_target_pairs={{0,8},{4,12},{8,0},{12,4},{1,9},{5,13},{9,1},{13,5},{2,10},{6,14},... | collective-permute-start | bytes 393224 | tf_op jit(solution)/shard_map/ppermute | solution.py:86
  129.4 7.5 %collective-permute-start.32 = (bf16[512,128]{1,0:T(8,128)(2,1)S(1)}, bf16[512,128]{1,0:T(8,128)(2,1)S(1)}, u32[]{:S(2)}, u32[]{:S(2)}) collective-permute-start(bf16[512,128]{1,0:T(8,128)(2,1)S(1)} %get-tuple-element.106), channel_id=1, source_target_pairs={{0,12},{4,8},{8,4},{12,0},{1,13},{5,9},{9,5},{13,1},{2,14},{6,10},... | collective-permute-start | bytes 393224 | tf_op jit(solution)/shard_map/ppermute | solution.py:86
  137.3 1.9 %collective-permute-start.33 = (bf16[256,128]{1,0:T(8,128)(2,1)S(1)}, bf16[256,128]{1,0:T(8,128)(2,1)S(1)}, u32[]{:S(2)}, u32[]{:S(2)}) collective-permute-start(bf16[256,128]{1,0:T(8,128)(2,1)S(1)} %get-tuple-element.108), channel_id=1, source_target_pairs={{0,1},{1,0},{2,3},{3,2},{4,5},{5,4},{6,7},{7,6},{8,9},{9,8},{10,11... | collective-permute-start | bytes 196616 | tf_op jit(solution)/shard_map/ppermute | solution.py:83
  137.4 5.0 %collective-permute-start.34 = (bf16[256,128]{1,0:T(8,128)(2,1)S(1)}, bf16[256,128]{1,0:T(8,128)(2,1)S(1)}, u32[]{:S(2)}, u32[]{:S(2)}) collective-permute-start(bf16[256,128]{1,0:T(8,128)(2,1)S(1)} %get-tuple-element.109), channel_id=1, source_target_pairs={{0,2},{1,3},{2,0},{3,1},{4,6},{5,7},{6,4},{7,5},{8,10},{9,11},{10,... | collective-permute-start | bytes 196616 | tf_op jit(solution)/shard_map/ppermute | solution.py:83
  138.3 4.6 %collective-permute-start.35 = (bf16[256,128]{1,0:T(8,128)(2,1)S(1)}, bf16[256,128]{1,0:T(8,128)(2,1)S(1)}, u32[]{:S(2)}, u32[]{:S(2)}) collective-permute-start(bf16[256,128]{1,0:T(8,128)(2,1)S(1)} %get-tuple-element.110), channel_id=1, source_target_pairs={{0,3},{1,2},{2,1},{3,0},{4,7},{5,6},{6,5},{7,4},{8,11},{9,10},{10,... | collective-permute-start | bytes 196616 | tf_op jit(solution)/shard_map/ppermute | solution.py:83
  (34 other events, 44.9 us)
Sparse Core Ops, SparseCore 0:
  8.9 22.3 all-gather.2
  32.9 19.1 all-gather.4

commit v4 on v3

--- a/solution.py
+++ b/solution.py
@@ -10,6 +10,7 @@
 SMEM = pl.BlockSpec(memory_space=pltpu.SMEM)
 VMEM = pl.BlockSpec(memory_space=pltpu.VMEM)
 HBM = pl.BlockSpec(memory_space=pltpu.HBM)
+ANY = pl.BlockSpec(memory_space=pl.ANY)
 
 
 def dot(a, b):
@@ -56,19 +57,19 @@
     return parts[0] if len(parts) == 1 else jnp.concatenate(parts, axis=0)
 
 
-def call(body, name, me, ins, outs, scratch=(), flops=0, far=()):
+def call(body, name, me, ins, outs, scratch=(), flops=0, far=(), unread=()):
     size = lambda s: s.size * s.dtype.itemsize
     moved = sum(size(x) for x in ins) + sum(size(x) for x in outs)
     return pl.pallas_call(
         body,
         out_shape=list(outs),
-        in_specs=[SMEM] + [HBM if i in far else VMEM for i in range(len(ins))],
+        in_specs=[SMEM] + [HBM if i in far else ANY if i in unread else VMEM for i in range(len(ins))],
         out_specs=[VMEM] * len(outs),
         scratch_shapes=list(scratch),
         compiler_params=pltpu.CompilerParams(vmem_limit_bytes=24 * 2**20),
         cost_estimate=pl.CostEstimate(flops=flops, bytes_accessed=moved, transcendentals=0),
         name=name,
-    )(me, *ins)
+    )(me, *[pltpu.with_memory_space_constraint(x, pltpu.HBM) if i in far else x for i, x in enumerate(ins)])
 
 
 def shape(dims, dtype=BF):
@@ -203,11 +204,35 @@
 
         state_parts = member_gather_chips(grid_state)
         pack_parts = member_gather_chips(pack)
-        gather = lambda w: lax.all_gather(w, ("feat", "rep"), axis=0, tiled=True)
-        in_full = gather(edge_in_weight)
-        out_full = gather(edge_out_weight)
-        node_in_full = gather(node_in_weight)
-        node_out_full = gather(node_out_weight)
+
+        def relay(name, weights, arrived):
+            rows = [w.shape[0] for w in weights]
+            starts = [sum(rows[:i]) for i in range(len(rows))]
+
+            def relay_kernel(me_ref, *refs):
+                out, sems = refs[-2:]
+                copies = [
+                    pltpu.make_async_copy(refs[i], out.at[at : at + n, :], sems.at[i])
+                    for i, (at, n) in enumerate(zip(starts, rows))
+                ]
+                for copy in copies:
+                    copy.start()
+                for copy in copies:
+                    copy.wait()
+
+            return call(
+                relay_kernel,
+                name,
+                me1,
+                list(weights) + [arrived],
+                [shape((sum(rows), D))],
+                scratch=[pltpu.SemaphoreType.DMA((len(rows),))],
+                far=range(len(rows)),
+                unread=(len(rows),),
+            )[0]
+
+        edge_in_own = relay("relay_edge", [edge_in_weight], state_parts[n_rep])
+        in_parts = member_gather_chips(edge_in_own)
 
         def hots_kernel(me_ref, send_ref, recv_ref, sl_out, sh_out, r_out, slt_out, sht_out, rt_out):
             for i in range(E // T):
@@ -230,8 +255,8 @@
 
         def grid_kernel(me_ref, *refs):
             states, packs = refs[:M], refs[M : 2 * M]
-            enc_out, slope_out, table_out = refs[2 * M : 2 * M + 3]
-            outs, (own, sem) = refs[2 * M + 3 : 2 * M + 3 + n_dom], refs[2 * M + 3 + n_dom :]
+            enc_out, slope_out, table_out = refs[2 * M + 1 : 2 * M + 4]
+            outs, (own, sem) = refs[2 * M + 4 : 2 * M + 4 + n_dom], refs[2 * M + 4 + n_dom :]
             me = me_ref[0]
             copy = pltpu.make_async_copy(states[0], own, sem)
             copy.start()
@@ -256,14 +281,17 @@
             grid_kernel,
             "grid_messages",
             me1,
-            state_parts + pack_parts,
+            state_parts + pack_parts + [edge_in_own],
             [shape((D, D)), shape((M, G, C), F32), shape((M, 2, NS), jnp.int32)]
             + [shape((M * S, C))] * n_dom,
             scratch=[pltpu.VMEM((G, D), BF), pltpu.SemaphoreType.DMA(())],
             flops=2 * M * G * D * C + 2 * M * NS * G * C,
             far=(0,),
+            unread=(2 * M,),
         )
         incoming = dom_trade(outgoing)
+        rest = relay("relay_rest", [edge_out_weight, node_in_weight, node_out_weight], incoming[1])
+        rest_parts = member_gather_chips(rest)
 
         def encode_kernel(me_ref, base_ref, halo_ref, table_ref, *refs):
             arrived, state_out, outs = refs[:n_dom], refs[n_dom], refs[n_dom + 1 :]
@@ -290,43 +318,54 @@
         halo_cols = jnp.concatenate(halo_in, axis=0)
         halo_parts = member_gather_chips(halo_cols)
 
-        def local_kernel(me_ref, es_ref, send_ref, recv_ref, w_ref, *refs):
-            cols, (pre_out, state_out, parts) = refs[:M], refs[M:]
+        def local_kernel(me_ref, es_ref, send_ref, recv_ref, *refs):
+            cols, weights = refs[:M], refs[M : 2 * M]
+            pre_out, state_out, w_out, parts = refs[2 * M :]
             me = me_ref[0]
             for k in range(M):
                 parts[me ^ k] = cols[k][...]
+                w_out[rows_at(me ^ k, rows_in), :] = weights[k][...]
             state_out[...] = lanes([parts[j] for j in range(M)])
             for i in range(E // T):
                 at = slice(i * T, (i + 1) * T)
                 sent = dot(send_ref[at, :], state_out[...]).astype(BF)
                 got = dot(recv_ref[at, :], state_out[...]).astype(BF)
                 pre_out[at, :] = (
-                    dot(es_ref[at, :], w_ref[:D, :])
-                    + dot(sent, w_ref[D : 2 * D, :])
-                    + dot(got, w_ref[2 * D :, :])
+                    dot(es_ref[at, :], w_out[:D, :])
+                    + dot(sent, w_out[D : 2 * D, :])
+                    + dot(got, w_out[2 * D :, :])
                 )
 
-        local_pre, mesh_state = call(
+        local_pre, mesh_state, in_full = call(
             local_kernel,
             "edge_local",
             me1,
-            [edge_state, sl_hot, r_hot, in_full] + state_parts2,
-            [shape((E, D), F32), shape((N, D))],
+            [edge_state, sl_hot, r_hot] + state_parts2 + in_parts,
+            [shape((E, D), F32), shape((N, D)), shape((3 * D, D))],
             scratch=[pltpu.VMEM((M, N, C), BF)],
             flops=2 * E * D * (3 * D + 2 * N),
         )
 
-        def node_ahead_kernel(me_ref, state_ref, grad_ref, in_ref, out_ref, pre_out, cot_out):
-            mine = rows_at(me_ref[0], R)
-            pre_out[...] = dot(state_ref[mine, :], in_ref[:D, :])
-            cot_out[...] = dot_t(grad_ref[mine, :], out_ref[...])
-
-        node_pre, node_cot = call(
+        def node_ahead_kernel(me_ref, state_ref, grad_ref, *refs):
+            weights = refs[:M]
+            out_full, node_in_full, pre_out, cot_out, node_out_full = refs[M:]
+            me = me_ref[0]
+            for k in range(M):
+                first, second = rows_out, rows_out + rows_node
+                out_full[rows_at(me ^ k, rows_out), :] = weights[k][:first, :]
+                node_in_full[rows_at(me ^ k, rows_node), :] = weights[k][first:second, :]
+                node_out_full[rows_at(me ^ k, rows_out), :] = weights[k][second:, :]
+            mine = rows_at(me, R)
+            pre_out[...] = dot(state_ref[mine, :], node_in_full[:D, :])
+            cot_out[...] = dot_t(grad_ref[mine, :], node_out_full[...])
+
+        out_full, node_in_full, node_pre, node_cot = call(
             node_ahead_kernel,
             "node_ahead",
             me1,
-            [mesh_state, node_grad, node_in_full, node_out_full],
-            [shape((R, D), F32), shape((R, D), F32)],
+            [mesh_state, node_grad] + rest_parts,
+            [shape((D, D)), shape((2 * D, D)), shape((R, D), F32), shape((R, D), F32)],
+            scratch=[pltpu.VMEM((D, D), BF)],
             flops=4 * R * D * D,
         )
 

time: 151 us -> 120 us (0.79)
  local copies, waits for them, and re-layouts: 27.4 us -> 0.06 us
  blocking collectives: 16.9 us -> 0 us
  between operations: 13.7 us -> 0.31 us
  waiting for transfers between devices: 38.2 us -> 50.8 us
  starting transfers between devices: 31.1 us -> 43.4 us
    unnamed x91 -> x13, local copies, waits for them, and re-layouts: 27.4 us -> 0.05 us
    all_gather x2 -> x0, blocking collectives: 16.9 us -> none  [per_device(): gather = lambda w: lax.all_gather(w, ('feat', 'rep'), axis=0, tiled=True)]
    ppermute x12, waiting for transfers between devices: 16.1 us -> 22.7 us  [dom_swap(): return lax.ppermute(x, 'dom', [(i, i ^ k) for i in range(n_dom)])]
    ppermute x24 -> x30, waiting for transfers between devices: 21.4 us -> 28.1 us  [member_swap(): return lax.ppermute(x, ('feat', 'rep'), [(i, i ^ k) for i in range(M)])]
    ppermute x24 -> x30, starting transfers between devices: 13 us -> 19.5 us  [member_swap(): return lax.ppermute(x, ('feat', 'rep'), [(i, i ^ k) for i in range(M)])]
    ppermute x12, starting transfers between devices: 18.1 us -> 23.9 us  [dom_swap(): return lax.ppermute(x, 'dom', [(i, i ^ k) for i in range(n_dom)])]
    pallas_call x17 -> x19, Pallas kernels: 23.4 us -> 24.7 us  [call(): pl.pallas_call(body, out_shape=list(outs), in_specs=[SMEM] + [HBM if i in...]
  transfers between devices with their start and end apart: 38 -> 42, of which waited for: 17 -> 18; matrix products, arithmetic and copies ran while one was open for 0% -> 0% of each run, Pallas kernels for 11% -> 10%
where the time goes in v4:
time: 120 us; the launch traced here: 119 us
  waiting for transfers between devices  50.8 us (42%)
  starting transfers between devices  43.4 us (36%)
  Pallas kernels  24.7 us (21%)
    ppermute x30, waiting for transfers between devices, member_swap(): return lax.ppermute(x, ('feat', 'rep'), [(i, i ^ k) for i in range(M)])  28.1 us
    pallas_call x19, Pallas kernels, call(): pl.pallas_call(body, out_shape=list(outs), in_specs=[SMEM] + [HBM if i in...  24.7 us
    ppermute x12, starting transfers between devices, dom_swap(): return lax.ppermute(x, 'dom', [(i, i ^ k) for i in range(n_dom)])  23.9 us
    ppermute x12, waiting for transfers between devices, dom_swap(): return lax.ppermute(x, 'dom', [(i, i ^ k) for i in range(n_dom)])  22.7 us
    ppermute x30, starting transfers between devices, member_swap(): return lax.ppermute(x, ('feat', 'rep'), [(i, i ^ k) for i in range(M)])  19.5 us
  transfers between devices with their start and end apart: 42, of which 18 were waited for; matrix products, arithmetic and copies ran while one was open for 0% of the time, Pallas kernels for 10%

profile of v4, /device:TPU:0, one launch (start us, length us, event | category | flops | bytes accessed | tf_op | source)
XLA Modules:
  0.0 119.3 jit_solution(3855072962511397150)
XLA Ops:
  0.0 2.9 %collective-permute-start.1 = (bf16[256,512]{1,0:T(8,128)(2,1)}, bf16[256,512]{1,0:T(8,128)(2,1)S(1)}, u32[]{:S(2)}, u32[]{:S(2)}) collective-permute-start(bf16[256,512]{1,0:T(8,128)(2,1)} %refs_0_.4), channel_id=1, source_target_pairs={{0,2},{1,3},{2,0},{3,1},{4,6},{5,7},{6,4},{7,5},{8,10},{9,11},{10,... | collective-permute-start | bytes 786440 | tf_op jit(solution)/shard_map/ppermute | solution.py:84
  3.0 1.5 %tables.1 = (bf16[144,512]{1,0:T(8,128)(2,1)S(1)}, s32[1,512]{1,0:T(1,128)S(1)}, s32[1,1024]{1,0:T(1,128)S(1)}) custom-call(s32[2]{0:T(128)S(1)} %pad_add_fusion.where_ref, bf16[128,512]{1,0:T(8,128)(2,1)} %enc_ref.1, s32[1,4,128]{2,1,0:T(4,128)} %gs_ref.1, s32[1,4,128]{2,1,0:T(4,128)} %gr_ref.1, s32[1,4,128]{2,1,0:T(4,128)} %halo_ref.1, s32[1,1024]{1,0:T(1,128)} %bitcast.5), custom_call_target="tpu_custom_call" | custom-call | bytes 294912 | tf_op jit(solution)/shard_map/tables/pallas_call | solution.py:63
  4.7 5.6 %collective-permute-done.1.refs_1_.refs_2_ = bf16[256,512]{1,0:T(8,128)(2,1)S(1)} collective-permute-done((bf16[256,512]{1,0:T(8,128)(2,1)}, bf16[256,512]{1,0:T(8,128)(2,1)S(1)}, u32[]{:S(2)}, u32[]{:S(2)}) %collective-permute-start.1) | collective-permute-done | bytes 262176 | tf_op jit(solution)/shard_map/ppermute | solution.py:84
  10.8 1.8 %collective-permute-done.4.refs_6_ = bf16[144,512]{1,0:T(8,128)(2,1)S(1)} collective-permute-done((bf16[144,512]{1,0:T(8,128)(2,1)S(1)}, bf16[144,512]{1,0:T(8,128)(2,1)S(1)}, u32[]{:S(2)}, u32[]{:S(2)}) %collective-permute-start.4) | collective-permute-done | bytes 147488 | tf_op jit(solution)/shard_map/ppermute | solution.py:84
  12.6 1.0 relay_edge.1.refs_8_.refs_4_
  14.0 2.5 %grid_messages.1 = (bf16[512,512]{1,0:T(8,128)(2,1)S(1)}, f32[4,256,128]{2,1,0:T(8,128)S(1)}, s32[4,2,512]{2,1,0:T(2,128)S(1)}, bf16[512,128]{1,0:T(8,128)(2,1)S...) custom-call(s32[1]{0:T(128)} %bitcast.me_ref, ...), custom_call_target="tpu_custom_call" | custom-call | flops 268435456 | bytes 3620864 | tf_op jit(solution)/shard_map/grid_messages/pallas_call | solution.py:63
  16.5 1.9 %collective-permute-start.6 = (bf16[512,128]{1,0:T(8,128)(2,1)S(1)}, bf16[512,128]{1,0:T(8,128)(2,1)S(1)}, u32[]{:S(2)}, u32[]{:S(2)}) collective-permute-start(bf16[512,128]{1,0:T(8,128)(2,1)S(1)} %get-tuple-element.70), channel_id=1, source_target_pairs={{0,4},{4,0},{8,12},{12,8},{1,5},{5,1},{9,13},{13,9},{2,6},{6,2},{1... | collective-permute-start | bytes 393224 | tf_op jit(solution)/shard_map/ppermute | solution.py:87
  18.4 3.9 %collective-permute-done.6.refs_1_.refs_3_ = bf16[512,128]{1,0:T(8,128)(2,1)S(1)} collective-permute-done((bf16[512,128]{1,0:T(8,128)(2,1)S(1)}, bf16[512,128]{1,0:T(8,128)(2,1)S(1)}, u32[]{:S(2)}, u32[]{:S(2)}) %collective-permute-start.6) | collective-permute-done | bytes 131104 | tf_op jit(solution)/shard_map/ppermute | solution.py:87
  22.3 1.1 relay_rest.1.refs_0_
  23.4 1.7 %collective-permute-start.16 = (bf16[512,512]{1,0:T(8,128)(2,1)S(1)}, bf16[512,512]{1,0:T(8,128)(2,1)S(1)}, u32[]{:S(2)}, u32[]{:S(2)}) collective-permute-start(bf16[512,512]{1,0:T(8,128)(2,1)S(1)} %relay_rest.1.refs_0_), channel_id=1, source_target_pairs={{0,2},{1,3},{2,0},{3,1},{4,6},{5,7},{6,4},{7,5},{8,10},{9,11},{10,... | collective-permute-start | bytes 1572872 | tf_op jit(solution)/shard_map/ppermute | solution.py:84
  25.4 2.8 %collective-permute-start.7 = (bf16[512,128]{1,0:T(8,128)(2,1)S(1)}, bf16[512,128]{1,0:T(8,128)(2,1)S(1)}, u32[]{:S(2)}, u32[]{:S(2)}) collective-permute-start(bf16[512,128]{1,0:T(8,128)(2,1)S(1)} %get-tuple-element.71), channel_id=1, source_target_pairs={{0,8},{4,12},{8,0},{12,4},{1,9},{5,13},{9,1},{13,5},{2,10},{6,14},... | collective-permute-start | bytes 393224 | tf_op jit(solution)/shard_map/ppermute | solution.py:87
  28.2 1.3 %collective-permute-start.8 = (bf16[512,128]{1,0:T(8,128)(2,1)S(1)}, bf16[512,128]{1,0:T(8,128)(2,1)S(1)}, u32[]{:S(2)}, u32[]{:S(2)}) collective-permute-start(bf16[512,128]{1,0:T(8,128)(2,1)S(1)} %get-tuple-element.72), channel_id=1, source_target_pairs={{0,12},{4,8},{8,4},{12,0},{1,13},{5,9},{9,5},{13,1},{2,14},{6,10},... | collective-permute-start | bytes 393224 | tf_op jit(solution)/shard_map/ppermute | solution.py:87
  29.6 8.7 %collective-permute-done.7.refs_2_ = bf16[512,128]{1,0:T(8,128)(2,1)S(1)} collective-permute-done((bf16[512,128]{1,0:T(8,128)(2,1)S(1)}, bf16[512,128]{1,0:T(8,128)(2,1)S(1)}, u32[]{:S(2)}, u32[]{:S(2)}) %collective-permute-start.7) | collective-permute-done | bytes 131104 | tf_op jit(solution)/shard_map/ppermute | solution.py:87
  38.2 1.4 %encode.1 = (bf16[512,128]{1,0:T(8,128)(2,1)S(1)}, bf16[128,128]{1,0:T(8,128)(2,1)S(1)}, bf16[128,128]{1,0:T(8,128)(2,1)S(1)}, bf16[128,128]{1,0:T(8,128)(2,1)S(1)}, bf16[128,128]{1,0:T(8,128)(2,1)S(1)}) custom-call(s32[1]{0:T(128)} %bitcast.me_ref, bf16[512,512]{1,0:T(8,128)(2,1)S(1)} %copy-done.2, s32[1,512]{1,0:T(1,128)S(1)} %get-tuple-element.65.halo_ref, ...), custom_call_target="tpu_custom_call" | custom-call | flops 268435456 | bytes 1329152 | tf_op jit(solution)/shard_map/encode/pallas_call | solution.py:63
  39.6 3.4 %collective-permute-start.18 = (bf16[128,128]{1,0:T(8,128)(2,1)S(1)}, bf16[128,128]{1,0:T(8,128)(2,1)S(1)}, u32[]{:S(2)}, u32[]{:S(2)}) collective-permute-start(bf16[128,128]{1,0:T(8,128)(2,1)S(1)} %get-tuple-element.81), channel_id=1, source_target_pairs={{0,4},{4,0},{8,12},{12,8},{1,5},{5,1},{9,13},{13,9},{2,6},{6,2},{1... | collective-permute-start | bytes 98312 | tf_op jit(solution)/shard_map/ppermute | solution.py:87
  43.0 2.0 %collective-permute-start.19 = (bf16[128,128]{1,0:T(8,128)(2,1)S(1)}, bf16[128,128]{1,0:T(8,128)(2,1)S(1)}, u32[]{:S(2)}, u32[]{:S(2)}) collective-permute-start(bf16[128,128]{1,0:T(8,128)(2,1)S(1)} %get-tuple-element.82), channel_id=1, source_target_pairs={{0,8},{4,12},{8,0},{12,4},{1,9},{5,13},{9,1},{13,5},{2,10},{6,14},... | collective-permute-start | bytes 98312 | tf_op jit(solution)/shard_map/ppermute | solution.py:87
  45.2 3.7 %collective-permute-start.20 = (bf16[128,128]{1,0:T(8,128)(2,1)S(1)}, bf16[128,128]{1,0:T(8,128)(2,1)S(1)}, u32[]{:S(2)}, u32[]{:S(2)}) collective-permute-start(bf16[128,128]{1,0:T(8,128)(2,1)S(1)} %get-tuple-element.83), channel_id=1, source_target_pairs={{0,12},{4,8},{8,4},{12,0},{1,13},{5,9},{9,5},{13,1},{2,14},{6,10},... | collective-permute-start | bytes 98312 | tf_op jit(solution)/shard_map/ppermute | solution.py:87
  49.4 1.5 %collective-permute-start.10 = (bf16[512,128]{1,0:T(8,128)(2,1)S(1)}, bf16[512,128]{1,0:T(8,128)(2,1)S(1)}, u32[]{:S(2)}, u32[]{:S(2)}) collective-permute-start(bf16[512,128]{1,0:T(8,128)(2,1)S(1)} %get-tuple-element.73.refs_0_), channel_id=1, source_target_pairs={{0,2},{1,3},{2,0},{3,1},{4,6},{5,7},{6,4},{7,5},{8,10},{9,11},{10,... | collective-permute-start | bytes 393224 | tf_op jit(solution)/shard_map/ppermute | solution.py:84
  51.5 1.6 %collective-permute-start.22 = (bf16[512,128]{1,0:T(8,128)(2,1)S(1)}, bf16[512,128]{1,0:T(8,128)(2,1)S(1)}, u32[]{:S(2)}, u32[]{:S(2)}) collective-permute-start(bf16[512,128]{1,0:T(8,128)(2,1)S(1)} %constant_dynamic-update-slice_fusion.refs_0_), channel_id=1, source_target_pairs={{0,2},{1,3},{2,0},{3,1},{4,6},{5,7},{6,4},{7,5},{8,10},{9,11},{10,... | collective-permute-start | bytes 393224 | tf_op jit(solution)/shard_map/ppermute | solution.py:84
  53.1 2.6 %collective-permute-done.10.refs_2_ = bf16[512,128]{1,0:T(8,128)(2,1)S(1)} collective-permute-done((bf16[512,128]{1,0:T(8,128)(2,1)S(1)}, bf16[512,128]{1,0:T(8,128)(2,1)S(1)}, u32[]{:S(2)}, u32[]{:S(2)}) %collective-permute-start.10) | collective-permute-done | bytes 131104 | tf_op jit(solution)/shard_map/ppermute | solution.py:84
  55.6 2.1 %edge_hots.1 = (bf16[1024,512]{1,0:T(8,128)(2,1)S(1)}, bf16[1024,512]{1,0:T(8,128)(2,1)S(1)}, bf16[1024,512]{1,0:T(8,128)(2,1)S(1)}, bf16[512,1024]{1,0:T(8,128)...) custom-call(s32[1]{0:T(128)} %bitcast.me_ref, s32[1,1024]{1,0:T(1,128)S(1)} %get-tuple-element.66.send_ref, ...), custom_call_target="tpu_custom_call" | custom-call | bytes 6299648 | tf_op jit(solution)/shard_map/edge_hots/pallas_call | solution.py:63
  57.8 0.6 collective-permute-start.21
  58.4 3.0 %edge_local.1 = (f32[1024,512]{1,0:T(8,128)S(1)}, bf16[512,512]{1,0:T(8,128)(2,1)S(1)}, bf16[1536,512]{1,0:T(8,128)(2,1)S(1)}) custom-call(s32[1]{0:T(128)} %bitcast.me_ref, bf16[1024,512]{1,0:T(8,128)(2,1)S(1)} %copy-done.4, bf16[1024,512]{1,0:T(8,128)(2,1)S(1)} %get-tuple-element.67.send_ref, bf16[1024,512]{1,0:T(8,128)(2,1)S(1)} %get-tuple-element.68.recv_ref, ...), custom_call_target="tpu_custom_call" | custom-call | flops 2684354560 | bytes 9437184 | tf_op jit(solution)/shard_map/edge_local/pallas_call | solution.py:63
  62.0 3.2 %edge_update.1 = (f32[1024,512]{1,0:T(8,128)S(1)}, bf16[2,128,512]{2,1,0:T(8,128)(2,1)S(1)}, bf16[2,128,512]{2,1,0:T(8,128)(2,1)S(1)}) custom-call(s32[1]{0:T(128)} %bitcast.me_ref, f32[1024,512]{1,0:T(8,128)S(1)} %get-tuple-element.74.local_ref, bf16[1024,512]{1,0:T(8,128)(2,1)S(1)} %copy-done.4, bf16[1024,512]{1,0:T(8,128)(2,1)S(1)} %get-tuple-element.75.send_ref, ...), custom_call_target="tpu_custom_call" | custom-call | flops 2147483648 | bytes 10485760 | tf_op jit(solution)/shard_map/edge_update/pallas_call | solution.py:63
  65.7 1.2 collective-permute-done.24.refs_1_
  66.9 1.6 %collective-permute-start.25 = (bf16[128,512]{1,0:T(8,128)(2,1)S(1)}, bf16[128,512]{1,0:T(8,128)(2,1)S(1)}, u32[]{:S(2)}, u32[]{:S(2)}) collective-permute-start(bf16[128,512]{1,0:T(8,128)(2,1)S(1)} %get-tuple-element.92), channel_id=1, source_target_pairs={{0,2},{1,3},{2,0},{3,1},{4,6},{5,7},{6,4},{7,5},{8,10},{9,11},{10,... | collective-permute-start | bytes 393224 | tf_op jit(solution)/shard_map/ppermute | solution.py:84
  68.5 4.2 %collective-permute-done.25.refs_1_ = bf16[128,512]{1,0:T(8,128)(2,1)S(1)} collective-permute-done((bf16[128,512]{1,0:T(8,128)(2,1)S(1)}, bf16[128,512]{1,0:T(8,128)(2,1)S(1)}, u32[]{:S(2)}, u32[]{:S(2)}) %collective-permute-start.25) | collective-permute-done | bytes 131104 | tf_op jit(solution)/shard_map/ppermute | solution.py:84
  72.8 0.6 node_backward.1
  73.4 1.6 %collective-permute-start.27 = (bf16[128,512]{1,0:T(8,128)(2,1)S(1)}, bf16[128,512]{1,0:T(8,128)(2,1)S(1)}, u32[]{:S(2)}, u32[]{:S(2)}) collective-permute-start(bf16[128,512]{1,0:T(8,128)(2,1)S(1)} %get-tuple-element.93.refs_0_), channel_id=1, source_target_pairs={{0,2},{1,3},{2,0},{3,1},{4,6},{5,7},{6,4},{7,5},{8,10},{9,11},{10,... | collective-permute-start | bytes 393224 | tf_op jit(solution)/shard_map/ppermute | solution.py:84
  75.0 3.4 %collective-permute-done.27.refs_2_ = bf16[128,512]{1,0:T(8,128)(2,1)S(1)} collective-permute-done((bf16[128,512]{1,0:T(8,128)(2,1)S(1)}, bf16[128,512]{1,0:T(8,128)(2,1)S(1)}, u32[]{:S(2)}, u32[]{:S(2)}) %collective-permute-start.27) | collective-permute-done | bytes 131104 | tf_op jit(solution)/shard_map/ppermute | solution.py:84
  78.5 1.3 %collective-permute-done.28.refs_3_ = bf16[128,512]{1,0:T(8,128)(2,1)S(1)} collective-permute-done((bf16[128,512]{1,0:T(8,128)(2,1)S(1)}, bf16[128,512]{1,0:T(8,128)(2,1)S(1)}, u32[]{:S(2)}, u32[]{:S(2)}) %collective-permute-start.28) | collective-permute-done | bytes 131104 | tf_op jit(solution)/shard_map/ppermute | solution.py:84
  79.8 2.7 %edge_backward.1 = (bf16[1024,512]{1,0:T(8,128)(2,1)S(1)}, bf16[2,512,128]{2,1,0:T(8,128)(2,1)S(1)}, bf16[2,512,128]{2,1,0:T(8,128)(2,1)S(1)}) custom-call(s32[1]{0:T(128)} %bitcast.me_ref, bf16[1024,512]{1,0:T(8,128)(2,1)S(1)} %copy-done.1, f32[1024,512]{1,0:T(8,128)S(1)} %get-tuple-element.84.pre_ref, bf16[512,1024]{1,0:T(8,128)(2,1)S(1)} %get-tuple-element.85.send_ref, ...), custom_call_target="tpu_custom_call" | custom-call | flops 1879048192 | bytes 9437184 | tf_op jit(solution)/shard_map/edge_backward/pallas_call | solution.py:63
  82.7 2.1 %local_backward.1 = (bf16[2,512,128]{2,1,0:T(8,128)(2,1)S(1)}, bf16[2,512,128]{2,1,0:T(8,128)(2,1)S(1)}) custom-call(s32[1]{0:T(128)} %bitcast.me_ref, bf16[1024,512]{1,0:T(8,128)(2,1)S(1)} %get-tuple-element.94.dpre_ref, bf16[512,1024]{1,0:T(8,128)(2,1)S(1)} %get-tuple-element.95.send_ref, bf16[512,1024]{1,0:T(8,128)(2,1)S(1)} %get-tuple-element.76.recv_ref, ...), custom_call_target="tpu_custom_call" | custom-call | flops 1610612736 | bytes 5505024 | tf_op jit(solution)/shard_map/local_backward/pallas_call | solution.py:63
  85.4 1.6 %collective-permute-start.32 = (bf16[512,128]{1,0:T(8,128)(2,1)S(1)}, bf16[512,128]{1,0:T(8,128)(2,1)S(1)}, u32[]{:S(2)}, u32[]{:S(2)}) collective-permute-start(bf16[512,128]{1,0:T(8,128)(2,1)S(1)} %get-tuple-element.104), channel_id=1, source_target_pairs={{0,2},{1,3},{2,0},{3,1},{4,6},{5,7},{6,4},{7,5},{8,10},{9,11},{10,... | collective-permute-start | bytes 393224 | tf_op jit(solution)/shard_map/ppermute | solution.py:84
  87.0 1.1 collective-permute-start.30
  88.1 3.6 %collective-permute-done.32.refs_1_ = bf16[512,128]{1,0:T(8,128)(2,1)S(1)} collective-permute-done((bf16[512,128]{1,0:T(8,128)(2,1)S(1)}, bf16[512,128]{1,0:T(8,128)(2,1)S(1)}, u32[]{:S(2)}, u32[]{:S(2)}) %collective-permute-start.32) | collective-permute-done | bytes 131104 | tf_op jit(solution)/shard_map/ppermute | solution.py:84
  91.9 2.9 %collective-permute-start.34 = (bf16[128,128]{1,0:T(8,128)(2,1)S(1)}, bf16[128,128]{1,0:T(8,128)(2,1)S(1)}, u32[]{:S(2)}, u32[]{:S(2)}) collective-permute-start(bf16[128,128]{1,0:T(8,128)(2,1)S(1)} %get-tuple-element.107), channel_id=1, source_target_pairs={{0,8},{4,12},{8,0},{12,4},{1,9},{5,13},{9,1},{13,5},{2,10},{6,14},... | collective-permute-start | bytes 98312 | tf_op jit(solution)/shard_map/ppermute | solution.py:87
  94.8 1.4 %collective-permute-start.35 = (bf16[128,128]{1,0:T(8,128)(2,1)S(1)}, bf16[128,128]{1,0:T(8,128)(2,1)S(1)}, u32[]{:S(2)}, u32[]{:S(2)}) collective-permute-start(bf16[128,128]{1,0:T(8,128)(2,1)S(1)} %get-tuple-element.108), channel_id=1, source_target_pairs={{0,12},{4,8},{8,4},{12,0},{1,13},{5,9},{9,5},{13,1},{2,14},{6,10},... | collective-permute-start | bytes 98312 | tf_op jit(solution)/shard_map/ppermute | solution.py:87
  96.8 3.8 %collective-permute-done.35.refs_5_ = bf16[128,128]{1,0:T(8,128)(2,1)S(1)} collective-permute-done((bf16[128,128]{1,0:T(8,128)(2,1)S(1)}, bf16[128,128]{1,0:T(8,128)(2,1)S(1)}, u32[]{:S(2)}, u32[]{:S(2)}) %collective-permute-start.35) | collective-permute-done | bytes 32800 | tf_op jit(solution)/shard_map/ppermute | solution.py:87
  100.5 1.2 owed_rows.1
  101.8 2.0 %collective-permute-start.37 = (bf16[512,128]{1,0:T(8,128)(2,1)S(1)}, bf16[512,128]{1,0:T(8,128)(2,1)S(1)}, u32[]{:S(2)}, u32[]{:S(2)}) collective-permute-start(bf16[512,128]{1,0:T(8,128)(2,1)S(1)} %get-tuple-element.111), channel_id=1, source_target_pairs={{0,8},{4,12},{8,0},{12,4},{1,9},{5,13},{9,1},{13,5},{2,10},{6,14},... | collective-permute-start | bytes 393224 | tf_op jit(solution)/shard_map/ppermute | solution.py:87
  103.8 2.4 %collective-permute-start.38 = (bf16[512,128]{1,0:T(8,128)(2,1)S(1)}, bf16[512,128]{1,0:T(8,128)(2,1)S(1)}, u32[]{:S(2)}, u32[]{:S(2)}) collective-permute-start(bf16[512,128]{1,0:T(8,128)(2,1)S(1)} %get-tuple-element.112), channel_id=1, source_target_pairs={{0,12},{4,8},{8,4},{12,0},{1,13},{5,9},{9,5},{13,1},{2,14},{6,10},... | collective-permute-start | bytes 393224 | tf_op jit(solution)/shard_map/ppermute | solution.py:87
  106.2 2.1 %collective-permute-done.36.refs_1_ = bf16[512,128]{1,0:T(8,128)(2,1)S(1)} collective-permute-done((bf16[512,128]{1,0:T(8,128)(2,1)S(1)}, bf16[512,128]{1,0:T(8,128)(2,1)S(1)}, u32[]{:S(2)}, u32[]{:S(2)}) %collective-permute-start.36) | collective-permute-done | bytes 131104 | tf_op jit(solution)/shard_map/ppermute | solution.py:87
  108.2 3.8 %collective-permute-done.37.refs_2_ = bf16[512,128]{1,0:T(8,128)(2,1)S(1)} collective-permute-done((bf16[512,128]{1,0:T(8,128)(2,1)S(1)}, bf16[512,128]{1,0:T(8,128)(2,1)S(1)}, u32[]{:S(2)}, u32[]{:S(2)}) %collective-permute-start.37) | collective-permute-done | bytes 131104 | tf_op jit(solution)/shard_map/ppermute | solution.py:87
  112.6 1.5 %collective-permute-start.40 = (bf16[256,128]{1,0:T(8,128)(2,1)S(1)}, bf16[256,128]{1,0:T(8,128)(2,1)S(1)}, u32[]{:S(2)}, u32[]{:S(2)}) collective-permute-start(bf16[256,128]{1,0:T(8,128)(2,1)S(1)} %get-tuple-element.115), channel_id=1, source_target_pairs={{0,2},{1,3},{2,0},{3,1},{4,6},{5,7},{6,4},{7,5},{8,10},{9,11},{10,... | collective-permute-start | bytes 196616 | tf_op jit(solution)/shard_map/ppermute | solution.py:84
  114.4 2.6 %collective-permute-done.40.refs_2_ = bf16[256,128]{1,0:T(8,128)(2,1)S(1)} collective-permute-done((bf16[256,128]{1,0:T(8,128)(2,1)S(1)}, bf16[256,128]{1,0:T(8,128)(2,1)S(1)}, u32[]{:S(2)}, u32[]{:S(2)}) %collective-permute-start.40) | collective-permute-done | bytes 65568 | tf_op jit(solution)/shard_map/ppermute | solution.py:84
  117.1 1.1 collective-permute-done.41.refs_3_
  118.2 1.1 adjoint.1
  (70 shorter events, 6.2 us)
Async XLA Ops:
  0.0 10.3 %collective-permute-start.1 = (bf16[256,512]{1,0:T(8,128)(2,1)}, bf16[256,512]{1,0:T(8,128)(2,1)S(1)}, u32[]{:S(2)}, u32[]{:S(2)}) collective-permute-start(bf16[256,512]{1,0:T(8,128)(2,1)} %refs_0_.4), channel_id=1, source_target_pairs={{0,2},{1,3},{2,0},{3,1},{4,6},{5,7},{6,4},{7,5},{8,10},{9,11},{10,... | collective-permute-start | bytes 786440 | tf_op jit(solution)/shard_map/ppermute | solution.py:84
  4.5 33.7 %copy-start.2 = (bf16[512,512]{1,0:T(8,128)(2,1)S(1)}, bf16[512,512]{1,0:T(8,128)(2,1)}, u32[]{:S(2)}) copy-start(bf16[512,512]{1,0:T(8,128)(2,1)} %base_ref.1) | copy-start | bytes 1572868
  4.6 8.1 %collective-permute-start.4 = (bf16[144,512]{1,0:T(8,128)(2,1)S(1)}, bf16[144,512]{1,0:T(8,128)(2,1)S(1)}, u32[]{:S(2)}, u32[]{:S(2)}) collective-permute-start(bf16[144,512]{1,0:T(8,128)(2,1)S(1)} %get-tuple-element.61.refs_4_), channel_id=1, source_target_pairs={{0,2},{1,3},{2,0},{3,1},{4,6},{5,7},{6,4},{7,5},{8,10},{9,11},{10,... | collective-permute-start | bytes 442376 | tf_op jit(solution)/shard_map/ppermute | solution.py:84
  4.6 9.0 %collective-permute-start = (bf16[256,512]{1,0:T(8,128)(2,1)}, bf16[256,512]{1,0:T(8,128)(2,1)S(1)}, u32[]{:S(2)}, u32[]{:S(2)}) collective-permute-start(bf16[256,512]{1,0:T(8,128)(2,1)} %refs_0_.4), channel_id=1, source_target_pairs={{0,1},{1,0},{2,3},{3,2},{4,5},{5,4},{6,7},{7,6},{8,9},{9,8},{10,11... | collective-permute-start | bytes 786440 | tf_op jit(solution)/shard_map/ppermute | solution.py:84
  10.3 3.7 %collective-permute-start.2 = (bf16[256,512]{1,0:T(8,128)(2,1)S(1)}, bf16[256,512]{1,0:T(8,128)(2,1)S(1)}, u32[]{:S(2)}, u32[]{:S(2)}) collective-permute-start(bf16[256,512]{1,0:T(8,128)(2,1)S(1)} %collective-permute-done.1.refs_1_.refs_2_), channel_id=1, source_target_pairs={{0,1},{1,0},{2,3},{3,2},{4,5},{5,4},{6,7},{7,6},{8,9},{9,8},{10,11... | collective-permute-start | bytes 786440 | tf_op jit(solution)/shard_map/ppermute | solution.py:84
  10.3 3.4 %collective-permute-start.3 = (bf16[144,512]{1,0:T(8,128)(2,1)S(1)}, bf16[144,512]{1,0:T(8,128)(2,1)S(1)}, u32[]{:S(2)}, u32[]{:S(2)}) collective-permute-start(bf16[144,512]{1,0:T(8,128)(2,1)S(1)} %get-tuple-element.61.refs_4_), channel_id=1, source_target_pairs={{0,1},{1,0},{2,3},{3,2},{4,5},{5,4},{6,7},{7,6},{8,9},{9,8},{10,11... | collective-permute-start | bytes 442376 | tf_op jit(solution)/shard_map/ppermute | solution.py:84
  12.6 1.4 %collective-permute-start.5 = (bf16[144,512]{1,0:T(8,128)(2,1)S(1)}, bf16[144,512]{1,0:T(8,128)(2,1)S(1)}, u32[]{:S(2)}, u32[]{:S(2)}) collective-permute-start(bf16[144,512]{1,0:T(8,128)(2,1)S(1)} %collective-permute-done.4.refs_6_), channel_id=1, source_target_pairs={{0,1},{1,0},{2,3},{3,2},{4,5},{5,4},{6,7},{7,6},{8,9},{9,8},{10,11... | collective-permute-start | bytes 442376 | tf_op jit(solution)/shard_map/ppermute | solution.py:84
  13.6 42.0 %copy-start.3 = (s32[1024]{0:T(1024)S(1)}, s32[1024]{0:T(1024)}, u32[]{:S(2)}) copy-start(s32[1024]{0:T(1024)} %param.27) | copy-start | bytes 12292
  13.6 44.8 %copy-start.4 = (bf16[1024,512]{1,0:T(8,128)(2,1)S(1)}, bf16[1024,512]{1,0:T(8,128)(2,1)}, u32[]{:S(2)}) copy-start(bf16[1024,512]{1,0:T(8,128)(2,1)} %es_ref.3) | copy-start | bytes 3145732
  16.5 5.8 %collective-permute-start.6 = (bf16[512,128]{1,0:T(8,128)(2,1)S(1)}, bf16[512,128]{1,0:T(8,128)(2,1)S(1)}, u32[]{:S(2)}, u32[]{:S(2)}) collective-permute-start(bf16[512,128]{1,0:T(8,128)(2,1)S(1)} %get-tuple-element.70), channel_id=1, source_target_pairs={{0,4},{4,0},{8,12},{12,8},{1,5},{5,1},{9,13},{13,9},{2,6},{6,2},{1... | collective-permute-start | bytes 393224 | tf_op jit(solution)/shard_map/ppermute | solution.py:87
  23.4 27.6 %collective-permute-start.16 = (bf16[512,512]{1,0:T(8,128)(2,1)S(1)}, bf16[512,512]{1,0:T(8,128)(2,1)S(1)}, u32[]{:S(2)}, u32[]{:S(2)}) collective-permute-start(bf16[512,512]{1,0:T(8,128)(2,1)S(1)} %relay_rest.1.refs_0_), channel_id=1, source_target_pairs={{0,2},{1,3},{2,0},{3,1},{4,6},{5,7},{6,4},{7,5},{8,10},{9,11},{10,... | collective-permute-start | bytes 1572872 | tf_op jit(solution)/shard_map/ppermute | solution.py:84
  25.1 20.1 %collective-permute-start.13 = (bf16[384,512]{1,0:T(8,128)(2,1)S(1)}, bf16[384,512]{1,0:T(8,128)(2,1)S(1)}, u32[]{:S(2)}, u32[]{:S(2)}) collective-permute-start(bf16[384,512]{1,0:T(8,128)(2,1)S(1)} %relay_edge.1.refs_8_.refs_4_), channel_id=1, source_target_pairs={{0,2},{1,3},{2,0},{3,1},{4,6},{5,7},{6,4},{7,5},{8,10},{9,11},{10,... | collective-permute-start | bytes 1179656 | tf_op jit(solution)/shard_map/ppermute | solution.py:84
  25.4 23.4 %collective-permute-start.12 = (bf16[384,512]{1,0:T(8,128)(2,1)S(1)}, bf16[384,512]{1,0:T(8,128)(2,1)S(1)}, u32[]{:S(2)}, u32[]{:S(2)}) collective-permute-start(bf16[384,512]{1,0:T(8,128)(2,1)S(1)} %relay_edge.1.refs_8_.refs_4_), channel_id=1, source_target_pairs={{0,1},{1,0},{2,3},{3,2},{4,5},{5,4},{6,7},{7,6},{8,9},{9,8},{10,11... | collective-permute-start | bytes 1179656 | tf_op jit(solution)/shard_map/ppermute | solution.py:84
  25.4 12.8 %collective-permute-start.7 = (bf16[512,128]{1,0:T(8,128)(2,1)S(1)}, bf16[512,128]{1,0:T(8,128)(2,1)S(1)}, u32[]{:S(2)}, u32[]{:S(2)}) collective-permute-start(bf16[512,128]{1,0:T(8,128)(2,1)S(1)} %get-tuple-element.71), channel_id=1, source_target_pairs={{0,8},{4,12},{8,0},{12,4},{1,9},{5,13},{9,1},{13,5},{2,10},{6,14},... | collective-permute-start | bytes 393224 | tf_op jit(solution)/shard_map/ppermute | solution.py:87
  28.2 10.0 %collective-permute-start.8 = (bf16[512,128]{1,0:T(8,128)(2,1)S(1)}, bf16[512,128]{1,0:T(8,128)(2,1)S(1)}, u32[]{:S(2)}, u32[]{:S(2)}) collective-permute-start(bf16[512,128]{1,0:T(8,128)(2,1)S(1)} %get-tuple-element.72), channel_id=1, source_target_pairs={{0,12},{4,8},{8,4},{12,0},{1,13},{5,9},{9,5},{13,1},{2,14},{6,10},... | collective-permute-start | bytes 393224 | tf_op jit(solution)/shard_map/ppermute | solution.py:87
  39.6 9.2 %collective-permute-start.18 = (bf16[128,128]{1,0:T(8,128)(2,1)S(1)}, bf16[128,128]{1,0:T(8,128)(2,1)S(1)}, u32[]{:S(2)}, u32[]{:S(2)}) collective-permute-start(bf16[128,128]{1,0:T(8,128)(2,1)S(1)} %get-tuple-element.81), channel_id=1, source_target_pairs={{0,4},{4,0},{8,12},{12,8},{1,5},{5,1},{9,13},{13,9},{2,6},{6,2},{1... | collective-permute-start | bytes 98312 | tf_op jit(solution)/shard_map/ppermute | solution.py:87
  43.0 6.5 %collective-permute-start.19 = (bf16[128,128]{1,0:T(8,128)(2,1)S(1)}, bf16[128,128]{1,0:T(8,128)(2,1)S(1)}, u32[]{:S(2)}, u32[]{:S(2)}) collective-permute-start(bf16[128,128]{1,0:T(8,128)(2,1)S(1)} %get-tuple-element.82), channel_id=1, source_target_pairs={{0,8},{4,12},{8,0},{12,4},{1,9},{5,13},{9,1},{13,5},{2,10},{6,14},... | collective-permute-start | bytes 98312 | tf_op jit(solution)/shard_map/ppermute | solution.py:87
  45.2 5.8 %collective-permute-start.20 = (bf16[128,128]{1,0:T(8,128)(2,1)S(1)}, bf16[128,128]{1,0:T(8,128)(2,1)S(1)}, u32[]{:S(2)}, u32[]{:S(2)}) collective-permute-start(bf16[128,128]{1,0:T(8,128)(2,1)S(1)} %get-tuple-element.83), channel_id=1, source_target_pairs={{0,12},{4,8},{8,4},{12,0},{1,13},{5,9},{9,5},{13,1},{2,14},{6,10},... | collective-permute-start | bytes 98312 | tf_op jit(solution)/shard_map/ppermute | solution.py:87
  48.8 9.6 %collective-permute-start.14 = (bf16[384,512]{1,0:T(8,128)(2,1)S(1)}, bf16[384,512]{1,0:T(8,128)(2,1)S(1)}, u32[]{:S(2)}, u32[]{:S(2)}) collective-permute-start(bf16[384,512]{1,0:T(8,128)(2,1)S(1)} %collective-permute-done.13.refs_6_), channel_id=1, source_target_pairs={{0,1},{1,0},{2,3},{3,2},{4,5},{5,4},{6,7},{7,6},{8,9},{9,8},{10,11... | collective-permute-start | bytes 1179656 | tf_op jit(solution)/shard_map/ppermute | solution.py:84
  48.9 2.6 %collective-permute-start.9 = (bf16[512,128]{1,0:T(8,128)(2,1)S(1)}, bf16[512,128]{1,0:T(8,128)(2,1)S(1)}, u32[]{:S(2)}, u32[]{:S(2)}) collective-permute-start(bf16[512,128]{1,0:T(8,128)(2,1)S(1)} %get-tuple-element.73.refs_0_), channel_id=1, source_target_pairs={{0,1},{1,0},{2,3},{3,2},{4,5},{5,4},{6,7},{7,6},{8,9},{9,8},{10,11... | collective-permute-start | bytes 393224 | tf_op jit(solution)/shard_map/ppermute | solution.py:84
  49.4 6.2 %collective-permute-start.10 = (bf16[512,128]{1,0:T(8,128)(2,1)S(1)}, bf16[512,128]{1,0:T(8,128)(2,1)S(1)}, u32[]{:S(2)}, u32[]{:S(2)}) collective-permute-start(bf16[512,128]{1,0:T(8,128)(2,1)S(1)} %get-tuple-element.73.refs_0_), channel_id=1, source_target_pairs={{0,2},{1,3},{2,0},{3,1},{4,6},{5,7},{6,4},{7,5},{8,10},{9,11},{10,... | collective-permute-start | bytes 393224 | tf_op jit(solution)/shard_map/ppermute | solution.py:84
  50.9 10.5 %collective-permute-start.15 = (bf16[512,512]{1,0:T(8,128)(2,1)S(1)}, bf16[512,512]{1,0:T(8,128)(2,1)S(1)}, u32[]{:S(2)}, u32[]{:S(2)}) collective-permute-start(bf16[512,512]{1,0:T(8,128)(2,1)S(1)} %relay_rest.1.refs_0_), channel_id=1, source_target_pairs={{0,1},{1,0},{2,3},{3,2},{4,5},{5,4},{6,7},{7,6},{8,9},{9,8},{10,11... | collective-permute-start | bytes 1572872 | tf_op jit(solution)/shard_map/ppermute | solution.py:84
  50.9 10.5 %collective-permute-start.17 = (bf16[512,512]{1,0:T(8,128)(2,1)S(1)}, bf16[512,512]{1,0:T(8,128)(2,1)S(1)}, u32[]{:S(2)}, u32[]{:S(2)}) collective-permute-start(bf16[512,512]{1,0:T(8,128)(2,1)S(1)} %collective-permute-done.16.refs_2_), channel_id=1, source_target_pairs={{0,1},{1,0},{2,3},{3,2},{4,5},{5,4},{6,7},{7,6},{8,9},{9,8},{10,11... | collective-permute-start | bytes 1572872 | tf_op jit(solution)/shard_map/ppermute | solution.py:84
  51.5 6.3 %collective-permute-start.22 = (bf16[512,128]{1,0:T(8,128)(2,1)S(1)}, bf16[512,128]{1,0:T(8,128)(2,1)S(1)}, u32[]{:S(2)}, u32[]{:S(2)}) collective-permute-start(bf16[512,128]{1,0:T(8,128)(2,1)S(1)} %constant_dynamic-update-slice_fusion.refs_0_), channel_id=1, source_target_pairs={{0,2},{1,3},{2,0},{3,1},{4,6},{5,7},{6,4},{7,5},{8,10},{9,11},{10,... | collective-permute-start | bytes 393224 | tf_op jit(solution)/shard_map/ppermute | solution.py:84
  55.6 2.7 %collective-permute-start.11 = (bf16[512,128]{1,0:T(8,128)(2,1)S(1)}, bf16[512,128]{1,0:T(8,128)(2,1)S(1)}, u32[]{:S(2)}, u32[]{:S(2)}) collective-permute-start(bf16[512,128]{1,0:T(8,128)(2,1)S(1)} %collective-permute-done.10.refs_2_), channel_id=1, source_target_pairs={{0,1},{1,0},{2,3},{3,2},{4,5},{5,4},{6,7},{7,6},{8,9},{9,8},{10,11... | collective-permute-start | bytes 393224 | tf_op jit(solution)/shard_map/ppermute | solution.py:84
  57.8 4.2 %collective-permute-start.21 = (bf16[512,128]{1,0:T(8,128)(2,1)S(1)}, bf16[512,128]{1,0:T(8,128)(2,1)S(1)}, u32[]{:S(2)}, u32[]{:S(2)}) collective-permute-start(bf16[512,128]{1,0:T(8,128)(2,1)S(1)} %constant_dynamic-update-slice_fusion.refs_0_), channel_id=1, source_target_pairs={{0,1},{1,0},{2,3},{3,2},{4,5},{5,4},{6,7},{7,6},{8,9},{9,8},{10,11... | collective-permute-start | bytes 393224 | tf_op jit(solution)/shard_map/ppermute | solution.py:84
  58.3 3.7 %collective-permute-start.23 = (bf16[512,128]{1,0:T(8,128)(2,1)S(1)}, bf16[512,128]{1,0:T(8,128)(2,1)S(1)}, u32[]{:S(2)}, u32[]{:S(2)}) collective-permute-start(bf16[512,128]{1,0:T(8,128)(2,1)S(1)} %collective-permute-done.22.refs_2_), channel_id=1, source_target_pairs={{0,1},{1,0},{2,3},{3,2},{4,5},{5,4},{6,7},{7,6},{8,9},{9,8},{10,11... | collective-permute-start | bytes 393224 | tf_op jit(solution)/shard_map/ppermute | solution.py:84
  58.4 3.0 %copy-start = (bf16[512,512]{1,0:T(8,128)(2,1)S(1)}, bf16[512,512]{1,0:T(8,128)(2,1)}, u32[]{:S(2)}) copy-start(bf16[512,512]{1,0:T(8,128)(2,1)} %grad_ref.4) | copy-start | bytes 1572868
  65.2 14.6 %copy-start.1 = (bf16[1024,512]{1,0:T(8,128)(2,1)S(1)}, bf16[1024,512]{1,0:T(8,128)(2,1)}, u32[]{:S(2)}) copy-start(bf16[1024,512]{1,0:T(8,128)(2,1)} %grad_ref.5) | copy-start | bytes 3145732
  65.2 1.7 %collective-permute-start.24 = (bf16[2,128,512]{2,1,0:T(8,128)(2,1)S(1)}, bf16[2,128,512]{2,1,0:T(8,128)(2,1)S(1)}, u32[]{:S(2)}, u32[]{:S(2)}) collective-permute-start(bf16[2,128,512]{2,1,0:T(8,128)(2,1)S(1)} %get-tuple-element.90), channel_id=1, source_target_pairs={{0,1},{1,0},{2,3},{3,2},{4,5},{5,4},{6,7},{7,6},{8,9},{9,8},{10,11... | collective-permute-start | bytes 786440 | tf_op jit(solution)/shard_map/ppermute | solution.py:84
  66.9 5.8 %collective-permute-start.25 = (bf16[128,512]{1,0:T(8,128)(2,1)S(1)}, bf16[128,512]{1,0:T(8,128)(2,1)S(1)}, u32[]{:S(2)}, u32[]{:S(2)}) collective-permute-start(bf16[128,512]{1,0:T(8,128)(2,1)S(1)} %get-tuple-element.92), channel_id=1, source_target_pairs={{0,2},{1,3},{2,0},{3,1},{4,6},{5,7},{6,4},{7,5},{8,10},{9,11},{10,... | collective-permute-start | bytes 393224 | tf_op jit(solution)/shard_map/ppermute | solution.py:84
  73.4 5.0 %collective-permute-start.27 = (bf16[128,512]{1,0:T(8,128)(2,1)S(1)}, bf16[128,512]{1,0:T(8,128)(2,1)S(1)}, u32[]{:S(2)}, u32[]{:S(2)}) collective-permute-start(bf16[128,512]{1,0:T(8,128)(2,1)S(1)} %get-tuple-element.93.refs_0_), channel_id=1, source_target_pairs={{0,2},{1,3},{2,0},{3,1},{4,6},{5,7},{6,4},{7,5},{8,10},{9,11},{10,... | collective-permute-start | bytes 393224 | tf_op jit(solution)/shard_map/ppermute | solution.py:84
  75.0 3.4 %collective-permute-start.26 = (bf16[128,512]{1,0:T(8,128)(2,1)S(1)}, bf16[128,512]{1,0:T(8,128)(2,1)S(1)}, u32[]{:S(2)}, u32[]{:S(2)}) collective-permute-start(bf16[128,512]{1,0:T(8,128)(2,1)S(1)} %get-tuple-element.93.refs_0_), channel_id=1, source_target_pairs={{0,1},{1,0},{2,3},{3,2},{4,5},{5,4},{6,7},{7,6},{8,9},{9,8},{10,11... | collective-permute-start | bytes 393224 | tf_op jit(solution)/shard_map/ppermute | solution.py:84
  78.4 1.3 %collective-permute-start.28 = (bf16[128,512]{1,0:T(8,128)(2,1)S(1)}, bf16[128,512]{1,0:T(8,128)(2,1)S(1)}, u32[]{:S(2)}, u32[]{:S(2)}) collective-permute-start(bf16[128,512]{1,0:T(8,128)(2,1)S(1)} %collective-permute-done.27.refs_2_), channel_id=1, source_target_pairs={{0,1},{1,0},{2,3},{3,2},{4,5},{5,4},{6,7},{7,6},{8,9},{9,8},{10,11... | collective-permute-start | bytes 393224 | tf_op jit(solution)/shard_map/ppermute | solution.py:84
  82.5 2.8 %collective-permute-start.31 = (bf16[2,512,128]{2,1,0:T(8,128)(2,1)S(1)}, bf16[2,512,128]{2,1,0:T(8,128)(2,1)S(1)}, u32[]{:S(2)}, u32[]{:S(2)}) collective-permute-start(bf16[2,512,128]{2,1,0:T(8,128)(2,1)S(1)} %get-tuple-element.102), channel_id=1, source_target_pairs={{0,1},{1,0},{2,3},{3,2},{4,5},{5,4},{6,7},{7,6},{8,9},{9,8},{10,11... | collective-permute-start | bytes 786440 | tf_op jit(solution)/shard_map/ppermute | solution.py:84
  84.9 2.1 %collective-permute-start.29 = (bf16[2,512,128]{2,1,0:T(8,128)(2,1)S(1)}, bf16[2,512,128]{2,1,0:T(8,128)(2,1)S(1)}, u32[]{:S(2)}, u32[]{:S(2)}) collective-permute-start(bf16[2,512,128]{2,1,0:T(8,128)(2,1)S(1)} %get-tuple-element.98), channel_id=1, source_target_pairs={{0,1},{1,0},{2,3},{3,2},{4,5},{5,4},{6,7},{7,6},{8,9},{9,8},{10,11... | collective-permute-start | bytes 786440 | tf_op jit(solution)/shard_map/ppermute | solution.py:84
  85.4 6.4 %collective-permute-start.32 = (bf16[512,128]{1,0:T(8,128)(2,1)S(1)}, bf16[512,128]{1,0:T(8,128)(2,1)S(1)}, u32[]{:S(2)}, u32[]{:S(2)}) collective-permute-start(bf16[512,128]{1,0:T(8,128)(2,1)S(1)} %get-tuple-element.104), channel_id=1, source_target_pairs={{0,2},{1,3},{2,0},{3,1},{4,6},{5,7},{6,4},{7,5},{8,10},{9,11},{10,... | collective-permute-start | bytes 393224 | tf_op jit(solution)/shard_map/ppermute | solution.py:84
  87.0 9.2 %collective-permute-start.30 = (bf16[512,128]{1,0:T(8,128)(2,1)S(1)}, bf16[512,128]{1,0:T(8,128)(2,1)S(1)}, u32[]{:S(2)}, u32[]{:S(2)}) collective-permute-start(bf16[512,128]{1,0:T(8,128)(2,1)S(1)} %get-tuple-element.100), channel_id=1, source_target_pairs={{0,2},{1,3},{2,0},{3,1},{4,6},{5,7},{6,4},{7,5},{8,10},{9,11},{10,... | collective-permute-start | bytes 393224 | tf_op jit(solution)/shard_map/ppermute | solution.py:84
  91.8 4.5 %collective-permute-start.33 = (bf16[128,128]{1,0:T(8,128)(2,1)S(1)}, bf16[128,128]{1,0:T(8,128)(2,1)S(1)}, u32[]{:S(2)}, u32[]{:S(2)}) collective-permute-start(bf16[128,128]{1,0:T(8,128)(2,1)S(1)} %get-tuple-element.106), channel_id=1, source_target_pairs={{0,4},{4,0},{8,12},{12,8},{1,5},{5,1},{9,13},{13,9},{2,6},{6,2},{1... | collective-permute-start | bytes 98312 | tf_op jit(solution)/shard_map/ppermute | solution.py:87
  91.9 4.9 %collective-permute-start.34 = (bf16[128,128]{1,0:T(8,128)(2,1)S(1)}, bf16[128,128]{1,0:T(8,128)(2,1)S(1)}, u32[]{:S(2)}, u32[]{:S(2)}) collective-permute-start(bf16[128,128]{1,0:T(8,128)(2,1)S(1)} %get-tuple-element.107), channel_id=1, source_target_pairs={{0,8},{4,12},{8,0},{12,4},{1,9},{5,13},{9,1},{13,5},{2,10},{6,14},... | collective-permute-start | bytes 98312 | tf_op jit(solution)/shard_map/ppermute | solution.py:87
  94.8 5.7 %collective-permute-start.35 = (bf16[128,128]{1,0:T(8,128)(2,1)S(1)}, bf16[128,128]{1,0:T(8,128)(2,1)S(1)}, u32[]{:S(2)}, u32[]{:S(2)}) collective-permute-start(bf16[128,128]{1,0:T(8,128)(2,1)S(1)} %get-tuple-element.108), channel_id=1, source_target_pairs={{0,12},{4,8},{8,4},{12,0},{1,13},{5,9},{9,5},{13,1},{2,14},{6,10},... | collective-permute-start | bytes 98312 | tf_op jit(solution)/shard_map/ppermute | solution.py:87
  101.7 6.5 %collective-permute-start.36 = (bf16[512,128]{1,0:T(8,128)(2,1)S(1)}, bf16[512,128]{1,0:T(8,128)(2,1)S(1)}, u32[]{:S(2)}, u32[]{:S(2)}) collective-permute-start(bf16[512,128]{1,0:T(8,128)(2,1)S(1)} %get-tuple-element.110), channel_id=1, source_target_pairs={{0,4},{4,0},{8,12},{12,8},{1,5},{5,1},{9,13},{13,9},{2,6},{6,2},{1... | collective-permute-start | bytes 393224 | tf_op jit(solution)/shard_map/ppermute | solution.py:87
  101.8 10.3 %collective-permute-start.37 = (bf16[512,128]{1,0:T(8,128)(2,1)S(1)}, bf16[512,128]{1,0:T(8,128)(2,1)S(1)}, u32[]{:S(2)}, u32[]{:S(2)}) collective-permute-start(bf16[512,128]{1,0:T(8,128)(2,1)S(1)} %get-tuple-element.111), channel_id=1, source_target_pairs={{0,8},{4,12},{8,0},{12,4},{1,9},{5,13},{9,1},{13,5},{2,10},{6,14},... | collective-permute-start | bytes 393224 | tf_op jit(solution)/shard_map/ppermute | solution.py:87
  103.8 8.3 %collective-permute-start.38 = (bf16[512,128]{1,0:T(8,128)(2,1)S(1)}, bf16[512,128]{1,0:T(8,128)(2,1)S(1)}, u32[]{:S(2)}, u32[]{:S(2)}) collective-permute-start(bf16[512,128]{1,0:T(8,128)(2,1)S(1)} %get-tuple-element.112), channel_id=1, source_target_pairs={{0,12},{4,8},{8,4},{12,0},{1,13},{5,9},{9,5},{13,1},{2,14},{6,10},... | collective-permute-start | bytes 393224 | tf_op jit(solution)/shard_map/ppermute | solution.py:87
  112.5 1.9 %collective-permute-start.39 = (bf16[256,128]{1,0:T(8,128)(2,1)S(1)}, bf16[256,128]{1,0:T(8,128)(2,1)S(1)}, u32[]{:S(2)}, u32[]{:S(2)}) collective-permute-start(bf16[256,128]{1,0:T(8,128)(2,1)S(1)} %get-tuple-element.114), channel_id=1, source_target_pairs={{0,1},{1,0},{2,3},{3,2},{4,5},{5,4},{6,7},{7,6},{8,9},{9,8},{10,11... | collective-permute-start | bytes 196616 | tf_op jit(solution)/shard_map/ppermute | solution.py:84
  112.6 4.5 %collective-permute-start.40 = (bf16[256,128]{1,0:T(8,128)(2,1)S(1)}, bf16[256,128]{1,0:T(8,128)(2,1)S(1)}, u32[]{:S(2)}, u32[]{:S(2)}) collective-permute-start(bf16[256,128]{1,0:T(8,128)(2,1)S(1)} %get-tuple-element.115), channel_id=1, source_target_pairs={{0,2},{1,3},{2,0},{3,1},{4,6},{5,7},{6,4},{7,5},{8,10},{9,11},{10,... | collective-permute-start | bytes 196616 | tf_op jit(solution)/shard_map/ppermute | solution.py:84
  114.1 4.0 %collective-permute-start.41 = (bf16[256,128]{1,0:T(8,128)(2,1)S(1)}, bf16[256,128]{1,0:T(8,128)(2,1)S(1)}, u32[]{:S(2)}, u32[]{:S(2)}) collective-permute-start(bf16[256,128]{1,0:T(8,128)(2,1)S(1)} %get-tuple-element.116), channel_id=1, source_target_pairs={{0,3},{1,2},{2,1},{3,0},{4,7},{5,6},{6,5},{7,4},{8,11},{9,10},{10,... | collective-permute-start | bytes 196616 | tf_op jit(solution)/shard_map/ppermute | solution.py:84

commit v5 on v3

--- a/solution.py
+++ b/solution.py
@@ -10,6 +10,7 @@
 SMEM = pl.BlockSpec(memory_space=pltpu.SMEM)
 VMEM = pl.BlockSpec(memory_space=pltpu.VMEM)
 HBM = pl.BlockSpec(memory_space=pltpu.HBM)
+ANY = pl.BlockSpec(memory_space=pl.ANY)
 
 
 def dot(a, b):
@@ -56,19 +57,19 @@
     return parts[0] if len(parts) == 1 else jnp.concatenate(parts, axis=0)
 
 
-def call(body, name, me, ins, outs, scratch=(), flops=0, far=()):
+def call(body, name, me, ins, outs, scratch=(), flops=0, far=(), unread=()):
     size = lambda s: s.size * s.dtype.itemsize
     moved = sum(size(x) for x in ins) + sum(size(x) for x in outs)
     return pl.pallas_call(
         body,
         out_shape=list(outs),
-        in_specs=[SMEM] + [HBM if i in far else VMEM for i in range(len(ins))],
+        in_specs=[SMEM] + [HBM if i in far else ANY if i in unread else VMEM for i in range(len(ins))],
         out_specs=[VMEM] * len(outs),
         scratch_shapes=list(scratch),
         compiler_params=pltpu.CompilerParams(vmem_limit_bytes=24 * 2**20),
         cost_estimate=pl.CostEstimate(flops=flops, bytes_accessed=moved, transcendentals=0),
         name=name,
-    )(me, *ins)
+    )(me, *[pltpu.with_memory_space_constraint(x, pltpu.HBM) if i in far else x for i, x in enumerate(ins)])
 
 
 def shape(dims, dtype=BF):
@@ -203,30 +204,6 @@
 
         state_parts = member_gather_chips(grid_state)
         pack_parts = member_gather_chips(pack)
-        gather = lambda w: lax.all_gather(w, ("feat", "rep"), axis=0, tiled=True)
-        in_full = gather(edge_in_weight)
-        out_full = gather(edge_out_weight)
-        node_in_full = gather(node_in_weight)
-        node_out_full = gather(node_out_weight)
-
-        def hots_kernel(me_ref, send_ref, recv_ref, sl_out, sh_out, r_out, slt_out, sht_out, rt_out):
-            for i in range(E // T):
-                at = slice(i * T, (i + 1) * T)
-                sent, got = send_ref[:, at], recv_ref[:, at]
-                sl_out[at, :] = hot_rows(sent, N)
-                sh_out[at, :] = hot_rows(sent - N, NH)
-                r_out[at, :] = hot_rows(got, N)
-                slt_out[:, at] = hot_columns(sent, N)
-                sht_out[:, at] = hot_columns(sent - N, NH)
-                rt_out[:, at] = hot_columns(got, N)
-
-        sl_hot, sh_hot, r_hot, slt_hot, sht_hot, rt_hot = call(
-            hots_kernel,
-            "edge_hots",
-            me1,
-            [send_row, recv_row],
-            [shape((E, N)), shape((E, NH)), shape((E, N)), shape((N, E)), shape((NH, E)), shape((N, E))],
-        )
 
         def grid_kernel(me_ref, *refs):
             states, packs = refs[:M], refs[M : 2 * M]
@@ -264,70 +241,151 @@
             far=(0,),
         )
         incoming = dom_trade(outgoing)
-
-        def encode_kernel(me_ref, base_ref, halo_ref, table_ref, *refs):
-            arrived, state_out, outs = refs[:n_dom], refs[n_dom], refs[n_dom + 1 :]
+        near, others = range(n_rep), range(n_rep, M)
+
+        def hots_kernel(me_ref, send_ref, recv_ref, after_ref, sl_out, sh_out, r_out, slt_out, sht_out, rt_out):
+            for i in range(E // T):
+                at = slice(i * T, (i + 1) * T)
+                sent, got = send_ref[:, at], recv_ref[:, at]
+                sl_out[at, :] = hot_rows(sent, N)
+                sh_out[at, :] = hot_rows(sent - N, NH)
+                r_out[at, :] = hot_rows(got, N)
+                slt_out[:, at] = hot_columns(sent, N)
+                sht_out[:, at] = hot_columns(sent - N, NH)
+                rt_out[:, at] = hot_columns(got, N)
+
+        sl_hot, sh_hot, r_hot, slt_hot, sht_hot, rt_hot = call(
+            hots_kernel,
+            "edge_hots",
+            me1,
+            [send_row, recv_row, grid_slope],
+            [shape((E, N)), shape((E, NH)), shape((E, N)), shape((N, E)), shape((NH, E)), shape((N, E))],
+            unread=(2,),
+        )
+
+        firsts = [kf * n_rep for kf in range(1, n_feat)]
+
+        def relay_kernel(me_ref, in_ref, out_ref, after_ref, edge_out, sems):
+            pairs = [(in_ref, edge_out.at[:rows_in, :]), (out_ref, edge_out.at[rows_in:, :])]
+            copies = [pltpu.make_async_copy(a, b, sems.at[i]) for i, (a, b) in enumerate(pairs)]
+            for copy in copies:
+                copy.start()
+            for copy in copies:
+                copy.wait()
+
+        edge_own = call(
+            relay_kernel,
+            "relay",
+            me1,
+            [edge_in_weight, edge_out_weight, sl_hot],
+            [shape((rows_in + rows_out, D))],
+            scratch=[pltpu.SemaphoreType.DMA((2,))],
+            far=range(2),
+            unread=(2,),
+        )[0]
+        edge_chips = [edge_own] + [member_swap(edge_own, k) for k in firsts]
+
+        def encode_kernel(me_ref, base_ref, table_ref, *refs):
+            arrived, state_out = refs[:n_dom], refs[-1]
             total = dot(base_ref[...], column_pick(me_ref[0], D, C))
             for k in range(M):
                 rows = stack([arrived[j][k * S : (k + 1) * S, :] for j in range(n_dom)])
                 total += dot(hot_columns(table_ref[k, 1:2, :], N), rows)
-            state = total.astype(BF)
-            state_out[...] = state
-            rows = dot(hot_rows(halo_ref[...], N), state).astype(BF)
+            state_out[...] = total.astype(BF)
+
+        state_cols = call(
+            encode_kernel,
+            "encode",
+            me1,
+            [mesh_base, slots] + incoming + [sl_hot],
+            [shape((N, C))],
+            flops=2 * M * N * NS * C,
+            unread=(2 + n_dom,),
+        )[0]
+        state_parts2 = member_gather_chips(state_cols)
+
+        def halo_kernel(me_ref, state_ref, halo_ref, *outs):
+            rows = dot(hot_rows(halo_ref[...], N), state_ref[...]).astype(BF)
             for j in range(n_dom):
                 outs[j][...] = rows[j * H : (j + 1) * H]
 
-        state_cols, *halo_out = call(
-            encode_kernel,
-            "encode",
-            me1,
-            [mesh_base, halo_row, slots] + incoming,
-            [shape((N, C))] + [shape((H, C))] * n_dom,
-            flops=2 * M * N * NS * C,
+        halo_out = call(
+            halo_kernel,
+            "halo_rows",
+            me1,
+            [state_cols, halo_row],
+            [shape((H, C))] * n_dom,
+            flops=2 * N * NH * C,
         )
         halo_in = dom_trade(halo_out)
-        state_parts2 = member_gather_chips(state_cols)
-        halo_cols = jnp.concatenate(halo_in, axis=0)
+
+        def join_kernel(me_ref, *refs):
+            for j in range(n_dom):
+                refs[-1][j * H : (j + 1) * H, :] = refs[j][...]
+
+        halo_cols = call(
+            join_kernel,
+            "halo_join",
+            me1,
+            halo_in + [state_parts2[n_rep]],
+            [shape((NH, C))],
+            unread=(n_dom,),
+        )[0]
         halo_parts = member_gather_chips(halo_cols)
 
-        def local_kernel(me_ref, es_ref, send_ref, recv_ref, w_ref, *refs):
-            cols, (pre_out, state_out, parts) = refs[:M], refs[M:]
+        def weights_kernel(me_ref, in_ref, out_ref, *refs):
+            chips, (pair_out, node_out, sems) = refs[:n_feat], refs[-3:]
+            pairs = [(in_ref, node_out.at[:rows_node, :]), (out_ref, node_out.at[rows_node:, :])]
+            copies = [pltpu.make_async_copy(a, b, sems.at[i]) for i, (a, b) in enumerate(pairs)]
+            for copy in copies:
+                copy.start()
+            for kf in range(n_feat):
+                pair_out[kf] = chips[kf][...]
+            for copy in copies:
+                copy.wait()
+
+        edge_pair, node_own = call(
+            weights_kernel,
+            "join_weights",
+            me1,
+            [node_in_weight, node_out_weight] + edge_chips + [halo_cols],
+            [shape((n_feat, rows_in + rows_out, D)), shape((rows_node + rows_out, D))],
+            scratch=[pltpu.SemaphoreType.DMA((2,))],
+            far=range(2),
+            unread=(2 + n_feat,),
+        )
+        edge_pairs = [edge_pair] + [member_swap(edge_pair, kr) for kr in range(1, n_rep)]
+        node_chips = [node_own] + [member_swap(node_own, k) for k in firsts]
+
+
+        def local_kernel(me_ref, es_ref, send_ref, recv_ref, *refs):
+            cols, weights = refs[:M], refs[M : M + n_rep]
+            pre_out, state_out, w_out, out_out, parts = refs[M + n_rep :]
             me = me_ref[0]
             for k in range(M):
+                kf, kr = divmod(k, n_rep)
                 parts[me ^ k] = cols[k][...]
+                w_out[rows_at(me ^ k, rows_in), :] = weights[kr][kf, :rows_in, :]
+                out_out[rows_at(me ^ k, rows_out), :] = weights[kr][kf, rows_in:, :]
             state_out[...] = lanes([parts[j] for j in range(M)])
             for i in range(E // T):
                 at = slice(i * T, (i + 1) * T)
                 sent = dot(send_ref[at, :], state_out[...]).astype(BF)
                 got = dot(recv_ref[at, :], state_out[...]).astype(BF)
                 pre_out[at, :] = (
-                    dot(es_ref[at, :], w_ref[:D, :])
-                    + dot(sent, w_ref[D : 2 * D, :])
-                    + dot(got, w_ref[2 * D :, :])
+                    dot(es_ref[at, :], w_out[:D, :])
+                    + dot(sent, w_out[D : 2 * D, :])
+                    + dot(got, w_out[2 * D :, :])
                 )
 
-        local_pre, mesh_state = call(
+        local_pre, mesh_state, in_full, out_full = call(
             local_kernel,
             "edge_local",
             me1,
-            [edge_state, sl_hot, r_hot, in_full] + state_parts2,
-            [shape((E, D), F32), shape((N, D))],
+            [edge_state, sl_hot, r_hot] + state_parts2 + edge_pairs,
+            [shape((E, D), F32), shape((N, D)), shape((3 * D, D)), shape((D, D))],
             scratch=[pltpu.VMEM((M, N, C), BF)],
             flops=2 * E * D * (3 * D + 2 * N),
-        )
-
-        def node_ahead_kernel(me_ref, state_ref, grad_ref, in_ref, out_ref, pre_out, cot_out):
-            mine = rows_at(me_ref[0], R)
-            pre_out[...] = dot(state_ref[mine, :], in_ref[:D, :])
-            cot_out[...] = dot_t(grad_ref[mine, :], out_ref[...])
-
-        node_pre, node_cot = call(
-            node_ahead_kernel,
-            "node_ahead",
-            me1,
-            [mesh_state, node_grad, node_in_full, node_out_full],
-            [shape((R, D), F32), shape((R, D), F32)],
-            flops=4 * R * D * D,
         )
 
         def edge_kernel(me_ref, local_ref, es_ref, send_ref, recv_ref, w_ref, out_ref, *refs):
@@ -366,6 +424,42 @@
             ],
             flops=2 * E * D * (NH + D + D + N),
         )
+        def node_weights_kernel(me_ref, *refs):
+            for kf in range(n_feat):
+                refs[-1][kf] = refs[kf][...]
+
+        node_pair = call(
+            node_weights_kernel,
+            "join_node_weights",
+            me1,
+            node_chips + [sums[0]],
+            [shape((n_feat, rows_node + rows_out, D))],
+            unread=(n_feat,),
+        )[0]
+        node_pairs = [node_pair] + [member_swap(node_pair, kr) for kr in range(1, n_rep)]
+
+        def node_ahead_kernel(me_ref, state_ref, grad_ref, *refs):
+            weights = refs[:n_rep]
+            node_in_full, pre_out, cot_out, node_out_full = refs[n_rep:]
+            me = me_ref[0]
+            for k in range(M):
+                kf, kr = divmod(k, n_rep)
+                node_in_full[rows_at(me ^ k, rows_node), :] = weights[kr][kf, :rows_node, :]
+                node_out_full[rows_at(me ^ k, rows_out), :] = weights[kr][kf, rows_node:, :]
+            mine = rows_at(me, R)
+            pre_out[...] = dot(state_ref[mine, :], node_in_full[:D, :])
+            cot_out[...] = dot_t(grad_ref[mine, :], node_out_full[...])
+
+        node_in_full, node_pre, node_cot = call(
+            node_ahead_kernel,
+            "node_ahead",
+            me1,
+            [mesh_state, node_grad] + node_pairs,
+            [shape((2 * D, D)), shape((R, D), F32), shape((R, D), F32)],
+            scratch=[pltpu.VMEM((D, D), BF)],
+            flops=4 * R * D * D,
+        )
+
         sums = member_sums(sums, me1, "node_sums")
 
         def node_kernel(me_ref, pre_ref, cot_ref, w_ref, grad_ref, *refs):
@@ -460,7 +554,7 @@
 
         def owed_kernel(me_ref, halo_ref, table_ref, *refs):
             local, back = refs[:n_feat], refs[n_feat : n_feat + n_dom]
-            outs = refs[n_feat + n_dom :]
+            first, second = refs[n_feat + n_dom : -n_dom], refs[-n_dom:]
             total = local[0][...].astype(F32)
             for k in range(1, n_feat):
                 total += local[k][...].astype(F32)
@@ -468,35 +562,44 @@
             cot = (total + dot(hot_columns(halo_ref[...], N), rows)).astype(BF)
             for k in range(M):
                 owed = dot(hot_rows(table_ref[k, 1:2, :], N), cot).astype(BF)
+                outs, at = (first, k) if k < n_rep else (second, k - n_rep)
                 for j in range(n_dom):
-                    outs[j][k * S : (k + 1) * S, :] = owed[j * S : (j + 1) * S]
+                    outs[j][at * S : (at + 1) * S, :] = owed[j * S : (j + 1) * S]
 
         owed = call(
             owed_kernel,
             "owed_rows",
             me1,
             [halo_row, slots] + local_grads + halo_back,
-            [shape((M * S, C))] * n_dom,
+            [shape((n_rep * S, C))] * n_dom + [shape((len(others) * S, C))] * n_dom,
             flops=2 * M * NS * N * C,
         )
-        owed = dom_trade(owed)
-
-        def grid_back_kernel(me_ref, slope_ref, table_ref, *refs):
-            back, outs = refs[:n_dom], refs[n_dom:]
-            for k in range(M):
-                rows = stack([back[j][k * S : (k + 1) * S, :] for j in range(n_dom)])
-                cot = dot(hot_columns(table_ref[k, 0:1, :], G), rows)
-                outs[k][...] = (cot * slope_ref[k]).astype(BF)
-
-        grid_dpre = call(
-            grid_back_kernel,
-            "grid_backward",
-            me1,
-            [grid_slope, slots] + owed,
-            [shape((G, C))] * M,
-            flops=2 * M * G * NS * C,
-        )
-        grid_dpre = member_trade(grid_dpre)
+        far_owed = dom_trade(owed[n_dom:])
+        near_owed = dom_trade(owed[:n_dom])
+
+        def grid_back(name, members, back, after=()):
+            def kernel(me_ref, slope_ref, table_ref, *refs):
+                arrived, outs = refs[:n_dom], refs[n_dom + len(after) :]
+                for at, k in enumerate(members):
+                    rows = stack([arrived[j][at * S : (at + 1) * S, :] for j in range(n_dom)])
+                    cot = dot(hot_columns(table_ref[k, 0:1, :], G), rows)
+                    outs[at][...] = (cot * slope_ref[k]).astype(BF)
+
+            return call(
+                kernel,
+                name,
+                me1,
+                [grid_slope, slots] + back + list(after),
+                [shape((G, C))] * len(members),
+                flops=2 * len(members) * G * NS * C,
+                unread=range(2 + n_dom, 2 + n_dom + len(after)),
+            )
+
+        far_dpre = grid_back("grid_back_far", others, far_owed)
+        near_dpre = grid_back("grid_back_near", near, near_owed, far_dpre[:1])
+        far_dpre = [member_swap(x, k) for x, k in zip(far_dpre, others)]
+        near_dpre = [member_swap(x, k) if k else x for x, k in zip(near_dpre, near)]
+        grid_dpre = near_dpre + far_dpre
 
         def adjoint_kernel(me_ref, enc_ref, *refs):
             cols, out, parts = refs[:M], refs[M], refs[M + 1]

time: 151 us -> 122 us (0.81)
  local copies, waits for them, and re-layouts: 27.4 us -> 0.7 us
  blocking collectives: 16.9 us -> 0 us
  waiting for transfers between devices: 38.2 us -> 53.4 us
  between operations: 13.7 us -> 0.29 us
  starting transfers between devices: 31.1 us -> 42.2 us
  Pallas kernels: 23.4 us -> 25 us
    unnamed x91 -> x10, local copies, waits for them, and re-layouts: 27.4 us -> 0.7 us
    all_gather x2 -> x0, blocking collectives: 16.9 us -> none  [per_device(): gather = lambda w: lax.all_gather(w, ('feat', 'rep'), axis=0, tiled=True)]
    ppermute x24 -> x28, waiting for transfers between devices: 21.4 us -> 32.9 us  [member_swap(): return lax.ppermute(x, ('feat', 'rep'), [(i, i ^ k) for i in range(M)])]
    ppermute x24 -> x28, starting transfers between devices: 13 us -> 20 us  [member_swap(): return lax.ppermute(x, ('feat', 'rep'), [(i, i ^ k) for i in range(M)])]
    ppermute x12 -> x15, waiting for transfers between devices: 16.1 us -> 20.5 us  [dom_swap(): return lax.ppermute(x, 'dom', [(i, i ^ k) for i in range(n_dom)])]
    ppermute x12 -> x15, starting transfers between devices: 18.1 us -> 22.2 us  [dom_swap(): return lax.ppermute(x, 'dom', [(i, i ^ k) for i in range(n_dom)])]
    pallas_call x17 -> x23, Pallas kernels: 23.4 us -> 25 us  [call(): pl.pallas_call(body, out_shape=list(outs), in_specs=[SMEM] + [HBM if i in...]
  transfers between devices with their start and end apart: 38 -> 43, of which waited for: 17 -> 20; matrix products, arithmetic and copies ran while one was open for 0% -> 0% of each run, Pallas kernels for 11% -> 10%
where the time goes in v5:
time: 122 us
  waiting for transfers between devices  53.4 us (44%)
  starting transfers between devices  42.2 us (35%)
  Pallas kernels  25 us (20%)
    ppermute x28, waiting for transfers between devices, member_swap(): return lax.ppermute(x, ('feat', 'rep'), [(i, i ^ k) for i in range(M)])  32.9 us
    pallas_call x23, Pallas kernels, call(): pl.pallas_call(body, out_shape=list(outs), in_specs=[SMEM] + [HBM if i in...  25 us
    ppermute x15, starting transfers between devices, dom_swap(): return lax.ppermute(x, 'dom', [(i, i ^ k) for i in range(n_dom)])  22.2 us
    ppermute x15, waiting for transfers between devices, dom_swap(): return lax.ppermute(x, 'dom', [(i, i ^ k) for i in range(n_dom)])  20.5 us
    ppermute x28, starting transfers between devices, member_swap(): return lax.ppermute(x, ('feat', 'rep'), [(i, i ^ k) for i in range(M)])  20 us
  transfers between devices with their start and end apart: 43, of which 20 were waited for; matrix products, arithmetic and copies ran while one was open for 0% of the time, Pallas kernels for 10%

profile of v5, /device:TPU:0, one launch (start us, length us, event | category | flops | bytes accessed | tf_op | source)
XLA Modules:
  0.0 121.6 jit_solution(3164251883845176836)
XLA Ops:
  0.0 2.9 %collective-permute-start.1 = (bf16[256,512]{1,0:T(8,128)(2,1)}, bf16[256,512]{1,0:T(8,128)(2,1)S(1)}, u32[]{:S(2)}, u32[]{:S(2)}) collective-permute-start(bf16[256,512]{1,0:T(8,128)(2,1)} %refs_0_.1), channel_id=1, source_target_pairs={{0,2},{1,3},{2,0},{3,1},{4,6},{5,7},{6,4},{7,5},{8,10},{9,11},{10,... | collective-permute-start | bytes 786440 | tf_op jit(solution)/shard_map/ppermute | solution.py:84
  3.0 1.5 %tables.1 = (bf16[144,512]{1,0:T(8,128)(2,1)S(1)}, s32[1,512]{1,0:T(1,128)S(1)}, s32[1,1024]{1,0:T(1,128)S(1)}) custom-call(s32[2]{0:T(128)S(1)} %pad_add_fusion.where_ref, bf16[128,512]{1,0:T(8,128)(2,1)} %enc_ref.1, s32[1,4,128]{2,1,0:T(4,128)} %gs_ref.1, s32[1,4,128]{2,1,0:T(4,128)} %gr_ref.1, s32[1,4,128]{2,1,0:T(4,128)} %halo_ref.1, s32[1,1024]{1,0:T(1,128)} %bitcast.5), custom_call_target="tpu_custom_call" | custom-call | bytes 294912 | tf_op jit(solution)/shard_map/tables/pallas_call | solution.py:63
  4.7 5.6 %collective-permute-done.1.refs_2_ = bf16[256,512]{1,0:T(8,128)(2,1)S(1)} collective-permute-done((bf16[256,512]{1,0:T(8,128)(2,1)}, bf16[256,512]{1,0:T(8,128)(2,1)S(1)}, u32[]{:S(2)}, u32[]{:S(2)}) %collective-permute-start.1) | collective-permute-done | bytes 262176 | tf_op jit(solution)/shard_map/ppermute | solution.py:84
  10.8 1.8 %collective-permute-done.4.refs_6_ = bf16[144,512]{1,0:T(8,128)(2,1)S(1)} collective-permute-done((bf16[144,512]{1,0:T(8,128)(2,1)S(1)}, bf16[144,512]{1,0:T(8,128)(2,1)S(1)}, u32[]{:S(2)}, u32[]{:S(2)}) %collective-permute-start.4) | collective-permute-done | bytes 147488 | tf_op jit(solution)/shard_map/ppermute | solution.py:84
  12.6 1.4 %collective-permute-done.5.refs_7_ = bf16[144,512]{1,0:T(8,128)(2,1)S(1)} collective-permute-done((bf16[144,512]{1,0:T(8,128)(2,1)S(1)}, bf16[144,512]{1,0:T(8,128)(2,1)S(1)}, u32[]{:S(2)}, u32[]{:S(2)}) %collective-permute-start.5) | collective-permute-done | bytes 147488 | tf_op jit(solution)/shard_map/ppermute | solution.py:84
  14.0 2.5 %grid_messages.1 = (bf16[512,512]{1,0:T(8,128)(2,1)S(1)}, f32[4,256,128]{2,1,0:T(8,128)S(1)}, s32[4,2,512]{2,1,0:T(2,128)S(1)}, bf16[512,128]{1,0:T(8,128)(2,1)S...) custom-call(s32[1]{0:T(128)} %bitcast.me_ref, ...), custom_call_target="tpu_custom_call" | custom-call | flops 268435456 | bytes 3227648 | tf_op jit(solution)/shard_map/grid_messages/pallas_call | solution.py:63
  17.2 2.1 %edge_hots.1 = (bf16[1024,512]{1,0:T(8,128)(2,1)S(1)}, bf16[1024,512]{1,0:T(8,128)(2,1)S(1)}, bf16[1024,512]{1,0:T(8,128)(2,1)S(1)}, bf16[512,1024]{1,0:T(8,128)...) custom-call(s32[1]{0:T(128)} %bitcast.me_ref, s32[1,1024]{1,0:T(1,128)S(1)} %get-tuple-element.71.send_ref, ...), custom_call_target="tpu_custom_call" | custom-call | bytes 6823936 | tf_op jit(solution)/shard_map/edge_hots/pallas_call | solution.py:63
  19.3 1.0 relay.1.refs_0_
  20.4 1.8 %collective-permute-start.12 = (bf16[512,512]{1,0:T(8,128)(2,1)S(1)}, bf16[512,512]{1,0:T(8,128)(2,1)S(1)}, u32[]{:S(2)}, u32[]{:S(2)}) collective-permute-start(bf16[512,512]{1,0:T(8,128)(2,1)S(1)} %relay.1.refs_0_), channel_id=1, source_target_pairs={{0,2},{1,3},{2,0},{3,1},{4,6},{5,7},{6,4},{7,5},{8,10},{9,11},{10,... | collective-permute-start | bytes 1572872 | tf_op jit(solution)/shard_map/ppermute | solution.py:84
  22.2 1.6 %collective-permute-start.6 = (bf16[512,128]{1,0:T(8,128)(2,1)S(1)}, bf16[512,128]{1,0:T(8,128)(2,1)S(1)}, u32[]{:S(2)}, u32[]{:S(2)}) collective-permute-start(bf16[512,128]{1,0:T(8,128)(2,1)S(1)} %get-tuple-element.75), channel_id=1, source_target_pairs={{0,4},{4,0},{8,12},{12,8},{1,5},{5,1},{9,13},{13,9},{2,6},{6,2},{1... | collective-permute-start | bytes 393224 | tf_op jit(solution)/shard_map/ppermute | solution.py:87
  23.7 2.6 %collective-permute-start.7 = (bf16[512,128]{1,0:T(8,128)(2,1)S(1)}, bf16[512,128]{1,0:T(8,128)(2,1)S(1)}, u32[]{:S(2)}, u32[]{:S(2)}) collective-permute-start(bf16[512,128]{1,0:T(8,128)(2,1)S(1)} %get-tuple-element.76), channel_id=1, source_target_pairs={{0,8},{4,12},{8,0},{12,4},{1,9},{5,13},{9,1},{13,5},{2,10},{6,14},... | collective-permute-start | bytes 393224 | tf_op jit(solution)/shard_map/ppermute | solution.py:87
  26.6 2.5 %collective-permute-done.6.refs_1_ = bf16[512,128]{1,0:T(8,128)(2,1)S(1)} collective-permute-done((bf16[512,128]{1,0:T(8,128)(2,1)S(1)}, bf16[512,128]{1,0:T(8,128)(2,1)S(1)}, u32[]{:S(2)}, u32[]{:S(2)}) %collective-permute-start.6) | collective-permute-done | bytes 131104 | tf_op jit(solution)/shard_map/ppermute | solution.py:87
  29.1 7.6 %collective-permute-done.7.refs_2_ = bf16[512,128]{1,0:T(8,128)(2,1)S(1)} collective-permute-done((bf16[512,128]{1,0:T(8,128)(2,1)S(1)}, bf16[512,128]{1,0:T(8,128)(2,1)S(1)}, u32[]{:S(2)}, u32[]{:S(2)}) %collective-permute-start.7) | collective-permute-done | bytes 131104 | tf_op jit(solution)/shard_map/ppermute | solution.py:87
  38.7 2.0 %collective-permute-start.13 = (bf16[128,128]{1,0:T(8,128)(2,1)S(1)}, bf16[128,128]{1,0:T(8,128)(2,1)S(1)}, u32[]{:S(2)}, u32[]{:S(2)}) collective-permute-start(bf16[128,128]{1,0:T(8,128)(2,1)S(1)} %get-tuple-element.79), channel_id=1, source_target_pairs={{0,4},{4,0},{8,12},{12,8},{1,5},{5,1},{9,13},{13,9},{2,6},{6,2},{1... | collective-permute-start | bytes 98312 | tf_op jit(solution)/shard_map/ppermute | solution.py:87
  40.8 1.1 collective-permute-start.14
  41.8 1.4 %collective-permute-start.15 = (bf16[128,128]{1,0:T(8,128)(2,1)S(1)}, bf16[128,128]{1,0:T(8,128)(2,1)S(1)}, u32[]{:S(2)}, u32[]{:S(2)}) collective-permute-start(bf16[128,128]{1,0:T(8,128)(2,1)S(1)} %get-tuple-element.81), channel_id=1, source_target_pairs={{0,12},{4,8},{8,4},{12,0},{1,13},{5,9},{9,5},{13,1},{2,14},{6,10},... | collective-permute-start | bytes 98312 | tf_op jit(solution)/shard_map/ppermute | solution.py:87
  43.2 2.7 %collective-permute-done.14.refs_2_ = bf16[128,128]{1,0:T(8,128)(2,1)S(1)} collective-permute-done((bf16[128,128]{1,0:T(8,128)(2,1)S(1)}, bf16[128,128]{1,0:T(8,128)(2,1)S(1)}, u32[]{:S(2)}, u32[]{:S(2)}) %collective-permute-start.14) | collective-permute-done | bytes 32800 | tf_op jit(solution)/shard_map/ppermute | solution.py:87
  45.9 1.6 %collective-permute-done.15.refs_3_ = bf16[128,128]{1,0:T(8,128)(2,1)S(1)} collective-permute-done((bf16[128,128]{1,0:T(8,128)(2,1)S(1)}, bf16[128,128]{1,0:T(8,128)(2,1)S(1)}, u32[]{:S(2)}, u32[]{:S(2)}) %collective-permute-start.15) | collective-permute-done | bytes 32800 | tf_op jit(solution)/shard_map/ppermute | solution.py:87
  48.7 1.5 %collective-permute-start.18 = (bf16[512,128]{1,0:T(8,128)(2,1)S(1)}, bf16[512,128]{1,0:T(8,128)(2,1)S(1)}, u32[]{:S(2)}, u32[]{:S(2)}) collective-permute-start(bf16[512,128]{1,0:T(8,128)(2,1)S(1)} %halo_join.1.refs_2_.refs_0_), channel_id=1, source_target_pairs={{0,2},{1,3},{2,0},{3,1},{4,6},{5,7},{6,4},{7,5},{8,10},{9,11},{10,... | collective-permute-start | bytes 393224 | tf_op jit(solution)/shard_map/ppermute | solution.py:84
  50.9 3.7 %collective-permute-done.18.refs_2_ = bf16[512,128]{1,0:T(8,128)(2,1)S(1)} collective-permute-done((bf16[512,128]{1,0:T(8,128)(2,1)S(1)}, bf16[512,128]{1,0:T(8,128)(2,1)S(1)}, u32[]{:S(2)}, u32[]{:S(2)}) %collective-permute-start.18) | collective-permute-done | bytes 131104 | tf_op jit(solution)/shard_map/ppermute | solution.py:84
  54.6 1.5 %collective-permute-start.20 = (bf16[384,512]{1,0:T(8,128)(2,1)S(1)}, bf16[384,512]{1,0:T(8,128)(2,1)S(1)}, u32[]{:S(2)}, u32[]{:S(2)}) collective-permute-start(bf16[384,512]{1,0:T(8,128)(2,1)S(1)} %get-tuple-element.91.refs_0_), channel_id=1, source_target_pairs={{0,2},{1,3},{2,0},{3,1},{4,6},{5,7},{6,4},{7,5},{8,10},{9,11},{10,... | collective-permute-start | bytes 1179656 | tf_op jit(solution)/shard_map/ppermute | solution.py:84
  56.1 3.0 %edge_local.1 = (f32[1024,512]{1,0:T(8,128)S(1)}, bf16[512,512]{1,0:T(8,128)(2,1)S(1)}, bf16[1536,512]{1,0:T(8,128)(2,1)S(1)}, bf16[512,512]{1,0:T(8,128)(2,1)S(1)}) custom-call(s32[1]{0:T(128)} %bitcast.me_ref, bf16[1024,512]{1,0:T(8,128)(2,1)S(1)} %copy-done.4, bf16[1024,512]{1,0:T(8,128)(2,1)S(1)} %get-tuple-element.72.refs_4_.after_ref.send_ref, ...), custom_call_target="tpu_custom_call" | custom-call | flops 2684354560 | bytes 10485760 | tf_op jit(solution)/shard_map/edge_local/pallas_call | solution.py:63
  59.1 3.1 %edge_update.1 = (f32[1024,512]{1,0:T(8,128)S(1)}, bf16[2,128,512]{2,1,0:T(8,128)(2,1)S(1)}, bf16[2,128,512]{2,1,0:T(8,128)(2,1)S(1)}) custom-call(s32[1]{0:T(128)} %bitcast.me_ref, f32[1024,512]{1,0:T(8,128)S(1)} %get-tuple-element.83.local_ref, bf16[1024,512]{1,0:T(8,128)(2,1)S(1)} %copy-done.4, bf16[1024,512]{1,0:T(8,128)(2,1)S(1)} %get-tuple-element.84.send_ref, ...), custom_call_target="tpu_custom_call" | custom-call | flops 2147483648 | bytes 10485760 | tf_op jit(solution)/shard_map/edge_update/pallas_call | solution.py:63
  62.3 3.9 %collective-permute-done.20.refs_1_ = bf16[384,512]{1,0:T(8,128)(2,1)S(1)} collective-permute-done((bf16[384,512]{1,0:T(8,128)(2,1)S(1)}, bf16[384,512]{1,0:T(8,128)(2,1)S(1)}, u32[]{:S(2)}, u32[]{:S(2)}) %collective-permute-start.20) | collective-permute-done | bytes 393248 | tf_op jit(solution)/shard_map/ppermute | solution.py:84
  66.8 2.1 %collective-permute-done.22.refs_1_ = bf16[2,128,512]{2,1,0:T(8,128)(2,1)S(1)} collective-permute-done((bf16[2,128,512]{2,1,0:T(8,128)(2,1)S(1)}, bf16[2,128,512]{2,1,0:T(8,128)(2,1)S(1)}, u32[]{:S(2)}, u32[]{:S(2)}) %collective-permute-start.22) | collective-permute-done | bytes 262176 | tf_op jit(solution)/shard_map/ppermute | solution.py:84
  69.0 1.5 %collective-permute-start.23 = (bf16[128,512]{1,0:T(8,128)(2,1)S(1)}, bf16[128,512]{1,0:T(8,128)(2,1)S(1)}, u32[]{:S(2)}, u32[]{:S(2)}) collective-permute-start(bf16[128,512]{1,0:T(8,128)(2,1)S(1)} %get-tuple-element.98), channel_id=1, source_target_pairs={{0,2},{1,3},{2,0},{3,1},{4,6},{5,7},{6,4},{7,5},{8,10},{9,11},{10,... | collective-permute-start | bytes 393224 | tf_op jit(solution)/shard_map/ppermute | solution.py:84
  71.0 3.6 %collective-permute-done.23.refs_1_ = bf16[128,512]{1,0:T(8,128)(2,1)S(1)} collective-permute-done((bf16[128,512]{1,0:T(8,128)(2,1)S(1)}, bf16[128,512]{1,0:T(8,128)(2,1)S(1)}, u32[]{:S(2)}, u32[]{:S(2)}) %collective-permute-start.23) | collective-permute-done | bytes 131104 | tf_op jit(solution)/shard_map/ppermute | solution.py:84
  75.2 1.5 %collective-permute-start.25 = (bf16[128,512]{1,0:T(8,128)(2,1)S(1)}, bf16[128,512]{1,0:T(8,128)(2,1)S(1)}, u32[]{:S(2)}, u32[]{:S(2)}) collective-permute-start(bf16[128,512]{1,0:T(8,128)(2,1)S(1)} %get-tuple-element.99.refs_0_), channel_id=1, source_target_pairs={{0,2},{1,3},{2,0},{3,1},{4,6},{5,7},{6,4},{7,5},{8,10},{9,11},{10,... | collective-permute-start | bytes 393224 | tf_op jit(solution)/shard_map/ppermute | solution.py:84
  76.8 3.5 %collective-permute-done.25.refs_2_ = bf16[128,512]{1,0:T(8,128)(2,1)S(1)} collective-permute-done((bf16[128,512]{1,0:T(8,128)(2,1)S(1)}, bf16[128,512]{1,0:T(8,128)(2,1)S(1)}, u32[]{:S(2)}, u32[]{:S(2)}) %collective-permute-start.25) | collective-permute-done | bytes 131104 | tf_op jit(solution)/shard_map/ppermute | solution.py:84
  80.3 1.3 %collective-permute-done.26.refs_3_ = bf16[128,512]{1,0:T(8,128)(2,1)S(1)} collective-permute-done((bf16[128,512]{1,0:T(8,128)(2,1)S(1)}, bf16[128,512]{1,0:T(8,128)(2,1)S(1)}, u32[]{:S(2)}, u32[]{:S(2)}) %collective-permute-start.26) | collective-permute-done | bytes 131104 | tf_op jit(solution)/shard_map/ppermute | solution.py:84
  81.6 2.9 %edge_backward.1 = (bf16[1024,512]{1,0:T(8,128)(2,1)S(1)}, bf16[2,512,128]{2,1,0:T(8,128)(2,1)S(1)}, bf16[2,512,128]{2,1,0:T(8,128)(2,1)S(1)}) custom-call(s32[1]{0:T(128)} %bitcast.me_ref, bf16[1024,512]{1,0:T(8,128)(2,1)S(1)} %copy-done.1, f32[1024,512]{1,0:T(8,128)S(1)} %get-tuple-element.88.pre_ref, bf16[512,1024]{1,0:T(8,128)(2,1)S(1)} %get-tuple-element.89.send_ref, ...), custom_call_target="tpu_custom_call" | custom-call | flops 1879048192 | bytes 9437184 | tf_op jit(solution)/shard_map/edge_backward/pallas_call | solution.py:63
  84.7 2.1 %local_backward.1 = (bf16[2,512,128]{2,1,0:T(8,128)(2,1)S(1)}, bf16[2,512,128]{2,1,0:T(8,128)(2,1)S(1)}) custom-call(s32[1]{0:T(128)} %bitcast.me_ref, bf16[1024,512]{1,0:T(8,128)(2,1)S(1)} %get-tuple-element.100.dpre_ref, bf16[512,1024]{1,0:T(8,128)(2,1)S(1)} %get-tuple-element.101.send_ref, bf16[512,1024]{1,0:T(8,128)(2,1)S(1)} %get-tuple-element.85.recv_ref, ...), custom_call_target="tpu_custom_call" | custom-call | flops 1610612736 | bytes 5505024 | tf_op jit(solution)/shard_map/local_backward/pallas_call | solution.py:63
  87.3 1.5 %collective-permute-start.30 = (bf16[512,128]{1,0:T(8,128)(2,1)S(1)}, bf16[512,128]{1,0:T(8,128)(2,1)S(1)}, u32[]{:S(2)}, u32[]{:S(2)}) collective-permute-start(bf16[512,128]{1,0:T(8,128)(2,1)S(1)} %get-tuple-element.110), channel_id=1, source_target_pairs={{0,2},{1,3},{2,0},{3,1},{4,6},{5,7},{6,4},{7,5},{8,10},{9,11},{10,... | collective-permute-start | bytes 393224 | tf_op jit(solution)/shard_map/ppermute | solution.py:84
  88.9 1.1 collective-permute-start.28
  90.1 3.7 %collective-permute-done.30.refs_1_ = bf16[512,128]{1,0:T(8,128)(2,1)S(1)} collective-permute-done((bf16[512,128]{1,0:T(8,128)(2,1)S(1)}, bf16[512,128]{1,0:T(8,128)(2,1)S(1)}, u32[]{:S(2)}, u32[]{:S(2)}) %collective-permute-start.30) | collective-permute-done | bytes 131104 | tf_op jit(solution)/shard_map/ppermute | solution.py:84
  94.0 1.8 %collective-permute-start.32 = (bf16[128,128]{1,0:T(8,128)(2,1)S(1)}, bf16[128,128]{1,0:T(8,128)(2,1)S(1)}, u32[]{:S(2)}, u32[]{:S(2)}) collective-permute-start(bf16[128,128]{1,0:T(8,128)(2,1)S(1)} %get-tuple-element.113), channel_id=1, source_target_pairs={{0,8},{4,12},{8,0},{12,4},{1,9},{5,13},{9,1},{13,5},{2,10},{6,14},... | collective-permute-start | bytes 98312 | tf_op jit(solution)/shard_map/ppermute | solution.py:87
  95.8 2.4 %collective-permute-start.33 = (bf16[128,128]{1,0:T(8,128)(2,1)S(1)}, bf16[128,128]{1,0:T(8,128)(2,1)S(1)}, u32[]{:S(2)}, u32[]{:S(2)}) collective-permute-start(bf16[128,128]{1,0:T(8,128)(2,1)S(1)} %get-tuple-element.114), channel_id=1, source_target_pairs={{0,12},{4,8},{8,4},{12,0},{1,13},{5,9},{9,5},{13,1},{2,14},{6,10},... | collective-permute-start | bytes 98312 | tf_op jit(solution)/shard_map/ppermute | solution.py:87
  98.9 2.6 %collective-permute-done.33.refs_5_ = bf16[128,128]{1,0:T(8,128)(2,1)S(1)} collective-permute-done((bf16[128,128]{1,0:T(8,128)(2,1)S(1)}, bf16[128,128]{1,0:T(8,128)(2,1)S(1)}, u32[]{:S(2)}, u32[]{:S(2)}) %collective-permute-start.33) | collective-permute-done | bytes 32800 | tf_op jit(solution)/shard_map/ppermute | solution.py:87
  101.5 1.2 owed_rows.1
  102.8 3.0 %collective-permute-start.38 = (bf16[256,128]{1,0:T(8,128)(2,1)S(1)}, bf16[256,128]{1,0:T(8,128)(2,1)S(1)}, u32[]{:S(2)}, u32[]{:S(2)}) collective-permute-start(bf16[256,128]{1,0:T(8,128)(2,1)S(1)} %get-tuple-element.121), channel_id=1, source_target_pairs={{0,8},{4,12},{8,0},{12,4},{1,9},{5,13},{9,1},{13,5},{2,10},{6,14},... | collective-permute-start | bytes 196616 | tf_op jit(solution)/shard_map/ppermute | solution.py:87
  105.8 1.4 %collective-permute-start.39 = (bf16[256,128]{1,0:T(8,128)(2,1)S(1)}, bf16[256,128]{1,0:T(8,128)(2,1)S(1)}, u32[]{:S(2)}, u32[]{:S(2)}) collective-permute-start(bf16[256,128]{1,0:T(8,128)(2,1)S(1)} %get-tuple-element.122), channel_id=1, source_target_pairs={{0,12},{4,8},{8,4},{12,0},{1,13},{5,9},{9,5},{13,1},{2,14},{6,10},... | collective-permute-start | bytes 196616 | tf_op jit(solution)/shard_map/ppermute | solution.py:87
  107.2 3.0 %collective-permute-start.35 = (bf16[256,128]{1,0:T(8,128)(2,1)S(1)}, bf16[256,128]{1,0:T(8,128)(2,1)S(1)}, u32[]{:S(2)}, u32[]{:S(2)}) collective-permute-start(bf16[256,128]{1,0:T(8,128)(2,1)S(1)} %get-tuple-element.117), channel_id=1, source_target_pairs={{0,8},{4,12},{8,0},{12,4},{1,9},{5,13},{9,1},{13,5},{2,10},{6,14},... | collective-permute-start | bytes 196616 | tf_op jit(solution)/shard_map/ppermute | solution.py:87
  110.2 1.4 %collective-permute-start.36 = (bf16[256,128]{1,0:T(8,128)(2,1)S(1)}, bf16[256,128]{1,0:T(8,128)(2,1)S(1)}, u32[]{:S(2)}, u32[]{:S(2)}) collective-permute-start(bf16[256,128]{1,0:T(8,128)(2,1)S(1)} %get-tuple-element.118), channel_id=1, source_target_pairs={{0,12},{4,8},{8,4},{12,0},{1,13},{5,9},{9,5},{13,1},{2,14},{6,10},... | collective-permute-start | bytes 196616 | tf_op jit(solution)/shard_map/ppermute | solution.py:87
  112.3 1.5 %collective-permute-start.41 = (bf16[256,128]{1,0:T(8,128)(2,1)S(1)}, bf16[256,128]{1,0:T(8,128)(2,1)S(1)}, u32[]{:S(2)}, u32[]{:S(2)}) collective-permute-start(bf16[256,128]{1,0:T(8,128)(2,1)S(1)} %get-tuple-element.123.refs_4_), channel_id=1, source_target_pairs={{0,2},{1,3},{2,0},{3,1},{4,6},{5,7},{6,4},{7,5},{8,10},{9,11},{10,... | collective-permute-start | bytes 196616 | tf_op jit(solution)/shard_map/ppermute | solution.py:84
  114.2 2.0 %collective-permute-done.36.refs_3_ = bf16[256,128]{1,0:T(8,128)(2,1)S(1)} collective-permute-done((bf16[256,128]{1,0:T(8,128)(2,1)S(1)}, bf16[256,128]{1,0:T(8,128)(2,1)S(1)}, u32[]{:S(2)}, u32[]{:S(2)}) %collective-permute-start.36) | collective-permute-done | bytes 65568 | tf_op jit(solution)/shard_map/ppermute | solution.py:87
  116.6 1.6 %collective-permute-start.42 = (bf16[256,128]{1,0:T(8,128)(2,1)S(1)}, bf16[256,128]{1,0:T(8,128)(2,1)S(1)}, u32[]{:S(2)}, u32[]{:S(2)}) collective-permute-start(bf16[256,128]{1,0:T(8,128)(2,1)S(1)} %get-tuple-element.126), channel_id=1, source_target_pairs={{0,3},{1,2},{2,1},{3,0},{4,7},{5,6},{6,5},{7,4},{8,11},{9,10},{10,... | collective-permute-start | bytes 196616 | tf_op jit(solution)/shard_map/ppermute | solution.py:84
  118.2 2.3 %collective-permute-done.42.refs_3_ = bf16[256,128]{1,0:T(8,128)(2,1)S(1)} collective-permute-done((bf16[256,128]{1,0:T(8,128)(2,1)S(1)}, bf16[256,128]{1,0:T(8,128)(2,1)S(1)}, u32[]{:S(2)}, u32[]{:S(2)}) %collective-permute-start.42) | collective-permute-done | bytes 65568 | tf_op jit(solution)/shard_map/ppermute | solution.py:84
  120.5 1.1 adjoint.1
  (72 shorter events, 10.4 us)
Async XLA Ops:
  0.0 10.3 %collective-permute-start.1 = (bf16[256,512]{1,0:T(8,128)(2,1)}, bf16[256,512]{1,0:T(8,128)(2,1)S(1)}, u32[]{:S(2)}, u32[]{:S(2)}) collective-permute-start(bf16[256,512]{1,0:T(8,128)(2,1)} %refs_0_.1), channel_id=1, source_target_pairs={{0,2},{1,3},{2,0},{3,1},{4,6},{5,7},{6,4},{7,5},{8,10},{9,11},{10,... | collective-permute-start | bytes 786440 | tf_op jit(solution)/shard_map/ppermute | solution.py:84
  4.5 32.1 %copy-start.2 = (bf16[512,512]{1,0:T(8,128)(2,1)S(1)}, bf16[512,512]{1,0:T(8,128)(2,1)}, u32[]{:S(2)}) copy-start(bf16[512,512]{1,0:T(8,128)(2,1)} %base_ref.1) | copy-start | bytes 1572868
  4.6 8.1 %collective-permute-start.4 = (bf16[144,512]{1,0:T(8,128)(2,1)S(1)}, bf16[144,512]{1,0:T(8,128)(2,1)S(1)}, u32[]{:S(2)}, u32[]{:S(2)}) collective-permute-start(bf16[144,512]{1,0:T(8,128)(2,1)S(1)} %get-tuple-element.66.refs_4_), channel_id=1, source_target_pairs={{0,2},{1,3},{2,0},{3,1},{4,6},{5,7},{6,4},{7,5},{8,10},{9,11},{10,... | collective-permute-start | bytes 442376 | tf_op jit(solution)/shard_map/ppermute | solution.py:84
  4.6 8.0 %collective-permute-start = (bf16[256,512]{1,0:T(8,128)(2,1)}, bf16[256,512]{1,0:T(8,128)(2,1)S(1)}, u32[]{:S(2)}, u32[]{:S(2)}) collective-permute-start(bf16[256,512]{1,0:T(8,128)(2,1)} %refs_0_.1), channel_id=1, source_target_pairs={{0,1},{1,0},{2,3},{3,2},{4,5},{5,4},{6,7},{7,6},{8,9},{9,8},{10,11... | collective-permute-start | bytes 786440 | tf_op jit(solution)/shard_map/ppermute | solution.py:84
  10.3 3.7 %collective-permute-start.2 = (bf16[256,512]{1,0:T(8,128)(2,1)S(1)}, bf16[256,512]{1,0:T(8,128)(2,1)S(1)}, u32[]{:S(2)}, u32[]{:S(2)}) collective-permute-start(bf16[256,512]{1,0:T(8,128)(2,1)S(1)} %collective-permute-done.1.refs_2_), channel_id=1, source_target_pairs={{0,1},{1,0},{2,3},{3,2},{4,5},{5,4},{6,7},{7,6},{8,9},{9,8},{10,11... | collective-permute-start | bytes 786440 | tf_op jit(solution)/shard_map/ppermute | solution.py:84
  10.3 2.3 %collective-permute-start.3 = (bf16[144,512]{1,0:T(8,128)(2,1)S(1)}, bf16[144,512]{1,0:T(8,128)(2,1)S(1)}, u32[]{:S(2)}, u32[]{:S(2)}) collective-permute-start(bf16[144,512]{1,0:T(8,128)(2,1)S(1)} %get-tuple-element.66.refs_4_), channel_id=1, source_target_pairs={{0,1},{1,0},{2,3},{3,2},{4,5},{5,4},{6,7},{7,6},{8,9},{9,8},{10,11... | collective-permute-start | bytes 442376 | tf_op jit(solution)/shard_map/ppermute | solution.py:84
  12.6 1.4 %collective-permute-start.5 = (bf16[144,512]{1,0:T(8,128)(2,1)S(1)}, bf16[144,512]{1,0:T(8,128)(2,1)S(1)}, u32[]{:S(2)}, u32[]{:S(2)}) collective-permute-start(bf16[144,512]{1,0:T(8,128)(2,1)S(1)} %collective-permute-done.4.refs_6_), channel_id=1, source_target_pairs={{0,1},{1,0},{2,3},{3,2},{4,5},{5,4},{6,7},{7,6},{8,9},{9,8},{10,11... | collective-permute-start | bytes 442376 | tf_op jit(solution)/shard_map/ppermute | solution.py:84
  16.5 0.7 copy-start.3
  20.4 27.2 %collective-permute-start.12 = (bf16[512,512]{1,0:T(8,128)(2,1)S(1)}, bf16[512,512]{1,0:T(8,128)(2,1)S(1)}, u32[]{:S(2)}, u32[]{:S(2)}) collective-permute-start(bf16[512,512]{1,0:T(8,128)(2,1)S(1)} %relay.1.refs_0_), channel_id=1, source_target_pairs={{0,2},{1,3},{2,0},{3,1},{4,6},{5,7},{6,4},{7,5},{8,10},{9,11},{10,... | collective-permute-start | bytes 1572872 | tf_op jit(solution)/shard_map/ppermute | solution.py:84
  22.2 6.9 %collective-permute-start.6 = (bf16[512,128]{1,0:T(8,128)(2,1)S(1)}, bf16[512,128]{1,0:T(8,128)(2,1)S(1)}, u32[]{:S(2)}, u32[]{:S(2)}) collective-permute-start(bf16[512,128]{1,0:T(8,128)(2,1)S(1)} %get-tuple-element.75), channel_id=1, source_target_pairs={{0,4},{4,0},{8,12},{12,8},{1,5},{5,1},{9,13},{13,9},{2,6},{6,2},{1... | collective-permute-start | bytes 393224 | tf_op jit(solution)/shard_map/ppermute | solution.py:87
  23.7 12.9 %collective-permute-start.7 = (bf16[512,128]{1,0:T(8,128)(2,1)S(1)}, bf16[512,128]{1,0:T(8,128)(2,1)S(1)}, u32[]{:S(2)}, u32[]{:S(2)}) collective-permute-start(bf16[512,128]{1,0:T(8,128)(2,1)S(1)} %get-tuple-element.76), channel_id=1, source_target_pairs={{0,8},{4,12},{8,0},{12,4},{1,9},{5,13},{9,1},{13,5},{2,10},{6,14},... | collective-permute-start | bytes 393224 | tf_op jit(solution)/shard_map/ppermute | solution.py:87
  26.3 10.3 %collective-permute-start.8 = (bf16[512,128]{1,0:T(8,128)(2,1)S(1)}, bf16[512,128]{1,0:T(8,128)(2,1)S(1)}, u32[]{:S(2)}, u32[]{:S(2)}) collective-permute-start(bf16[512,128]{1,0:T(8,128)(2,1)S(1)} %get-tuple-element.77), channel_id=1, source_target_pairs={{0,12},{4,8},{8,4},{12,0},{1,13},{5,9},{9,5},{13,1},{2,14},{6,10},... | collective-permute-start | bytes 393224 | tf_op jit(solution)/shard_map/ppermute | solution.py:87
  36.7 19.4 %copy-start.4 = (bf16[1024,512]{1,0:T(8,128)(2,1)S(1)}, bf16[1024,512]{1,0:T(8,128)(2,1)}, u32[]{:S(2)}) copy-start(bf16[1024,512]{1,0:T(8,128)(2,1)} %es_ref.3) | copy-start | bytes 3145732
  37.5 10.0 %collective-permute-start.10 = (bf16[512,128]{1,0:T(8,128)(2,1)S(1)}, bf16[512,128]{1,0:T(8,128)(2,1)S(1)}, u32[]{:S(2)}, u32[]{:S(2)}) collective-permute-start(bf16[512,128]{1,0:T(8,128)(2,1)S(1)} %encode.1.state_ref.refs_0_), channel_id=1, source_target_pairs={{0,2},{1,3},{2,0},{3,1},{4,6},{5,7},{6,4},{7,5},{8,10},{9,11},{10,... | collective-permute-start | bytes 393224 | tf_op jit(solution)/shard_map/ppermute | solution.py:84
  38.7 4.5 %collective-permute-start.13 = (bf16[128,128]{1,0:T(8,128)(2,1)S(1)}, bf16[128,128]{1,0:T(8,128)(2,1)S(1)}, u32[]{:S(2)}, u32[]{:S(2)}) collective-permute-start(bf16[128,128]{1,0:T(8,128)(2,1)S(1)} %get-tuple-element.79), channel_id=1, source_target_pairs={{0,4},{4,0},{8,12},{12,8},{1,5},{5,1},{9,13},{13,9},{2,6},{6,2},{1... | collective-permute-start | bytes 98312 | tf_op jit(solution)/shard_map/ppermute | solution.py:87
  40.8 5.2 %collective-permute-start.14 = (bf16[128,128]{1,0:T(8,128)(2,1)S(1)}, bf16[128,128]{1,0:T(8,128)(2,1)S(1)}, u32[]{:S(2)}, u32[]{:S(2)}) collective-permute-start(bf16[128,128]{1,0:T(8,128)(2,1)S(1)} %get-tuple-element.80), channel_id=1, source_target_pairs={{0,8},{4,12},{8,0},{12,4},{1,9},{5,13},{9,1},{13,5},{2,10},{6,14},... | collective-permute-start | bytes 98312 | tf_op jit(solution)/shard_map/ppermute | solution.py:87
  41.8 5.7 %collective-permute-start.15 = (bf16[128,128]{1,0:T(8,128)(2,1)S(1)}, bf16[128,128]{1,0:T(8,128)(2,1)S(1)}, u32[]{:S(2)}, u32[]{:S(2)}) collective-permute-start(bf16[128,128]{1,0:T(8,128)(2,1)S(1)} %get-tuple-element.81), channel_id=1, source_target_pairs={{0,12},{4,8},{8,4},{12,0},{1,13},{5,9},{9,5},{13,1},{2,14},{6,10},... | collective-permute-start | bytes 98312 | tf_op jit(solution)/shard_map/ppermute | solution.py:87
  48.6 7.5 %collective-permute-start.16 = (bf16[2,512,512]{2,1,0:T(8,128)(2,1)S(1)}, bf16[2,512,512]{2,1,0:T(8,128)(2,1)S(1)}, u32[]{:S(2)}, u32[]{:S(2)}) collective-permute-start(bf16[2,512,512]{2,1,0:T(8,128)(2,1)S(1)} %get-tuple-element.82.refs_4_), channel_id=1, source_target_pairs={{0,1},{1,0},{2,3},{3,2},{4,5},{5,4},{6,7},{7,6},{8,9},{9,8},{10,11... | collective-permute-start | bytes 3145736 | tf_op jit(solution)/shard_map/ppermute | solution.py:84
  48.7 5.9 %collective-permute-start.18 = (bf16[512,128]{1,0:T(8,128)(2,1)S(1)}, bf16[512,128]{1,0:T(8,128)(2,1)S(1)}, u32[]{:S(2)}, u32[]{:S(2)}) collective-permute-start(bf16[512,128]{1,0:T(8,128)(2,1)S(1)} %halo_join.1.refs_2_.refs_0_), channel_id=1, source_target_pairs={{0,2},{1,3},{2,0},{3,1},{4,6},{5,7},{6,4},{7,5},{8,10},{9,11},{10,... | collective-permute-start | bytes 393224 | tf_op jit(solution)/shard_map/ppermute | solution.py:84
  50.2 4.4 %collective-permute-start.9 = (bf16[512,128]{1,0:T(8,128)(2,1)S(1)}, bf16[512,128]{1,0:T(8,128)(2,1)S(1)}, u32[]{:S(2)}, u32[]{:S(2)}) collective-permute-start(bf16[512,128]{1,0:T(8,128)(2,1)S(1)} %encode.1.state_ref.refs_0_), channel_id=1, source_target_pairs={{0,1},{1,0},{2,3},{3,2},{4,5},{5,4},{6,7},{7,6},{8,9},{9,8},{10,11... | collective-permute-start | bytes 393224 | tf_op jit(solution)/shard_map/ppermute | solution.py:84
  50.4 5.7 %collective-permute-start.11 = (bf16[512,128]{1,0:T(8,128)(2,1)S(1)}, bf16[512,128]{1,0:T(8,128)(2,1)S(1)}, u32[]{:S(2)}, u32[]{:S(2)}) collective-permute-start(bf16[512,128]{1,0:T(8,128)(2,1)S(1)} %collective-permute-done.10.refs_4_.refs_2_), channel_id=1, source_target_pairs={{0,1},{1,0},{2,3},{3,2},{4,5},{5,4},{6,7},{7,6},{8,9},{9,8},{10,11... | collective-permute-start | bytes 393224 | tf_op jit(solution)/shard_map/ppermute | solution.py:84
  50.7 8.4 %collective-permute-start.17 = (bf16[512,128]{1,0:T(8,128)(2,1)S(1)}, bf16[512,128]{1,0:T(8,128)(2,1)S(1)}, u32[]{:S(2)}, u32[]{:S(2)}) collective-permute-start(bf16[512,128]{1,0:T(8,128)(2,1)S(1)} %halo_join.1.refs_2_.refs_0_), channel_id=1, source_target_pairs={{0,1},{1,0},{2,3},{3,2},{4,5},{5,4},{6,7},{7,6},{8,9},{9,8},{10,11... | collective-permute-start | bytes 393224 | tf_op jit(solution)/shard_map/ppermute | solution.py:84
  54.6 4.5 %collective-permute-start.19 = (bf16[512,128]{1,0:T(8,128)(2,1)S(1)}, bf16[512,128]{1,0:T(8,128)(2,1)S(1)}, u32[]{:S(2)}, u32[]{:S(2)}) collective-permute-start(bf16[512,128]{1,0:T(8,128)(2,1)S(1)} %collective-permute-done.18.refs_2_), channel_id=1, source_target_pairs={{0,1},{1,0},{2,3},{3,2},{4,5},{5,4},{6,7},{7,6},{8,9},{9,8},{10,11... | collective-permute-start | bytes 393224 | tf_op jit(solution)/shard_map/ppermute | solution.py:84
  54.6 11.5 %collective-permute-start.20 = (bf16[384,512]{1,0:T(8,128)(2,1)S(1)}, bf16[384,512]{1,0:T(8,128)(2,1)S(1)}, u32[]{:S(2)}, u32[]{:S(2)}) collective-permute-start(bf16[384,512]{1,0:T(8,128)(2,1)S(1)} %get-tuple-element.91.refs_0_), channel_id=1, source_target_pairs={{0,2},{1,3},{2,0},{3,1},{4,6},{5,7},{6,4},{7,5},{8,10},{9,11},{10,... | collective-permute-start | bytes 1179656 | tf_op jit(solution)/shard_map/ppermute | solution.py:84
  62.2 8.3 %copy-start = (bf16[512,512]{1,0:T(8,128)(2,1)S(1)}, bf16[512,512]{1,0:T(8,128)(2,1)}, u32[]{:S(2)}) copy-start(bf16[512,512]{1,0:T(8,128)(2,1)} %grad_ref.4) | copy-start | bytes 1572868
  66.2 4.3 %collective-permute-start.21 = (bf16[2,384,512]{2,1,0:T(8,128)(2,1)S(1)}, bf16[2,384,512]{2,1,0:T(8,128)(2,1)S(1)}, u32[]{:S(2)}, u32[]{:S(2)}) collective-permute-start(bf16[2,384,512]{2,1,0:T(8,128)(2,1)S(1)} %join_node_weights.1.refs_0_), channel_id=1, source_target_pairs={{0,1},{1,0},{2,3},{3,2},{4,5},{5,4},{6,7},{7,6},{8,9},{9,8},{10,11... | collective-permute-start | bytes 2359304 | tf_op jit(solution)/shard_map/ppermute | solution.py:84
  66.3 2.6 %collective-permute-start.22 = (bf16[2,128,512]{2,1,0:T(8,128)(2,1)S(1)}, bf16[2,128,512]{2,1,0:T(8,128)(2,1)S(1)}, u32[]{:S(2)}, u32[]{:S(2)}) collective-permute-start(bf16[2,128,512]{2,1,0:T(8,128)(2,1)S(1)} %get-tuple-element.96), channel_id=1, source_target_pairs={{0,1},{1,0},{2,3},{3,2},{4,5},{5,4},{6,7},{7,6},{8,9},{9,8},{10,11... | collective-permute-start | bytes 786440 | tf_op jit(solution)/shard_map/ppermute | solution.py:84
  69.0 5.6 %collective-permute-start.23 = (bf16[128,512]{1,0:T(8,128)(2,1)S(1)}, bf16[128,512]{1,0:T(8,128)(2,1)S(1)}, u32[]{:S(2)}, u32[]{:S(2)}) collective-permute-start(bf16[128,512]{1,0:T(8,128)(2,1)S(1)} %get-tuple-element.98), channel_id=1, source_target_pairs={{0,2},{1,3},{2,0},{3,1},{4,6},{5,7},{6,4},{7,5},{8,10},{9,11},{10,... | collective-permute-start | bytes 393224 | tf_op jit(solution)/shard_map/ppermute | solution.py:84
  70.5 11.1 %copy-start.1 = (bf16[1024,512]{1,0:T(8,128)(2,1)S(1)}, bf16[1024,512]{1,0:T(8,128)(2,1)}, u32[]{:S(2)}) copy-start(bf16[1024,512]{1,0:T(8,128)(2,1)} %grad_ref.5) | copy-start | bytes 3145732
  75.2 5.0 %collective-permute-start.25 = (bf16[128,512]{1,0:T(8,128)(2,1)S(1)}, bf16[128,512]{1,0:T(8,128)(2,1)S(1)}, u32[]{:S(2)}, u32[]{:S(2)}) collective-permute-start(bf16[128,512]{1,0:T(8,128)(2,1)S(1)} %get-tuple-element.99.refs_0_), channel_id=1, source_target_pairs={{0,2},{1,3},{2,0},{3,1},{4,6},{5,7},{6,4},{7,5},{8,10},{9,11},{10,... | collective-permute-start | bytes 393224 | tf_op jit(solution)/shard_map/ppermute | solution.py:84
  76.8 3.5 %collective-permute-start.24 = (bf16[128,512]{1,0:T(8,128)(2,1)S(1)}, bf16[128,512]{1,0:T(8,128)(2,1)S(1)}, u32[]{:S(2)}, u32[]{:S(2)}) collective-permute-start(bf16[128,512]{1,0:T(8,128)(2,1)S(1)} %get-tuple-element.99.refs_0_), channel_id=1, source_target_pairs={{0,1},{1,0},{2,3},{3,2},{4,5},{5,4},{6,7},{7,6},{8,9},{9,8},{10,11... | collective-permute-start | bytes 393224 | tf_op jit(solution)/shard_map/ppermute | solution.py:84
  80.3 1.3 %collective-permute-start.26 = (bf16[128,512]{1,0:T(8,128)(2,1)S(1)}, bf16[128,512]{1,0:T(8,128)(2,1)S(1)}, u32[]{:S(2)}, u32[]{:S(2)}) collective-permute-start(bf16[128,512]{1,0:T(8,128)(2,1)S(1)} %collective-permute-done.25.refs_2_), channel_id=1, source_target_pairs={{0,1},{1,0},{2,3},{3,2},{4,5},{5,4},{6,7},{7,6},{8,9},{9,8},{10,11... | collective-permute-start | bytes 393224 | tf_op jit(solution)/shard_map/ppermute | solution.py:84
  84.5 2.7 %collective-permute-start.29 = (bf16[2,512,128]{2,1,0:T(8,128)(2,1)S(1)}, bf16[2,512,128]{2,1,0:T(8,128)(2,1)S(1)}, u32[]{:S(2)}, u32[]{:S(2)}) collective-permute-start(bf16[2,512,128]{2,1,0:T(8,128)(2,1)S(1)} %get-tuple-element.108), channel_id=1, source_target_pairs={{0,1},{1,0},{2,3},{3,2},{4,5},{5,4},{6,7},{7,6},{8,9},{9,8},{10,11... | collective-permute-start | bytes 786440 | tf_op jit(solution)/shard_map/ppermute | solution.py:84
  86.8 2.0 %collective-permute-start.27 = (bf16[2,512,128]{2,1,0:T(8,128)(2,1)S(1)}, bf16[2,512,128]{2,1,0:T(8,128)(2,1)S(1)}, u32[]{:S(2)}, u32[]{:S(2)}) collective-permute-start(bf16[2,512,128]{2,1,0:T(8,128)(2,1)S(1)} %get-tuple-element.104), channel_id=1, source_target_pairs={{0,1},{1,0},{2,3},{3,2},{4,5},{5,4},{6,7},{7,6},{8,9},{9,8},{10,11... | collective-permute-start | bytes 786440 | tf_op jit(solution)/shard_map/ppermute | solution.py:84
  87.3 6.4 %collective-permute-start.30 = (bf16[512,128]{1,0:T(8,128)(2,1)S(1)}, bf16[512,128]{1,0:T(8,128)(2,1)S(1)}, u32[]{:S(2)}, u32[]{:S(2)}) collective-permute-start(bf16[512,128]{1,0:T(8,128)(2,1)S(1)} %get-tuple-element.110), channel_id=1, source_target_pairs={{0,2},{1,3},{2,0},{3,1},{4,6},{5,7},{6,4},{7,5},{8,10},{9,11},{10,... | collective-permute-start | bytes 393224 | tf_op jit(solution)/shard_map/ppermute | solution.py:84
  88.9 9.3 %collective-permute-start.28 = (bf16[512,128]{1,0:T(8,128)(2,1)S(1)}, bf16[512,128]{1,0:T(8,128)(2,1)S(1)}, u32[]{:S(2)}, u32[]{:S(2)}) collective-permute-start(bf16[512,128]{1,0:T(8,128)(2,1)S(1)} %get-tuple-element.106), channel_id=1, source_target_pairs={{0,2},{1,3},{2,0},{3,1},{4,6},{5,7},{6,4},{7,5},{8,10},{9,11},{10,... | collective-permute-start | bytes 393224 | tf_op jit(solution)/shard_map/ppermute | solution.py:84
  93.8 4.5 %collective-permute-start.31 = (bf16[128,128]{1,0:T(8,128)(2,1)S(1)}, bf16[128,128]{1,0:T(8,128)(2,1)S(1)}, u32[]{:S(2)}, u32[]{:S(2)}) collective-permute-start(bf16[128,128]{1,0:T(8,128)(2,1)S(1)} %get-tuple-element.112), channel_id=1, source_target_pairs={{0,4},{4,0},{8,12},{12,8},{1,5},{5,1},{9,13},{13,9},{2,6},{6,2},{1... | collective-permute-start | bytes 98312 | tf_op jit(solution)/shard_map/ppermute | solution.py:87
  94.0 4.9 %collective-permute-start.32 = (bf16[128,128]{1,0:T(8,128)(2,1)S(1)}, bf16[128,128]{1,0:T(8,128)(2,1)S(1)}, u32[]{:S(2)}, u32[]{:S(2)}) collective-permute-start(bf16[128,128]{1,0:T(8,128)(2,1)S(1)} %get-tuple-element.113), channel_id=1, source_target_pairs={{0,8},{4,12},{8,0},{12,4},{1,9},{5,13},{9,1},{13,5},{2,10},{6,14},... | collective-permute-start | bytes 98312 | tf_op jit(solution)/shard_map/ppermute | solution.py:87
  95.8 5.7 %collective-permute-start.33 = (bf16[128,128]{1,0:T(8,128)(2,1)S(1)}, bf16[128,128]{1,0:T(8,128)(2,1)S(1)}, u32[]{:S(2)}, u32[]{:S(2)}) collective-permute-start(bf16[128,128]{1,0:T(8,128)(2,1)S(1)} %get-tuple-element.114), channel_id=1, source_target_pairs={{0,12},{4,8},{8,4},{12,0},{1,13},{5,9},{9,5},{13,1},{2,14},{6,10},... | collective-permute-start | bytes 98312 | tf_op jit(solution)/shard_map/ppermute | solution.py:87
  102.7 7.5 %collective-permute-start.37 = (bf16[256,128]{1,0:T(8,128)(2,1)S(1)}, bf16[256,128]{1,0:T(8,128)(2,1)S(1)}, u32[]{:S(2)}, u32[]{:S(2)}) collective-permute-start(bf16[256,128]{1,0:T(8,128)(2,1)S(1)} %get-tuple-element.120), channel_id=1, source_target_pairs={{0,4},{4,0},{8,12},{12,8},{1,5},{5,1},{9,13},{13,9},{2,6},{6,2},{1... | collective-permute-start | bytes 196616 | tf_op jit(solution)/shard_map/ppermute | solution.py:87
  102.8 8.8 %collective-permute-start.38 = (bf16[256,128]{1,0:T(8,128)(2,1)S(1)}, bf16[256,128]{1,0:T(8,128)(2,1)S(1)}, u32[]{:S(2)}, u32[]{:S(2)}) collective-permute-start(bf16[256,128]{1,0:T(8,128)(2,1)S(1)} %get-tuple-element.121), channel_id=1, source_target_pairs={{0,8},{4,12},{8,0},{12,4},{1,9},{5,13},{9,1},{13,5},{2,10},{6,14},... | collective-permute-start | bytes 196616 | tf_op jit(solution)/shard_map/ppermute | solution.py:87
  105.8 6.2 %collective-permute-start.39 = (bf16[256,128]{1,0:T(8,128)(2,1)S(1)}, bf16[256,128]{1,0:T(8,128)(2,1)S(1)}, u32[]{:S(2)}, u32[]{:S(2)}) collective-permute-start(bf16[256,128]{1,0:T(8,128)(2,1)S(1)} %get-tuple-element.122), channel_id=1, source_target_pairs={{0,12},{4,8},{8,4},{12,0},{1,13},{5,9},{9,5},{13,1},{2,14},{6,10},... | collective-permute-start | bytes 196616 | tf_op jit(solution)/shard_map/ppermute | solution.py:87
  107.2 6.7 %collective-permute-start.34 = (bf16[256,128]{1,0:T(8,128)(2,1)S(1)}, bf16[256,128]{1,0:T(8,128)(2,1)S(1)}, u32[]{:S(2)}, u32[]{:S(2)}) collective-permute-start(bf16[256,128]{1,0:T(8,128)(2,1)S(1)} %get-tuple-element.116), channel_id=1, source_target_pairs={{0,4},{4,0},{8,12},{12,8},{1,5},{5,1},{9,13},{13,9},{2,6},{6,2},{1... | collective-permute-start | bytes 196616 | tf_op jit(solution)/shard_map/ppermute | solution.py:87
  107.2 7.0 %collective-permute-start.35 = (bf16[256,128]{1,0:T(8,128)(2,1)S(1)}, bf16[256,128]{1,0:T(8,128)(2,1)S(1)}, u32[]{:S(2)}, u32[]{:S(2)}) collective-permute-start(bf16[256,128]{1,0:T(8,128)(2,1)S(1)} %get-tuple-element.117), channel_id=1, source_target_pairs={{0,8},{4,12},{8,0},{12,4},{1,9},{5,13},{9,1},{13,5},{2,10},{6,14},... | collective-permute-start | bytes 196616 | tf_op jit(solution)/shard_map/ppermute | solution.py:87
  110.2 6.1 %collective-permute-start.36 = (bf16[256,128]{1,0:T(8,128)(2,1)S(1)}, bf16[256,128]{1,0:T(8,128)(2,1)S(1)}, u32[]{:S(2)}, u32[]{:S(2)}) collective-permute-start(bf16[256,128]{1,0:T(8,128)(2,1)S(1)} %get-tuple-element.118), channel_id=1, source_target_pairs={{0,12},{4,8},{8,4},{12,0},{1,13},{5,9},{9,5},{13,1},{2,14},{6,10},... | collective-permute-start | bytes 196616 | tf_op jit(solution)/shard_map/ppermute | solution.py:87
  112.3 6.0 %collective-permute-start.41 = (bf16[256,128]{1,0:T(8,128)(2,1)S(1)}, bf16[256,128]{1,0:T(8,128)(2,1)S(1)}, u32[]{:S(2)}, u32[]{:S(2)}) collective-permute-start(bf16[256,128]{1,0:T(8,128)(2,1)S(1)} %get-tuple-element.123.refs_4_), channel_id=1, source_target_pairs={{0,2},{1,3},{2,0},{3,1},{4,6},{5,7},{6,4},{7,5},{8,10},{9,11},{10,... | collective-permute-start | bytes 196616 | tf_op jit(solution)/shard_map/ppermute | solution.py:84
  116.5 1.7 %collective-permute-start.40 = (bf16[256,128]{1,0:T(8,128)(2,1)S(1)}, bf16[256,128]{1,0:T(8,128)(2,1)S(1)}, u32[]{:S(2)}, u32[]{:S(2)}) collective-permute-start(bf16[256,128]{1,0:T(8,128)(2,1)S(1)} %get-tuple-element.125), channel_id=1, source_target_pairs={{0,1},{1,0},{2,3},{3,2},{4,5},{5,4},{6,7},{7,6},{8,9},{9,8},{10,11... | collective-permute-start | bytes 196616 | tf_op jit(solution)/shard_map/ppermute | solution.py:84
  116.6 3.9 %collective-permute-start.42 = (bf16[256,128]{1,0:T(8,128)(2,1)S(1)}, bf16[256,128]{1,0:T(8,128)(2,1)S(1)}, u32[]{:S(2)}, u32[]{:S(2)}) collective-permute-start(bf16[256,128]{1,0:T(8,128)(2,1)S(1)} %get-tuple-element.126), channel_id=1, source_target_pairs={{0,3},{1,2},{2,1},{3,0},{4,7},{5,6},{6,5},{7,4},{8,11},{9,10},{10,... | collective-permute-start | bytes 196616 | tf_op jit(solution)/shard_map/ppermute | solution.py:84

commit v6 on v5

--- a/solution.py
+++ b/solution.py
@@ -60,7 +60,7 @@
 def call(body, name, me, ins, outs, scratch=(), flops=0, far=(), unread=()):
     size = lambda s: s.size * s.dtype.itemsize
     moved = sum(size(x) for x in ins) + sum(size(x) for x in outs)
-    return pl.pallas_call(
+    result = pl.pallas_call(
         body,
         out_shape=list(outs),
         in_specs=[SMEM] + [HBM if i in far else ANY if i in unread else VMEM for i in range(len(ins))],
@@ -70,6 +70,7 @@
         cost_estimate=pl.CostEstimate(flops=flops, bytes_accessed=moved, transcendentals=0),
         name=name,
     )(me, *[pltpu.with_memory_space_constraint(x, pltpu.HBM) if i in far else x for i, x in enumerate(ins)])
+    return list(result)
 
 
 def shape(dims, dtype=BF):
@@ -205,13 +206,44 @@
         state_parts = member_gather_chips(grid_state)
         pack_parts = member_gather_chips(pack)
 
+        def hots_kernel(me_ref, send_ref, recv_ref, sl_out, sh_out, r_out, slt_out, sht_out, rt_out):
+            for i in range(E // T):
+                at = slice(i * T, (i + 1) * T)
+                sent, got = send_ref[:, at], recv_ref[:, at]
+                sl_out[at, :] = hot_rows(sent, N)
+                sh_out[at, :] = hot_rows(sent - N, NH)
+                r_out[at, :] = hot_rows(got, N)
+                slt_out[:, at] = hot_columns(sent, N)
+                sht_out[:, at] = hot_columns(sent - N, NH)
+                rt_out[:, at] = hot_columns(got, N)
+
+        sl_hot, sh_hot, r_hot, slt_hot, sht_hot, rt_hot = call(
+            hots_kernel,
+            "edge_hots",
+            me1,
+            [send_row, recv_row],
+            [shape((E, N)), shape((E, NH)), shape((E, N)), shape((N, E)), shape((NH, E)), shape((N, E))],
+        )
+
+        firsts = [kf * n_rep for kf in range(1, n_feat)]
+
+        def stacked(pairs, out, sems):
+            copies, at = [], 0
+            for i, ref in enumerate(pairs):
+                copies.append(pltpu.make_async_copy(ref, out.at[at : at + ref.shape[0], :], sems.at[i]))
+                at += ref.shape[0]
+            return copies
+
         def grid_kernel(me_ref, *refs):
             states, packs = refs[:M], refs[M : 2 * M]
-            enc_out, slope_out, table_out = refs[2 * M : 2 * M + 3]
-            outs, (own, sem) = refs[2 * M + 3 : 2 * M + 3 + n_dom], refs[2 * M + 3 + n_dom :]
+            enc_out, slope_out, table_out, edge_out = refs[2 * M + 3 : 2 * M + 7]
+            outs, (own, sem, sems) = refs[2 * M + 7 : 2 * M + 7 + n_dom], refs[2 * M + 7 + n_dom :]
             me = me_ref[0]
             copy = pltpu.make_async_copy(states[0], own, sem)
             copy.start()
+            weight_copies = stacked(refs[2 * M : 2 * M + 2], edge_out, sems)
+            for each in weight_copies:
+                each.start()
             for k in range(M):
                 enc_out[rows_at(me ^ k, rows_enc), :] = packs[k][:rows_enc, :]
                 rows = packs[k][rows_enc:, :].astype(F32).astype(jnp.int32)
@@ -228,61 +260,23 @@
                 rows = dot(hot_rows(table_out[k, 0:1, :], G), message).astype(BF)
                 for j in range(n_dom):
                     outs[j][k * S : (k + 1) * S, :] = rows[j * S : (j + 1) * S]
-
-        enc_full, grid_slope, slots, *outgoing = call(
+            for each in weight_copies:
+                each.wait()
+
+        enc_full, grid_slope, slots, edge_own, *outgoing = call(
             grid_kernel,
             "grid_messages",
             me1,
-            state_parts + pack_parts,
-            [shape((D, D)), shape((M, G, C), F32), shape((M, 2, NS), jnp.int32)]
+            state_parts + pack_parts + [edge_in_weight, edge_out_weight, sl_hot],
+            [shape((D, D)), shape((M, G, C), F32), shape((M, 2, NS), jnp.int32), shape((rows_in + rows_out, D))]
             + [shape((M * S, C))] * n_dom,
-            scratch=[pltpu.VMEM((G, D), BF), pltpu.SemaphoreType.DMA(())],
+            scratch=[pltpu.VMEM((G, D), BF), pltpu.SemaphoreType.DMA(()), pltpu.SemaphoreType.DMA((2,))],
             flops=2 * M * G * D * C + 2 * M * NS * G * C,
-            far=(0,),
+            far=(0, 2 * M, 2 * M + 1),
+            unread=(2 * M + 2,),
         )
         incoming = dom_trade(outgoing)
         near, others = range(n_rep), range(n_rep, M)
-
-        def hots_kernel(me_ref, send_ref, recv_ref, after_ref, sl_out, sh_out, r_out, slt_out, sht_out, rt_out):
-            for i in range(E // T):
-                at = slice(i * T, (i + 1) * T)
-                sent, got = send_ref[:, at], recv_ref[:, at]
-                sl_out[at, :] = hot_rows(sent, N)
-                sh_out[at, :] = hot_rows(sent - N, NH)
-                r_out[at, :] = hot_rows(got, N)
-                slt_out[:, at] = hot_columns(sent, N)
-                sht_out[:, at] = hot_columns(sent - N, NH)
-                rt_out[:, at] = hot_columns(got, N)
-
-        sl_hot, sh_hot, r_hot, slt_hot, sht_hot, rt_hot = call(
-            hots_kernel,
-            "edge_hots",
-            me1,
-            [send_row, recv_row, grid_slope],
-            [shape((E, N)), shape((E, NH)), shape((E, N)), shape((N, E)), shape((NH, E)), shape((N, E))],
-            unread=(2,),
-        )
-
-        firsts = [kf * n_rep for kf in range(1, n_feat)]
-
-        def relay_kernel(me_ref, in_ref, out_ref, after_ref, edge_out, sems):
-            pairs = [(in_ref, edge_out.at[:rows_in, :]), (out_ref, edge_out.at[rows_in:, :])]
-            copies = [pltpu.make_async_copy(a, b, sems.at[i]) for i, (a, b) in enumerate(pairs)]
-            for copy in copies:
-                copy.start()
-            for copy in copies:
-                copy.wait()
-
-        edge_own = call(
-            relay_kernel,
-            "relay",
-            me1,
-            [edge_in_weight, edge_out_weight, sl_hot],
-            [shape((rows_in + rows_out, D))],
-            scratch=[pltpu.SemaphoreType.DMA((2,))],
-            far=range(2),
-            unread=(2,),
-        )[0]
         edge_chips = [edge_own] + [member_swap(edge_own, k) for k in firsts]
 
         def encode_kernel(me_ref, base_ref, table_ref, *refs):
@@ -297,12 +291,11 @@
             encode_kernel,
             "encode",
             me1,
-            [mesh_base, slots] + incoming + [sl_hot],
+            [mesh_base, slots] + incoming,
             [shape((N, C))],
             flops=2 * M * N * NS * C,
-            unread=(2 + n_dom,),
         )[0]
-        state_parts2 = member_gather_chips(state_cols)
+        state_chips = [state_cols] + [member_swap(state_cols, k) for k in firsts]
 
         def halo_kernel(me_ref, state_ref, halo_ref, *outs):
             rows = dot(hot_rows(halo_ref[...], N), state_ref[...]).astype(BF)
@@ -318,53 +311,42 @@
             flops=2 * N * NH * C,
         )
         halo_in = dom_trade(halo_out)
+        core_swaps = lambda x: [x] + [member_swap(x, kr) for kr in range(1, n_rep)]
+
+        def pair_kernel(me_ref, *refs):
+            for kf in range(n_feat):
+                refs[-1][kf] = refs[kf][...]
 
         def join_kernel(me_ref, *refs):
+            halo, chips, weights = refs[:n_dom], refs[n_dom : n_dom + n_feat], refs[n_dom + n_feat : -3]
+            halo_out_ref, pair_out, weights_out = refs[-3:]
             for j in range(n_dom):
-                refs[-1][j * H : (j + 1) * H, :] = refs[j][...]
-
-        halo_cols = call(
+                halo_out_ref[j * H : (j + 1) * H, :] = halo[j][...]
+            for kf in range(n_feat):
+                pair_out[kf] = chips[kf][...]
+                weights_out[kf] = weights[kf][...]
+
+        halo_cols, state_pair, edge_pair = call(
             join_kernel,
             "halo_join",
             me1,
-            halo_in + [state_parts2[n_rep]],
-            [shape((NH, C))],
-            unread=(n_dom,),
-        )[0]
-        halo_parts = member_gather_chips(halo_cols)
-
-        def weights_kernel(me_ref, in_ref, out_ref, *refs):
-            chips, (pair_out, node_out, sems) = refs[:n_feat], refs[-3:]
-            pairs = [(in_ref, node_out.at[:rows_node, :]), (out_ref, node_out.at[rows_node:, :])]
-            copies = [pltpu.make_async_copy(a, b, sems.at[i]) for i, (a, b) in enumerate(pairs)]
+            halo_in + state_chips + edge_chips,
+            [shape((NH, C)), shape((n_feat, N, C)), shape((n_feat, rows_in + rows_out, D))],
+        )
+        halo_chips = [halo_cols] + [member_swap(halo_cols, k) for k in firsts]
+        state_pairs = core_swaps(state_pair)
+        edge_pairs = core_swaps(edge_pair)
+
+        def local_kernel(me_ref, in_ref, out_ref, es_ref, send_ref, recv_ref, *refs):
+            cols, weights = refs[:n_rep], refs[n_rep : 2 * n_rep]
+            pre_out, state_out, w_out, out_out, node_out, parts, sems = refs[2 * n_rep :]
+            copies = stacked([in_ref, out_ref], node_out, sems)
             for copy in copies:
                 copy.start()
-            for kf in range(n_feat):
-                pair_out[kf] = chips[kf][...]
-            for copy in copies:
-                copy.wait()
-
-        edge_pair, node_own = call(
-            weights_kernel,
-            "join_weights",
-            me1,
-            [node_in_weight, node_out_weight] + edge_chips + [halo_cols],
-            [shape((n_feat, rows_in + rows_out, D)), shape((rows_node + rows_out, D))],
-            scratch=[pltpu.SemaphoreType.DMA((2,))],
-            far=range(2),
-            unread=(2 + n_feat,),
-        )
-        edge_pairs = [edge_pair] + [member_swap(edge_pair, kr) for kr in range(1, n_rep)]
-        node_chips = [node_own] + [member_swap(node_own, k) for k in firsts]
-
-
-        def local_kernel(me_ref, es_ref, send_ref, recv_ref, *refs):
-            cols, weights = refs[:M], refs[M : M + n_rep]
-            pre_out, state_out, w_out, out_out, parts = refs[M + n_rep :]
             me = me_ref[0]
             for k in range(M):
                 kf, kr = divmod(k, n_rep)
-                parts[me ^ k] = cols[k][...]
+                parts[me ^ k] = cols[kr][kf]
                 w_out[rows_at(me ^ k, rows_in), :] = weights[kr][kf, :rows_in, :]
                 out_out[rows_at(me ^ k, rows_out), :] = weights[kr][kf, rows_in:, :]
             state_out[...] = lanes([parts[j] for j in range(M)])
@@ -377,24 +359,40 @@
                     + dot(sent, w_out[D : 2 * D, :])
                     + dot(got, w_out[2 * D :, :])
                 )
-
-        local_pre, mesh_state, in_full, out_full = call(
+            for copy in copies:
+                copy.wait()
+
+        local_pre, mesh_state, in_full, out_full, node_own = call(
             local_kernel,
             "edge_local",
             me1,
-            [edge_state, sl_hot, r_hot] + state_parts2 + edge_pairs,
-            [shape((E, D), F32), shape((N, D)), shape((3 * D, D)), shape((D, D))],
-            scratch=[pltpu.VMEM((M, N, C), BF)],
+            [node_in_weight, node_out_weight, edge_state, sl_hot, r_hot] + state_pairs + edge_pairs,
+            [shape((E, D), F32), shape((N, D)), shape((3 * D, D)), shape((D, D))]
+            + [shape((rows_node + rows_out, D))],
+            scratch=[pltpu.VMEM((M, N, C), BF), pltpu.SemaphoreType.DMA((2,))],
             flops=2 * E * D * (3 * D + 2 * N),
-        )
+            far=range(2),
+        )
+        node_chips = [node_own] + [member_swap(node_own, k) for k in firsts]
+
+        halo_pair = call(
+            pair_kernel,
+            "halo_pair",
+            me1,
+            halo_chips + [local_pre],
+            [shape((n_feat, NH, C))],
+            unread=(n_feat,),
+        )[0]
+        halo_pairs = core_swaps(halo_pair)
 
         def edge_kernel(me_ref, local_ref, es_ref, send_ref, recv_ref, w_ref, out_ref, *refs):
-            cols = refs[:M]
-            pre_out, outs = refs[M], refs[M + 1 : M + 1 + n_rep]
-            parts, halo, new, total = refs[M + 1 + n_rep :]
+            cols = refs[:n_rep]
+            pre_out, outs = refs[n_rep], refs[n_rep + 1 : 2 * n_rep + 1]
+            parts, halo, new, total = refs[2 * n_rep + 1 :]
             me = me_ref[0]
             for k in range(M):
-                parts[me ^ k] = cols[k][...]
+                kf, kr = divmod(k, n_rep)
+                parts[me ^ k] = cols[kr][kf]
             halo[...] = lanes([parts[j] for j in range(M)])
             for i in range(E // T):
                 at = slice(i * T, (i + 1) * T)
@@ -414,7 +412,7 @@
             edge_kernel,
             "edge_update",
             me1,
-            [local_pre, edge_state, sh_hot, rt_hot, in_full, out_full] + halo_parts,
+            [local_pre, edge_state, sh_hot, rt_hot, in_full, out_full] + halo_pairs,
             [shape((E, D), F32)] + [shape((n_feat, R, D))] * n_rep,
             scratch=[
                 pltpu.VMEM((M, NH, C), BF),
@@ -424,19 +422,17 @@
             ],
             flops=2 * E * D * (NH + D + D + N),
         )
-        def node_weights_kernel(me_ref, *refs):
-            for kf in range(n_feat):
-                refs[-1][kf] = refs[kf][...]
+        sums = member_sums(sums, me1, "node_sums")
 
         node_pair = call(
-            node_weights_kernel,
-            "join_node_weights",
+            pair_kernel,
+            "node_pair",
             me1,
             node_chips + [sums[0]],
             [shape((n_feat, rows_node + rows_out, D))],
             unread=(n_feat,),
         )[0]
-        node_pairs = [node_pair] + [member_swap(node_pair, kr) for kr in range(1, n_rep)]
+        node_pairs = core_swaps(node_pair)
 
         def node_ahead_kernel(me_ref, state_ref, grad_ref, *refs):
             weights = refs[:n_rep]
@@ -459,8 +455,6 @@
             scratch=[pltpu.VMEM((D, D), BF)],
             flops=4 * R * D * D,
         )
-
-        sums = member_sums(sums, me1, "node_sums")
 
         def node_kernel(me_ref, pre_ref, cot_ref, w_ref, grad_ref, *refs):
             first_out, second_out = refs[n_feat:]
@@ -577,41 +571,56 @@
         far_owed = dom_trade(owed[n_dom:])
         near_owed = dom_trade(owed[:n_dom])
 
-        def grid_back(name, members, back, after=()):
+        def cotangents(table_ref, slope_ref, arrived, at, k):
+            rows = stack([arrived[j][at * S : (at + 1) * S, :] for j in range(n_dom)])
+            cot = dot(hot_columns(table_ref[k, 0:1, :], G), rows)
+            return (cot * slope_ref[k]).astype(BF)
+
+        def grid_back(name, members, back, after):
             def kernel(me_ref, slope_ref, table_ref, *refs):
-                arrived, outs = refs[:n_dom], refs[n_dom + len(after) :]
+                outs = refs[n_dom + len(after) :]
                 for at, k in enumerate(members):
-                    rows = stack([arrived[j][at * S : (at + 1) * S, :] for j in range(n_dom)])
-                    cot = dot(hot_columns(table_ref[k, 0:1, :], G), rows)
-                    outs[at][...] = (cot * slope_ref[k]).astype(BF)
+                    outs[at][...] = cotangents(table_ref, slope_ref, refs[:n_dom], at, k)
 
             return call(
                 kernel,
                 name,
                 me1,
-                [grid_slope, slots] + back + list(after),
+                [grid_slope, slots] + back + after,
                 [shape((G, C))] * len(members),
                 flops=2 * len(members) * G * NS * C,
                 unread=range(2 + n_dom, 2 + n_dom + len(after)),
             )
 
-        far_dpre = grid_back("grid_back_far", others, far_owed)
+        far_dpre = grid_back("grid_back_far", others, far_owed, [])
         near_dpre = grid_back("grid_back_near", near, near_owed, far_dpre[:1])
         far_dpre = [member_swap(x, k) for x, k in zip(far_dpre, others)]
+
+        def far_join_kernel(me_ref, *refs):
+            for at in range(len(others)):
+                refs[-1][at] = refs[at][...]
+
+        far_dpre = call(
+            far_join_kernel,
+            "far_join",
+            me1,
+            far_dpre + near_dpre[:1],
+            [shape((len(others), G, C))],
+            unread=(len(others),),
+        )
         near_dpre = [member_swap(x, k) if k else x for x, k in zip(near_dpre, near)]
-        grid_dpre = near_dpre + far_dpre
-
-        def adjoint_kernel(me_ref, enc_ref, *refs):
-            cols, out, parts = refs[:M], refs[M], refs[M + 1]
-            for k in range(M):
-                parts[me_ref[0] ^ k] = cols[k][...]
+
+        def adjoint_kernel(me_ref, enc_ref, far_ref, *refs):
+            cols, (out, parts) = refs[:n_rep], refs[n_rep:]
+            for k in range(M):
+                parts[me_ref[0] ^ k] = cols[k][...] if k < n_rep else far_ref[k - n_rep]
             out[...] = dot_t(lanes([parts[j] for j in range(M)]), enc_ref[...])
 
         return call(
             adjoint_kernel,
             "adjoint",
             me1,
-            [enc_full] + grid_dpre,
+            [enc_full] + far_dpre + near_dpre,
             [shape((G, D), F32)],
             scratch=[pltpu.VMEM((M, G, C), BF)],
             flops=2 * G * D * D,

time: 122 us -> 114 us (0.934)
  waiting for transfers between devices: 53.4 us -> 49.3 us
  Pallas kernels: 25 us -> 22.6 us
  starting transfers between devices: 42.2 us -> 40.7 us
    ppermute x28 -> x26, waiting for transfers between devices: 32.9 us -> 28.8 us  [member_swap(): return lax.ppermute(x, ('feat', 'rep'), [(i, i ^ k) for i in range(M)])]
    pallas_call x23, Pallas kernels: 25 us -> 22.6 us  [call(): pl.pallas_call(body, out_shape=list(outs), in_specs=[SMEM] + [HBM if i in...]
    ppermute x28 -> x26, starting transfers between devices: 20 us -> 18.1 us  [member_swap(): return lax.ppermute(x, ('feat', 'rep'), [(i, i ^ k) for i in range(M)])]
  transfers between devices with their start and end apart: 43 -> 41, of which waited for: 20 -> 20; matrix products, arithmetic and copies ran while one was open for 0% -> 0% of each run, Pallas kernels for 10% -> 13%
where the time goes in v6:
time: 114 us
  waiting for transfers between devices  49.3 us (43%)
  starting transfers between devices  40.7 us (36%)
  Pallas kernels  22.6 us (20%)
    ppermute x26, waiting for transfers between devices, member_swap(): return lax.ppermute(x, ('feat', 'rep'), [(i, i ^ k) for i in range(M)])  28.8 us
    ppermute x15, starting transfers between devices, dom_swap(): return lax.ppermute(x, 'dom', [(i, i ^ k) for i in range(n_dom)])  22.6 us
    pallas_call x23, Pallas kernels, call(): pl.pallas_call(body, out_shape=list(outs), in_specs=[SMEM] + [HBM if i in...  22.6 us
    ppermute x15, waiting for transfers between devices, dom_swap(): return lax.ppermute(x, 'dom', [(i, i ^ k) for i in range(n_dom)])  20.5 us
    ppermute x26, starting transfers between devices, member_swap(): return lax.ppermute(x, ('feat', 'rep'), [(i, i ^ k) for i in range(M)])  18.1 us
  transfers between devices with their start and end apart: 41, of which 20 were waited for; matrix products, arithmetic and copies ran while one was open for 0% of the time, Pallas kernels for 13%

profile of v6, /device:TPU:0, one launch (start us, length us, event | category | flops | bytes accessed | tf_op | source)
XLA Modules:
  0.0 113.6 jit_solution(733908739208227858)
XLA Ops:
  0.0 2.9 %collective-permute-start.1 = (bf16[256,512]{1,0:T(8,128)(2,1)}, bf16[256,512]{1,0:T(8,128)(2,1)S(1)}, u32[]{:S(2)}, u32[]{:S(2)}) collective-permute-start(bf16[256,512]{1,0:T(8,128)(2,1)} %refs_0_.1), channel_id=1, source_target_pairs={{0,2},{1,3},{2,0},{3,1},{4,6},{5,7},{6,4},{7,5},{8,10},{9,11},{10,... | collective-permute-start | bytes 786440 | tf_op jit(solution)/shard_map/ppermute | solution.py:85
  3.0 1.5 %tables.1 = (bf16[144,512]{1,0:T(8,128)(2,1)S(1)}, s32[1,512]{1,0:T(1,128)S(1)}, s32[1,1024]{1,0:T(1,128)S(1)}) custom-call(s32[2]{0:T(128)S(1)} %pad_add_fusion.where_ref, bf16[128,512]{1,0:T(8,128)(2,1)} %enc_ref.1, s32[1,4,128]{2,1,0:T(4,128)} %gs_ref.1, s32[1,4,128]{2,1,0:T(4,128)} %gr_ref.1, s32[1,4,128]{2,1,0:T(4,128)} %halo_ref.1, s32[1,1024]{1,0:T(1,128)} %bitcast.5), custom_call_target="tpu_custom_call" | custom-call | bytes 294912 | tf_op jit(solution)/shard_map/tables/pallas_call | solution.py:63
  4.7 5.6 %collective-permute-done.1.refs_2_ = bf16[256,512]{1,0:T(8,128)(2,1)S(1)} collective-permute-done((bf16[256,512]{1,0:T(8,128)(2,1)}, bf16[256,512]{1,0:T(8,128)(2,1)S(1)}, u32[]{:S(2)}, u32[]{:S(2)}) %collective-permute-start.1) | collective-permute-done | bytes 262176 | tf_op jit(solution)/shard_map/ppermute | solution.py:85
  10.8 1.8 %collective-permute-done.4.refs_6_ = bf16[144,512]{1,0:T(8,128)(2,1)S(1)} collective-permute-done((bf16[144,512]{1,0:T(8,128)(2,1)S(1)}, bf16[144,512]{1,0:T(8,128)(2,1)S(1)}, u32[]{:S(2)}, u32[]{:S(2)}) %collective-permute-start.4) | collective-permute-done | bytes 147488 | tf_op jit(solution)/shard_map/ppermute | solution.py:85
  12.6 0.7 copy-done.3
  13.3 2.1 %edge_hots.1 = (bf16[1024,512]{1,0:T(8,128)(2,1)S(1)}, bf16[1024,512]{1,0:T(8,128)(2,1)S(1)}, bf16[1024,512]{1,0:T(8,128)(2,1)S(1)}, bf16[512,1024]{1,0:T(8,128)...) custom-call(s32[1]{0:T(128)} %bitcast.me_ref, s32[1,1024]{1,0:T(1,128)S(1)} %get-tuple-element.70.send_ref, ...), custom_call_target="tpu_custom_call" | custom-call | bytes 6299648 | tf_op jit(solution)/shard_map/edge_hots/pallas_call | solution.py:63
  15.5 2.0 %grid_messages.1 = (bf16[512,512]{1,0:T(8,128)(2,1)S(1)}, f32[4,256,128]{2,1,0:T(8,128)S(1)}, s32[4,2,512]{2,1,0:T(2,128)S(1)}, bf16[512,512]{1,0:T(8,128)(2,1)S...) custom-call(s32[1]{0:T(128)} %bitcast.me_ref, ...), custom_call_target="tpu_custom_call" | custom-call | flops 268435456 | bytes 5324800 | tf_op jit(solution)/shard_map/grid_messages/pallas_call | solution.py:63
  17.5 1.8 %collective-permute-start.13 = (bf16[512,512]{1,0:T(8,128)(2,1)S(1)}, bf16[512,512]{1,0:T(8,128)(2,1)S(1)}, u32[]{:S(2)}, u32[]{:S(2)}) collective-permute-start(bf16[512,512]{1,0:T(8,128)(2,1)S(1)} %get-tuple-element.85.refs_6_), channel_id=1, source_target_pairs={{0,2},{1,3},{2,0},{3,1},{4,6},{5,7},{6,4},{7,5},{8,10},{9,11},{10,... | collective-permute-start | bytes 1572872 | tf_op jit(solution)/shard_map/ppermute | solution.py:85
  19.3 1.6 %collective-permute-start.6 = (bf16[512,128]{1,0:T(8,128)(2,1)S(1)}, bf16[512,128]{1,0:T(8,128)(2,1)S(1)}, u32[]{:S(2)}, u32[]{:S(2)}) collective-permute-start(bf16[512,128]{1,0:T(8,128)(2,1)S(1)} %get-tuple-element.78), channel_id=1, source_target_pairs={{0,4},{4,0},{8,12},{12,8},{1,5},{5,1},{9,13},{13,9},{2,6},{6,2},{1... | collective-permute-start | bytes 393224 | tf_op jit(solution)/shard_map/ppermute | solution.py:88
  20.9 2.6 %collective-permute-start.7 = (bf16[512,128]{1,0:T(8,128)(2,1)S(1)}, bf16[512,128]{1,0:T(8,128)(2,1)S(1)}, u32[]{:S(2)}, u32[]{:S(2)}) collective-permute-start(bf16[512,128]{1,0:T(8,128)(2,1)S(1)} %get-tuple-element.79), channel_id=1, source_target_pairs={{0,8},{4,12},{8,0},{12,4},{1,9},{5,13},{9,1},{13,5},{2,10},{6,14},... | collective-permute-start | bytes 393224 | tf_op jit(solution)/shard_map/ppermute | solution.py:88
  23.7 3.3 %collective-permute-done.6.refs_1_ = bf16[512,128]{1,0:T(8,128)(2,1)S(1)} collective-permute-done((bf16[512,128]{1,0:T(8,128)(2,1)S(1)}, bf16[512,128]{1,0:T(8,128)(2,1)S(1)}, u32[]{:S(2)}, u32[]{:S(2)}) %collective-permute-start.6) | collective-permute-done | bytes 131104 | tf_op jit(solution)/shard_map/ppermute | solution.py:88
  27.0 6.8 %collective-permute-done.7.refs_2_ = bf16[512,128]{1,0:T(8,128)(2,1)S(1)} collective-permute-done((bf16[512,128]{1,0:T(8,128)(2,1)S(1)}, bf16[512,128]{1,0:T(8,128)(2,1)S(1)}, u32[]{:S(2)}, u32[]{:S(2)}) %collective-permute-start.7) | collective-permute-done | bytes 131104 | tf_op jit(solution)/shard_map/ppermute | solution.py:88
  33.8 0.8 encode.1.state_ref.refs_4_
  35.8 2.5 %collective-permute-start.9 = (bf16[128,128]{1,0:T(8,128)(2,1)S(1)}, bf16[128,128]{1,0:T(8,128)(2,1)S(1)}, u32[]{:S(2)}, u32[]{:S(2)}) collective-permute-start(bf16[128,128]{1,0:T(8,128)(2,1)S(1)} %get-tuple-element.82), channel_id=1, source_target_pairs={{0,4},{4,0},{8,12},{12,8},{1,5},{5,1},{9,13},{13,9},{2,6},{6,2},{1... | collective-permute-start | bytes 98312 | tf_op jit(solution)/shard_map/ppermute | solution.py:88
  38.2 1.1 collective-permute-start.10
  39.3 1.4 %collective-permute-start.11 = (bf16[128,128]{1,0:T(8,128)(2,1)S(1)}, bf16[128,128]{1,0:T(8,128)(2,1)S(1)}, u32[]{:S(2)}, u32[]{:S(2)}) collective-permute-start(bf16[128,128]{1,0:T(8,128)(2,1)S(1)} %get-tuple-element.84), channel_id=1, source_target_pairs={{0,12},{4,8},{8,4},{12,0},{1,13},{5,9},{9,5},{13,1},{2,14},{6,10},... | collective-permute-start | bytes 98312 | tf_op jit(solution)/shard_map/ppermute | solution.py:88
  40.7 2.8 %collective-permute-done.10.refs_2_ = bf16[128,128]{1,0:T(8,128)(2,1)S(1)} collective-permute-done((bf16[128,128]{1,0:T(8,128)(2,1)S(1)}, bf16[128,128]{1,0:T(8,128)(2,1)S(1)}, u32[]{:S(2)}, u32[]{:S(2)}) %collective-permute-start.10) | collective-permute-done | bytes 32800 | tf_op jit(solution)/shard_map/ppermute | solution.py:88
  43.5 1.5 %collective-permute-done.11.refs_3_ = bf16[128,128]{1,0:T(8,128)(2,1)S(1)} collective-permute-done((bf16[128,128]{1,0:T(8,128)(2,1)S(1)}, bf16[128,128]{1,0:T(8,128)(2,1)S(1)}, u32[]{:S(2)}, u32[]{:S(2)}) %collective-permute-start.11) | collective-permute-done | bytes 32800 | tf_op jit(solution)/shard_map/ppermute | solution.py:88
  45.7 1.5 %collective-permute-start.16 = (bf16[512,128]{1,0:T(8,128)(2,1)S(1)}, bf16[512,128]{1,0:T(8,128)(2,1)S(1)}, u32[]{:S(2)}, u32[]{:S(2)}) collective-permute-start(bf16[512,128]{1,0:T(8,128)(2,1)S(1)} %get-tuple-element.93.refs_0_), channel_id=1, source_target_pairs={{0,2},{1,3},{2,0},{3,1},{4,6},{5,7},{6,4},{7,5},{8,10},{9,11},{10,... | collective-permute-start | bytes 393224 | tf_op jit(solution)/shard_map/ppermute | solution.py:85
  47.2 1.0 collective-permute-done.14.refs_1_
  48.2 3.0 %edge_local.1 = (f32[1024,512]{1,0:T(8,128)S(1)}, bf16[512,512]{1,0:T(8,128)(2,1)S(1)}, bf16[1536,512]{1,0:T(8,128)(2,1)S(1)}, bf16[512,512]{1,0:T(8,128)(2,1)S(1)}, bf16[384,512]{1,0:T(8,128)(2,1)S(1)}) custom-call(s32[1]{0:T(128)} %bitcast.me_ref, bf16[256,512]{1,0:T(8,128)(2,1)} %in_ref.1, bf16[128,512]{1,0:T(8,128)(2,1)} %out_ref.1, ...), custom_call_target="tpu_custom_call" | custom-call | flops 2684354560 | bytes 11272192 | tf_op jit(solution)/shard_map/edge_local/pallas_call | solution.py:63
  51.5 1.5 %collective-permute-start.18 = (bf16[384,512]{1,0:T(8,128)(2,1)S(1)}, bf16[384,512]{1,0:T(8,128)(2,1)S(1)}, u32[]{:S(2)}, u32[]{:S(2)}) collective-permute-start(bf16[384,512]{1,0:T(8,128)(2,1)S(1)} %get-tuple-element.97.refs_0_), channel_id=1, source_target_pairs={{0,2},{1,3},{2,0},{3,1},{4,6},{5,7},{6,4},{7,5},{8,10},{9,11},{10,... | collective-permute-start | bytes 1179656 | tf_op jit(solution)/shard_map/ppermute | solution.py:85
  53.0 3.1 %edge_update.1 = (f32[1024,512]{1,0:T(8,128)S(1)}, bf16[2,128,512]{2,1,0:T(8,128)(2,1)S(1)}, bf16[2,128,512]{2,1,0:T(8,128)(2,1)S(1)}) custom-call(s32[1]{0:T(128)} %bitcast.me_ref, f32[1024,512]{1,0:T(8,128)S(1)} %get-tuple-element.88.refs_2_.local_ref, bf16[1024,512]{1,0:T(8,128)(2,1)S(1)} %copy-done.4, bf16[1024,512]{1,0:T(8,128)(2,1)S(1)} %get-tuple-element.89.send_ref, ...), custom_call_target="tpu_custom_call" | custom-call | flops 2147483648 | bytes 10485760 | tf_op jit(solution)/shard_map/edge_update/pallas_call | solution.py:63
  56.3 1.5 %collective-permute-done.19.refs_1_ = bf16[2,128,512]{2,1,0:T(8,128)(2,1)S(1)} collective-permute-done((bf16[2,128,512]{2,1,0:T(8,128)(2,1)S(1)}, bf16[2,128,512]{2,1,0:T(8,128)(2,1)S(1)}, u32[]{:S(2)}, u32[]{:S(2)}) %collective-permute-start.19) | collective-permute-done | bytes 262176 | tf_op jit(solution)/shard_map/ppermute | solution.py:85
  57.8 5.1 %collective-permute-done.18.refs_1_ = bf16[384,512]{1,0:T(8,128)(2,1)S(1)} collective-permute-done((bf16[384,512]{1,0:T(8,128)(2,1)S(1)}, bf16[384,512]{1,0:T(8,128)(2,1)S(1)}, u32[]{:S(2)}, u32[]{:S(2)}) %collective-permute-start.18) | collective-permute-done | bytes 393248 | tf_op jit(solution)/shard_map/ppermute | solution.py:85
  63.0 1.6 %collective-permute-start.21 = (bf16[128,512]{1,0:T(8,128)(2,1)S(1)}, bf16[128,512]{1,0:T(8,128)(2,1)S(1)}, u32[]{:S(2)}, u32[]{:S(2)}) collective-permute-start(bf16[128,512]{1,0:T(8,128)(2,1)S(1)} %get-tuple-element.104), channel_id=1, source_target_pairs={{0,2},{1,3},{2,0},{3,1},{4,6},{5,7},{6,4},{7,5},{8,10},{9,11},{10,... | collective-permute-start | bytes 393224 | tf_op jit(solution)/shard_map/ppermute | solution.py:85
  64.6 0.7 collective-permute-done.20.refs_1_
  65.8 3.2 %collective-permute-done.21.refs_1_ = bf16[128,512]{1,0:T(8,128)(2,1)S(1)} collective-permute-done((bf16[128,512]{1,0:T(8,128)(2,1)S(1)}, bf16[128,512]{1,0:T(8,128)(2,1)S(1)}, u32[]{:S(2)}, u32[]{:S(2)}) %collective-permute-start.21) | collective-permute-done | bytes 131104 | tf_op jit(solution)/shard_map/ppermute | solution.py:85
  69.6 1.6 %collective-permute-start.23 = (bf16[128,512]{1,0:T(8,128)(2,1)S(1)}, bf16[128,512]{1,0:T(8,128)(2,1)S(1)}, u32[]{:S(2)}, u32[]{:S(2)}) collective-permute-start(bf16[128,512]{1,0:T(8,128)(2,1)S(1)} %get-tuple-element.105.refs_0_), channel_id=1, source_target_pairs={{0,2},{1,3},{2,0},{3,1},{4,6},{5,7},{6,4},{7,5},{8,10},{9,11},{10,... | collective-permute-start | bytes 393224 | tf_op jit(solution)/shard_map/ppermute | solution.py:85
  71.2 3.6 %collective-permute-done.23.refs_2_ = bf16[128,512]{1,0:T(8,128)(2,1)S(1)} collective-permute-done((bf16[128,512]{1,0:T(8,128)(2,1)S(1)}, bf16[128,512]{1,0:T(8,128)(2,1)S(1)}, u32[]{:S(2)}, u32[]{:S(2)}) %collective-permute-start.23) | collective-permute-done | bytes 131104 | tf_op jit(solution)/shard_map/ppermute | solution.py:85
  74.7 1.3 %collective-permute-done.24.refs_3_ = bf16[128,512]{1,0:T(8,128)(2,1)S(1)} collective-permute-done((bf16[128,512]{1,0:T(8,128)(2,1)S(1)}, bf16[128,512]{1,0:T(8,128)(2,1)S(1)}, u32[]{:S(2)}, u32[]{:S(2)}) %collective-permute-start.24) | collective-permute-done | bytes 131104 | tf_op jit(solution)/shard_map/ppermute | solution.py:85
  76.1 2.9 %edge_backward.1 = (bf16[1024,512]{1,0:T(8,128)(2,1)S(1)}, bf16[2,512,128]{2,1,0:T(8,128)(2,1)S(1)}, bf16[2,512,128]{2,1,0:T(8,128)(2,1)S(1)}) custom-call(s32[1]{0:T(128)} %bitcast.me_ref, bf16[1024,512]{1,0:T(8,128)(2,1)S(1)} %copy-done.1, f32[1024,512]{1,0:T(8,128)S(1)} %get-tuple-element.94.pre_ref, bf16[512,1024]{1,0:T(8,128)(2,1)S(1)} %get-tuple-element.95.send_ref, ...), custom_call_target="tpu_custom_call" | custom-call | flops 1879048192 | bytes 9437184 | tf_op jit(solution)/shard_map/edge_backward/pallas_call | solution.py:63
  79.2 2.1 %local_backward.1 = (bf16[2,512,128]{2,1,0:T(8,128)(2,1)S(1)}, bf16[2,512,128]{2,1,0:T(8,128)(2,1)S(1)}) custom-call(s32[1]{0:T(128)} %bitcast.me_ref, bf16[1024,512]{1,0:T(8,128)(2,1)S(1)} %get-tuple-element.106.dpre_ref, bf16[512,1024]{1,0:T(8,128)(2,1)S(1)} %get-tuple-element.107.send_ref, bf16[512,1024]{1,0:T(8,128)(2,1)S(1)} %get-tuple-element.90.recv_ref, ...), custom_call_target="tpu_custom_call" | custom-call | flops 1610612736 | bytes 5505024 | tf_op jit(solution)/shard_map/local_backward/pallas_call | solution.py:63
  81.8 1.6 %collective-permute-start.28 = (bf16[512,128]{1,0:T(8,128)(2,1)S(1)}, bf16[512,128]{1,0:T(8,128)(2,1)S(1)}, u32[]{:S(2)}, u32[]{:S(2)}) collective-permute-start(bf16[512,128]{1,0:T(8,128)(2,1)S(1)} %get-tuple-element.116), channel_id=1, source_target_pairs={{0,2},{1,3},{2,0},{3,1},{4,6},{5,7},{6,4},{7,5},{8,10},{9,11},{10,... | collective-permute-start | bytes 393224 | tf_op jit(solution)/shard_map/ppermute | solution.py:85
  83.4 1.1 collective-permute-start.26
  84.5 3.7 %collective-permute-done.28.refs_1_ = bf16[512,128]{1,0:T(8,128)(2,1)S(1)} collective-permute-done((bf16[512,128]{1,0:T(8,128)(2,1)S(1)}, bf16[512,128]{1,0:T(8,128)(2,1)S(1)}, u32[]{:S(2)}, u32[]{:S(2)}) %collective-permute-start.28) | collective-permute-done | bytes 131104 | tf_op jit(solution)/shard_map/ppermute | solution.py:85
  88.5 1.8 %collective-permute-start.30 = (bf16[128,128]{1,0:T(8,128)(2,1)S(1)}, bf16[128,128]{1,0:T(8,128)(2,1)S(1)}, u32[]{:S(2)}, u32[]{:S(2)}) collective-permute-start(bf16[128,128]{1,0:T(8,128)(2,1)S(1)} %get-tuple-element.119), channel_id=1, source_target_pairs={{0,8},{4,12},{8,0},{12,4},{1,9},{5,13},{9,1},{13,5},{2,10},{6,14},... | collective-permute-start | bytes 98312 | tf_op jit(solution)/shard_map/ppermute | solution.py:88
  90.3 2.5 %collective-permute-start.31 = (bf16[128,128]{1,0:T(8,128)(2,1)S(1)}, bf16[128,128]{1,0:T(8,128)(2,1)S(1)}, u32[]{:S(2)}, u32[]{:S(2)}) collective-permute-start(bf16[128,128]{1,0:T(8,128)(2,1)S(1)} %get-tuple-element.120), channel_id=1, source_target_pairs={{0,12},{4,8},{8,4},{12,0},{1,13},{5,9},{9,5},{13,1},{2,14},{6,10},... | collective-permute-start | bytes 98312 | tf_op jit(solution)/shard_map/ppermute | solution.py:88
  93.3 2.7 %collective-permute-done.31.refs_5_ = bf16[128,128]{1,0:T(8,128)(2,1)S(1)} collective-permute-done((bf16[128,128]{1,0:T(8,128)(2,1)S(1)}, bf16[128,128]{1,0:T(8,128)(2,1)S(1)}, u32[]{:S(2)}, u32[]{:S(2)}) %collective-permute-start.31) | collective-permute-done | bytes 32800 | tf_op jit(solution)/shard_map/ppermute | solution.py:88
  96.0 1.2 %owed_rows.1 = (bf16[256,128]{1,0:T(8,128)(2,1)S(1)}, bf16[256,128]{1,0:T(8,128)(2,1)S(1)}, bf16[256,128]{1,0:T(8,128)(2,1)S(1)}, bf16[256,128]{1,0:T(8,128)(2,1...) custom-call(s32[1]{0:T(128)} %bitcast.me_ref, ...), custom_call_target="tpu_custom_call" | custom-call | flops 268435456 | bytes 935936 | tf_op jit(solution)/shard_map/owed_rows/pallas_call | solution.py:63
  97.2 3.0 %collective-permute-start.33 = (bf16[256,128]{1,0:T(8,128)(2,1)S(1)}, bf16[256,128]{1,0:T(8,128)(2,1)S(1)}, u32[]{:S(2)}, u32[]{:S(2)}) collective-permute-start(bf16[256,128]{1,0:T(8,128)(2,1)S(1)} %get-tuple-element.123), channel_id=1, source_target_pairs={{0,8},{4,12},{8,0},{12,4},{1,9},{5,13},{9,1},{13,5},{2,10},{6,14},... | collective-permute-start | bytes 196616 | tf_op jit(solution)/shard_map/ppermute | solution.py:88
  100.2 1.4 %collective-permute-start.34 = (bf16[256,128]{1,0:T(8,128)(2,1)S(1)}, bf16[256,128]{1,0:T(8,128)(2,1)S(1)}, u32[]{:S(2)}, u32[]{:S(2)}) collective-permute-start(bf16[256,128]{1,0:T(8,128)(2,1)S(1)} %get-tuple-element.124), channel_id=1, source_target_pairs={{0,12},{4,8},{8,4},{12,0},{1,13},{5,9},{9,5},{13,1},{2,14},{6,10},... | collective-permute-start | bytes 196616 | tf_op jit(solution)/shard_map/ppermute | solution.py:88
  101.6 3.0 %collective-permute-start.38 = (bf16[256,128]{1,0:T(8,128)(2,1)S(1)}, bf16[256,128]{1,0:T(8,128)(2,1)S(1)}, u32[]{:S(2)}, u32[]{:S(2)}) collective-permute-start(bf16[256,128]{1,0:T(8,128)(2,1)S(1)} %get-tuple-element.129), channel_id=1, source_target_pairs={{0,8},{4,12},{8,0},{12,4},{1,9},{5,13},{9,1},{13,5},{2,10},{6,14},... | collective-permute-start | bytes 196616 | tf_op jit(solution)/shard_map/ppermute | solution.py:88
  104.6 1.4 %collective-permute-start.39 = (bf16[256,128]{1,0:T(8,128)(2,1)S(1)}, bf16[256,128]{1,0:T(8,128)(2,1)S(1)}, u32[]{:S(2)}, u32[]{:S(2)}) collective-permute-start(bf16[256,128]{1,0:T(8,128)(2,1)S(1)} %get-tuple-element.130), channel_id=1, source_target_pairs={{0,12},{4,8},{8,4},{12,0},{1,13},{5,9},{9,5},{13,1},{2,14},{6,10},... | collective-permute-start | bytes 196616 | tf_op jit(solution)/shard_map/ppermute | solution.py:88
  106.7 1.6 %collective-permute-start.35 = (bf16[256,128]{1,0:T(8,128)(2,1)S(1)}, bf16[256,128]{1,0:T(8,128)(2,1)S(1)}, u32[]{:S(2)}, u32[]{:S(2)}) collective-permute-start(bf16[256,128]{1,0:T(8,128)(2,1)S(1)} %get-tuple-element.125.refs_4_), channel_id=1, source_target_pairs={{0,2},{1,3},{2,0},{3,1},{4,6},{5,7},{6,4},{7,5},{8,10},{9,11},{10,... | collective-permute-start | bytes 196616 | tf_op jit(solution)/shard_map/ppermute | solution.py:85
  108.6 2.1 %collective-permute-done.39.refs_3_ = bf16[256,128]{1,0:T(8,128)(2,1)S(1)} collective-permute-done((bf16[256,128]{1,0:T(8,128)(2,1)S(1)}, bf16[256,128]{1,0:T(8,128)(2,1)S(1)}, u32[]{:S(2)}, u32[]{:S(2)}) %collective-permute-start.39) | collective-permute-done | bytes 65568 | tf_op jit(solution)/shard_map/ppermute | solution.py:88
  111.1 1.4 %collective-permute-done.36.refs_1_ = bf16[256,128]{1,0:T(8,128)(2,1)S(1)} collective-permute-done((bf16[256,128]{1,0:T(8,128)(2,1)S(1)}, bf16[256,128]{1,0:T(8,128)(2,1)S(1)}, u32[]{:S(2)}, u32[]{:S(2)}) %collective-permute-start.36) | collective-permute-done | bytes 65568 | tf_op jit(solution)/shard_map/ppermute | solution.py:85
  112.5 1.1 adjoint.1
  (68 shorter events, 7.7 us)
Async XLA Ops:
  0.0 33.8 %copy-start.2 = (bf16[512,512]{1,0:T(8,128)(2,1)S(1)}, bf16[512,512]{1,0:T(8,128)(2,1)}, u32[]{:S(2)}) copy-start(bf16[512,512]{1,0:T(8,128)(2,1)} %base_ref.1) | copy-start | bytes 1572868
  0.0 10.3 %collective-permute-start.1 = (bf16[256,512]{1,0:T(8,128)(2,1)}, bf16[256,512]{1,0:T(8,128)(2,1)S(1)}, u32[]{:S(2)}, u32[]{:S(2)}) collective-permute-start(bf16[256,512]{1,0:T(8,128)(2,1)} %refs_0_.1), channel_id=1, source_target_pairs={{0,2},{1,3},{2,0},{3,1},{4,6},{5,7},{6,4},{7,5},{8,10},{9,11},{10,... | collective-permute-start | bytes 786440 | tf_op jit(solution)/shard_map/ppermute | solution.py:85
  4.5 8.1 %collective-permute-start.4 = (bf16[144,512]{1,0:T(8,128)(2,1)S(1)}, bf16[144,512]{1,0:T(8,128)(2,1)S(1)}, u32[]{:S(2)}, u32[]{:S(2)}) collective-permute-start(bf16[144,512]{1,0:T(8,128)(2,1)S(1)} %get-tuple-element.69.refs_4_), channel_id=1, source_target_pairs={{0,2},{1,3},{2,0},{3,1},{4,6},{5,7},{6,4},{7,5},{8,10},{9,11},{10,... | collective-permute-start | bytes 442376 | tf_op jit(solution)/shard_map/ppermute | solution.py:85
  4.6 10.8 %collective-permute-start = (bf16[256,512]{1,0:T(8,128)(2,1)}, bf16[256,512]{1,0:T(8,128)(2,1)S(1)}, u32[]{:S(2)}, u32[]{:S(2)}) collective-permute-start(bf16[256,512]{1,0:T(8,128)(2,1)} %refs_0_.1), channel_id=1, source_target_pairs={{0,1},{1,0},{2,3},{3,2},{4,5},{5,4},{6,7},{7,6},{8,9},{9,8},{10,11... | collective-permute-start | bytes 786440 | tf_op jit(solution)/shard_map/ppermute | solution.py:85
  10.3 5.2 %collective-permute-start.2 = (bf16[256,512]{1,0:T(8,128)(2,1)S(1)}, bf16[256,512]{1,0:T(8,128)(2,1)S(1)}, u32[]{:S(2)}, u32[]{:S(2)}) collective-permute-start(bf16[256,512]{1,0:T(8,128)(2,1)S(1)} %collective-permute-done.1.refs_2_), channel_id=1, source_target_pairs={{0,1},{1,0},{2,3},{3,2},{4,5},{5,4},{6,7},{7,6},{8,9},{9,8},{10,11... | collective-permute-start | bytes 786440 | tf_op jit(solution)/shard_map/ppermute | solution.py:85
  10.3 5.2 %collective-permute-start.3 = (bf16[144,512]{1,0:T(8,128)(2,1)S(1)}, bf16[144,512]{1,0:T(8,128)(2,1)S(1)}, u32[]{:S(2)}, u32[]{:S(2)}) collective-permute-start(bf16[144,512]{1,0:T(8,128)(2,1)S(1)} %get-tuple-element.69.refs_4_), channel_id=1, source_target_pairs={{0,1},{1,0},{2,3},{3,2},{4,5},{5,4},{6,7},{7,6},{8,9},{9,8},{10,11... | collective-permute-start | bytes 442376 | tf_op jit(solution)/shard_map/ppermute | solution.py:85
  12.6 2.8 %collective-permute-start.5 = (bf16[144,512]{1,0:T(8,128)(2,1)S(1)}, bf16[144,512]{1,0:T(8,128)(2,1)S(1)}, u32[]{:S(2)}, u32[]{:S(2)}) collective-permute-start(bf16[144,512]{1,0:T(8,128)(2,1)S(1)} %collective-permute-done.4.refs_6_), channel_id=1, source_target_pairs={{0,1},{1,0},{2,3},{3,2},{4,5},{5,4},{6,7},{7,6},{8,9},{9,8},{10,11... | collective-permute-start | bytes 442376 | tf_op jit(solution)/shard_map/ppermute | solution.py:85
  12.6 0.7 copy-start.3
  17.5 30.8 %copy-start.4 = (bf16[1024,512]{1,0:T(8,128)(2,1)S(1)}, bf16[1024,512]{1,0:T(8,128)(2,1)}, u32[]{:S(2)}) copy-start(bf16[1024,512]{1,0:T(8,128)(2,1)} %es_ref.3) | copy-start | bytes 3145732
  17.5 27.6 %collective-permute-start.13 = (bf16[512,512]{1,0:T(8,128)(2,1)S(1)}, bf16[512,512]{1,0:T(8,128)(2,1)S(1)}, u32[]{:S(2)}, u32[]{:S(2)}) collective-permute-start(bf16[512,512]{1,0:T(8,128)(2,1)S(1)} %get-tuple-element.85.refs_6_), channel_id=1, source_target_pairs={{0,2},{1,3},{2,0},{3,1},{4,6},{5,7},{6,4},{7,5},{8,10},{9,11},{10,... | collective-permute-start | bytes 1572872 | tf_op jit(solution)/shard_map/ppermute | solution.py:85
  19.3 7.7 %collective-permute-start.6 = (bf16[512,128]{1,0:T(8,128)(2,1)S(1)}, bf16[512,128]{1,0:T(8,128)(2,1)S(1)}, u32[]{:S(2)}, u32[]{:S(2)}) collective-permute-start(bf16[512,128]{1,0:T(8,128)(2,1)S(1)} %get-tuple-element.78), channel_id=1, source_target_pairs={{0,4},{4,0},{8,12},{12,8},{1,5},{5,1},{9,13},{13,9},{2,6},{6,2},{1... | collective-permute-start | bytes 393224 | tf_op jit(solution)/shard_map/ppermute | solution.py:88
  20.9 12.9 %collective-permute-start.7 = (bf16[512,128]{1,0:T(8,128)(2,1)S(1)}, bf16[512,128]{1,0:T(8,128)(2,1)S(1)}, u32[]{:S(2)}, u32[]{:S(2)}) collective-permute-start(bf16[512,128]{1,0:T(8,128)(2,1)S(1)} %get-tuple-element.79), channel_id=1, source_target_pairs={{0,8},{4,12},{8,0},{12,4},{1,9},{5,13},{9,1},{13,5},{2,10},{6,14},... | collective-permute-start | bytes 393224 | tf_op jit(solution)/shard_map/ppermute | solution.py:88
  23.5 10.3 %collective-permute-start.8 = (bf16[512,128]{1,0:T(8,128)(2,1)S(1)}, bf16[512,128]{1,0:T(8,128)(2,1)S(1)}, u32[]{:S(2)}, u32[]{:S(2)}) collective-permute-start(bf16[512,128]{1,0:T(8,128)(2,1)S(1)} %get-tuple-element.80), channel_id=1, source_target_pairs={{0,12},{4,8},{8,4},{12,0},{1,13},{5,9},{9,5},{13,1},{2,14},{6,10},... | collective-permute-start | bytes 393224 | tf_op jit(solution)/shard_map/ppermute | solution.py:88
  34.6 10.4 %collective-permute-start.12 = (bf16[512,128]{1,0:T(8,128)(2,1)S(1)}, bf16[512,128]{1,0:T(8,128)(2,1)S(1)}, u32[]{:S(2)}, u32[]{:S(2)}) collective-permute-start(bf16[512,128]{1,0:T(8,128)(2,1)S(1)} %encode.1.state_ref.refs_4_), channel_id=1, source_target_pairs={{0,2},{1,3},{2,0},{3,1},{4,6},{5,7},{6,4},{7,5},{8,10},{9,11},{10,... | collective-permute-start | bytes 393224 | tf_op jit(solution)/shard_map/ppermute | solution.py:85
  35.8 4.9 %collective-permute-start.9 = (bf16[128,128]{1,0:T(8,128)(2,1)S(1)}, bf16[128,128]{1,0:T(8,128)(2,1)S(1)}, u32[]{:S(2)}, u32[]{:S(2)}) collective-permute-start(bf16[128,128]{1,0:T(8,128)(2,1)S(1)} %get-tuple-element.82), channel_id=1, source_target_pairs={{0,4},{4,0},{8,12},{12,8},{1,5},{5,1},{9,13},{13,9},{2,6},{6,2},{1... | collective-permute-start | bytes 98312 | tf_op jit(solution)/shard_map/ppermute | solution.py:88
  38.2 5.3 %collective-permute-start.10 = (bf16[128,128]{1,0:T(8,128)(2,1)S(1)}, bf16[128,128]{1,0:T(8,128)(2,1)S(1)}, u32[]{:S(2)}, u32[]{:S(2)}) collective-permute-start(bf16[128,128]{1,0:T(8,128)(2,1)S(1)} %get-tuple-element.83), channel_id=1, source_target_pairs={{0,8},{4,12},{8,0},{12,4},{1,9},{5,13},{9,1},{13,5},{2,10},{6,14},... | collective-permute-start | bytes 98312 | tf_op jit(solution)/shard_map/ppermute | solution.py:88
  39.3 5.7 %collective-permute-start.11 = (bf16[128,128]{1,0:T(8,128)(2,1)S(1)}, bf16[128,128]{1,0:T(8,128)(2,1)S(1)}, u32[]{:S(2)}, u32[]{:S(2)}) collective-permute-start(bf16[128,128]{1,0:T(8,128)(2,1)S(1)} %get-tuple-element.84), channel_id=1, source_target_pairs={{0,12},{4,8},{8,4},{12,0},{1,13},{5,9},{9,5},{13,1},{2,14},{6,10},... | collective-permute-start | bytes 98312 | tf_op jit(solution)/shard_map/ppermute | solution.py:88
  45.1 3.1 %collective-permute-start.15 = (bf16[2,512,512]{2,1,0:T(8,128)(2,1)S(1)}, bf16[2,512,512]{2,1,0:T(8,128)(2,1)S(1)}, u32[]{:S(2)}, u32[]{:S(2)}) collective-permute-start(bf16[2,512,512]{2,1,0:T(8,128)(2,1)S(1)} %get-tuple-element.87.refs_2_), channel_id=1, source_target_pairs={{0,1},{1,0},{2,3},{3,2},{4,5},{5,4},{6,7},{7,6},{8,9},{9,8},{10,11... | collective-permute-start | bytes 3145736 | tf_op jit(solution)/shard_map/ppermute | solution.py:85
  45.2 3.0 %collective-permute-start.14 = (bf16[2,512,128]{2,1,0:T(8,128)(2,1)S(1)}, bf16[2,512,128]{2,1,0:T(8,128)(2,1)S(1)}, u32[]{:S(2)}, u32[]{:S(2)}) collective-permute-start(bf16[2,512,128]{2,1,0:T(8,128)(2,1)S(1)} %get-tuple-element.86.refs_0_), channel_id=1, source_target_pairs={{0,1},{1,0},{2,3},{3,2},{4,5},{5,4},{6,7},{7,6},{8,9},{9,8},{10,11... | collective-permute-start | bytes 786440 | tf_op jit(solution)/shard_map/ppermute | solution.py:85
  45.7 5.6 %collective-permute-start.16 = (bf16[512,128]{1,0:T(8,128)(2,1)S(1)}, bf16[512,128]{1,0:T(8,128)(2,1)S(1)}, u32[]{:S(2)}, u32[]{:S(2)}) collective-permute-start(bf16[512,128]{1,0:T(8,128)(2,1)S(1)} %get-tuple-element.93.refs_0_), channel_id=1, source_target_pairs={{0,2},{1,3},{2,0},{3,1},{4,6},{5,7},{6,4},{7,5},{8,10},{9,11},{10,... | collective-permute-start | bytes 393224 | tf_op jit(solution)/shard_map/ppermute | solution.py:85
  51.3 1.7 %collective-permute-start.17 = (bf16[2,512,128]{2,1,0:T(8,128)(2,1)S(1)}, bf16[2,512,128]{2,1,0:T(8,128)(2,1)S(1)}, u32[]{:S(2)}, u32[]{:S(2)}) collective-permute-start(bf16[2,512,128]{2,1,0:T(8,128)(2,1)S(1)} %halo_pair.1.refs_0_), channel_id=1, source_target_pairs={{0,1},{1,0},{2,3},{3,2},{4,5},{5,4},{6,7},{7,6},{8,9},{9,8},{10,11... | collective-permute-start | bytes 786440 | tf_op jit(solution)/shard_map/ppermute | solution.py:85
  51.5 11.4 %collective-permute-start.18 = (bf16[384,512]{1,0:T(8,128)(2,1)S(1)}, bf16[384,512]{1,0:T(8,128)(2,1)S(1)}, u32[]{:S(2)}, u32[]{:S(2)}) collective-permute-start(bf16[384,512]{1,0:T(8,128)(2,1)S(1)} %get-tuple-element.97.refs_0_), channel_id=1, source_target_pairs={{0,2},{1,3},{2,0},{3,1},{4,6},{5,7},{6,4},{7,5},{8,10},{9,11},{10,... | collective-permute-start | bytes 1179656 | tf_op jit(solution)/shard_map/ppermute | solution.py:85
  56.1 9.2 %copy-start = (bf16[512,512]{1,0:T(8,128)(2,1)S(1)}, bf16[512,512]{1,0:T(8,128)(2,1)}, u32[]{:S(2)}) copy-start(bf16[512,512]{1,0:T(8,128)(2,1)} %grad_ref.4) | copy-start | bytes 1572868
  56.1 1.6 %collective-permute-start.19 = (bf16[2,128,512]{2,1,0:T(8,128)(2,1)S(1)}, bf16[2,128,512]{2,1,0:T(8,128)(2,1)S(1)}, u32[]{:S(2)}, u32[]{:S(2)}) collective-permute-start(bf16[2,128,512]{2,1,0:T(8,128)(2,1)S(1)} %get-tuple-element.99), channel_id=1, source_target_pairs={{0,1},{1,0},{2,3},{3,2},{4,5},{5,4},{6,7},{7,6},{8,9},{9,8},{10,11... | collective-permute-start | bytes 786440 | tf_op jit(solution)/shard_map/ppermute | solution.py:85
  63.0 2.4 %collective-permute-start.20 = (bf16[2,384,512]{2,1,0:T(8,128)(2,1)S(1)}, bf16[2,384,512]{2,1,0:T(8,128)(2,1)S(1)}, u32[]{:S(2)}, u32[]{:S(2)}) collective-permute-start(bf16[2,384,512]{2,1,0:T(8,128)(2,1)S(1)} %node_pair.1.refs_0_), channel_id=1, source_target_pairs={{0,1},{1,0},{2,3},{3,2},{4,5},{5,4},{6,7},{7,6},{8,9},{9,8},{10,11... | collective-permute-start | bytes 2359304 | tf_op jit(solution)/shard_map/ppermute | solution.py:85
  63.0 5.9 %collective-permute-start.21 = (bf16[128,512]{1,0:T(8,128)(2,1)S(1)}, bf16[128,512]{1,0:T(8,128)(2,1)S(1)}, u32[]{:S(2)}, u32[]{:S(2)}) collective-permute-start(bf16[128,512]{1,0:T(8,128)(2,1)S(1)} %get-tuple-element.104), channel_id=1, source_target_pairs={{0,2},{1,3},{2,0},{3,1},{4,6},{5,7},{6,4},{7,5},{8,10},{9,11},{10,... | collective-permute-start | bytes 393224 | tf_op jit(solution)/shard_map/ppermute | solution.py:85
  65.3 10.8 %copy-start.1 = (bf16[1024,512]{1,0:T(8,128)(2,1)S(1)}, bf16[1024,512]{1,0:T(8,128)(2,1)}, u32[]{:S(2)}) copy-start(bf16[1024,512]{1,0:T(8,128)(2,1)} %grad_ref.5) | copy-start | bytes 3145732
  69.6 5.1 %collective-permute-start.23 = (bf16[128,512]{1,0:T(8,128)(2,1)S(1)}, bf16[128,512]{1,0:T(8,128)(2,1)S(1)}, u32[]{:S(2)}, u32[]{:S(2)}) collective-permute-start(bf16[128,512]{1,0:T(8,128)(2,1)S(1)} %get-tuple-element.105.refs_0_), channel_id=1, source_target_pairs={{0,2},{1,3},{2,0},{3,1},{4,6},{5,7},{6,4},{7,5},{8,10},{9,11},{10,... | collective-permute-start | bytes 393224 | tf_op jit(solution)/shard_map/ppermute | solution.py:85
  71.2 3.6 %collective-permute-start.22 = (bf16[128,512]{1,0:T(8,128)(2,1)S(1)}, bf16[128,512]{1,0:T(8,128)(2,1)S(1)}, u32[]{:S(2)}, u32[]{:S(2)}) collective-permute-start(bf16[128,512]{1,0:T(8,128)(2,1)S(1)} %get-tuple-element.105.refs_0_), channel_id=1, source_target_pairs={{0,1},{1,0},{2,3},{3,2},{4,5},{5,4},{6,7},{7,6},{8,9},{9,8},{10,11... | collective-permute-start | bytes 393224 | tf_op jit(solution)/shard_map/ppermute | solution.py:85
  74.7 1.3 %collective-permute-start.24 = (bf16[128,512]{1,0:T(8,128)(2,1)S(1)}, bf16[128,512]{1,0:T(8,128)(2,1)S(1)}, u32[]{:S(2)}, u32[]{:S(2)}) collective-permute-start(bf16[128,512]{1,0:T(8,128)(2,1)S(1)} %collective-permute-done.23.refs_2_), channel_id=1, source_target_pairs={{0,1},{1,0},{2,3},{3,2},{4,5},{5,4},{6,7},{7,6},{8,9},{9,8},{10,11... | collective-permute-start | bytes 393224 | tf_op jit(solution)/shard_map/ppermute | solution.py:85
  79.0 2.7 %collective-permute-start.27 = (bf16[2,512,128]{2,1,0:T(8,128)(2,1)S(1)}, bf16[2,512,128]{2,1,0:T(8,128)(2,1)S(1)}, u32[]{:S(2)}, u32[]{:S(2)}) collective-permute-start(bf16[2,512,128]{2,1,0:T(8,128)(2,1)S(1)} %get-tuple-element.114), channel_id=1, source_target_pairs={{0,1},{1,0},{2,3},{3,2},{4,5},{5,4},{6,7},{7,6},{8,9},{9,8},{10,11... | collective-permute-start | bytes 786440 | tf_op jit(solution)/shard_map/ppermute | solution.py:85
  81.3 2.1 %collective-permute-start.25 = (bf16[2,512,128]{2,1,0:T(8,128)(2,1)S(1)}, bf16[2,512,128]{2,1,0:T(8,128)(2,1)S(1)}, u32[]{:S(2)}, u32[]{:S(2)}) collective-permute-start(bf16[2,512,128]{2,1,0:T(8,128)(2,1)S(1)} %get-tuple-element.110), channel_id=1, source_target_pairs={{0,1},{1,0},{2,3},{3,2},{4,5},{5,4},{6,7},{7,6},{8,9},{9,8},{10,11... | collective-permute-start | bytes 786440 | tf_op jit(solution)/shard_map/ppermute | solution.py:85
  81.8 6.4 %collective-permute-start.28 = (bf16[512,128]{1,0:T(8,128)(2,1)S(1)}, bf16[512,128]{1,0:T(8,128)(2,1)S(1)}, u32[]{:S(2)}, u32[]{:S(2)}) collective-permute-start(bf16[512,128]{1,0:T(8,128)(2,1)S(1)} %get-tuple-element.116), channel_id=1, source_target_pairs={{0,2},{1,3},{2,0},{3,1},{4,6},{5,7},{6,4},{7,5},{8,10},{9,11},{10,... | collective-permute-start | bytes 393224 | tf_op jit(solution)/shard_map/ppermute | solution.py:85
  83.4 9.3 %collective-permute-start.26 = (bf16[512,128]{1,0:T(8,128)(2,1)S(1)}, bf16[512,128]{1,0:T(8,128)(2,1)S(1)}, u32[]{:S(2)}, u32[]{:S(2)}) collective-permute-start(bf16[512,128]{1,0:T(8,128)(2,1)S(1)} %get-tuple-element.112), channel_id=1, source_target_pairs={{0,2},{1,3},{2,0},{3,1},{4,6},{5,7},{6,4},{7,5},{8,10},{9,11},{10,... | collective-permute-start | bytes 393224 | tf_op jit(solution)/shard_map/ppermute | solution.py:85
  88.2 4.5 %collective-permute-start.29 = (bf16[128,128]{1,0:T(8,128)(2,1)S(1)}, bf16[128,128]{1,0:T(8,128)(2,1)S(1)}, u32[]{:S(2)}, u32[]{:S(2)}) collective-permute-start(bf16[128,128]{1,0:T(8,128)(2,1)S(1)} %get-tuple-element.118), channel_id=1, source_target_pairs={{0,4},{4,0},{8,12},{12,8},{1,5},{5,1},{9,13},{13,9},{2,6},{6,2},{1... | collective-permute-start | bytes 98312 | tf_op jit(solution)/shard_map/ppermute | solution.py:88
  88.5 4.8 %collective-permute-start.30 = (bf16[128,128]{1,0:T(8,128)(2,1)S(1)}, bf16[128,128]{1,0:T(8,128)(2,1)S(1)}, u32[]{:S(2)}, u32[]{:S(2)}) collective-permute-start(bf16[128,128]{1,0:T(8,128)(2,1)S(1)} %get-tuple-element.119), channel_id=1, source_target_pairs={{0,8},{4,12},{8,0},{12,4},{1,9},{5,13},{9,1},{13,5},{2,10},{6,14},... | collective-permute-start | bytes 98312 | tf_op jit(solution)/shard_map/ppermute | solution.py:88
  90.3 5.7 %collective-permute-start.31 = (bf16[128,128]{1,0:T(8,128)(2,1)S(1)}, bf16[128,128]{1,0:T(8,128)(2,1)S(1)}, u32[]{:S(2)}, u32[]{:S(2)}) collective-permute-start(bf16[128,128]{1,0:T(8,128)(2,1)S(1)} %get-tuple-element.120), channel_id=1, source_target_pairs={{0,12},{4,8},{8,4},{12,0},{1,13},{5,9},{9,5},{13,1},{2,14},{6,10},... | collective-permute-start | bytes 98312 | tf_op jit(solution)/shard_map/ppermute | solution.py:88
  97.1 7.5 %collective-permute-start.32 = (bf16[256,128]{1,0:T(8,128)(2,1)S(1)}, bf16[256,128]{1,0:T(8,128)(2,1)S(1)}, u32[]{:S(2)}, u32[]{:S(2)}) collective-permute-start(bf16[256,128]{1,0:T(8,128)(2,1)S(1)} %get-tuple-element.122), channel_id=1, source_target_pairs={{0,4},{4,0},{8,12},{12,8},{1,5},{5,1},{9,13},{13,9},{2,6},{6,2},{1... | collective-permute-start | bytes 196616 | tf_op jit(solution)/shard_map/ppermute | solution.py:88
  97.2 8.8 %collective-permute-start.33 = (bf16[256,128]{1,0:T(8,128)(2,1)S(1)}, bf16[256,128]{1,0:T(8,128)(2,1)S(1)}, u32[]{:S(2)}, u32[]{:S(2)}) collective-permute-start(bf16[256,128]{1,0:T(8,128)(2,1)S(1)} %get-tuple-element.123), channel_id=1, source_target_pairs={{0,8},{4,12},{8,0},{12,4},{1,9},{5,13},{9,1},{13,5},{2,10},{6,14},... | collective-permute-start | bytes 196616 | tf_op jit(solution)/shard_map/ppermute | solution.py:88
  100.2 6.2 %collective-permute-start.34 = (bf16[256,128]{1,0:T(8,128)(2,1)S(1)}, bf16[256,128]{1,0:T(8,128)(2,1)S(1)}, u32[]{:S(2)}, u32[]{:S(2)}) collective-permute-start(bf16[256,128]{1,0:T(8,128)(2,1)S(1)} %get-tuple-element.124), channel_id=1, source_target_pairs={{0,12},{4,8},{8,4},{12,0},{1,13},{5,9},{9,5},{13,1},{2,14},{6,10},... | collective-permute-start | bytes 196616 | tf_op jit(solution)/shard_map/ppermute | solution.py:88
  101.6 6.7 %collective-permute-start.37 = (bf16[256,128]{1,0:T(8,128)(2,1)S(1)}, bf16[256,128]{1,0:T(8,128)(2,1)S(1)}, u32[]{:S(2)}, u32[]{:S(2)}) collective-permute-start(bf16[256,128]{1,0:T(8,128)(2,1)S(1)} %get-tuple-element.128), channel_id=1, source_target_pairs={{0,4},{4,0},{8,12},{12,8},{1,5},{5,1},{9,13},{13,9},{2,6},{6,2},{1... | collective-permute-start | bytes 196616 | tf_op jit(solution)/shard_map/ppermute | solution.py:88
  101.6 7.0 %collective-permute-start.38 = (bf16[256,128]{1,0:T(8,128)(2,1)S(1)}, bf16[256,128]{1,0:T(8,128)(2,1)S(1)}, u32[]{:S(2)}, u32[]{:S(2)}) collective-permute-start(bf16[256,128]{1,0:T(8,128)(2,1)S(1)} %get-tuple-element.129), channel_id=1, source_target_pairs={{0,8},{4,12},{8,0},{12,4},{1,9},{5,13},{9,1},{13,5},{2,10},{6,14},... | collective-permute-start | bytes 196616 | tf_op jit(solution)/shard_map/ppermute | solution.py:88
  104.6 6.1 %collective-permute-start.39 = (bf16[256,128]{1,0:T(8,128)(2,1)S(1)}, bf16[256,128]{1,0:T(8,128)(2,1)S(1)}, u32[]{:S(2)}, u32[]{:S(2)}) collective-permute-start(bf16[256,128]{1,0:T(8,128)(2,1)S(1)} %get-tuple-element.130), channel_id=1, source_target_pairs={{0,12},{4,8},{8,4},{12,0},{1,13},{5,9},{9,5},{13,1},{2,14},{6,10},... | collective-permute-start | bytes 196616 | tf_op jit(solution)/shard_map/ppermute | solution.py:88
  106.7 4.4 %collective-permute-start.35 = (bf16[256,128]{1,0:T(8,128)(2,1)S(1)}, bf16[256,128]{1,0:T(8,128)(2,1)S(1)}, u32[]{:S(2)}, u32[]{:S(2)}) collective-permute-start(bf16[256,128]{1,0:T(8,128)(2,1)S(1)} %get-tuple-element.125.refs_4_), channel_id=1, source_target_pairs={{0,2},{1,3},{2,0},{3,1},{4,6},{5,7},{6,4},{7,5},{8,10},{9,11},{10,... | collective-permute-start | bytes 196616 | tf_op jit(solution)/shard_map/ppermute | solution.py:85
  108.3 4.2 %collective-permute-start.36 = (bf16[256,128]{1,0:T(8,128)(2,1)S(1)}, bf16[256,128]{1,0:T(8,128)(2,1)S(1)}, u32[]{:S(2)}, u32[]{:S(2)}) collective-permute-start(bf16[256,128]{1,0:T(8,128)(2,1)S(1)} %get-tuple-element.126), channel_id=1, source_target_pairs={{0,3},{1,2},{2,1},{3,0},{4,7},{5,6},{6,5},{7,4},{8,11},{9,10},{10,... | collective-permute-start | bytes 196616 | tf_op jit(solution)/shard_map/ppermute | solution.py:85
  111.0 1.5 %collective-permute-start.40 = (bf16[256,128]{1,0:T(8,128)(2,1)S(1)}, bf16[256,128]{1,0:T(8,128)(2,1)S(1)}, u32[]{:S(2)}, u32[]{:S(2)}) collective-permute-start(bf16[256,128]{1,0:T(8,128)(2,1)S(1)} %get-tuple-element.132), channel_id=1, source_target_pairs={{0,1},{1,0},{2,3},{3,2},{4,5},{5,4},{6,7},{7,6},{8,9},{9,8},{10,11... | collective-permute-start | bytes 196616 | tf_op jit(solution)/shard_map/ppermute | solution.py:85

commit v7 on v6

--- a/solution.py
+++ b/solution.py
@@ -154,6 +154,7 @@
             edge_out_weight.shape[0],
             node_in_weight.shape[0],
         )
+        rows_edge, rows_mlp = rows_in + rows_out, rows_node + rows_out
         me = lax.axis_index(("feat", "rep")).astype(jnp.int32)
         dom = lax.axis_index("dom").astype(jnp.int32)
         me1 = me.reshape(1)
@@ -203,10 +204,10 @@
             far=range(5),
         )
 
-        state_parts = member_gather_chips(grid_state)
-        pack_parts = member_gather_chips(pack)
-
-        def hots_kernel(me_ref, send_ref, recv_ref, sl_out, sh_out, r_out, slt_out, sht_out, rt_out):
+        def hots_kernel(me_ref, state_ref, send_ref, recv_ref, *refs):
+            sl_out, sh_out, r_out, slt_out, sht_out, rt_out, state_out, sem = refs
+            copy = pltpu.make_async_copy(state_ref, state_out, sem)
+            copy.start()
             for i in range(E // T):
                 at = slice(i * T, (i + 1) * T)
                 sent, got = send_ref[:, at], recv_ref[:, at]
@@ -216,14 +217,26 @@
                 slt_out[:, at] = hot_columns(sent, N)
                 sht_out[:, at] = hot_columns(sent - N, NH)
                 rt_out[:, at] = hot_columns(got, N)
-
-        sl_hot, sh_hot, r_hot, slt_hot, sht_hot, rt_hot = call(
+            copy.wait()
+
+        sl_hot, sh_hot, r_hot, slt_hot, sht_hot, rt_hot, state_own = call(
             hots_kernel,
             "edge_hots",
             me1,
-            [send_row, recv_row],
-            [shape((E, N)), shape((E, NH)), shape((E, N)), shape((N, E)), shape((NH, E)), shape((N, E))],
-        )
+            [grid_state, send_row, recv_row],
+            [shape((E, N)), shape((E, NH)), shape((E, N)), shape((N, E)), shape((NH, E)), shape((N, E))]
+            + [shape((G, D))],
+            scratch=[pltpu.SemaphoreType.DMA(())],
+            far=(0,),
+        )
+
+        state_parts = [state_own] + [None] * (M - 1)
+        for kf in range(n_feat):
+            if kf:
+                state_parts[kf * n_rep] = member_swap(grid_state, kf * n_rep)
+            for kr in range(1, n_rep):
+                state_parts[kf * n_rep + kr] = member_swap(state_parts[kf * n_rep], kr)
+        pack_parts = member_gather_chips(pack)
 
         firsts = [kf * n_rep for kf in range(1, n_feat)]
 
@@ -236,12 +249,10 @@
 
         def grid_kernel(me_ref, *refs):
             states, packs = refs[:M], refs[M : 2 * M]
-            enc_out, slope_out, table_out, edge_out = refs[2 * M + 3 : 2 * M + 7]
-            outs, (own, sem, sems) = refs[2 * M + 7 : 2 * M + 7 + n_dom], refs[2 * M + 7 + n_dom :]
+            enc_out, slope_out, table_out, weights_out = refs[2 * M + 4 : 2 * M + 8]
+            outs, sems = refs[2 * M + 8 : 2 * M + 8 + n_dom], refs[-1]
             me = me_ref[0]
-            copy = pltpu.make_async_copy(states[0], own, sem)
-            copy.start()
-            weight_copies = stacked(refs[2 * M : 2 * M + 2], edge_out, sems)
+            weight_copies = stacked(refs[2 * M : 2 * M + 4], weights_out, sems)
             for each in weight_copies:
                 each.start()
             for k in range(M):
@@ -250,10 +261,8 @@
                 table_out[k, 0:1, :] = rows[0:1]
                 table_out[k, 1:2, :] = 2 * rows[1:2] + rows[2:3]
             enc_cols = dot(enc_out[...], column_pick(me, D, C)).astype(BF)
-            for k in list(range(1, M)) + [0]:
-                if k == 0:
-                    copy.wait()
-                pre = dot(states[k][...] if k else own[...], enc_cols)
+            for k in range(M):
+                pre = dot(states[k][...], enc_cols)
                 logistic = jax.nn.sigmoid(pre)
                 slope_out[k] = logistic * (1.0 + pre * (1.0 - logistic))
                 message = (pre * logistic).astype(BF)
@@ -263,21 +272,20 @@
             for each in weight_copies:
                 each.wait()
 
-        enc_full, grid_slope, slots, edge_own, *outgoing = call(
+        enc_full, grid_slope, slots, weights_own, *outgoing = call(
             grid_kernel,
             "grid_messages",
             me1,
-            state_parts + pack_parts + [edge_in_weight, edge_out_weight, sl_hot],
-            [shape((D, D)), shape((M, G, C), F32), shape((M, 2, NS), jnp.int32), shape((rows_in + rows_out, D))]
+            state_parts + pack_parts + [edge_in_weight, edge_out_weight, node_in_weight, node_out_weight],
+            [shape((D, D)), shape((M, G, C), F32), shape((M, 2, NS), jnp.int32), shape((rows_edge + rows_mlp, D))]
             + [shape((M * S, C))] * n_dom,
-            scratch=[pltpu.VMEM((G, D), BF), pltpu.SemaphoreType.DMA(()), pltpu.SemaphoreType.DMA((2,))],
+            scratch=[pltpu.SemaphoreType.DMA((4,))],
             flops=2 * M * G * D * C + 2 * M * NS * G * C,
-            far=(0, 2 * M, 2 * M + 1),
-            unread=(2 * M + 2,),
+            far=range(2 * M, 2 * M + 4),
         )
         incoming = dom_trade(outgoing)
         near, others = range(n_rep), range(n_rep, M)
-        edge_chips = [edge_own] + [member_swap(edge_own, k) for k in firsts]
+        weight_chips = [weights_own] + [member_swap(weights_own, k) for k in firsts]
 
         def encode_kernel(me_ref, base_ref, table_ref, *refs):
             arrived, state_out = refs[:n_dom], refs[-1]
@@ -318,31 +326,31 @@
                 refs[-1][kf] = refs[kf][...]
 
         def join_kernel(me_ref, *refs):
-            halo, chips, weights = refs[:n_dom], refs[n_dom : n_dom + n_feat], refs[n_dom + n_feat : -3]
-            halo_out_ref, pair_out, weights_out = refs[-3:]
+            halo, chips, weights = refs[:n_dom], refs[n_dom : n_dom + n_feat], refs[n_dom + n_feat : -4]
+            halo_out_ref, pair_out, edge_out, node_out = refs[-4:]
             for j in range(n_dom):
                 halo_out_ref[j * H : (j + 1) * H, :] = halo[j][...]
             for kf in range(n_feat):
                 pair_out[kf] = chips[kf][...]
-                weights_out[kf] = weights[kf][...]
-
-        halo_cols, state_pair, edge_pair = call(
+                edge_out[kf] = weights[kf][:rows_edge, :]
+                node_out[kf] = weights[kf][rows_edge:, :]
+
+        halo_cols, state_pair, edge_pair, node_pair = call(
             join_kernel,
             "halo_join",
             me1,
-            halo_in + state_chips + edge_chips,
-            [shape((NH, C)), shape((n_feat, N, C)), shape((n_feat, rows_in + rows_out, D))],
+            halo_in + state_chips + weight_chips,
+            [shape((NH, C)), shape((n_feat, N, C))]
+            + [shape((n_feat, rows_edge, D)), shape((n_feat, rows_mlp, D))],
         )
         halo_chips = [halo_cols] + [member_swap(halo_cols, k) for k in firsts]
         state_pairs = core_swaps(state_pair)
         edge_pairs = core_swaps(edge_pair)
-
-        def local_kernel(me_ref, in_ref, out_ref, es_ref, send_ref, recv_ref, *refs):
+        node_pairs = core_swaps(node_pair)
+
+        def local_kernel(me_ref, es_ref, send_ref, recv_ref, *refs):
             cols, weights = refs[:n_rep], refs[n_rep : 2 * n_rep]
-            pre_out, state_out, w_out, out_out, node_out, parts, sems = refs[2 * n_rep :]
-            copies = stacked([in_ref, out_ref], node_out, sems)
-            for copy in copies:
-                copy.start()
+            pre_out, state_out, w_out, out_out, parts = refs[2 * n_rep :]
             me = me_ref[0]
             for k in range(M):
                 kf, kr = divmod(k, n_rep)
@@ -359,21 +367,16 @@
                     + dot(sent, w_out[D : 2 * D, :])
                     + dot(got, w_out[2 * D :, :])
                 )
-            for copy in copies:
-                copy.wait()
-
-        local_pre, mesh_state, in_full, out_full, node_own = call(
+
+        local_pre, mesh_state, in_full, out_full = call(
             local_kernel,
             "edge_local",
             me1,
-            [node_in_weight, node_out_weight, edge_state, sl_hot, r_hot] + state_pairs + edge_pairs,
-            [shape((E, D), F32), shape((N, D)), shape((3 * D, D)), shape((D, D))]
-            + [shape((rows_node + rows_out, D))],
-            scratch=[pltpu.VMEM((M, N, C), BF), pltpu.SemaphoreType.DMA((2,))],
+            [edge_state, sl_hot, r_hot] + state_pairs + edge_pairs,
+            [shape((E, D), F32), shape((N, D)), shape((3 * D, D)), shape((D, D))],
+            scratch=[pltpu.VMEM((M, N, C), BF)],
             flops=2 * E * D * (3 * D + 2 * N),
-            far=range(2),
-        )
-        node_chips = [node_own] + [member_swap(node_own, k) for k in firsts]
+        )
 
         halo_pair = call(
             pair_kernel,
@@ -424,19 +427,9 @@
         )
         sums = member_sums(sums, me1, "node_sums")
 
-        node_pair = call(
-            pair_kernel,
-            "node_pair",
-            me1,
-            node_chips + [sums[0]],
-            [shape((n_feat, rows_node + rows_out, D))],
-            unread=(n_feat,),
-        )[0]
-        node_pairs = core_swaps(node_pair)
-
         def node_ahead_kernel(me_ref, state_ref, grad_ref, *refs):
             weights = refs[:n_rep]
-            node_in_full, pre_out, cot_out, node_out_full = refs[n_rep:]
+            node_in_full, pre_out, cot_out, node_out_full = refs[n_rep + 1 :]
             me = me_ref[0]
             for k in range(M):
                 kf, kr = divmod(k, n_rep)
@@ -450,10 +443,11 @@
             node_ahead_kernel,
             "node_ahead",
             me1,
-            [mesh_state, node_grad] + node_pairs,
+            [mesh_state, node_grad] + node_pairs + [sums[0]],
             [shape((2 * D, D)), shape((R, D), F32), shape((R, D), F32)],
             scratch=[pltpu.VMEM((D, D), BF)],
             flops=4 * R * D * D,
+            unread=(2 + n_rep,),
         )
 
         def node_kernel(me_ref, pre_ref, cot_ref, w_ref, grad_ref, *refs):

time: 114 us -> 107 us (0.939)
  waiting for transfers between devices: 49.3 us -> 43.5 us
  starting transfers between devices: 40.7 us -> 39.1 us
    ppermute x26 -> x25, waiting for transfers between devices: 28.8 us -> 22.9 us  [member_swap(): return lax.ppermute(x, ('feat', 'rep'), [(i, i ^ k) for i in range(M)])]
    ppermute x26 -> x25, starting transfers between devices: 18.1 us -> 16.9 us  [member_swap(): return lax.ppermute(x, ('feat', 'rep'), [(i, i ^ k) for i in range(M)])]
    pallas_call x23 -> x22, Pallas kernels: 22.6 us -> 23.1 us  [call(): pl.pallas_call(body, out_shape=list(outs), in_specs=[SMEM] + [HBM if i in...]
  transfers between devices with their start and end apart: 41 -> 40, of which waited for: 20 -> 19; matrix products, arithmetic and copies ran while one was open for 0% -> 0% of each run, Pallas kernels for 13% -> 14%
where the time goes in v7:
time: 107 us
  waiting for transfers between devices  43.5 us (41%)
  starting transfers between devices  39.1 us (37%)
  Pallas kernels  23.1 us (22%)
    pallas_call x22, Pallas kernels, call(): pl.pallas_call(body, out_shape=list(outs), in_specs=[SMEM] + [HBM if i in...  23.1 us
    ppermute x25, waiting for transfers between devices, member_swap(): return lax.ppermute(x, ('feat', 'rep'), [(i, i ^ k) for i in range(M)])  22.9 us
    ppermute x15, starting transfers between devices, dom_swap(): return lax.ppermute(x, 'dom', [(i, i ^ k) for i in range(n_dom)])  22.2 us
    ppermute x15, waiting for transfers between devices, dom_swap(): return lax.ppermute(x, 'dom', [(i, i ^ k) for i in range(n_dom)])  20.5 us
    ppermute x25, starting transfers between devices, member_swap(): return lax.ppermute(x, ('feat', 'rep'), [(i, i ^ k) for i in range(M)])  16.9 us
  transfers between devices with their start and end apart: 40, of which 19 were waited for; matrix products, arithmetic and copies ran while one was open for 0% of the time, Pallas kernels for 14%

profile of v7, /device:TPU:0, one launch (start us, length us, event | category | flops | bytes accessed | tf_op | source)
XLA Modules:
  0.0 106.7 jit_solution(1259868083925870903)
XLA Ops:
  0.0 2.9 %collective-permute-start.1 = (bf16[256,512]{1,0:T(8,128)(2,1)}, bf16[256,512]{1,0:T(8,128)(2,1)S(1)}, u32[]{:S(2)}, u32[]{:S(2)}) collective-permute-start(bf16[256,512]{1,0:T(8,128)(2,1)} %state_ref.1), channel_id=1, source_target_pairs={{0,2},{1,3},{2,0},{3,1},{4,6},{5,7},{6,4},{7,5},{8,10},{9,11},{10,... | collective-permute-start | bytes 786440 | tf_op jit(solution)/shard_map/ppermute | solution.py:85
  3.0 1.5 %tables.1 = (bf16[144,512]{1,0:T(8,128)(2,1)S(1)}, s32[1,512]{1,0:T(1,128)S(1)}, s32[1,1024]{1,0:T(1,128)S(1)}) custom-call(s32[2]{0:T(128)S(1)} %pad_add_fusion.where_ref, bf16[128,512]{1,0:T(8,128)(2,1)} %enc_ref.1, s32[1,4,128]{2,1,0:T(4,128)} %gs_ref.1, s32[1,4,128]{2,1,0:T(4,128)} %gr_ref.1, s32[1,4,128]{2,1,0:T(4,128)} %halo_ref.1, s32[1,1024]{1,0:T(1,128)} %bitcast.5), custom_call_target="tpu_custom_call" | custom-call | bytes 294912 | tf_op jit(solution)/shard_map/tables/pallas_call | solution.py:63
  4.6 0.7 copy-done.3
  5.3 2.1 %edge_hots.1 = (bf16[1024,512]{1,0:T(8,128)(2,1)S(1)}, bf16[1024,512]{1,0:T(8,128)(2,1)S(1)}, bf16[1024,512]{1,0:T(8,128)(2,1)S(1)}, bf16[512,1024]{1,0:T(8,128)...) custom-call(s32[1]{0:T(128)} %bitcast.me_ref, ...), custom_call_target="tpu_custom_call" | custom-call | bytes 6823936 | tf_op jit(solution)/shard_map/edge_hots/pallas_call | solution.py:63
  7.5 2.7 %collective-permute-done.1.refs_2_ = bf16[256,512]{1,0:T(8,128)(2,1)S(1)} collective-permute-done((bf16[256,512]{1,0:T(8,128)(2,1)}, bf16[256,512]{1,0:T(8,128)(2,1)S(1)}, u32[]{:S(2)}, u32[]{:S(2)}) %collective-permute-start.1) | collective-permute-done | bytes 262176 | tf_op jit(solution)/shard_map/ppermute | solution.py:85
  10.8 1.8 %collective-permute-done.4.refs_6_ = bf16[144,512]{1,0:T(8,128)(2,1)S(1)} collective-permute-done((bf16[144,512]{1,0:T(8,128)(2,1)S(1)}, bf16[144,512]{1,0:T(8,128)(2,1)S(1)}, u32[]{:S(2)}, u32[]{:S(2)}) %collective-permute-start.4) | collective-permute-done | bytes 147488 | tf_op jit(solution)/shard_map/ppermute | solution.py:85
  12.6 1.4 %collective-permute-done.5.refs_7_ = bf16[144,512]{1,0:T(8,128)(2,1)S(1)} collective-permute-done((bf16[144,512]{1,0:T(8,128)(2,1)S(1)}, bf16[144,512]{1,0:T(8,128)(2,1)S(1)}, u32[]{:S(2)}, u32[]{:S(2)}) %collective-permute-start.5) | collective-permute-done | bytes 147488 | tf_op jit(solution)/shard_map/ppermute | solution.py:85
  14.0 2.5 %grid_messages.1 = (bf16[512,512]{1,0:T(8,128)(2,1)S(1)}, f32[4,256,128]{2,1,0:T(8,128)S(1)}, s32[4,2,512]{2,1,0:T(2,128)S(1)}, bf16[896,512]{1,0:T(8,128)(2,1)S...) custom-call(s32[1]{0:T(128)} %bitcast.me_ref, ...), custom_call_target="tpu_custom_call" | custom-call | flops 268435456 | bytes 5062656 | tf_op jit(solution)/shard_map/grid_messages/pallas_call | solution.py:63
  16.5 1.8 %collective-permute-start.13 = (bf16[896,512]{1,0:T(8,128)(2,1)S(1)}, bf16[896,512]{1,0:T(8,128)(2,1)S(1)}, u32[]{:S(2)}, u32[]{:S(2)}) collective-permute-start(bf16[896,512]{1,0:T(8,128)(2,1)S(1)} %get-tuple-element.87.refs_6_), channel_id=1, source_target_pairs={{0,2},{1,3},{2,0},{3,1},{4,6},{5,7},{6,4},{7,5},{8,10},{9,11},{10,... | collective-permute-start | bytes 2752520 | tf_op jit(solution)/shard_map/ppermute | solution.py:85
  18.3 1.6 %collective-permute-start.6 = (bf16[512,128]{1,0:T(8,128)(2,1)S(1)}, bf16[512,128]{1,0:T(8,128)(2,1)S(1)}, u32[]{:S(2)}, u32[]{:S(2)}) collective-permute-start(bf16[512,128]{1,0:T(8,128)(2,1)S(1)} %get-tuple-element.80), channel_id=1, source_target_pairs={{0,4},{4,0},{8,12},{12,8},{1,5},{5,1},{9,13},{13,9},{2,6},{6,2},{1... | collective-permute-start | bytes 393224 | tf_op jit(solution)/shard_map/ppermute | solution.py:88
  19.9 2.6 %collective-permute-start.7 = (bf16[512,128]{1,0:T(8,128)(2,1)S(1)}, bf16[512,128]{1,0:T(8,128)(2,1)S(1)}, u32[]{:S(2)}, u32[]{:S(2)}) collective-permute-start(bf16[512,128]{1,0:T(8,128)(2,1)S(1)} %get-tuple-element.81), channel_id=1, source_target_pairs={{0,8},{4,12},{8,0},{12,4},{1,9},{5,13},{9,1},{13,5},{2,10},{6,14},... | collective-permute-start | bytes 393224 | tf_op jit(solution)/shard_map/ppermute | solution.py:88
  22.7 2.5 %collective-permute-done.6.refs_1_ = bf16[512,128]{1,0:T(8,128)(2,1)S(1)} collective-permute-done((bf16[512,128]{1,0:T(8,128)(2,1)S(1)}, bf16[512,128]{1,0:T(8,128)(2,1)S(1)}, u32[]{:S(2)}, u32[]{:S(2)}) %collective-permute-start.6) | collective-permute-done | bytes 131104 | tf_op jit(solution)/shard_map/ppermute | solution.py:88
  25.2 7.6 %collective-permute-done.7.refs_2_ = bf16[512,128]{1,0:T(8,128)(2,1)S(1)} collective-permute-done((bf16[512,128]{1,0:T(8,128)(2,1)S(1)}, bf16[512,128]{1,0:T(8,128)(2,1)S(1)}, u32[]{:S(2)}, u32[]{:S(2)}) %collective-permute-start.7) | collective-permute-done | bytes 131104 | tf_op jit(solution)/shard_map/ppermute | solution.py:88
  32.8 0.8 encode.1.state_ref.refs_4_
  34.8 2.0 %collective-permute-start.9 = (bf16[128,128]{1,0:T(8,128)(2,1)S(1)}, bf16[128,128]{1,0:T(8,128)(2,1)S(1)}, u32[]{:S(2)}, u32[]{:S(2)}) collective-permute-start(bf16[128,128]{1,0:T(8,128)(2,1)S(1)} %get-tuple-element.84), channel_id=1, source_target_pairs={{0,4},{4,0},{8,12},{12,8},{1,5},{5,1},{9,13},{13,9},{2,6},{6,2},{1... | collective-permute-start | bytes 98312 | tf_op jit(solution)/shard_map/ppermute | solution.py:88
  36.9 1.1 %collective-permute-start.10 = (bf16[128,128]{1,0:T(8,128)(2,1)S(1)}, bf16[128,128]{1,0:T(8,128)(2,1)S(1)}, u32[]{:S(2)}, u32[]{:S(2)}) collective-permute-start(bf16[128,128]{1,0:T(8,128)(2,1)S(1)} %get-tuple-element.85), channel_id=1, source_target_pairs={{0,8},{4,12},{8,0},{12,4},{1,9},{5,13},{9,1},{13,5},{2,10},{6,14},... | collective-permute-start | bytes 98312 | tf_op jit(solution)/shard_map/ppermute | solution.py:88
  38.0 1.4 %collective-permute-start.11 = (bf16[128,128]{1,0:T(8,128)(2,1)S(1)}, bf16[128,128]{1,0:T(8,128)(2,1)S(1)}, u32[]{:S(2)}, u32[]{:S(2)}) collective-permute-start(bf16[128,128]{1,0:T(8,128)(2,1)S(1)} %get-tuple-element.86), channel_id=1, source_target_pairs={{0,12},{4,8},{8,4},{12,0},{1,13},{5,9},{9,5},{13,1},{2,14},{6,10},... | collective-permute-start | bytes 98312 | tf_op jit(solution)/shard_map/ppermute | solution.py:88
  39.4 2.7 %collective-permute-done.10.refs_2_ = bf16[128,128]{1,0:T(8,128)(2,1)S(1)} collective-permute-done((bf16[128,128]{1,0:T(8,128)(2,1)S(1)}, bf16[128,128]{1,0:T(8,128)(2,1)S(1)}, u32[]{:S(2)}, u32[]{:S(2)}) %collective-permute-start.10) | collective-permute-done | bytes 32800 | tf_op jit(solution)/shard_map/ppermute | solution.py:88
  42.1 1.6 %collective-permute-done.11.refs_3_ = bf16[128,128]{1,0:T(8,128)(2,1)S(1)} collective-permute-done((bf16[128,128]{1,0:T(8,128)(2,1)S(1)}, bf16[128,128]{1,0:T(8,128)(2,1)S(1)}, u32[]{:S(2)}, u32[]{:S(2)}) %collective-permute-start.11) | collective-permute-done | bytes 32800 | tf_op jit(solution)/shard_map/ppermute | solution.py:88
  44.4 1.5 %collective-permute-start.16 = (bf16[512,128]{1,0:T(8,128)(2,1)S(1)}, bf16[512,128]{1,0:T(8,128)(2,1)S(1)}, u32[]{:S(2)}, u32[]{:S(2)}) collective-permute-start(bf16[512,128]{1,0:T(8,128)(2,1)S(1)} %get-tuple-element.95.refs_0_), channel_id=1, source_target_pairs={{0,2},{1,3},{2,0},{3,1},{4,6},{5,7},{6,4},{7,5},{8,10},{9,11},{10,... | collective-permute-start | bytes 393224 | tf_op jit(solution)/shard_map/ppermute | solution.py:85
  45.9 1.0 collective-permute-done.14.refs_1_
  47.0 3.0 %edge_local.1 = (f32[1024,512]{1,0:T(8,128)S(1)}, bf16[512,512]{1,0:T(8,128)(2,1)S(1)}, bf16[1536,512]{1,0:T(8,128)(2,1)S(1)}, bf16[512,512]{1,0:T(8,128)(2,1)S(1)}) custom-call(s32[1]{0:T(128)} %bitcast.me_ref, bf16[1024,512]{1,0:T(8,128)(2,1)S(1)} %copy-done.4, bf16[1024,512]{1,0:T(8,128)(2,1)S(1)} %get-tuple-element.77.send_ref, ...), custom_call_target="tpu_custom_call" | custom-call | flops 2684354560 | bytes 10485760 | tf_op jit(solution)/shard_map/edge_local/pallas_call | solution.py:63
  50.6 1.0 collective-permute-done.17.refs_1_
  51.6 3.1 %edge_update.1 = (f32[1024,512]{1,0:T(8,128)S(1)}, bf16[2,128,512]{2,1,0:T(8,128)(2,1)S(1)}, bf16[2,128,512]{2,1,0:T(8,128)(2,1)S(1)}) custom-call(s32[1]{0:T(128)} %bitcast.me_ref, f32[1024,512]{1,0:T(8,128)S(1)} %get-tuple-element.90.refs_2_.local_ref, bf16[1024,512]{1,0:T(8,128)(2,1)S(1)} %copy-done.4, bf16[1024,512]{1,0:T(8,128)(2,1)S(1)} %get-tuple-element.91.send_ref, ...), custom_call_target="tpu_custom_call" | custom-call | flops 2147483648 | bytes 10485760 | tf_op jit(solution)/shard_map/edge_update/pallas_call | solution.py:63
  54.9 1.4 %collective-permute-done.19.refs_1_ = bf16[2,128,512]{2,1,0:T(8,128)(2,1)S(1)} collective-permute-done((bf16[2,128,512]{2,1,0:T(8,128)(2,1)S(1)}, bf16[2,128,512]{2,1,0:T(8,128)(2,1)S(1)}, u32[]{:S(2)}, u32[]{:S(2)}) %collective-permute-start.19) | collective-permute-done | bytes 262176 | tf_op jit(solution)/shard_map/ppermute | solution.py:85
  56.4 1.6 %collective-permute-start.20 = (bf16[128,512]{1,0:T(8,128)(2,1)S(1)}, bf16[128,512]{1,0:T(8,128)(2,1)S(1)}, u32[]{:S(2)}, u32[]{:S(2)}) collective-permute-start(bf16[128,512]{1,0:T(8,128)(2,1)S(1)} %get-tuple-element.106), channel_id=1, source_target_pairs={{0,2},{1,3},{2,0},{3,1},{4,6},{5,7},{6,4},{7,5},{8,10},{9,11},{10,... | collective-permute-start | bytes 393224 | tf_op jit(solution)/shard_map/ppermute | solution.py:85
  58.4 3.6 %collective-permute-done.20.refs_1_ = bf16[128,512]{1,0:T(8,128)(2,1)S(1)} collective-permute-done((bf16[128,512]{1,0:T(8,128)(2,1)S(1)}, bf16[128,512]{1,0:T(8,128)(2,1)S(1)}, u32[]{:S(2)}, u32[]{:S(2)}) %collective-permute-start.20) | collective-permute-done | bytes 131104 | tf_op jit(solution)/shard_map/ppermute | solution.py:85
  62.6 1.6 %collective-permute-start.22 = (bf16[128,512]{1,0:T(8,128)(2,1)S(1)}, bf16[128,512]{1,0:T(8,128)(2,1)S(1)}, u32[]{:S(2)}, u32[]{:S(2)}) collective-permute-start(bf16[128,512]{1,0:T(8,128)(2,1)S(1)} %get-tuple-element.107.refs_0_), channel_id=1, source_target_pairs={{0,2},{1,3},{2,0},{3,1},{4,6},{5,7},{6,4},{7,5},{8,10},{9,11},{10,... | collective-permute-start | bytes 393224 | tf_op jit(solution)/shard_map/ppermute | solution.py:85
  64.2 3.5 %collective-permute-done.22.refs_2_ = bf16[128,512]{1,0:T(8,128)(2,1)S(1)} collective-permute-done((bf16[128,512]{1,0:T(8,128)(2,1)S(1)}, bf16[128,512]{1,0:T(8,128)(2,1)S(1)}, u32[]{:S(2)}, u32[]{:S(2)}) %collective-permute-start.22) | collective-permute-done | bytes 131104 | tf_op jit(solution)/shard_map/ppermute | solution.py:85
  67.7 1.3 %collective-permute-done.23.refs_3_ = bf16[128,512]{1,0:T(8,128)(2,1)S(1)} collective-permute-done((bf16[128,512]{1,0:T(8,128)(2,1)S(1)}, bf16[128,512]{1,0:T(8,128)(2,1)S(1)}, u32[]{:S(2)}, u32[]{:S(2)}) %collective-permute-start.23) | collective-permute-done | bytes 131104 | tf_op jit(solution)/shard_map/ppermute | solution.py:85
  69.0 2.9 %edge_backward.1 = (bf16[1024,512]{1,0:T(8,128)(2,1)S(1)}, bf16[2,512,128]{2,1,0:T(8,128)(2,1)S(1)}, bf16[2,512,128]{2,1,0:T(8,128)(2,1)S(1)}) custom-call(s32[1]{0:T(128)} %bitcast.me_ref, bf16[1024,512]{1,0:T(8,128)(2,1)S(1)} %copy-done.1, f32[1024,512]{1,0:T(8,128)S(1)} %get-tuple-element.96.pre_ref, bf16[512,1024]{1,0:T(8,128)(2,1)S(1)} %get-tuple-element.97.send_ref, ...), custom_call_target="tpu_custom_call" | custom-call | flops 1879048192 | bytes 9437184 | tf_op jit(solution)/shard_map/edge_backward/pallas_call | solution.py:63
  72.1 2.1 %local_backward.1 = (bf16[2,512,128]{2,1,0:T(8,128)(2,1)S(1)}, bf16[2,512,128]{2,1,0:T(8,128)(2,1)S(1)}) custom-call(s32[1]{0:T(128)} %bitcast.me_ref, bf16[1024,512]{1,0:T(8,128)(2,1)S(1)} %get-tuple-element.108.dpre_ref, bf16[512,1024]{1,0:T(8,128)(2,1)S(1)} %get-tuple-element.109.send_ref, bf16[512,1024]{1,0:T(8,128)(2,1)S(1)} %get-tuple-element.92.recv_ref, ...), custom_call_target="tpu_custom_call" | custom-call | flops 1610612736 | bytes 5505024 | tf_op jit(solution)/shard_map/local_backward/pallas_call | solution.py:63
  74.7 1.6 %collective-permute-start.27 = (bf16[512,128]{1,0:T(8,128)(2,1)S(1)}, bf16[512,128]{1,0:T(8,128)(2,1)S(1)}, u32[]{:S(2)}, u32[]{:S(2)}) collective-permute-start(bf16[512,128]{1,0:T(8,128)(2,1)S(1)} %get-tuple-element.118), channel_id=1, source_target_pairs={{0,2},{1,3},{2,0},{3,1},{4,6},{5,7},{6,4},{7,5},{8,10},{9,11},{10,... | collective-permute-start | bytes 393224 | tf_op jit(solution)/shard_map/ppermute | solution.py:85
  76.4 1.1 %collective-permute-start.25 = (bf16[512,128]{1,0:T(8,128)(2,1)S(1)}, bf16[512,128]{1,0:T(8,128)(2,1)S(1)}, u32[]{:S(2)}, u32[]{:S(2)}) collective-permute-start(bf16[512,128]{1,0:T(8,128)(2,1)S(1)} %get-tuple-element.114), channel_id=1, source_target_pairs={{0,2},{1,3},{2,0},{3,1},{4,6},{5,7},{6,4},{7,5},{8,10},{9,11},{10,... | collective-permute-start | bytes 393224 | tf_op jit(solution)/shard_map/ppermute | solution.py:85
  77.5 3.7 %collective-permute-done.27.refs_1_ = bf16[512,128]{1,0:T(8,128)(2,1)S(1)} collective-permute-done((bf16[512,128]{1,0:T(8,128)(2,1)S(1)}, bf16[512,128]{1,0:T(8,128)(2,1)S(1)}, u32[]{:S(2)}, u32[]{:S(2)}) %collective-permute-start.27) | collective-permute-done | bytes 131104 | tf_op jit(solution)/shard_map/ppermute | solution.py:85
  81.4 2.3 %collective-permute-start.29 = (bf16[128,128]{1,0:T(8,128)(2,1)S(1)}, bf16[128,128]{1,0:T(8,128)(2,1)S(1)}, u32[]{:S(2)}, u32[]{:S(2)}) collective-permute-start(bf16[128,128]{1,0:T(8,128)(2,1)S(1)} %get-tuple-element.121), channel_id=1, source_target_pairs={{0,8},{4,12},{8,0},{12,4},{1,9},{5,13},{9,1},{13,5},{2,10},{6,14},... | collective-permute-start | bytes 98312 | tf_op jit(solution)/shard_map/ppermute | solution.py:88
  83.8 1.9 %collective-permute-start.30 = (bf16[128,128]{1,0:T(8,128)(2,1)S(1)}, bf16[128,128]{1,0:T(8,128)(2,1)S(1)}, u32[]{:S(2)}, u32[]{:S(2)}) collective-permute-start(bf16[128,128]{1,0:T(8,128)(2,1)S(1)} %get-tuple-element.122), channel_id=1, source_target_pairs={{0,12},{4,8},{8,4},{12,0},{1,13},{5,9},{9,5},{13,1},{2,14},{6,10},... | collective-permute-start | bytes 98312 | tf_op jit(solution)/shard_map/ppermute | solution.py:88
  85.6 0.9 collective-permute-done.29.refs_4_
  86.6 2.9 %collective-permute-done.30.refs_5_ = bf16[128,128]{1,0:T(8,128)(2,1)S(1)} collective-permute-done((bf16[128,128]{1,0:T(8,128)(2,1)S(1)}, bf16[128,128]{1,0:T(8,128)(2,1)S(1)}, u32[]{:S(2)}, u32[]{:S(2)}) %collective-permute-start.30) | collective-permute-done | bytes 32800 | tf_op jit(solution)/shard_map/ppermute | solution.py:88
  89.5 1.2 %owed_rows.1 = (bf16[256,128]{1,0:T(8,128)(2,1)S(1)}, bf16[256,128]{1,0:T(8,128)(2,1)S(1)}, bf16[256,128]{1,0:T(8,128)(2,1)S(1)}, bf16[256,128]{1,0:T(8,128)(2,1...) custom-call(s32[1]{0:T(128)} %bitcast.me_ref, ...), custom_call_target="tpu_custom_call" | custom-call | flops 268435456 | bytes 935936 | tf_op jit(solution)/shard_map/owed_rows/pallas_call | solution.py:63
  90.7 2.5 %collective-permute-start.32 = (bf16[256,128]{1,0:T(8,128)(2,1)S(1)}, bf16[256,128]{1,0:T(8,128)(2,1)S(1)}, u32[]{:S(2)}, u32[]{:S(2)}) collective-permute-start(bf16[256,128]{1,0:T(8,128)(2,1)S(1)} %get-tuple-element.125), channel_id=1, source_target_pairs={{0,8},{4,12},{8,0},{12,4},{1,9},{5,13},{9,1},{13,5},{2,10},{6,14},... | collective-permute-start | bytes 196616 | tf_op jit(solution)/shard_map/ppermute | solution.py:88
  93.2 1.9 %collective-permute-start.33 = (bf16[256,128]{1,0:T(8,128)(2,1)S(1)}, bf16[256,128]{1,0:T(8,128)(2,1)S(1)}, u32[]{:S(2)}, u32[]{:S(2)}) collective-permute-start(bf16[256,128]{1,0:T(8,128)(2,1)S(1)} %get-tuple-element.126), channel_id=1, source_target_pairs={{0,12},{4,8},{8,4},{12,0},{1,13},{5,9},{9,5},{13,1},{2,14},{6,10},... | collective-permute-start | bytes 196616 | tf_op jit(solution)/shard_map/ppermute | solution.py:88
  95.1 2.5 %collective-permute-start.37 = (bf16[256,128]{1,0:T(8,128)(2,1)S(1)}, bf16[256,128]{1,0:T(8,128)(2,1)S(1)}, u32[]{:S(2)}, u32[]{:S(2)}) collective-permute-start(bf16[256,128]{1,0:T(8,128)(2,1)S(1)} %get-tuple-element.131), channel_id=1, source_target_pairs={{0,8},{4,12},{8,0},{12,4},{1,9},{5,13},{9,1},{13,5},{2,10},{6,14},... | collective-permute-start | bytes 196616 | tf_op jit(solution)/shard_map/ppermute | solution.py:88
  97.6 1.9 %collective-permute-start.38 = (bf16[256,128]{1,0:T(8,128)(2,1)S(1)}, bf16[256,128]{1,0:T(8,128)(2,1)S(1)}, u32[]{:S(2)}, u32[]{:S(2)}) collective-permute-start(bf16[256,128]{1,0:T(8,128)(2,1)S(1)} %get-tuple-element.132), channel_id=1, source_target_pairs={{0,12},{4,8},{8,4},{12,0},{1,13},{5,9},{9,5},{13,1},{2,14},{6,10},... | collective-permute-start | bytes 196616 | tf_op jit(solution)/shard_map/ppermute | solution.py:88
  99.8 1.6 %collective-permute-start.34 = (bf16[256,128]{1,0:T(8,128)(2,1)S(1)}, bf16[256,128]{1,0:T(8,128)(2,1)S(1)}, u32[]{:S(2)}, u32[]{:S(2)}) collective-permute-start(bf16[256,128]{1,0:T(8,128)(2,1)S(1)} %get-tuple-element.127.refs_4_), channel_id=1, source_target_pairs={{0,2},{1,3},{2,0},{3,1},{4,6},{5,7},{6,4},{7,5},{8,10},{9,11},{10,... | collective-permute-start | bytes 196616 | tf_op jit(solution)/shard_map/ppermute | solution.py:85
  101.4 2.3 %collective-permute-done.38.refs_3_ = bf16[256,128]{1,0:T(8,128)(2,1)S(1)} collective-permute-done((bf16[256,128]{1,0:T(8,128)(2,1)S(1)}, bf16[256,128]{1,0:T(8,128)(2,1)S(1)}, u32[]{:S(2)}, u32[]{:S(2)}) %collective-permute-start.38) | collective-permute-done | bytes 65568 | tf_op jit(solution)/shard_map/ppermute | solution.py:88
  104.1 1.4 %collective-permute-done.35.refs_1_ = bf16[256,128]{1,0:T(8,128)(2,1)S(1)} collective-permute-done((bf16[256,128]{1,0:T(8,128)(2,1)S(1)}, bf16[256,128]{1,0:T(8,128)(2,1)S(1)}, u32[]{:S(2)}, u32[]{:S(2)}) %collective-permute-start.35) | collective-permute-done | bytes 65568 | tf_op jit(solution)/shard_map/ppermute | solution.py:85
  105.6 1.1 %adjoint.1 = f32[256,512]{1,0:T(8,128)} custom-call(s32[1]{0:T(128)} %bitcast.me_ref, bf16[512,512]{1,0:T(8,128)(2,1)S(1)} %get-tuple-element.73.enc_ref, bf16[2,256,128]{2,1,0:T(8,128)(2,1)S(1)} %far_join.1.far_ref, bf16[256,128]{1,0:T(8,128)(2,1)S(1)} %get-tuple-element.133.refs_2_.refs_0_, bf16[256,128]{1,0:T(8,128)(2,1)S(1)} %collective-permute-done.39.refs_1_), custom_call_target="tpu_custom_call" | custom-call | flops 134217728 | bytes 1310720 | tf_op jit(solution)/shard_map/adjoint/pallas_call | solution.py:63
  (65 shorter events, 6.8 us)
Async XLA Ops:
  0.0 32.8 %copy-start.2 = (bf16[512,512]{1,0:T(8,128)(2,1)S(1)}, bf16[512,512]{1,0:T(8,128)(2,1)}, u32[]{:S(2)}) copy-start(bf16[512,512]{1,0:T(8,128)(2,1)} %base_ref.1) | copy-start | bytes 1572868
  0.0 10.3 %collective-permute-start.1 = (bf16[256,512]{1,0:T(8,128)(2,1)}, bf16[256,512]{1,0:T(8,128)(2,1)S(1)}, u32[]{:S(2)}, u32[]{:S(2)}) collective-permute-start(bf16[256,512]{1,0:T(8,128)(2,1)} %state_ref.1), channel_id=1, source_target_pairs={{0,2},{1,3},{2,0},{3,1},{4,6},{5,7},{6,4},{7,5},{8,10},{9,11},{10,... | collective-permute-start | bytes 786440 | tf_op jit(solution)/shard_map/ppermute | solution.py:85
  4.5 8.1 %collective-permute-start.4 = (bf16[144,512]{1,0:T(8,128)(2,1)S(1)}, bf16[144,512]{1,0:T(8,128)(2,1)S(1)}, u32[]{:S(2)}, u32[]{:S(2)}) collective-permute-start(bf16[144,512]{1,0:T(8,128)(2,1)S(1)} %get-tuple-element.72.refs_4_), channel_id=1, source_target_pairs={{0,2},{1,3},{2,0},{3,1},{4,6},{5,7},{6,4},{7,5},{8,10},{9,11},{10,... | collective-permute-start | bytes 442376 | tf_op jit(solution)/shard_map/ppermute | solution.py:85
  4.6 0.7 copy-start.3
  7.5 5.2 %collective-permute-start = (bf16[256,512]{1,0:T(8,128)(2,1)S(1)}, bf16[256,512]{1,0:T(8,128)(2,1)S(1)}, u32[]{:S(2)}, u32[]{:S(2)}) collective-permute-start(bf16[256,512]{1,0:T(8,128)(2,1)S(1)} %get-tuple-element.71.refs_0_), channel_id=1, source_target_pairs={{0,1},{1,0},{2,3},{3,2},{4,5},{5,4},{6,7},{7,6},{8,9},{9,8},{10,11... | collective-permute-start | bytes 786440 | tf_op jit(solution)/shard_map/ppermute | solution.py:85
  10.3 3.7 %collective-permute-start.2 = (bf16[256,512]{1,0:T(8,128)(2,1)S(1)}, bf16[256,512]{1,0:T(8,128)(2,1)S(1)}, u32[]{:S(2)}, u32[]{:S(2)}) collective-permute-start(bf16[256,512]{1,0:T(8,128)(2,1)S(1)} %collective-permute-done.1.refs_2_), channel_id=1, source_target_pairs={{0,1},{1,0},{2,3},{3,2},{4,5},{5,4},{6,7},{7,6},{8,9},{9,8},{10,11... | collective-permute-start | bytes 786440 | tf_op jit(solution)/shard_map/ppermute | solution.py:85
  10.3 2.3 %collective-permute-start.3 = (bf16[144,512]{1,0:T(8,128)(2,1)S(1)}, bf16[144,512]{1,0:T(8,128)(2,1)S(1)}, u32[]{:S(2)}, u32[]{:S(2)}) collective-permute-start(bf16[144,512]{1,0:T(8,128)(2,1)S(1)} %get-tuple-element.72.refs_4_), channel_id=1, source_target_pairs={{0,1},{1,0},{2,3},{3,2},{4,5},{5,4},{6,7},{7,6},{8,9},{9,8},{10,11... | collective-permute-start | bytes 442376 | tf_op jit(solution)/shard_map/ppermute | solution.py:85
  12.6 1.4 %collective-permute-start.5 = (bf16[144,512]{1,0:T(8,128)(2,1)S(1)}, bf16[144,512]{1,0:T(8,128)(2,1)S(1)}, u32[]{:S(2)}, u32[]{:S(2)}) collective-permute-start(bf16[144,512]{1,0:T(8,128)(2,1)S(1)} %collective-permute-done.4.refs_6_), channel_id=1, source_target_pairs={{0,1},{1,0},{2,3},{3,2},{4,5},{5,4},{6,7},{7,6},{8,9},{9,8},{10,11... | collective-permute-start | bytes 442376 | tf_op jit(solution)/shard_map/ppermute | solution.py:85
  16.5 30.5 %copy-start.4 = (bf16[1024,512]{1,0:T(8,128)(2,1)S(1)}, bf16[1024,512]{1,0:T(8,128)(2,1)}, u32[]{:S(2)}) copy-start(bf16[1024,512]{1,0:T(8,128)(2,1)} %es_ref.3) | copy-start | bytes 3145732
  16.5 27.2 %collective-permute-start.13 = (bf16[896,512]{1,0:T(8,128)(2,1)S(1)}, bf16[896,512]{1,0:T(8,128)(2,1)S(1)}, u32[]{:S(2)}, u32[]{:S(2)}) collective-permute-start(bf16[896,512]{1,0:T(8,128)(2,1)S(1)} %get-tuple-element.87.refs_6_), channel_id=1, source_target_pairs={{0,2},{1,3},{2,0},{3,1},{4,6},{5,7},{6,4},{7,5},{8,10},{9,11},{10,... | collective-permute-start | bytes 2752520 | tf_op jit(solution)/shard_map/ppermute | solution.py:85
  18.3 6.9 %collective-permute-start.6 = (bf16[512,128]{1,0:T(8,128)(2,1)S(1)}, bf16[512,128]{1,0:T(8,128)(2,1)S(1)}, u32[]{:S(2)}, u32[]{:S(2)}) collective-permute-start(bf16[512,128]{1,0:T(8,128)(2,1)S(1)} %get-tuple-element.80), channel_id=1, source_target_pairs={{0,4},{4,0},{8,12},{12,8},{1,5},{5,1},{9,13},{13,9},{2,6},{6,2},{1... | collective-permute-start | bytes 393224 | tf_op jit(solution)/shard_map/ppermute | solution.py:88
  19.9 12.9 %collective-permute-start.7 = (bf16[512,128]{1,0:T(8,128)(2,1)S(1)}, bf16[512,128]{1,0:T(8,128)(2,1)S(1)}, u32[]{:S(2)}, u32[]{:S(2)}) collective-permute-start(bf16[512,128]{1,0:T(8,128)(2,1)S(1)} %get-tuple-element.81), channel_id=1, source_target_pairs={{0,8},{4,12},{8,0},{12,4},{1,9},{5,13},{9,1},{13,5},{2,10},{6,14},... | collective-permute-start | bytes 393224 | tf_op jit(solution)/shard_map/ppermute | solution.py:88
  22.5 10.4 %collective-permute-start.8 = (bf16[512,128]{1,0:T(8,128)(2,1)S(1)}, bf16[512,128]{1,0:T(8,128)(2,1)S(1)}, u32[]{:S(2)}, u32[]{:S(2)}) collective-permute-start(bf16[512,128]{1,0:T(8,128)(2,1)S(1)} %get-tuple-element.82), channel_id=1, source_target_pairs={{0,12},{4,8},{8,4},{12,0},{1,13},{5,9},{9,5},{13,1},{2,14},{6,10},... | collective-permute-start | bytes 393224 | tf_op jit(solution)/shard_map/ppermute | solution.py:88
  33.7 10.0 %collective-permute-start.12 = (bf16[512,128]{1,0:T(8,128)(2,1)S(1)}, bf16[512,128]{1,0:T(8,128)(2,1)S(1)}, u32[]{:S(2)}, u32[]{:S(2)}) collective-permute-start(bf16[512,128]{1,0:T(8,128)(2,1)S(1)} %encode.1.state_ref.refs_4_), channel_id=1, source_target_pairs={{0,2},{1,3},{2,0},{3,1},{4,6},{5,7},{6,4},{7,5},{8,10},{9,11},{10,... | collective-permute-start | bytes 393224 | tf_op jit(solution)/shard_map/ppermute | solution.py:85
  34.8 4.5 %collective-permute-start.9 = (bf16[128,128]{1,0:T(8,128)(2,1)S(1)}, bf16[128,128]{1,0:T(8,128)(2,1)S(1)}, u32[]{:S(2)}, u32[]{:S(2)}) collective-permute-start(bf16[128,128]{1,0:T(8,128)(2,1)S(1)} %get-tuple-element.84), channel_id=1, source_target_pairs={{0,4},{4,0},{8,12},{12,8},{1,5},{5,1},{9,13},{13,9},{2,6},{6,2},{1... | collective-permute-start | bytes 98312 | tf_op jit(solution)/shard_map/ppermute | solution.py:88
  36.9 5.2 %collective-permute-start.10 = (bf16[128,128]{1,0:T(8,128)(2,1)S(1)}, bf16[128,128]{1,0:T(8,128)(2,1)S(1)}, u32[]{:S(2)}, u32[]{:S(2)}) collective-permute-start(bf16[128,128]{1,0:T(8,128)(2,1)S(1)} %get-tuple-element.85), channel_id=1, source_target_pairs={{0,8},{4,12},{8,0},{12,4},{1,9},{5,13},{9,1},{13,5},{2,10},{6,14},... | collective-permute-start | bytes 98312 | tf_op jit(solution)/shard_map/ppermute | solution.py:88
  38.0 5.7 %collective-permute-start.11 = (bf16[128,128]{1,0:T(8,128)(2,1)S(1)}, bf16[128,128]{1,0:T(8,128)(2,1)S(1)}, u32[]{:S(2)}, u32[]{:S(2)}) collective-permute-start(bf16[128,128]{1,0:T(8,128)(2,1)S(1)} %get-tuple-element.86), channel_id=1, source_target_pairs={{0,12},{4,8},{8,4},{12,0},{1,13},{5,9},{9,5},{13,1},{2,14},{6,10},... | collective-permute-start | bytes 98312 | tf_op jit(solution)/shard_map/ppermute | solution.py:88
  43.8 3.1 %collective-permute-start.15 = (bf16[2,512,512]{2,1,0:T(8,128)(2,1)S(1)}, bf16[2,512,512]{2,1,0:T(8,128)(2,1)S(1)}, u32[]{:S(2)}, u32[]{:S(2)}) collective-permute-start(bf16[2,512,512]{2,1,0:T(8,128)(2,1)S(1)} %get-tuple-element.89.refs_2_), channel_id=1, source_target_pairs={{0,1},{1,0},{2,3},{3,2},{4,5},{5,4},{6,7},{7,6},{8,9},{9,8},{10,11... | collective-permute-start | bytes 3145736 | tf_op jit(solution)/shard_map/ppermute | solution.py:85
  43.9 3.0 %collective-permute-start.14 = (bf16[2,512,128]{2,1,0:T(8,128)(2,1)S(1)}, bf16[2,512,128]{2,1,0:T(8,128)(2,1)S(1)}, u32[]{:S(2)}, u32[]{:S(2)}) collective-permute-start(bf16[2,512,128]{2,1,0:T(8,128)(2,1)S(1)} %get-tuple-element.88.refs_0_), channel_id=1, source_target_pairs={{0,1},{1,0},{2,3},{3,2},{4,5},{5,4},{6,7},{7,6},{8,9},{9,8},{10,11... | collective-permute-start | bytes 786440 | tf_op jit(solution)/shard_map/ppermute | solution.py:85
  44.4 5.5 %collective-permute-start.16 = (bf16[512,128]{1,0:T(8,128)(2,1)S(1)}, bf16[512,128]{1,0:T(8,128)(2,1)S(1)}, u32[]{:S(2)}, u32[]{:S(2)}) collective-permute-start(bf16[512,128]{1,0:T(8,128)(2,1)S(1)} %get-tuple-element.95.refs_0_), channel_id=1, source_target_pairs={{0,2},{1,3},{2,0},{3,1},{4,6},{5,7},{6,4},{7,5},{8,10},{9,11},{10,... | collective-permute-start | bytes 393224 | tf_op jit(solution)/shard_map/ppermute | solution.py:85
  50.0 1.6 %collective-permute-start.17 = (bf16[2,512,128]{2,1,0:T(8,128)(2,1)S(1)}, bf16[2,512,128]{2,1,0:T(8,128)(2,1)S(1)}, u32[]{:S(2)}, u32[]{:S(2)}) collective-permute-start(bf16[2,512,128]{2,1,0:T(8,128)(2,1)S(1)} %halo_pair.1.refs_0_), channel_id=1, source_target_pairs={{0,1},{1,0},{2,3},{3,2},{4,5},{5,4},{6,7},{7,6},{8,9},{9,8},{10,11... | collective-permute-start | bytes 786440 | tf_op jit(solution)/shard_map/ppermute | solution.py:85
  50.2 7.7 %collective-permute-start.18 = (bf16[2,384,512]{2,1,0:T(8,128)(2,1)S(1)}, bf16[2,384,512]{2,1,0:T(8,128)(2,1)S(1)}, u32[]{:S(2)}, u32[]{:S(2)}) collective-permute-start(bf16[2,384,512]{2,1,0:T(8,128)(2,1)S(1)} %get-tuple-element.99.refs_0_), channel_id=1, source_target_pairs={{0,1},{1,0},{2,3},{3,2},{4,5},{5,4},{6,7},{7,6},{8,9},{9,8},{10,11... | collective-permute-start | bytes 2359304 | tf_op jit(solution)/shard_map/ppermute | solution.py:85
  51.6 6.3 %copy-start = (bf16[512,512]{1,0:T(8,128)(2,1)S(1)}, bf16[512,512]{1,0:T(8,128)(2,1)}, u32[]{:S(2)}) copy-start(bf16[512,512]{1,0:T(8,128)(2,1)} %grad_ref.4) | copy-start | bytes 1572868
  54.7 1.6 %collective-permute-start.19 = (bf16[2,128,512]{2,1,0:T(8,128)(2,1)S(1)}, bf16[2,128,512]{2,1,0:T(8,128)(2,1)S(1)}, u32[]{:S(2)}, u32[]{:S(2)}) collective-permute-start(bf16[2,128,512]{2,1,0:T(8,128)(2,1)S(1)} %get-tuple-element.101), channel_id=1, source_target_pairs={{0,1},{1,0},{2,3},{3,2},{4,5},{5,4},{6,7},{7,6},{8,9},{9,8},{10,11... | collective-permute-start | bytes 786440 | tf_op jit(solution)/shard_map/ppermute | solution.py:85
  56.4 5.6 %collective-permute-start.20 = (bf16[128,512]{1,0:T(8,128)(2,1)S(1)}, bf16[128,512]{1,0:T(8,128)(2,1)S(1)}, u32[]{:S(2)}, u32[]{:S(2)}) collective-permute-start(bf16[128,512]{1,0:T(8,128)(2,1)S(1)} %get-tuple-element.106), channel_id=1, source_target_pairs={{0,2},{1,3},{2,0},{3,1},{4,6},{5,7},{6,4},{7,5},{8,10},{9,11},{10,... | collective-permute-start | bytes 393224 | tf_op jit(solution)/shard_map/ppermute | solution.py:85
  57.9 11.1 %copy-start.1 = (bf16[1024,512]{1,0:T(8,128)(2,1)S(1)}, bf16[1024,512]{1,0:T(8,128)(2,1)}, u32[]{:S(2)}) copy-start(bf16[1024,512]{1,0:T(8,128)(2,1)} %grad_ref.5) | copy-start | bytes 3145732
  62.6 5.0 %collective-permute-start.22 = (bf16[128,512]{1,0:T(8,128)(2,1)S(1)}, bf16[128,512]{1,0:T(8,128)(2,1)S(1)}, u32[]{:S(2)}, u32[]{:S(2)}) collective-permute-start(bf16[128,512]{1,0:T(8,128)(2,1)S(1)} %get-tuple-element.107.refs_0_), channel_id=1, source_target_pairs={{0,2},{1,3},{2,0},{3,1},{4,6},{5,7},{6,4},{7,5},{8,10},{9,11},{10,... | collective-permute-start | bytes 393224 | tf_op jit(solution)/shard_map/ppermute | solution.py:85
  64.2 3.5 %collective-permute-start.21 = (bf16[128,512]{1,0:T(8,128)(2,1)S(1)}, bf16[128,512]{1,0:T(8,128)(2,1)S(1)}, u32[]{:S(2)}, u32[]{:S(2)}) collective-permute-start(bf16[128,512]{1,0:T(8,128)(2,1)S(1)} %get-tuple-element.107.refs_0_), channel_id=1, source_target_pairs={{0,1},{1,0},{2,3},{3,2},{4,5},{5,4},{6,7},{7,6},{8,9},{9,8},{10,11... | collective-permute-start | bytes 393224 | tf_op jit(solution)/shard_map/ppermute | solution.py:85
  67.7 1.3 %collective-permute-start.23 = (bf16[128,512]{1,0:T(8,128)(2,1)S(1)}, bf16[128,512]{1,0:T(8,128)(2,1)S(1)}, u32[]{:S(2)}, u32[]{:S(2)}) collective-permute-start(bf16[128,512]{1,0:T(8,128)(2,1)S(1)} %collective-permute-done.22.refs_2_), channel_id=1, source_target_pairs={{0,1},{1,0},{2,3},{3,2},{4,5},{5,4},{6,7},{7,6},{8,9},{9,8},{10,11... | collective-permute-start | bytes 393224 | tf_op jit(solution)/shard_map/ppermute | solution.py:85
  71.9 2.7 %collective-permute-start.26 = (bf16[2,512,128]{2,1,0:T(8,128)(2,1)S(1)}, bf16[2,512,128]{2,1,0:T(8,128)(2,1)S(1)}, u32[]{:S(2)}, u32[]{:S(2)}) collective-permute-start(bf16[2,512,128]{2,1,0:T(8,128)(2,1)S(1)} %get-tuple-element.116), channel_id=1, source_target_pairs={{0,1},{1,0},{2,3},{3,2},{4,5},{5,4},{6,7},{7,6},{8,9},{9,8},{10,11... | collective-permute-start | bytes 786440 | tf_op jit(solution)/shard_map/ppermute | solution.py:85
  74.2 2.1 %collective-permute-start.24 = (bf16[2,512,128]{2,1,0:T(8,128)(2,1)S(1)}, bf16[2,512,128]{2,1,0:T(8,128)(2,1)S(1)}, u32[]{:S(2)}, u32[]{:S(2)}) collective-permute-start(bf16[2,512,128]{2,1,0:T(8,128)(2,1)S(1)} %get-tuple-element.112), channel_id=1, source_target_pairs={{0,1},{1,0},{2,3},{3,2},{4,5},{5,4},{6,7},{7,6},{8,9},{9,8},{10,11... | collective-permute-start | bytes 786440 | tf_op jit(solution)/shard_map/ppermute | solution.py:85
  74.7 6.4 %collective-permute-start.27 = (bf16[512,128]{1,0:T(8,128)(2,1)S(1)}, bf16[512,128]{1,0:T(8,128)(2,1)S(1)}, u32[]{:S(2)}, u32[]{:S(2)}) collective-permute-start(bf16[512,128]{1,0:T(8,128)(2,1)S(1)} %get-tuple-element.118), channel_id=1, source_target_pairs={{0,2},{1,3},{2,0},{3,1},{4,6},{5,7},{6,4},{7,5},{8,10},{9,11},{10,... | collective-permute-start | bytes 393224 | tf_op jit(solution)/shard_map/ppermute | solution.py:85
  76.4 9.3 %collective-permute-start.25 = (bf16[512,128]{1,0:T(8,128)(2,1)S(1)}, bf16[512,128]{1,0:T(8,128)(2,1)S(1)}, u32[]{:S(2)}, u32[]{:S(2)}) collective-permute-start(bf16[512,128]{1,0:T(8,128)(2,1)S(1)} %get-tuple-element.114), channel_id=1, source_target_pairs={{0,2},{1,3},{2,0},{3,1},{4,6},{5,7},{6,4},{7,5},{8,10},{9,11},{10,... | collective-permute-start | bytes 393224 | tf_op jit(solution)/shard_map/ppermute | solution.py:85
  81.2 4.5 %collective-permute-start.28 = (bf16[128,128]{1,0:T(8,128)(2,1)S(1)}, bf16[128,128]{1,0:T(8,128)(2,1)S(1)}, u32[]{:S(2)}, u32[]{:S(2)}) collective-permute-start(bf16[128,128]{1,0:T(8,128)(2,1)S(1)} %get-tuple-element.120), channel_id=1, source_target_pairs={{0,4},{4,0},{8,12},{12,8},{1,5},{5,1},{9,13},{13,9},{2,6},{6,2},{1... | collective-permute-start | bytes 98312 | tf_op jit(solution)/shard_map/ppermute | solution.py:88
  81.4 5.2 %collective-permute-start.29 = (bf16[128,128]{1,0:T(8,128)(2,1)S(1)}, bf16[128,128]{1,0:T(8,128)(2,1)S(1)}, u32[]{:S(2)}, u32[]{:S(2)}) collective-permute-start(bf16[128,128]{1,0:T(8,128)(2,1)S(1)} %get-tuple-element.121), channel_id=1, source_target_pairs={{0,8},{4,12},{8,0},{12,4},{1,9},{5,13},{9,1},{13,5},{2,10},{6,14},... | collective-permute-start | bytes 98312 | tf_op jit(solution)/shard_map/ppermute | solution.py:88
  83.8 5.7 %collective-permute-start.30 = (bf16[128,128]{1,0:T(8,128)(2,1)S(1)}, bf16[128,128]{1,0:T(8,128)(2,1)S(1)}, u32[]{:S(2)}, u32[]{:S(2)}) collective-permute-start(bf16[128,128]{1,0:T(8,128)(2,1)S(1)} %get-tuple-element.122), channel_id=1, source_target_pairs={{0,12},{4,8},{8,4},{12,0},{1,13},{5,9},{9,5},{13,1},{2,14},{6,10},... | collective-permute-start | bytes 98312 | tf_op jit(solution)/shard_map/ppermute | solution.py:88
  90.6 6.9 %collective-permute-start.31 = (bf16[256,128]{1,0:T(8,128)(2,1)S(1)}, bf16[256,128]{1,0:T(8,128)(2,1)S(1)}, u32[]{:S(2)}, u32[]{:S(2)}) collective-permute-start(bf16[256,128]{1,0:T(8,128)(2,1)S(1)} %get-tuple-element.124), channel_id=1, source_target_pairs={{0,4},{4,0},{8,12},{12,8},{1,5},{5,1},{9,13},{13,9},{2,6},{6,2},{1... | collective-permute-start | bytes 196616 | tf_op jit(solution)/shard_map/ppermute | solution.py:88
  90.7 8.8 %collective-permute-start.32 = (bf16[256,128]{1,0:T(8,128)(2,1)S(1)}, bf16[256,128]{1,0:T(8,128)(2,1)S(1)}, u32[]{:S(2)}, u32[]{:S(2)}) collective-permute-start(bf16[256,128]{1,0:T(8,128)(2,1)S(1)} %get-tuple-element.125), channel_id=1, source_target_pairs={{0,8},{4,12},{8,0},{12,4},{1,9},{5,13},{9,1},{13,5},{2,10},{6,14},... | collective-permute-start | bytes 196616 | tf_op jit(solution)/shard_map/ppermute | solution.py:88
  93.2 6.3 %collective-permute-start.33 = (bf16[256,128]{1,0:T(8,128)(2,1)S(1)}, bf16[256,128]{1,0:T(8,128)(2,1)S(1)}, u32[]{:S(2)}, u32[]{:S(2)}) collective-permute-start(bf16[256,128]{1,0:T(8,128)(2,1)S(1)} %get-tuple-element.126), channel_id=1, source_target_pairs={{0,12},{4,8},{8,4},{12,0},{1,13},{5,9},{9,5},{13,1},{2,14},{6,10},... | collective-permute-start | bytes 196616 | tf_op jit(solution)/shard_map/ppermute | solution.py:88
  95.1 6.3 %collective-permute-start.36 = (bf16[256,128]{1,0:T(8,128)(2,1)S(1)}, bf16[256,128]{1,0:T(8,128)(2,1)S(1)}, u32[]{:S(2)}, u32[]{:S(2)}) collective-permute-start(bf16[256,128]{1,0:T(8,128)(2,1)S(1)} %get-tuple-element.130), channel_id=1, source_target_pairs={{0,4},{4,0},{8,12},{12,8},{1,5},{5,1},{9,13},{13,9},{2,6},{6,2},{1... | collective-permute-start | bytes 196616 | tf_op jit(solution)/shard_map/ppermute | solution.py:88
  95.1 6.3 %collective-permute-start.37 = (bf16[256,128]{1,0:T(8,128)(2,1)S(1)}, bf16[256,128]{1,0:T(8,128)(2,1)S(1)}, u32[]{:S(2)}, u32[]{:S(2)}) collective-permute-start(bf16[256,128]{1,0:T(8,128)(2,1)S(1)} %get-tuple-element.131), channel_id=1, source_target_pairs={{0,8},{4,12},{8,0},{12,4},{1,9},{5,13},{9,1},{13,5},{2,10},{6,14},... | collective-permute-start | bytes 196616 | tf_op jit(solution)/shard_map/ppermute | solution.py:88
  97.6 6.1 %collective-permute-start.38 = (bf16[256,128]{1,0:T(8,128)(2,1)S(1)}, bf16[256,128]{1,0:T(8,128)(2,1)S(1)}, u32[]{:S(2)}, u32[]{:S(2)}) collective-permute-start(bf16[256,128]{1,0:T(8,128)(2,1)S(1)} %get-tuple-element.132), channel_id=1, source_target_pairs={{0,12},{4,8},{8,4},{12,0},{1,13},{5,9},{9,5},{13,1},{2,14},{6,10},... | collective-permute-start | bytes 196616 | tf_op jit(solution)/shard_map/ppermute | solution.py:88
  99.8 4.3 %collective-permute-start.34 = (bf16[256,128]{1,0:T(8,128)(2,1)S(1)}, bf16[256,128]{1,0:T(8,128)(2,1)S(1)}, u32[]{:S(2)}, u32[]{:S(2)}) collective-permute-start(bf16[256,128]{1,0:T(8,128)(2,1)S(1)} %get-tuple-element.127.refs_4_), channel_id=1, source_target_pairs={{0,2},{1,3},{2,0},{3,1},{4,6},{5,7},{6,4},{7,5},{8,10},{9,11},{10,... | collective-permute-start | bytes 196616 | tf_op jit(solution)/shard_map/ppermute | solution.py:85
  101.4 4.2 %collective-permute-start.35 = (bf16[256,128]{1,0:T(8,128)(2,1)S(1)}, bf16[256,128]{1,0:T(8,128)(2,1)S(1)}, u32[]{:S(2)}, u32[]{:S(2)}) collective-permute-start(bf16[256,128]{1,0:T(8,128)(2,1)S(1)} %get-tuple-element.128), channel_id=1, source_target_pairs={{0,3},{1,2},{2,1},{3,0},{4,7},{5,6},{6,5},{7,4},{8,11},{9,10},{10,... | collective-permute-start | bytes 196616 | tf_op jit(solution)/shard_map/ppermute | solution.py:85
  104.0 1.6 %collective-permute-start.39 = (bf16[256,128]{1,0:T(8,128)(2,1)S(1)}, bf16[256,128]{1,0:T(8,128)(2,1)S(1)}, u32[]{:S(2)}, u32[]{:S(2)}) collective-permute-start(bf16[256,128]{1,0:T(8,128)(2,1)S(1)} %get-tuple-element.134), channel_id=1, source_target_pairs={{0,1},{1,0},{2,3},{3,2},{4,5},{5,4},{6,7},{7,6},{8,9},{9,8},{10,11... | collective-permute-start | bytes 196616 | tf_op jit(solution)/shard_map/ppermute | solution.py:85

commit v8 on v7

--- a/solution.py
+++ b/solution.py
@@ -116,7 +116,11 @@
         return [halves[0]] + [member_swap(halves[kf], kf * n_rep) for kf in range(1, n_feat)]
 
     def dom_trade(parts):
-        return [parts[0]] + [dom_swap(parts[k], k) for k in range(1, n_dom)]
+        swapped = [dom_swap(parts[k], k) for k in reversed(range(1, n_dom))]
+        return [parts[0]] + swapped[::-1]
+
+    def far_first(parts):
+        return [parts[0]] + list(parts[:0:-1])
 
     def per_device(
         grid_state,
@@ -288,7 +292,7 @@
         weight_chips = [weights_own] + [member_swap(weights_own, k) for k in firsts]
 
         def encode_kernel(me_ref, base_ref, table_ref, *refs):
-            arrived, state_out = refs[:n_dom], refs[-1]
+            arrived, state_out = far_first(refs[:n_dom]), refs[-1]
             total = dot(base_ref[...], column_pick(me_ref[0], D, C))
             for k in range(M):
                 rows = stack([arrived[j][k * S : (k + 1) * S, :] for j in range(n_dom)])
@@ -299,7 +303,7 @@
             encode_kernel,
             "encode",
             me1,
-            [mesh_base, slots] + incoming,
+            [mesh_base, slots] + far_first(incoming),
             [shape((N, C))],
             flops=2 * M * N * NS * C,
         )[0]
@@ -326,7 +330,7 @@
                 refs[-1][kf] = refs[kf][...]
 
         def join_kernel(me_ref, *refs):
-            halo, chips, weights = refs[:n_dom], refs[n_dom : n_dom + n_feat], refs[n_dom + n_feat : -4]
+            halo, chips, weights = far_first(refs[:n_dom]), refs[n_dom : n_dom + n_feat], refs[n_dom + n_feat : -4]
             halo_out_ref, pair_out, edge_out, node_out = refs[-4:]
             for j in range(n_dom):
                 halo_out_ref[j * H : (j + 1) * H, :] = halo[j][...]
@@ -339,7 +343,7 @@
             join_kernel,
             "halo_join",
             me1,
-            halo_in + state_chips + weight_chips,
+            far_first(halo_in) + state_chips + weight_chips,
             [shape((NH, C)), shape((n_feat, N, C))]
             + [shape((n_feat, rows_edge, D)), shape((n_feat, rows_mlp, D))],
         )
@@ -541,7 +545,7 @@
         halo_back = dom_trade(halo_back)
 
         def owed_kernel(me_ref, halo_ref, table_ref, *refs):
-            local, back = refs[:n_feat], refs[n_feat : n_feat + n_dom]
+            local, back = refs[:n_feat], far_first(refs[n_feat : n_feat + n_dom])
             first, second = refs[n_feat + n_dom : -n_dom], refs[-n_dom:]
             total = local[0][...].astype(F32)
             for k in range(1, n_feat):
@@ -558,7 +562,7 @@
             owed_kernel,
             "owed_rows",
             me1,
-            [halo_row, slots] + local_grads + halo_back,
+            [halo_row, slots] + local_grads + far_first(halo_back),
             [shape((n_rep * S, C))] * n_dom + [shape((len(others) * S, C))] * n_dom,
             flops=2 * M * NS * N * C,
         )
@@ -574,13 +578,13 @@
             def kernel(me_ref, slope_ref, table_ref, *refs):
                 outs = refs[n_dom + len(after) :]
                 for at, k in enumerate(members):
-                    outs[at][...] = cotangents(table_ref, slope_ref, refs[:n_dom], at, k)
+                    outs[at][...] = cotangents(table_ref, slope_ref, far_first(refs[:n_dom]), at, k)
 
             return call(
                 kernel,
                 name,
                 me1,
-                [grid_slope, slots] + back + after,
+                [grid_slope, slots] + far_first(back) + after,
                 [shape((G, C))] * len(members),
                 flops=2 * len(members) * G * NS * C,
                 unread=range(2 + n_dom, 2 + n_dom + len(after)),

time: 107 us -> 106 us (level)
  starting transfers between devices: 39.1 us -> 38 us
    ppermute x25, waiting for transfers between devices: 22.9 us -> 24.3 us  [member_swap(): return lax.ppermute(x, ('feat', 'rep'), [(i, i ^ k) for i in range(M)])]
    ppermute x15, starting transfers between devices: 22.2 us -> 21.1 us  [dom_swap(): return lax.ppermute(x, 'dom', [(i, i ^ k) for i in range(n_dom)])]
  transfers between devices with their start and end apart: 40 -> 40, of which waited for: 19 -> 21; matrix products, arithmetic and copies ran while one was open for 0% -> 0% of each run, Pallas kernels for 14% -> 14%
where the time goes in v8:
time: 106 us
  waiting for transfers between devices  43.9 us (41%)
  starting transfers between devices  38 us (36%)
  Pallas kernels  23.1 us (22%)
    ppermute x25, waiting for transfers between devices, member_swap(): return lax.ppermute(x, ('feat', 'rep'), [(i, i ^ k) for i in range(M)])  24.3 us
    pallas_call x22, Pallas kernels, call(): pl.pallas_call(body, out_shape=list(outs), in_specs=[SMEM] + [HBM if i in...  23.1 us
    ppermute x15, starting transfers between devices, dom_swap(): return lax.ppermute(x, 'dom', [(i, i ^ k) for i in range(n_dom)])  21.1 us
    ppermute x15, waiting for transfers between devices, dom_swap(): return lax.ppermute(x, 'dom', [(i, i ^ k) for i in range(n_dom)])  19.6 us
    ppermute x25, starting transfers between devices, member_swap(): return lax.ppermute(x, ('feat', 'rep'), [(i, i ^ k) for i in range(M)])  16.9 us
  transfers between devices with their start and end apart: 40, of which 21 were waited for; matrix products, arithmetic and copies ran while one was open for 0% of the time, Pallas kernels for 14%

profile of v8, /device:TPU:0, one launch (start us, length us, event | category | flops | bytes accessed | tf_op | source)
XLA Modules:
  0.0 106.0 jit_solution(13615723182804483299)
XLA Ops:
  0.0 2.9 %collective-permute-start.1 = (bf16[256,512]{1,0:T(8,128)(2,1)}, bf16[256,512]{1,0:T(8,128)(2,1)S(1)}, u32[]{:S(2)}, u32[]{:S(2)}) collective-permute-start(bf16[256,512]{1,0:T(8,128)(2,1)} %state_ref.1), channel_id=1, source_target_pairs={{0,2},{1,3},{2,0},{3,1},{4,6},{5,7},{6,4},{7,5},{8,10},{9,11},{10,... | collective-permute-start | bytes 786440 | tf_op jit(solution)/shard_map/ppermute | solution.py:85
  3.0 1.5 %tables.1 = (bf16[144,512]{1,0:T(8,128)(2,1)S(1)}, s32[1,512]{1,0:T(1,128)S(1)}, s32[1,1024]{1,0:T(1,128)S(1)}) custom-call(s32[2]{0:T(128)S(1)} %pad_add_fusion.where_ref, bf16[128,512]{1,0:T(8,128)(2,1)} %enc_ref.1, s32[1,4,128]{2,1,0:T(4,128)} %gs_ref.1, s32[1,4,128]{2,1,0:T(4,128)} %gr_ref.1, s32[1,4,128]{2,1,0:T(4,128)} %halo_ref.1, s32[1,1024]{1,0:T(1,128)} %bitcast.5), custom_call_target="tpu_custom_call" | custom-call | bytes 294912 | tf_op jit(solution)/shard_map/tables/pallas_call | solution.py:63
  5.3 2.1 %edge_hots.1 = (bf16[1024,512]{1,0:T(8,128)(2,1)S(1)}, bf16[1024,512]{1,0:T(8,128)(2,1)S(1)}, bf16[1024,512]{1,0:T(8,128)(2,1)S(1)}, bf16[512,1024]{1,0:T(8,128)...) custom-call(s32[1]{0:T(128)} %bitcast.me_ref, ...), custom_call_target="tpu_custom_call" | custom-call | bytes 6823936 | tf_op jit(solution)/shard_map/edge_hots/pallas_call | solution.py:63
  7.5 2.7 %collective-permute-done.1.refs_2_ = bf16[256,512]{1,0:T(8,128)(2,1)S(1)} collective-permute-done((bf16[256,512]{1,0:T(8,128)(2,1)}, bf16[256,512]{1,0:T(8,128)(2,1)S(1)}, u32[]{:S(2)}, u32[]{:S(2)}) %collective-permute-start.1) | collective-permute-done | bytes 262176 | tf_op jit(solution)/shard_map/ppermute | solution.py:85
  10.8 1.8 %collective-permute-done.4.refs_6_ = bf16[144,512]{1,0:T(8,128)(2,1)S(1)} collective-permute-done((bf16[144,512]{1,0:T(8,128)(2,1)S(1)}, bf16[144,512]{1,0:T(8,128)(2,1)S(1)}, u32[]{:S(2)}, u32[]{:S(2)}) %collective-permute-start.4) | collective-permute-done | bytes 147488 | tf_op jit(solution)/shard_map/ppermute | solution.py:85
  12.6 1.4 %collective-permute-done.5.refs_7_ = bf16[144,512]{1,0:T(8,128)(2,1)S(1)} collective-permute-done((bf16[144,512]{1,0:T(8,128)(2,1)S(1)}, bf16[144,512]{1,0:T(8,128)(2,1)S(1)}, u32[]{:S(2)}, u32[]{:S(2)}) %collective-permute-start.5) | collective-permute-done | bytes 147488 | tf_op jit(solution)/shard_map/ppermute | solution.py:85
  14.0 2.5 %grid_messages.1 = (bf16[512,512]{1,0:T(8,128)(2,1)S(1)}, f32[4,256,128]{2,1,0:T(8,128)S(1)}, s32[4,2,512]{2,1,0:T(2,128)S(1)}, bf16[896,512]{1,0:T(8,128)(2,1)S...) custom-call(s32[1]{0:T(128)} %bitcast.me_ref, ...), custom_call_target="tpu_custom_call" | custom-call | flops 268435456 | bytes 5062656 | tf_op jit(solution)/shard_map/grid_messages/pallas_call | solution.py:63
  16.5 1.8 %collective-permute-start.13 = (bf16[896,512]{1,0:T(8,128)(2,1)S(1)}, bf16[896,512]{1,0:T(8,128)(2,1)S(1)}, u32[]{:S(2)}, u32[]{:S(2)}) collective-permute-start(bf16[896,512]{1,0:T(8,128)(2,1)S(1)} %get-tuple-element.87.refs_6_), channel_id=1, source_target_pairs={{0,2},{1,3},{2,0},{3,1},{4,6},{5,7},{6,4},{7,5},{8,10},{9,11},{10,... | collective-permute-start | bytes 2752520 | tf_op jit(solution)/shard_map/ppermute | solution.py:85
  18.3 3.6 %collective-permute-start.6 = (bf16[512,128]{1,0:T(8,128)(2,1)S(1)}, bf16[512,128]{1,0:T(8,128)(2,1)S(1)}, u32[]{:S(2)}, u32[]{:S(2)}) collective-permute-start(bf16[512,128]{1,0:T(8,128)(2,1)S(1)} %get-tuple-element.80), channel_id=1, source_target_pairs={{0,12},{4,8},{8,4},{12,0},{1,13},{5,9},{9,5},{13,1},{2,14},{6,10},... | collective-permute-start | bytes 393224 | tf_op jit(solution)/shard_map/ppermute | solution.py:88
  21.9 0.8 collective-permute-start.8
  22.7 3.8 %collective-permute-done.6.refs_1_ = bf16[512,128]{1,0:T(8,128)(2,1)S(1)} collective-permute-done((bf16[512,128]{1,0:T(8,128)(2,1)S(1)}, bf16[512,128]{1,0:T(8,128)(2,1)S(1)}, u32[]{:S(2)}, u32[]{:S(2)}) %collective-permute-start.6) | collective-permute-done | bytes 131104 | tf_op jit(solution)/shard_map/ppermute | solution.py:88
  26.5 6.5 %collective-permute-done.7.refs_2_ = bf16[512,128]{1,0:T(8,128)(2,1)S(1)} collective-permute-done((bf16[512,128]{1,0:T(8,128)(2,1)S(1)}, bf16[512,128]{1,0:T(8,128)(2,1)S(1)}, u32[]{:S(2)}, u32[]{:S(2)}) %collective-permute-start.7) | collective-permute-done | bytes 131104 | tf_op jit(solution)/shard_map/ppermute | solution.py:88
  33.0 0.8 encode.1.state_ref.refs_4_
  35.0 2.5 %collective-permute-start.9 = (bf16[128,128]{1,0:T(8,128)(2,1)S(1)}, bf16[128,128]{1,0:T(8,128)(2,1)S(1)}, u32[]{:S(2)}, u32[]{:S(2)}) collective-permute-start(bf16[128,128]{1,0:T(8,128)(2,1)S(1)} %get-tuple-element.84), channel_id=1, source_target_pairs={{0,12},{4,8},{8,4},{12,0},{1,13},{5,9},{9,5},{13,1},{2,14},{6,10},... | collective-permute-start | bytes 98312 | tf_op jit(solution)/shard_map/ppermute | solution.py:88
  37.6 1.9 %collective-permute-start.11 = (bf16[128,128]{1,0:T(8,128)(2,1)S(1)}, bf16[128,128]{1,0:T(8,128)(2,1)S(1)}, u32[]{:S(2)}, u32[]{:S(2)}) collective-permute-start(bf16[128,128]{1,0:T(8,128)(2,1)S(1)} %get-tuple-element.86), channel_id=1, source_target_pairs={{0,4},{4,0},{8,12},{12,8},{1,5},{5,1},{9,13},{13,9},{2,6},{6,2},{1... | collective-permute-start | bytes 98312 | tf_op jit(solution)/shard_map/ppermute | solution.py:88
  39.5 1.4 %collective-permute-done.9.refs_1_ = bf16[128,128]{1,0:T(8,128)(2,1)S(1)} collective-permute-done((bf16[128,128]{1,0:T(8,128)(2,1)S(1)}, bf16[128,128]{1,0:T(8,128)(2,1)S(1)}, u32[]{:S(2)}, u32[]{:S(2)}) %collective-permute-start.9) | collective-permute-done | bytes 32800 | tf_op jit(solution)/shard_map/ppermute | solution.py:88
  40.9 1.5 %collective-permute-done.10.refs_2_ = bf16[128,128]{1,0:T(8,128)(2,1)S(1)} collective-permute-done((bf16[128,128]{1,0:T(8,128)(2,1)S(1)}, bf16[128,128]{1,0:T(8,128)(2,1)S(1)}, u32[]{:S(2)}, u32[]{:S(2)}) %collective-permute-start.10) | collective-permute-done | bytes 32800 | tf_op jit(solution)/shard_map/ppermute | solution.py:88
  43.1 1.5 %collective-permute-start.16 = (bf16[512,128]{1,0:T(8,128)(2,1)S(1)}, bf16[512,128]{1,0:T(8,128)(2,1)S(1)}, u32[]{:S(2)}, u32[]{:S(2)}) collective-permute-start(bf16[512,128]{1,0:T(8,128)(2,1)S(1)} %get-tuple-element.95.refs_0_), channel_id=1, source_target_pairs={{0,2},{1,3},{2,0},{3,1},{4,6},{5,7},{6,4},{7,5},{8,10},{9,11},{10,... | collective-permute-start | bytes 393224 | tf_op jit(solution)/shard_map/ppermute | solution.py:85
  44.6 1.0 collective-permute-done.14.refs_1_
  45.7 3.0 %edge_local.1 = (f32[1024,512]{1,0:T(8,128)S(1)}, bf16[512,512]{1,0:T(8,128)(2,1)S(1)}, bf16[1536,512]{1,0:T(8,128)(2,1)S(1)}, bf16[512,512]{1,0:T(8,128)(2,1)S(1)}) custom-call(s32[1]{0:T(128)} %bitcast.me_ref, bf16[1024,512]{1,0:T(8,128)(2,1)S(1)} %copy-done.4, bf16[1024,512]{1,0:T(8,128)(2,1)S(1)} %get-tuple-element.77.send_ref, ...), custom_call_target="tpu_custom_call" | custom-call | flops 2684354560 | bytes 10485760 | tf_op jit(solution)/shard_map/edge_local/pallas_call | solution.py:63
  49.3 1.0 collective-permute-done.17.refs_1_
  50.3 3.1 %edge_update.1 = (f32[1024,512]{1,0:T(8,128)S(1)}, bf16[2,128,512]{2,1,0:T(8,128)(2,1)S(1)}, bf16[2,128,512]{2,1,0:T(8,128)(2,1)S(1)}) custom-call(s32[1]{0:T(128)} %bitcast.me_ref, f32[1024,512]{1,0:T(8,128)S(1)} %get-tuple-element.90.refs_2_.local_ref, bf16[1024,512]{1,0:T(8,128)(2,1)S(1)} %copy-done.4, bf16[1024,512]{1,0:T(8,128)(2,1)S(1)} %get-tuple-element.91.send_ref, ...), custom_call_target="tpu_custom_call" | custom-call | flops 2147483648 | bytes 10485760 | tf_op jit(solution)/shard_map/edge_update/pallas_call | solution.py:63
  53.6 1.4 %collective-permute-done.19.refs_1_ = bf16[2,128,512]{2,1,0:T(8,128)(2,1)S(1)} collective-permute-done((bf16[2,128,512]{2,1,0:T(8,128)(2,1)S(1)}, bf16[2,128,512]{2,1,0:T(8,128)(2,1)S(1)}, u32[]{:S(2)}, u32[]{:S(2)}) %collective-permute-start.19) | collective-permute-done | bytes 262176 | tf_op jit(solution)/shard_map/ppermute | solution.py:85
  55.1 1.6 %collective-permute-start.20 = (bf16[128,512]{1,0:T(8,128)(2,1)S(1)}, bf16[128,512]{1,0:T(8,128)(2,1)S(1)}, u32[]{:S(2)}, u32[]{:S(2)}) collective-permute-start(bf16[128,512]{1,0:T(8,128)(2,1)S(1)} %get-tuple-element.106), channel_id=1, source_target_pairs={{0,2},{1,3},{2,0},{3,1},{4,6},{5,7},{6,4},{7,5},{8,10},{9,11},{10,... | collective-permute-start | bytes 393224 | tf_op jit(solution)/shard_map/ppermute | solution.py:85
  57.1 3.6 %collective-permute-done.20.refs_1_ = bf16[128,512]{1,0:T(8,128)(2,1)S(1)} collective-permute-done((bf16[128,512]{1,0:T(8,128)(2,1)S(1)}, bf16[128,512]{1,0:T(8,128)(2,1)S(1)}, u32[]{:S(2)}, u32[]{:S(2)}) %collective-permute-start.20) | collective-permute-done | bytes 131104 | tf_op jit(solution)/shard_map/ppermute | solution.py:85
  61.3 1.6 %collective-permute-start.22 = (bf16[128,512]{1,0:T(8,128)(2,1)S(1)}, bf16[128,512]{1,0:T(8,128)(2,1)S(1)}, u32[]{:S(2)}, u32[]{:S(2)}) collective-permute-start(bf16[128,512]{1,0:T(8,128)(2,1)S(1)} %get-tuple-element.107.refs_0_), channel_id=1, source_target_pairs={{0,2},{1,3},{2,0},{3,1},{4,6},{5,7},{6,4},{7,5},{8,10},{9,11},{10,... | collective-permute-start | bytes 393224 | tf_op jit(solution)/shard_map/ppermute | solution.py:85
  62.9 3.5 %collective-permute-done.22.refs_2_ = bf16[128,512]{1,0:T(8,128)(2,1)S(1)} collective-permute-done((bf16[128,512]{1,0:T(8,128)(2,1)S(1)}, bf16[128,512]{1,0:T(8,128)(2,1)S(1)}, u32[]{:S(2)}, u32[]{:S(2)}) %collective-permute-start.22) | collective-permute-done | bytes 131104 | tf_op jit(solution)/shard_map/ppermute | solution.py:85
  66.4 1.3 %collective-permute-done.23.refs_3_ = bf16[128,512]{1,0:T(8,128)(2,1)S(1)} collective-permute-done((bf16[128,512]{1,0:T(8,128)(2,1)S(1)}, bf16[128,512]{1,0:T(8,128)(2,1)S(1)}, u32[]{:S(2)}, u32[]{:S(2)}) %collective-permute-start.23) | collective-permute-done | bytes 131104 | tf_op jit(solution)/shard_map/ppermute | solution.py:85
  67.7 2.9 %edge_backward.1 = (bf16[1024,512]{1,0:T(8,128)(2,1)S(1)}, bf16[2,512,128]{2,1,0:T(8,128)(2,1)S(1)}, bf16[2,512,128]{2,1,0:T(8,128)(2,1)S(1)}) custom-call(s32[1]{0:T(128)} %bitcast.me_ref, bf16[1024,512]{1,0:T(8,128)(2,1)S(1)} %copy-done.1, f32[1024,512]{1,0:T(8,128)S(1)} %get-tuple-element.96.pre_ref, bf16[512,1024]{1,0:T(8,128)(2,1)S(1)} %get-tuple-element.97.send_ref, ...), custom_call_target="tpu_custom_call" | custom-call | flops 1879048192 | bytes 9437184 | tf_op jit(solution)/shard_map/edge_backward/pallas_call | solution.py:63
  70.9 2.1 %local_backward.1 = (bf16[2,512,128]{2,1,0:T(8,128)(2,1)S(1)}, bf16[2,512,128]{2,1,0:T(8,128)(2,1)S(1)}) custom-call(s32[1]{0:T(128)} %bitcast.me_ref, bf16[1024,512]{1,0:T(8,128)(2,1)S(1)} %get-tuple-element.108.dpre_ref, bf16[512,1024]{1,0:T(8,128)(2,1)S(1)} %get-tuple-element.109.send_ref, bf16[512,1024]{1,0:T(8,128)(2,1)S(1)} %get-tuple-element.92.recv_ref, ...), custom_call_target="tpu_custom_call" | custom-call | flops 1610612736 | bytes 5505024 | tf_op jit(solution)/shard_map/local_backward/pallas_call | solution.py:63
  73.5 1.6 %collective-permute-start.27 = (bf16[512,128]{1,0:T(8,128)(2,1)S(1)}, bf16[512,128]{1,0:T(8,128)(2,1)S(1)}, u32[]{:S(2)}, u32[]{:S(2)}) collective-permute-start(bf16[512,128]{1,0:T(8,128)(2,1)S(1)} %get-tuple-element.118), channel_id=1, source_target_pairs={{0,2},{1,3},{2,0},{3,1},{4,6},{5,7},{6,4},{7,5},{8,10},{9,11},{10,... | collective-permute-start | bytes 393224 | tf_op jit(solution)/shard_map/ppermute | solution.py:85
  75.1 1.1 %collective-permute-start.25 = (bf16[512,128]{1,0:T(8,128)(2,1)S(1)}, bf16[512,128]{1,0:T(8,128)(2,1)S(1)}, u32[]{:S(2)}, u32[]{:S(2)}) collective-permute-start(bf16[512,128]{1,0:T(8,128)(2,1)S(1)} %get-tuple-element.114), channel_id=1, source_target_pairs={{0,2},{1,3},{2,0},{3,1},{4,6},{5,7},{6,4},{7,5},{8,10},{9,11},{10,... | collective-permute-start | bytes 393224 | tf_op jit(solution)/shard_map/ppermute | solution.py:85
  76.2 3.7 %collective-permute-done.27.refs_1_ = bf16[512,128]{1,0:T(8,128)(2,1)S(1)} collective-permute-done((bf16[512,128]{1,0:T(8,128)(2,1)S(1)}, bf16[512,128]{1,0:T(8,128)(2,1)S(1)}, u32[]{:S(2)}, u32[]{:S(2)}) %collective-permute-start.27) | collective-permute-done | bytes 131104 | tf_op jit(solution)/shard_map/ppermute | solution.py:85
  79.9 3.3 %collective-permute-start.28 = (bf16[128,128]{1,0:T(8,128)(2,1)S(1)}, bf16[128,128]{1,0:T(8,128)(2,1)S(1)}, u32[]{:S(2)}, u32[]{:S(2)}) collective-permute-start(bf16[128,128]{1,0:T(8,128)(2,1)S(1)} %get-tuple-element.120), channel_id=1, source_target_pairs={{0,12},{4,8},{8,4},{12,0},{1,13},{5,9},{9,5},{13,1},{2,14},{6,10},... | collective-permute-start | bytes 98312 | tf_op jit(solution)/shard_map/ppermute | solution.py:88
  83.2 1.2 %collective-permute-start.30 = (bf16[128,128]{1,0:T(8,128)(2,1)S(1)}, bf16[128,128]{1,0:T(8,128)(2,1)S(1)}, u32[]{:S(2)}, u32[]{:S(2)}) collective-permute-start(bf16[128,128]{1,0:T(8,128)(2,1)S(1)} %get-tuple-element.122), channel_id=1, source_target_pairs={{0,4},{4,0},{8,12},{12,8},{1,5},{5,1},{9,13},{13,9},{2,6},{6,2},{1... | collective-permute-start | bytes 98312 | tf_op jit(solution)/shard_map/ppermute | solution.py:88
  84.4 1.3 %collective-permute-done.28.refs_3_ = bf16[128,128]{1,0:T(8,128)(2,1)S(1)} collective-permute-done((bf16[128,128]{1,0:T(8,128)(2,1)S(1)}, bf16[128,128]{1,0:T(8,128)(2,1)S(1)}, u32[]{:S(2)}, u32[]{:S(2)}) %collective-permute-start.28) | collective-permute-done | bytes 32800 | tf_op jit(solution)/shard_map/ppermute | solution.py:88
  85.7 2.3 %collective-permute-done.29.refs_4_ = bf16[128,128]{1,0:T(8,128)(2,1)S(1)} collective-permute-done((bf16[128,128]{1,0:T(8,128)(2,1)S(1)}, bf16[128,128]{1,0:T(8,128)(2,1)S(1)}, u32[]{:S(2)}, u32[]{:S(2)}) %collective-permute-start.29) | collective-permute-done | bytes 32800 | tf_op jit(solution)/shard_map/ppermute | solution.py:88
  88.0 1.2 %owed_rows.1 = (bf16[256,128]{1,0:T(8,128)(2,1)S(1)}, bf16[256,128]{1,0:T(8,128)(2,1)S(1)}, bf16[256,128]{1,0:T(8,128)(2,1)S(1)}, bf16[256,128]{1,0:T(8,128)(2,1...) custom-call(s32[1]{0:T(128)} %bitcast.me_ref, ...), custom_call_target="tpu_custom_call" | custom-call | flops 268435456 | bytes 935936 | tf_op jit(solution)/shard_map/owed_rows/pallas_call | solution.py:63
  89.2 1.5 %collective-permute-start.31 = (bf16[256,128]{1,0:T(8,128)(2,1)S(1)}, bf16[256,128]{1,0:T(8,128)(2,1)S(1)}, u32[]{:S(2)}, u32[]{:S(2)}) collective-permute-start(bf16[256,128]{1,0:T(8,128)(2,1)S(1)} %get-tuple-element.124), channel_id=1, source_target_pairs={{0,12},{4,8},{8,4},{12,0},{1,13},{5,9},{9,5},{13,1},{2,14},{6,10},... | collective-permute-start | bytes 196616 | tf_op jit(solution)/shard_map/ppermute | solution.py:88
  91.3 2.3 %collective-permute-start.33 = (bf16[256,128]{1,0:T(8,128)(2,1)S(1)}, bf16[256,128]{1,0:T(8,128)(2,1)S(1)}, u32[]{:S(2)}, u32[]{:S(2)}) collective-permute-start(bf16[256,128]{1,0:T(8,128)(2,1)S(1)} %get-tuple-element.126), channel_id=1, source_target_pairs={{0,4},{4,0},{8,12},{12,8},{1,5},{5,1},{9,13},{13,9},{2,6},{6,2},{1... | collective-permute-start | bytes 196616 | tf_op jit(solution)/shard_map/ppermute | solution.py:88
  93.7 1.4 %collective-permute-start.36 = (bf16[256,128]{1,0:T(8,128)(2,1)S(1)}, bf16[256,128]{1,0:T(8,128)(2,1)S(1)}, u32[]{:S(2)}, u32[]{:S(2)}) collective-permute-start(bf16[256,128]{1,0:T(8,128)(2,1)S(1)} %get-tuple-element.130), channel_id=1, source_target_pairs={{0,12},{4,8},{8,4},{12,0},{1,13},{5,9},{9,5},{13,1},{2,14},{6,10},... | collective-permute-start | bytes 196616 | tf_op jit(solution)/shard_map/ppermute | solution.py:88
  95.1 1.1 %collective-permute-done.31.refs_1_ = bf16[256,128]{1,0:T(8,128)(2,1)S(1)} collective-permute-done((bf16[256,128]{1,0:T(8,128)(2,1)S(1)}, bf16[256,128]{1,0:T(8,128)(2,1)S(1)}, u32[]{:S(2)}, u32[]{:S(2)}) %collective-permute-start.31) | collective-permute-done | bytes 65568 | tf_op jit(solution)/shard_map/ppermute | solution.py:88
  96.2 1.9 %collective-permute-start.38 = (bf16[256,128]{1,0:T(8,128)(2,1)S(1)}, bf16[256,128]{1,0:T(8,128)(2,1)S(1)}, u32[]{:S(2)}, u32[]{:S(2)}) collective-permute-start(bf16[256,128]{1,0:T(8,128)(2,1)S(1)} %get-tuple-element.132), channel_id=1, source_target_pairs={{0,4},{4,0},{8,12},{12,8},{1,5},{5,1},{9,13},{13,9},{2,6},{6,2},{1... | collective-permute-start | bytes 196616 | tf_op jit(solution)/shard_map/ppermute | solution.py:88
  99.1 1.6 %collective-permute-start.34 = (bf16[256,128]{1,0:T(8,128)(2,1)S(1)}, bf16[256,128]{1,0:T(8,128)(2,1)S(1)}, u32[]{:S(2)}, u32[]{:S(2)}) collective-permute-start(bf16[256,128]{1,0:T(8,128)(2,1)S(1)} %get-tuple-element.127.refs_4_), channel_id=1, source_target_pairs={{0,2},{1,3},{2,0},{3,1},{4,6},{5,7},{6,4},{7,5},{8,10},{9,11},{10,... | collective-permute-start | bytes 196616 | tf_op jit(solution)/shard_map/ppermute | solution.py:85
  100.7 0.9 collective-permute-done.37.refs_2_
  102.0 1.4 %collective-permute-done.34.refs_0_ = bf16[256,128]{1,0:T(8,128)(2,1)S(1)} collective-permute-done((bf16[256,128]{1,0:T(8,128)(2,1)S(1)}, bf16[256,128]{1,0:T(8,128)(2,1)S(1)}, u32[]{:S(2)}, u32[]{:S(2)}) %collective-permute-start.34) | collective-permute-done | bytes 65568 | tf_op jit(solution)/shard_map/ppermute | solution.py:85
  103.4 1.4 %collective-permute-done.35.refs_1_ = bf16[256,128]{1,0:T(8,128)(2,1)S(1)} collective-permute-done((bf16[256,128]{1,0:T(8,128)(2,1)S(1)}, bf16[256,128]{1,0:T(8,128)(2,1)S(1)}, u32[]{:S(2)}, u32[]{:S(2)}) %collective-permute-start.35) | collective-permute-done | bytes 65568 | tf_op jit(solution)/shard_map/ppermute | solution.py:85
  104.9 1.1 %adjoint.1 = f32[256,512]{1,0:T(8,128)} custom-call(s32[1]{0:T(128)} %bitcast.me_ref, bf16[512,512]{1,0:T(8,128)(2,1)S(1)} %get-tuple-element.73.enc_ref, bf16[2,256,128]{2,1,0:T(8,128)(2,1)S(1)} %far_join.1.far_ref, bf16[256,128]{1,0:T(8,128)(2,1)S(1)} %get-tuple-element.133.refs_2_.refs_0_, bf16[256,128]{1,0:T(8,128)(2,1)S(1)} %collective-permute-done.39.refs_1_), custom_call_target="tpu_custom_call" | custom-call | flops 134217728 | bytes 1310720 | tf_op jit(solution)/shard_map/adjoint/pallas_call | solution.py:63
  (65 shorter events, 8.2 us)
Async XLA Ops:
  0.0 33.0 %copy-start.2 = (bf16[512,512]{1,0:T(8,128)(2,1)S(1)}, bf16[512,512]{1,0:T(8,128)(2,1)}, u32[]{:S(2)}) copy-start(bf16[512,512]{1,0:T(8,128)(2,1)} %base_ref.1) | copy-start | bytes 1572868
  0.0 10.3 %collective-permute-start.1 = (bf16[256,512]{1,0:T(8,128)(2,1)}, bf16[256,512]{1,0:T(8,128)(2,1)S(1)}, u32[]{:S(2)}, u32[]{:S(2)}) collective-permute-start(bf16[256,512]{1,0:T(8,128)(2,1)} %state_ref.1), channel_id=1, source_target_pairs={{0,2},{1,3},{2,0},{3,1},{4,6},{5,7},{6,4},{7,5},{8,10},{9,11},{10,... | collective-permute-start | bytes 786440 | tf_op jit(solution)/shard_map/ppermute | solution.py:85
  4.5 8.1 %collective-permute-start.4 = (bf16[144,512]{1,0:T(8,128)(2,1)S(1)}, bf16[144,512]{1,0:T(8,128)(2,1)S(1)}, u32[]{:S(2)}, u32[]{:S(2)}) collective-permute-start(bf16[144,512]{1,0:T(8,128)(2,1)S(1)} %get-tuple-element.72.refs_4_), channel_id=1, source_target_pairs={{0,2},{1,3},{2,0},{3,1},{4,6},{5,7},{6,4},{7,5},{8,10},{9,11},{10,... | collective-permute-start | bytes 442376 | tf_op jit(solution)/shard_map/ppermute | solution.py:85
  4.6 0.7 copy-start.3
  7.5 5.2 %collective-permute-start = (bf16[256,512]{1,0:T(8,128)(2,1)S(1)}, bf16[256,512]{1,0:T(8,128)(2,1)S(1)}, u32[]{:S(2)}, u32[]{:S(2)}) collective-permute-start(bf16[256,512]{1,0:T(8,128)(2,1)S(1)} %get-tuple-element.71.refs_0_), channel_id=1, source_target_pairs={{0,1},{1,0},{2,3},{3,2},{4,5},{5,4},{6,7},{7,6},{8,9},{9,8},{10,11... | collective-permute-start | bytes 786440 | tf_op jit(solution)/shard_map/ppermute | solution.py:85
  10.3 3.7 %collective-permute-start.2 = (bf16[256,512]{1,0:T(8,128)(2,1)S(1)}, bf16[256,512]{1,0:T(8,128)(2,1)S(1)}, u32[]{:S(2)}, u32[]{:S(2)}) collective-permute-start(bf16[256,512]{1,0:T(8,128)(2,1)S(1)} %collective-permute-done.1.refs_2_), channel_id=1, source_target_pairs={{0,1},{1,0},{2,3},{3,2},{4,5},{5,4},{6,7},{7,6},{8,9},{9,8},{10,11... | collective-permute-start | bytes 786440 | tf_op jit(solution)/shard_map/ppermute | solution.py:85
  10.3 2.3 %collective-permute-start.3 = (bf16[144,512]{1,0:T(8,128)(2,1)S(1)}, bf16[144,512]{1,0:T(8,128)(2,1)S(1)}, u32[]{:S(2)}, u32[]{:S(2)}) collective-permute-start(bf16[144,512]{1,0:T(8,128)(2,1)S(1)} %get-tuple-element.72.refs_4_), channel_id=1, source_target_pairs={{0,1},{1,0},{2,3},{3,2},{4,5},{5,4},{6,7},{7,6},{8,9},{9,8},{10,11... | collective-permute-start | bytes 442376 | tf_op jit(solution)/shard_map/ppermute | solution.py:85
  12.6 1.4 %collective-permute-start.5 = (bf16[144,512]{1,0:T(8,128)(2,1)S(1)}, bf16[144,512]{1,0:T(8,128)(2,1)S(1)}, u32[]{:S(2)}, u32[]{:S(2)}) collective-permute-start(bf16[144,512]{1,0:T(8,128)(2,1)S(1)} %collective-permute-done.4.refs_6_), channel_id=1, source_target_pairs={{0,1},{1,0},{2,3},{3,2},{4,5},{5,4},{6,7},{7,6},{8,9},{9,8},{10,11... | collective-permute-start | bytes 442376 | tf_op jit(solution)/shard_map/ppermute | solution.py:85
  16.5 29.2 %copy-start.4 = (bf16[1024,512]{1,0:T(8,128)(2,1)S(1)}, bf16[1024,512]{1,0:T(8,128)(2,1)}, u32[]{:S(2)}) copy-start(bf16[1024,512]{1,0:T(8,128)(2,1)} %es_ref.3) | copy-start | bytes 3145732
  16.5 25.9 %collective-permute-start.13 = (bf16[896,512]{1,0:T(8,128)(2,1)S(1)}, bf16[896,512]{1,0:T(8,128)(2,1)S(1)}, u32[]{:S(2)}, u32[]{:S(2)}) collective-permute-start(bf16[896,512]{1,0:T(8,128)(2,1)S(1)} %get-tuple-element.87.refs_6_), channel_id=1, source_target_pairs={{0,2},{1,3},{2,0},{3,1},{4,6},{5,7},{6,4},{7,5},{8,10},{9,11},{10,... | collective-permute-start | bytes 2752520 | tf_op jit(solution)/shard_map/ppermute | solution.py:85
  18.3 8.2 %collective-permute-start.6 = (bf16[512,128]{1,0:T(8,128)(2,1)S(1)}, bf16[512,128]{1,0:T(8,128)(2,1)S(1)}, u32[]{:S(2)}, u32[]{:S(2)}) collective-permute-start(bf16[512,128]{1,0:T(8,128)(2,1)S(1)} %get-tuple-element.80), channel_id=1, source_target_pairs={{0,12},{4,8},{8,4},{12,0},{1,13},{5,9},{9,5},{13,1},{2,14},{6,10},... | collective-permute-start | bytes 393224 | tf_op jit(solution)/shard_map/ppermute | solution.py:88
  21.9 11.1 %collective-permute-start.7 = (bf16[512,128]{1,0:T(8,128)(2,1)S(1)}, bf16[512,128]{1,0:T(8,128)(2,1)S(1)}, u32[]{:S(2)}, u32[]{:S(2)}) collective-permute-start(bf16[512,128]{1,0:T(8,128)(2,1)S(1)} %get-tuple-element.81), channel_id=1, source_target_pairs={{0,8},{4,12},{8,0},{12,4},{1,9},{5,13},{9,1},{13,5},{2,10},{6,14},... | collective-permute-start | bytes 393224 | tf_op jit(solution)/shard_map/ppermute | solution.py:88
  21.9 11.1 %collective-permute-start.8 = (bf16[512,128]{1,0:T(8,128)(2,1)S(1)}, bf16[512,128]{1,0:T(8,128)(2,1)S(1)}, u32[]{:S(2)}, u32[]{:S(2)}) collective-permute-start(bf16[512,128]{1,0:T(8,128)(2,1)S(1)} %get-tuple-element.82), channel_id=1, source_target_pairs={{0,4},{4,0},{8,12},{12,8},{1,5},{5,1},{9,13},{13,9},{2,6},{6,2},{1... | collective-permute-start | bytes 393224 | tf_op jit(solution)/shard_map/ppermute | solution.py:88
  33.9 8.5 %collective-permute-start.12 = (bf16[512,128]{1,0:T(8,128)(2,1)S(1)}, bf16[512,128]{1,0:T(8,128)(2,1)S(1)}, u32[]{:S(2)}, u32[]{:S(2)}) collective-permute-start(bf16[512,128]{1,0:T(8,128)(2,1)S(1)} %encode.1.state_ref.refs_4_), channel_id=1, source_target_pairs={{0,2},{1,3},{2,0},{3,1},{4,6},{5,7},{6,4},{7,5},{8,10},{9,11},{10,... | collective-permute-start | bytes 393224 | tf_op jit(solution)/shard_map/ppermute | solution.py:85
  35.0 5.9 %collective-permute-start.9 = (bf16[128,128]{1,0:T(8,128)(2,1)S(1)}, bf16[128,128]{1,0:T(8,128)(2,1)S(1)}, u32[]{:S(2)}, u32[]{:S(2)}) collective-permute-start(bf16[128,128]{1,0:T(8,128)(2,1)S(1)} %get-tuple-element.84), channel_id=1, source_target_pairs={{0,12},{4,8},{8,4},{12,0},{1,13},{5,9},{9,5},{13,1},{2,14},{6,10},... | collective-permute-start | bytes 98312 | tf_op jit(solution)/shard_map/ppermute | solution.py:88
  37.6 4.8 %collective-permute-start.10 = (bf16[128,128]{1,0:T(8,128)(2,1)S(1)}, bf16[128,128]{1,0:T(8,128)(2,1)S(1)}, u32[]{:S(2)}, u32[]{:S(2)}) collective-permute-start(bf16[128,128]{1,0:T(8,128)(2,1)S(1)} %get-tuple-element.85), channel_id=1, source_target_pairs={{0,8},{4,12},{8,0},{12,4},{1,9},{5,13},{9,1},{13,5},{2,10},{6,14},... | collective-permute-start | bytes 98312 | tf_op jit(solution)/shard_map/ppermute | solution.py:88
  37.6 4.8 %collective-permute-start.11 = (bf16[128,128]{1,0:T(8,128)(2,1)S(1)}, bf16[128,128]{1,0:T(8,128)(2,1)S(1)}, u32[]{:S(2)}, u32[]{:S(2)}) collective-permute-start(bf16[128,128]{1,0:T(8,128)(2,1)S(1)} %get-tuple-element.86), channel_id=1, source_target_pairs={{0,4},{4,0},{8,12},{12,8},{1,5},{5,1},{9,13},{13,9},{2,6},{6,2},{1... | collective-permute-start | bytes 98312 | tf_op jit(solution)/shard_map/ppermute | solution.py:88
  42.6 3.1 %collective-permute-start.15 = (bf16[2,512,512]{2,1,0:T(8,128)(2,1)S(1)}, bf16[2,512,512]{2,1,0:T(8,128)(2,1)S(1)}, u32[]{:S(2)}, u32[]{:S(2)}) collective-permute-start(bf16[2,512,512]{2,1,0:T(8,128)(2,1)S(1)} %get-tuple-element.89.refs_2_), channel_id=1, source_target_pairs={{0,1},{1,0},{2,3},{3,2},{4,5},{5,4},{6,7},{7,6},{8,9},{9,8},{10,11... | collective-permute-start | bytes 3145736 | tf_op jit(solution)/shard_map/ppermute | solution.py:85
  42.6 3.0 %collective-permute-start.14 = (bf16[2,512,128]{2,1,0:T(8,128)(2,1)S(1)}, bf16[2,512,128]{2,1,0:T(8,128)(2,1)S(1)}, u32[]{:S(2)}, u32[]{:S(2)}) collective-permute-start(bf16[2,512,128]{2,1,0:T(8,128)(2,1)S(1)} %get-tuple-element.88.refs_0_), channel_id=1, source_target_pairs={{0,1},{1,0},{2,3},{3,2},{4,5},{5,4},{6,7},{7,6},{8,9},{9,8},{10,11... | collective-permute-start | bytes 786440 | tf_op jit(solution)/shard_map/ppermute | solution.py:85
  43.1 5.5 %collective-permute-start.16 = (bf16[512,128]{1,0:T(8,128)(2,1)S(1)}, bf16[512,128]{1,0:T(8,128)(2,1)S(1)}, u32[]{:S(2)}, u32[]{:S(2)}) collective-permute-start(bf16[512,128]{1,0:T(8,128)(2,1)S(1)} %get-tuple-element.95.refs_0_), channel_id=1, source_target_pairs={{0,2},{1,3},{2,0},{3,1},{4,6},{5,7},{6,4},{7,5},{8,10},{9,11},{10,... | collective-permute-start | bytes 393224 | tf_op jit(solution)/shard_map/ppermute | solution.py:85
  48.7 1.6 %collective-permute-start.17 = (bf16[2,512,128]{2,1,0:T(8,128)(2,1)S(1)}, bf16[2,512,128]{2,1,0:T(8,128)(2,1)S(1)}, u32[]{:S(2)}, u32[]{:S(2)}) collective-permute-start(bf16[2,512,128]{2,1,0:T(8,128)(2,1)S(1)} %halo_pair.1.refs_0_), channel_id=1, source_target_pairs={{0,1},{1,0},{2,3},{3,2},{4,5},{5,4},{6,7},{7,6},{8,9},{9,8},{10,11... | collective-permute-start | bytes 786440 | tf_op jit(solution)/shard_map/ppermute | solution.py:85
  48.9 7.7 %collective-permute-start.18 = (bf16[2,384,512]{2,1,0:T(8,128)(2,1)S(1)}, bf16[2,384,512]{2,1,0:T(8,128)(2,1)S(1)}, u32[]{:S(2)}, u32[]{:S(2)}) collective-permute-start(bf16[2,384,512]{2,1,0:T(8,128)(2,1)S(1)} %get-tuple-element.99.refs_0_), channel_id=1, source_target_pairs={{0,1},{1,0},{2,3},{3,2},{4,5},{5,4},{6,7},{7,6},{8,9},{9,8},{10,11... | collective-permute-start | bytes 2359304 | tf_op jit(solution)/shard_map/ppermute | solution.py:85
  50.3 6.4 %copy-start = (bf16[512,512]{1,0:T(8,128)(2,1)S(1)}, bf16[512,512]{1,0:T(8,128)(2,1)}, u32[]{:S(2)}) copy-start(bf16[512,512]{1,0:T(8,128)(2,1)} %grad_ref.4) | copy-start | bytes 1572868
  53.4 1.6 %collective-permute-start.19 = (bf16[2,128,512]{2,1,0:T(8,128)(2,1)S(1)}, bf16[2,128,512]{2,1,0:T(8,128)(2,1)S(1)}, u32[]{:S(2)}, u32[]{:S(2)}) collective-permute-start(bf16[2,128,512]{2,1,0:T(8,128)(2,1)S(1)} %get-tuple-element.101), channel_id=1, source_target_pairs={{0,1},{1,0},{2,3},{3,2},{4,5},{5,4},{6,7},{7,6},{8,9},{9,8},{10,11... | collective-permute-start | bytes 786440 | tf_op jit(solution)/shard_map/ppermute | solution.py:85
  55.1 5.6 %collective-permute-start.20 = (bf16[128,512]{1,0:T(8,128)(2,1)S(1)}, bf16[128,512]{1,0:T(8,128)(2,1)S(1)}, u32[]{:S(2)}, u32[]{:S(2)}) collective-permute-start(bf16[128,512]{1,0:T(8,128)(2,1)S(1)} %get-tuple-element.106), channel_id=1, source_target_pairs={{0,2},{1,3},{2,0},{3,1},{4,6},{5,7},{6,4},{7,5},{8,10},{9,11},{10,... | collective-permute-start | bytes 393224 | tf_op jit(solution)/shard_map/ppermute | solution.py:85
  56.7 11.1 %copy-start.1 = (bf16[1024,512]{1,0:T(8,128)(2,1)S(1)}, bf16[1024,512]{1,0:T(8,128)(2,1)}, u32[]{:S(2)}) copy-start(bf16[1024,512]{1,0:T(8,128)(2,1)} %grad_ref.5) | copy-start | bytes 3145732
  61.3 5.0 %collective-permute-start.22 = (bf16[128,512]{1,0:T(8,128)(2,1)S(1)}, bf16[128,512]{1,0:T(8,128)(2,1)S(1)}, u32[]{:S(2)}, u32[]{:S(2)}) collective-permute-start(bf16[128,512]{1,0:T(8,128)(2,1)S(1)} %get-tuple-element.107.refs_0_), channel_id=1, source_target_pairs={{0,2},{1,3},{2,0},{3,1},{4,6},{5,7},{6,4},{7,5},{8,10},{9,11},{10,... | collective-permute-start | bytes 393224 | tf_op jit(solution)/shard_map/ppermute | solution.py:85
  62.9 3.5 %collective-permute-start.21 = (bf16[128,512]{1,0:T(8,128)(2,1)S(1)}, bf16[128,512]{1,0:T(8,128)(2,1)S(1)}, u32[]{:S(2)}, u32[]{:S(2)}) collective-permute-start(bf16[128,512]{1,0:T(8,128)(2,1)S(1)} %get-tuple-element.107.refs_0_), channel_id=1, source_target_pairs={{0,1},{1,0},{2,3},{3,2},{4,5},{5,4},{6,7},{7,6},{8,9},{9,8},{10,11... | collective-permute-start | bytes 393224 | tf_op jit(solution)/shard_map/ppermute | solution.py:85
  66.4 1.3 %collective-permute-start.23 = (bf16[128,512]{1,0:T(8,128)(2,1)S(1)}, bf16[128,512]{1,0:T(8,128)(2,1)S(1)}, u32[]{:S(2)}, u32[]{:S(2)}) collective-permute-start(bf16[128,512]{1,0:T(8,128)(2,1)S(1)} %collective-permute-done.22.refs_2_), channel_id=1, source_target_pairs={{0,1},{1,0},{2,3},{3,2},{4,5},{5,4},{6,7},{7,6},{8,9},{9,8},{10,11... | collective-permute-start | bytes 393224 | tf_op jit(solution)/shard_map/ppermute | solution.py:85
  70.6 2.7 %collective-permute-start.26 = (bf16[2,512,128]{2,1,0:T(8,128)(2,1)S(1)}, bf16[2,512,128]{2,1,0:T(8,128)(2,1)S(1)}, u32[]{:S(2)}, u32[]{:S(2)}) collective-permute-start(bf16[2,512,128]{2,1,0:T(8,128)(2,1)S(1)} %get-tuple-element.116), channel_id=1, source_target_pairs={{0,1},{1,0},{2,3},{3,2},{4,5},{5,4},{6,7},{7,6},{8,9},{9,8},{10,11... | collective-permute-start | bytes 786440 | tf_op jit(solution)/shard_map/ppermute | solution.py:85
  73.0 2.1 %collective-permute-start.24 = (bf16[2,512,128]{2,1,0:T(8,128)(2,1)S(1)}, bf16[2,512,128]{2,1,0:T(8,128)(2,1)S(1)}, u32[]{:S(2)}, u32[]{:S(2)}) collective-permute-start(bf16[2,512,128]{2,1,0:T(8,128)(2,1)S(1)} %get-tuple-element.112), channel_id=1, source_target_pairs={{0,1},{1,0},{2,3},{3,2},{4,5},{5,4},{6,7},{7,6},{8,9},{9,8},{10,11... | collective-permute-start | bytes 786440 | tf_op jit(solution)/shard_map/ppermute | solution.py:85
  73.5 6.4 %collective-permute-start.27 = (bf16[512,128]{1,0:T(8,128)(2,1)S(1)}, bf16[512,128]{1,0:T(8,128)(2,1)S(1)}, u32[]{:S(2)}, u32[]{:S(2)}) collective-permute-start(bf16[512,128]{1,0:T(8,128)(2,1)S(1)} %get-tuple-element.118), channel_id=1, source_target_pairs={{0,2},{1,3},{2,0},{3,1},{4,6},{5,7},{6,4},{7,5},{8,10},{9,11},{10,... | collective-permute-start | bytes 393224 | tf_op jit(solution)/shard_map/ppermute | solution.py:85
  75.1 9.3 %collective-permute-start.25 = (bf16[512,128]{1,0:T(8,128)(2,1)S(1)}, bf16[512,128]{1,0:T(8,128)(2,1)S(1)}, u32[]{:S(2)}, u32[]{:S(2)}) collective-permute-start(bf16[512,128]{1,0:T(8,128)(2,1)S(1)} %get-tuple-element.114), channel_id=1, source_target_pairs={{0,2},{1,3},{2,0},{3,1},{4,6},{5,7},{6,4},{7,5},{8,10},{9,11},{10,... | collective-permute-start | bytes 393224 | tf_op jit(solution)/shard_map/ppermute | solution.py:85
  79.9 5.8 %collective-permute-start.28 = (bf16[128,128]{1,0:T(8,128)(2,1)S(1)}, bf16[128,128]{1,0:T(8,128)(2,1)S(1)}, u32[]{:S(2)}, u32[]{:S(2)}) collective-permute-start(bf16[128,128]{1,0:T(8,128)(2,1)S(1)} %get-tuple-element.120), channel_id=1, source_target_pairs={{0,12},{4,8},{8,4},{12,0},{1,13},{5,9},{9,5},{13,1},{2,14},{6,10},... | collective-permute-start | bytes 98312 | tf_op jit(solution)/shard_map/ppermute | solution.py:88
  83.2 4.8 %collective-permute-start.29 = (bf16[128,128]{1,0:T(8,128)(2,1)S(1)}, bf16[128,128]{1,0:T(8,128)(2,1)S(1)}, u32[]{:S(2)}, u32[]{:S(2)}) collective-permute-start(bf16[128,128]{1,0:T(8,128)(2,1)S(1)} %get-tuple-element.121), channel_id=1, source_target_pairs={{0,8},{4,12},{8,0},{12,4},{1,9},{5,13},{9,1},{13,5},{2,10},{6,14},... | collective-permute-start | bytes 98312 | tf_op jit(solution)/shard_map/ppermute | solution.py:88
  83.2 4.8 %collective-permute-start.30 = (bf16[128,128]{1,0:T(8,128)(2,1)S(1)}, bf16[128,128]{1,0:T(8,128)(2,1)S(1)}, u32[]{:S(2)}, u32[]{:S(2)}) collective-permute-start(bf16[128,128]{1,0:T(8,128)(2,1)S(1)} %get-tuple-element.122), channel_id=1, source_target_pairs={{0,4},{4,0},{8,12},{12,8},{1,5},{5,1},{9,13},{13,9},{2,6},{6,2},{1... | collective-permute-start | bytes 98312 | tf_op jit(solution)/shard_map/ppermute | solution.py:88
  89.2 7.0 %collective-permute-start.31 = (bf16[256,128]{1,0:T(8,128)(2,1)S(1)}, bf16[256,128]{1,0:T(8,128)(2,1)S(1)}, u32[]{:S(2)}, u32[]{:S(2)}) collective-permute-start(bf16[256,128]{1,0:T(8,128)(2,1)S(1)} %get-tuple-element.124), channel_id=1, source_target_pairs={{0,12},{4,8},{8,4},{12,0},{1,13},{5,9},{9,5},{13,1},{2,14},{6,10},... | collective-permute-start | bytes 196616 | tf_op jit(solution)/shard_map/ppermute | solution.py:88
  90.7 8.1 %collective-permute-start.32 = (bf16[256,128]{1,0:T(8,128)(2,1)S(1)}, bf16[256,128]{1,0:T(8,128)(2,1)S(1)}, u32[]{:S(2)}, u32[]{:S(2)}) collective-permute-start(bf16[256,128]{1,0:T(8,128)(2,1)S(1)} %get-tuple-element.125), channel_id=1, source_target_pairs={{0,8},{4,12},{8,0},{12,4},{1,9},{5,13},{9,1},{13,5},{2,10},{6,14},... | collective-permute-start | bytes 196616 | tf_op jit(solution)/shard_map/ppermute | solution.py:88
  91.3 7.4 %collective-permute-start.33 = (bf16[256,128]{1,0:T(8,128)(2,1)S(1)}, bf16[256,128]{1,0:T(8,128)(2,1)S(1)}, u32[]{:S(2)}, u32[]{:S(2)}) collective-permute-start(bf16[256,128]{1,0:T(8,128)(2,1)S(1)} %get-tuple-element.126), channel_id=1, source_target_pairs={{0,4},{4,0},{8,12},{12,8},{1,5},{5,1},{9,13},{13,9},{2,6},{6,2},{1... | collective-permute-start | bytes 196616 | tf_op jit(solution)/shard_map/ppermute | solution.py:88
  93.7 7.0 %collective-permute-start.36 = (bf16[256,128]{1,0:T(8,128)(2,1)S(1)}, bf16[256,128]{1,0:T(8,128)(2,1)S(1)}, u32[]{:S(2)}, u32[]{:S(2)}) collective-permute-start(bf16[256,128]{1,0:T(8,128)(2,1)S(1)} %get-tuple-element.130), channel_id=1, source_target_pairs={{0,12},{4,8},{8,4},{12,0},{1,13},{5,9},{9,5},{13,1},{2,14},{6,10},... | collective-permute-start | bytes 196616 | tf_op jit(solution)/shard_map/ppermute | solution.py:88
  95.1 6.5 %collective-permute-start.37 = (bf16[256,128]{1,0:T(8,128)(2,1)S(1)}, bf16[256,128]{1,0:T(8,128)(2,1)S(1)}, u32[]{:S(2)}, u32[]{:S(2)}) collective-permute-start(bf16[256,128]{1,0:T(8,128)(2,1)S(1)} %get-tuple-element.131), channel_id=1, source_target_pairs={{0,8},{4,12},{8,0},{12,4},{1,9},{5,13},{9,1},{13,5},{2,10},{6,14},... | collective-permute-start | bytes 196616 | tf_op jit(solution)/shard_map/ppermute | solution.py:88
  96.2 5.4 %collective-permute-start.38 = (bf16[256,128]{1,0:T(8,128)(2,1)S(1)}, bf16[256,128]{1,0:T(8,128)(2,1)S(1)}, u32[]{:S(2)}, u32[]{:S(2)}) collective-permute-start(bf16[256,128]{1,0:T(8,128)(2,1)S(1)} %get-tuple-element.132), channel_id=1, source_target_pairs={{0,4},{4,0},{8,12},{12,8},{1,5},{5,1},{9,13},{13,9},{2,6},{6,2},{1... | collective-permute-start | bytes 196616 | tf_op jit(solution)/shard_map/ppermute | solution.py:88
  99.1 4.3 %collective-permute-start.34 = (bf16[256,128]{1,0:T(8,128)(2,1)S(1)}, bf16[256,128]{1,0:T(8,128)(2,1)S(1)}, u32[]{:S(2)}, u32[]{:S(2)}) collective-permute-start(bf16[256,128]{1,0:T(8,128)(2,1)S(1)} %get-tuple-element.127.refs_4_), channel_id=1, source_target_pairs={{0,2},{1,3},{2,0},{3,1},{4,6},{5,7},{6,4},{7,5},{8,10},{9,11},{10,... | collective-permute-start | bytes 196616 | tf_op jit(solution)/shard_map/ppermute | solution.py:85
  100.7 4.2 %collective-permute-start.35 = (bf16[256,128]{1,0:T(8,128)(2,1)S(1)}, bf16[256,128]{1,0:T(8,128)(2,1)S(1)}, u32[]{:S(2)}, u32[]{:S(2)}) collective-permute-start(bf16[256,128]{1,0:T(8,128)(2,1)S(1)} %get-tuple-element.128), channel_id=1, source_target_pairs={{0,3},{1,2},{2,1},{3,0},{4,7},{5,6},{6,5},{7,4},{8,11},{9,10},{10,... | collective-permute-start | bytes 196616 | tf_op jit(solution)/shard_map/ppermute | solution.py:85
  101.9 2.9 %collective-permute-start.39 = (bf16[256,128]{1,0:T(8,128)(2,1)S(1)}, bf16[256,128]{1,0:T(8,128)(2,1)S(1)}, u32[]{:S(2)}, u32[]{:S(2)}) collective-permute-start(bf16[256,128]{1,0:T(8,128)(2,1)S(1)} %get-tuple-element.134), channel_id=1, source_target_pairs={{0,1},{1,0},{2,3},{3,2},{4,5},{5,4},{6,7},{7,6},{8,9},{9,8},{10,11... | collective-permute-start | bytes 196616 | tf_op jit(solution)/shard_map/ppermute | solution.py:85

commit v9 on v8

--- a/solution.py
+++ b/solution.py
@@ -149,7 +149,7 @@
         NS = n_dom * S
         C = D // M
         R = N // M
-        T = 256
+        T = 512
         PACK = 16
         assert NS == D
         rows_enc, rows_in, rows_out, rows_node = (

time: 106 us -> 105 us (level)
  Pallas kernels: 23.1 us -> 21.9 us
    pallas_call x22, Pallas kernels: 23.1 us -> 21.9 us  [call(): pl.pallas_call(body, out_shape=list(outs), in_specs=[SMEM] + [HBM if i in...]
  transfers between devices with their start and end apart: 40 -> 40, of which waited for: 21 -> 21; matrix products, arithmetic and copies ran while one was open for 0% -> 0% of each run, Pallas kernels for 14% -> 13%
where the time goes in v9:
time: 105 us
  waiting for transfers between devices  43.9 us (42%)
  starting transfers between devices  38 us (36%)
  Pallas kernels  21.9 us (21%)
    ppermute x25, waiting for transfers between devices, member_swap(): return lax.ppermute(x, ('feat', 'rep'), [(i, i ^ k) for i in range(M)])  24.3 us
    pallas_call x22, Pallas kernels, call(): pl.pallas_call(body, out_shape=list(outs), in_specs=[SMEM] + [HBM if i in...  21.9 us
    ppermute x15, starting transfers between devices, dom_swap(): return lax.ppermute(x, 'dom', [(i, i ^ k) for i in range(n_dom)])  21.1 us
    ppermute x15, waiting for transfers between devices, dom_swap(): return lax.ppermute(x, 'dom', [(i, i ^ k) for i in range(n_dom)])  19.6 us
    ppermute x25, starting transfers between devices, member_swap(): return lax.ppermute(x, ('feat', 'rep'), [(i, i ^ k) for i in range(M)])  16.9 us
  transfers between devices with their start and end apart: 40, of which 21 were waited for; matrix products, arithmetic and copies ran while one was open for 0% of the time, Pallas kernels for 13%

profile of v9, /device:TPU:0, one launch (start us, length us, event | category | flops | bytes accessed | tf_op | source)
XLA Modules:
  0.0 104.8 jit_solution(14631362885011779251)
XLA Ops:
  0.0 2.9 %collective-permute-start.1 = (bf16[256,512]{1,0:T(8,128)(2,1)}, bf16[256,512]{1,0:T(8,128)(2,1)S(1)}, u32[]{:S(2)}, u32[]{:S(2)}) collective-permute-start(bf16[256,512]{1,0:T(8,128)(2,1)} %state_ref.1), channel_id=1, source_target_pairs={{0,2},{1,3},{2,0},{3,1},{4,6},{5,7},{6,4},{7,5},{8,10},{9,11},{10,... | collective-permute-start | bytes 786440 | tf_op jit(solution)/shard_map/ppermute | solution.py:85
  3.0 1.5 %tables.1 = (bf16[144,512]{1,0:T(8,128)(2,1)S(1)}, s32[1,512]{1,0:T(1,128)S(1)}, s32[1,1024]{1,0:T(1,128)S(1)}) custom-call(s32[2]{0:T(128)S(1)} %pad_add_fusion.where_ref, bf16[128,512]{1,0:T(8,128)(2,1)} %enc_ref.1, s32[1,4,128]{2,1,0:T(4,128)} %gs_ref.1, s32[1,4,128]{2,1,0:T(4,128)} %gr_ref.1, s32[1,4,128]{2,1,0:T(4,128)} %halo_ref.1, s32[1,1024]{1,0:T(1,128)} %bitcast.5), custom_call_target="tpu_custom_call" | custom-call | bytes 294912 | tf_op jit(solution)/shard_map/tables/pallas_call | solution.py:63
  5.3 2.1 %edge_hots.1 = (bf16[1024,512]{1,0:T(8,128)(2,1)S(1)}, bf16[1024,512]{1,0:T(8,128)(2,1)S(1)}, bf16[1024,512]{1,0:T(8,128)(2,1)S(1)}, bf16[512,1024]{1,0:T(8,128)...) custom-call(s32[1]{0:T(128)} %bitcast.me_ref, ...), custom_call_target="tpu_custom_call" | custom-call | bytes 6823936 | tf_op jit(solution)/shard_map/edge_hots/pallas_call | solution.py:63
  7.5 2.7 %collective-permute-done.1.refs_2_ = bf16[256,512]{1,0:T(8,128)(2,1)S(1)} collective-permute-done((bf16[256,512]{1,0:T(8,128)(2,1)}, bf16[256,512]{1,0:T(8,128)(2,1)S(1)}, u32[]{:S(2)}, u32[]{:S(2)}) %collective-permute-start.1) | collective-permute-done | bytes 262176 | tf_op jit(solution)/shard_map/ppermute | solution.py:85
  10.8 1.8 %collective-permute-done.4.refs_6_ = bf16[144,512]{1,0:T(8,128)(2,1)S(1)} collective-permute-done((bf16[144,512]{1,0:T(8,128)(2,1)S(1)}, bf16[144,512]{1,0:T(8,128)(2,1)S(1)}, u32[]{:S(2)}, u32[]{:S(2)}) %collective-permute-start.4) | collective-permute-done | bytes 147488 | tf_op jit(solution)/shard_map/ppermute | solution.py:85
  12.6 1.4 %collective-permute-done.5.refs_7_ = bf16[144,512]{1,0:T(8,128)(2,1)S(1)} collective-permute-done((bf16[144,512]{1,0:T(8,128)(2,1)S(1)}, bf16[144,512]{1,0:T(8,128)(2,1)S(1)}, u32[]{:S(2)}, u32[]{:S(2)}) %collective-permute-start.5) | collective-permute-done | bytes 147488 | tf_op jit(solution)/shard_map/ppermute | solution.py:85
  14.0 2.5 %grid_messages.1 = (bf16[512,512]{1,0:T(8,128)(2,1)S(1)}, f32[4,256,128]{2,1,0:T(8,128)S(1)}, s32[4,2,512]{2,1,0:T(2,128)S(1)}, bf16[896,512]{1,0:T(8,128)(2,1)S...) custom-call(s32[1]{0:T(128)} %bitcast.me_ref, ...), custom_call_target="tpu_custom_call" | custom-call | flops 268435456 | bytes 5062656 | tf_op jit(solution)/shard_map/grid_messages/pallas_call | solution.py:63
  16.5 1.8 %collective-permute-start.13 = (bf16[896,512]{1,0:T(8,128)(2,1)S(1)}, bf16[896,512]{1,0:T(8,128)(2,1)S(1)}, u32[]{:S(2)}, u32[]{:S(2)}) collective-permute-start(bf16[896,512]{1,0:T(8,128)(2,1)S(1)} %get-tuple-element.87.refs_6_), channel_id=1, source_target_pairs={{0,2},{1,3},{2,0},{3,1},{4,6},{5,7},{6,4},{7,5},{8,10},{9,11},{10,... | collective-permute-start | bytes 2752520 | tf_op jit(solution)/shard_map/ppermute | solution.py:85
  18.3 3.6 %collective-permute-start.6 = (bf16[512,128]{1,0:T(8,128)(2,1)S(1)}, bf16[512,128]{1,0:T(8,128)(2,1)S(1)}, u32[]{:S(2)}, u32[]{:S(2)}) collective-permute-start(bf16[512,128]{1,0:T(8,128)(2,1)S(1)} %get-tuple-element.80), channel_id=1, source_target_pairs={{0,12},{4,8},{8,4},{12,0},{1,13},{5,9},{9,5},{13,1},{2,14},{6,10},... | collective-permute-start | bytes 393224 | tf_op jit(solution)/shard_map/ppermute | solution.py:88
  21.9 0.8 collective-permute-start.8
  22.7 3.8 %collective-permute-done.6.refs_1_ = bf16[512,128]{1,0:T(8,128)(2,1)S(1)} collective-permute-done((bf16[512,128]{1,0:T(8,128)(2,1)S(1)}, bf16[512,128]{1,0:T(8,128)(2,1)S(1)}, u32[]{:S(2)}, u32[]{:S(2)}) %collective-permute-start.6) | collective-permute-done | bytes 131104 | tf_op jit(solution)/shard_map/ppermute | solution.py:88
  26.5 6.5 %collective-permute-done.7.refs_2_ = bf16[512,128]{1,0:T(8,128)(2,1)S(1)} collective-permute-done((bf16[512,128]{1,0:T(8,128)(2,1)S(1)}, bf16[512,128]{1,0:T(8,128)(2,1)S(1)}, u32[]{:S(2)}, u32[]{:S(2)}) %collective-permute-start.7) | collective-permute-done | bytes 131104 | tf_op jit(solution)/shard_map/ppermute | solution.py:88
  33.0 0.8 encode.1.state_ref.refs_4_
  35.0 2.5 %collective-permute-start.9 = (bf16[128,128]{1,0:T(8,128)(2,1)S(1)}, bf16[128,128]{1,0:T(8,128)(2,1)S(1)}, u32[]{:S(2)}, u32[]{:S(2)}) collective-permute-start(bf16[128,128]{1,0:T(8,128)(2,1)S(1)} %get-tuple-element.84), channel_id=1, source_target_pairs={{0,12},{4,8},{8,4},{12,0},{1,13},{5,9},{9,5},{13,1},{2,14},{6,10},... | collective-permute-start | bytes 98312 | tf_op jit(solution)/shard_map/ppermute | solution.py:88
  37.6 1.9 %collective-permute-start.11 = (bf16[128,128]{1,0:T(8,128)(2,1)S(1)}, bf16[128,128]{1,0:T(8,128)(2,1)S(1)}, u32[]{:S(2)}, u32[]{:S(2)}) collective-permute-start(bf16[128,128]{1,0:T(8,128)(2,1)S(1)} %get-tuple-element.86), channel_id=1, source_target_pairs={{0,4},{4,0},{8,12},{12,8},{1,5},{5,1},{9,13},{13,9},{2,6},{6,2},{1... | collective-permute-start | bytes 98312 | tf_op jit(solution)/shard_map/ppermute | solution.py:88
  39.5 1.4 %collective-permute-done.9.refs_1_ = bf16[128,128]{1,0:T(8,128)(2,1)S(1)} collective-permute-done((bf16[128,128]{1,0:T(8,128)(2,1)S(1)}, bf16[128,128]{1,0:T(8,128)(2,1)S(1)}, u32[]{:S(2)}, u32[]{:S(2)}) %collective-permute-start.9) | collective-permute-done | bytes 32800 | tf_op jit(solution)/shard_map/ppermute | solution.py:88
  40.9 1.5 %collective-permute-done.10.refs_2_ = bf16[128,128]{1,0:T(8,128)(2,1)S(1)} collective-permute-done((bf16[128,128]{1,0:T(8,128)(2,1)S(1)}, bf16[128,128]{1,0:T(8,128)(2,1)S(1)}, u32[]{:S(2)}, u32[]{:S(2)}) %collective-permute-start.10) | collective-permute-done | bytes 32800 | tf_op jit(solution)/shard_map/ppermute | solution.py:88
  43.1 1.5 %collective-permute-start.16 = (bf16[512,128]{1,0:T(8,128)(2,1)S(1)}, bf16[512,128]{1,0:T(8,128)(2,1)S(1)}, u32[]{:S(2)}, u32[]{:S(2)}) collective-permute-start(bf16[512,128]{1,0:T(8,128)(2,1)S(1)} %get-tuple-element.95.refs_0_), channel_id=1, source_target_pairs={{0,2},{1,3},{2,0},{3,1},{4,6},{5,7},{6,4},{7,5},{8,10},{9,11},{10,... | collective-permute-start | bytes 393224 | tf_op jit(solution)/shard_map/ppermute | solution.py:85
  44.6 1.0 collective-permute-done.14.refs_1_
  45.7 3.0 %edge_local.1 = (f32[1024,512]{1,0:T(8,128)S(1)}, bf16[512,512]{1,0:T(8,128)(2,1)S(1)}, bf16[1536,512]{1,0:T(8,128)(2,1)S(1)}, bf16[512,512]{1,0:T(8,128)(2,1)S(1)}) custom-call(s32[1]{0:T(128)} %bitcast.me_ref, bf16[1024,512]{1,0:T(8,128)(2,1)S(1)} %copy-done.4, bf16[1024,512]{1,0:T(8,128)(2,1)S(1)} %get-tuple-element.77.send_ref, ...), custom_call_target="tpu_custom_call" | custom-call | flops 2684354560 | bytes 10485760 | tf_op jit(solution)/shard_map/edge_local/pallas_call | solution.py:63
  49.3 1.0 collective-permute-done.17.refs_1_
  50.3 2.5 %edge_update.1 = (f32[1024,512]{1,0:T(8,128)S(1)}, bf16[2,128,512]{2,1,0:T(8,128)(2,1)S(1)}, bf16[2,128,512]{2,1,0:T(8,128)(2,1)S(1)}) custom-call(s32[1]{0:T(128)} %bitcast.me_ref, f32[1024,512]{1,0:T(8,128)S(1)} %get-tuple-element.90.refs_2_.local_ref, bf16[1024,512]{1,0:T(8,128)(2,1)S(1)} %copy-done.4, bf16[1024,512]{1,0:T(8,128)(2,1)S(1)} %get-tuple-element.91.send_ref, ...), custom_call_target="tpu_custom_call" | custom-call | flops 2147483648 | bytes 10485760 | tf_op jit(solution)/shard_map/edge_update/pallas_call | solution.py:63
  53.0 1.4 %collective-permute-done.19.refs_1_ = bf16[2,128,512]{2,1,0:T(8,128)(2,1)S(1)} collective-permute-done((bf16[2,128,512]{2,1,0:T(8,128)(2,1)S(1)}, bf16[2,128,512]{2,1,0:T(8,128)(2,1)S(1)}, u32[]{:S(2)}, u32[]{:S(2)}) %collective-permute-start.19) | collective-permute-done | bytes 262176 | tf_op jit(solution)/shard_map/ppermute | solution.py:85
  54.5 1.6 %collective-permute-start.20 = (bf16[128,512]{1,0:T(8,128)(2,1)S(1)}, bf16[128,512]{1,0:T(8,128)(2,1)S(1)}, u32[]{:S(2)}, u32[]{:S(2)}) collective-permute-start(bf16[128,512]{1,0:T(8,128)(2,1)S(1)} %get-tuple-element.106), channel_id=1, source_target_pairs={{0,2},{1,3},{2,0},{3,1},{4,6},{5,7},{6,4},{7,5},{8,10},{9,11},{10,... | collective-permute-start | bytes 393224 | tf_op jit(solution)/shard_map/ppermute | solution.py:85
  56.5 3.6 %collective-permute-done.20.refs_1_ = bf16[128,512]{1,0:T(8,128)(2,1)S(1)} collective-permute-done((bf16[128,512]{1,0:T(8,128)(2,1)S(1)}, bf16[128,512]{1,0:T(8,128)(2,1)S(1)}, u32[]{:S(2)}, u32[]{:S(2)}) %collective-permute-start.20) | collective-permute-done | bytes 131104 | tf_op jit(solution)/shard_map/ppermute | solution.py:85
  60.7 1.6 %collective-permute-start.22 = (bf16[128,512]{1,0:T(8,128)(2,1)S(1)}, bf16[128,512]{1,0:T(8,128)(2,1)S(1)}, u32[]{:S(2)}, u32[]{:S(2)}) collective-permute-start(bf16[128,512]{1,0:T(8,128)(2,1)S(1)} %get-tuple-element.107.refs_0_), channel_id=1, source_target_pairs={{0,2},{1,3},{2,0},{3,1},{4,6},{5,7},{6,4},{7,5},{8,10},{9,11},{10,... | collective-permute-start | bytes 393224 | tf_op jit(solution)/shard_map/ppermute | solution.py:85
  62.3 3.5 %collective-permute-done.22.refs_2_ = bf16[128,512]{1,0:T(8,128)(2,1)S(1)} collective-permute-done((bf16[128,512]{1,0:T(8,128)(2,1)S(1)}, bf16[128,512]{1,0:T(8,128)(2,1)S(1)}, u32[]{:S(2)}, u32[]{:S(2)}) %collective-permute-start.22) | collective-permute-done | bytes 131104 | tf_op jit(solution)/shard_map/ppermute | solution.py:85
  65.7 1.3 %collective-permute-done.23.refs_3_ = bf16[128,512]{1,0:T(8,128)(2,1)S(1)} collective-permute-done((bf16[128,512]{1,0:T(8,128)(2,1)S(1)}, bf16[128,512]{1,0:T(8,128)(2,1)S(1)}, u32[]{:S(2)}, u32[]{:S(2)}) %collective-permute-start.23) | collective-permute-done | bytes 131104 | tf_op jit(solution)/shard_map/ppermute | solution.py:85
  67.1 2.5 %edge_backward.1 = (bf16[1024,512]{1,0:T(8,128)(2,1)S(1)}, bf16[2,512,128]{2,1,0:T(8,128)(2,1)S(1)}, bf16[2,512,128]{2,1,0:T(8,128)(2,1)S(1)}) custom-call(s32[1]{0:T(128)} %bitcast.me_ref, bf16[1024,512]{1,0:T(8,128)(2,1)S(1)} %copy-done.1, f32[1024,512]{1,0:T(8,128)S(1)} %get-tuple-element.96.pre_ref, bf16[512,1024]{1,0:T(8,128)(2,1)S(1)} %get-tuple-element.97.send_ref, ...), custom_call_target="tpu_custom_call" | custom-call | flops 1879048192 | bytes 9437184 | tf_op jit(solution)/shard_map/edge_backward/pallas_call | solution.py:63
  69.8 1.9 %local_backward.1 = (bf16[2,512,128]{2,1,0:T(8,128)(2,1)S(1)}, bf16[2,512,128]{2,1,0:T(8,128)(2,1)S(1)}) custom-call(s32[1]{0:T(128)} %bitcast.me_ref, bf16[1024,512]{1,0:T(8,128)(2,1)S(1)} %get-tuple-element.108.dpre_ref, bf16[512,1024]{1,0:T(8,128)(2,1)S(1)} %get-tuple-element.109.send_ref, bf16[512,1024]{1,0:T(8,128)(2,1)S(1)} %get-tuple-element.92.recv_ref, ...), custom_call_target="tpu_custom_call" | custom-call | flops 1610612736 | bytes 5505024 | tf_op jit(solution)/shard_map/local_backward/pallas_call | solution.py:63
  72.2 1.6 %collective-permute-start.27 = (bf16[512,128]{1,0:T(8,128)(2,1)S(1)}, bf16[512,128]{1,0:T(8,128)(2,1)S(1)}, u32[]{:S(2)}, u32[]{:S(2)}) collective-permute-start(bf16[512,128]{1,0:T(8,128)(2,1)S(1)} %get-tuple-element.118), channel_id=1, source_target_pairs={{0,2},{1,3},{2,0},{3,1},{4,6},{5,7},{6,4},{7,5},{8,10},{9,11},{10,... | collective-permute-start | bytes 393224 | tf_op jit(solution)/shard_map/ppermute | solution.py:85
  73.9 1.1 %collective-permute-start.25 = (bf16[512,128]{1,0:T(8,128)(2,1)S(1)}, bf16[512,128]{1,0:T(8,128)(2,1)S(1)}, u32[]{:S(2)}, u32[]{:S(2)}) collective-permute-start(bf16[512,128]{1,0:T(8,128)(2,1)S(1)} %get-tuple-element.114), channel_id=1, source_target_pairs={{0,2},{1,3},{2,0},{3,1},{4,6},{5,7},{6,4},{7,5},{8,10},{9,11},{10,... | collective-permute-start | bytes 393224 | tf_op jit(solution)/shard_map/ppermute | solution.py:85
  75.0 3.7 %collective-permute-done.27.refs_1_ = bf16[512,128]{1,0:T(8,128)(2,1)S(1)} collective-permute-done((bf16[512,128]{1,0:T(8,128)(2,1)S(1)}, bf16[512,128]{1,0:T(8,128)(2,1)S(1)}, u32[]{:S(2)}, u32[]{:S(2)}) %collective-permute-start.27) | collective-permute-done | bytes 131104 | tf_op jit(solution)/shard_map/ppermute | solution.py:85
  78.7 3.3 %collective-permute-start.28 = (bf16[128,128]{1,0:T(8,128)(2,1)S(1)}, bf16[128,128]{1,0:T(8,128)(2,1)S(1)}, u32[]{:S(2)}, u32[]{:S(2)}) collective-permute-start(bf16[128,128]{1,0:T(8,128)(2,1)S(1)} %get-tuple-element.120), channel_id=1, source_target_pairs={{0,12},{4,8},{8,4},{12,0},{1,13},{5,9},{9,5},{13,1},{2,14},{6,10},... | collective-permute-start | bytes 98312 | tf_op jit(solution)/shard_map/ppermute | solution.py:88
  82.0 1.2 %collective-permute-start.30 = (bf16[128,128]{1,0:T(8,128)(2,1)S(1)}, bf16[128,128]{1,0:T(8,128)(2,1)S(1)}, u32[]{:S(2)}, u32[]{:S(2)}) collective-permute-start(bf16[128,128]{1,0:T(8,128)(2,1)S(1)} %get-tuple-element.122), channel_id=1, source_target_pairs={{0,4},{4,0},{8,12},{12,8},{1,5},{5,1},{9,13},{13,9},{2,6},{6,2},{1... | collective-permute-start | bytes 98312 | tf_op jit(solution)/shard_map/ppermute | solution.py:88
  83.1 1.3 %collective-permute-done.28.refs_3_ = bf16[128,128]{1,0:T(8,128)(2,1)S(1)} collective-permute-done((bf16[128,128]{1,0:T(8,128)(2,1)S(1)}, bf16[128,128]{1,0:T(8,128)(2,1)S(1)}, u32[]{:S(2)}, u32[]{:S(2)}) %collective-permute-start.28) | collective-permute-done | bytes 32800 | tf_op jit(solution)/shard_map/ppermute | solution.py:88
  84.5 2.3 %collective-permute-done.29.refs_4_ = bf16[128,128]{1,0:T(8,128)(2,1)S(1)} collective-permute-done((bf16[128,128]{1,0:T(8,128)(2,1)S(1)}, bf16[128,128]{1,0:T(8,128)(2,1)S(1)}, u32[]{:S(2)}, u32[]{:S(2)}) %collective-permute-start.29) | collective-permute-done | bytes 32800 | tf_op jit(solution)/shard_map/ppermute | solution.py:88
  86.8 1.2 %owed_rows.1 = (bf16[256,128]{1,0:T(8,128)(2,1)S(1)}, bf16[256,128]{1,0:T(8,128)(2,1)S(1)}, bf16[256,128]{1,0:T(8,128)(2,1)S(1)}, bf16[256,128]{1,0:T(8,128)(2,1...) custom-call(s32[1]{0:T(128)} %bitcast.me_ref, ...), custom_call_target="tpu_custom_call" | custom-call | flops 268435456 | bytes 935936 | tf_op jit(solution)/shard_map/owed_rows/pallas_call | solution.py:63
  88.0 1.5 %collective-permute-start.31 = (bf16[256,128]{1,0:T(8,128)(2,1)S(1)}, bf16[256,128]{1,0:T(8,128)(2,1)S(1)}, u32[]{:S(2)}, u32[]{:S(2)}) collective-permute-start(bf16[256,128]{1,0:T(8,128)(2,1)S(1)} %get-tuple-element.124), channel_id=1, source_target_pairs={{0,12},{4,8},{8,4},{12,0},{1,13},{5,9},{9,5},{13,1},{2,14},{6,10},... | collective-permute-start | bytes 196616 | tf_op jit(solution)/shard_map/ppermute | solution.py:88
  90.1 2.3 %collective-permute-start.33 = (bf16[256,128]{1,0:T(8,128)(2,1)S(1)}, bf16[256,128]{1,0:T(8,128)(2,1)S(1)}, u32[]{:S(2)}, u32[]{:S(2)}) collective-permute-start(bf16[256,128]{1,0:T(8,128)(2,1)S(1)} %get-tuple-element.126), channel_id=1, source_target_pairs={{0,4},{4,0},{8,12},{12,8},{1,5},{5,1},{9,13},{13,9},{2,6},{6,2},{1... | collective-permute-start | bytes 196616 | tf_op jit(solution)/shard_map/ppermute | solution.py:88
  92.4 1.4 %collective-permute-start.36 = (bf16[256,128]{1,0:T(8,128)(2,1)S(1)}, bf16[256,128]{1,0:T(8,128)(2,1)S(1)}, u32[]{:S(2)}, u32[]{:S(2)}) collective-permute-start(bf16[256,128]{1,0:T(8,128)(2,1)S(1)} %get-tuple-element.130), channel_id=1, source_target_pairs={{0,12},{4,8},{8,4},{12,0},{1,13},{5,9},{9,5},{13,1},{2,14},{6,10},... | collective-permute-start | bytes 196616 | tf_op jit(solution)/shard_map/ppermute | solution.py:88
  93.9 1.1 %collective-permute-done.31.refs_1_ = bf16[256,128]{1,0:T(8,128)(2,1)S(1)} collective-permute-done((bf16[256,128]{1,0:T(8,128)(2,1)S(1)}, bf16[256,128]{1,0:T(8,128)(2,1)S(1)}, u32[]{:S(2)}, u32[]{:S(2)}) %collective-permute-start.31) | collective-permute-done | bytes 65568 | tf_op jit(solution)/shard_map/ppermute | solution.py:88
  95.0 1.9 %collective-permute-start.38 = (bf16[256,128]{1,0:T(8,128)(2,1)S(1)}, bf16[256,128]{1,0:T(8,128)(2,1)S(1)}, u32[]{:S(2)}, u32[]{:S(2)}) collective-permute-start(bf16[256,128]{1,0:T(8,128)(2,1)S(1)} %get-tuple-element.132), channel_id=1, source_target_pairs={{0,4},{4,0},{8,12},{12,8},{1,5},{5,1},{9,13},{13,9},{2,6},{6,2},{1... | collective-permute-start | bytes 196616 | tf_op jit(solution)/shard_map/ppermute | solution.py:88
  97.9 1.6 %collective-permute-start.34 = (bf16[256,128]{1,0:T(8,128)(2,1)S(1)}, bf16[256,128]{1,0:T(8,128)(2,1)S(1)}, u32[]{:S(2)}, u32[]{:S(2)}) collective-permute-start(bf16[256,128]{1,0:T(8,128)(2,1)S(1)} %get-tuple-element.127.refs_4_), channel_id=1, source_target_pairs={{0,2},{1,3},{2,0},{3,1},{4,6},{5,7},{6,4},{7,5},{8,10},{9,11},{10,... | collective-permute-start | bytes 196616 | tf_op jit(solution)/shard_map/ppermute | solution.py:85
  99.5 0.9 collective-permute-done.37.refs_2_
  100.8 1.4 %collective-permute-done.34.refs_0_ = bf16[256,128]{1,0:T(8,128)(2,1)S(1)} collective-permute-done((bf16[256,128]{1,0:T(8,128)(2,1)S(1)}, bf16[256,128]{1,0:T(8,128)(2,1)S(1)}, u32[]{:S(2)}, u32[]{:S(2)}) %collective-permute-start.34) | collective-permute-done | bytes 65568 | tf_op jit(solution)/shard_map/ppermute | solution.py:85
  102.2 1.4 %collective-permute-done.35.refs_1_ = bf16[256,128]{1,0:T(8,128)(2,1)S(1)} collective-permute-done((bf16[256,128]{1,0:T(8,128)(2,1)S(1)}, bf16[256,128]{1,0:T(8,128)(2,1)S(1)}, u32[]{:S(2)}, u32[]{:S(2)}) %collective-permute-start.35) | collective-permute-done | bytes 65568 | tf_op jit(solution)/shard_map/ppermute | solution.py:85
  103.7 1.1 %adjoint.1 = f32[256,512]{1,0:T(8,128)} custom-call(s32[1]{0:T(128)} %bitcast.me_ref, bf16[512,512]{1,0:T(8,128)(2,1)S(1)} %get-tuple-element.73.enc_ref, bf16[2,256,128]{2,1,0:T(8,128)(2,1)S(1)} %far_join.1.far_ref, bf16[256,128]{1,0:T(8,128)(2,1)S(1)} %get-tuple-element.133.refs_2_.refs_0_, bf16[256,128]{1,0:T(8,128)(2,1)S(1)} %collective-permute-done.39.refs_1_), custom_call_target="tpu_custom_call" | custom-call | flops 134217728 | bytes 1310720 | tf_op jit(solution)/shard_map/adjoint/pallas_call | solution.py:63
  (65 shorter events, 8.2 us)
Async XLA Ops:
  0.0 33.0 %copy-start.2 = (bf16[512,512]{1,0:T(8,128)(2,1)S(1)}, bf16[512,512]{1,0:T(8,128)(2,1)}, u32[]{:S(2)}) copy-start(bf16[512,512]{1,0:T(8,128)(2,1)} %base_ref.1) | copy-start | bytes 1572868
  0.0 10.3 %collective-permute-start.1 = (bf16[256,512]{1,0:T(8,128)(2,1)}, bf16[256,512]{1,0:T(8,128)(2,1)S(1)}, u32[]{:S(2)}, u32[]{:S(2)}) collective-permute-start(bf16[256,512]{1,0:T(8,128)(2,1)} %state_ref.1), channel_id=1, source_target_pairs={{0,2},{1,3},{2,0},{3,1},{4,6},{5,7},{6,4},{7,5},{8,10},{9,11},{10,... | collective-permute-start | bytes 786440 | tf_op jit(solution)/shard_map/ppermute | solution.py:85
  4.5 8.1 %collective-permute-start.4 = (bf16[144,512]{1,0:T(8,128)(2,1)S(1)}, bf16[144,512]{1,0:T(8,128)(2,1)S(1)}, u32[]{:S(2)}, u32[]{:S(2)}) collective-permute-start(bf16[144,512]{1,0:T(8,128)(2,1)S(1)} %get-tuple-element.72.refs_4_), channel_id=1, source_target_pairs={{0,2},{1,3},{2,0},{3,1},{4,6},{5,7},{6,4},{7,5},{8,10},{9,11},{10,... | collective-permute-start | bytes 442376 | tf_op jit(solution)/shard_map/ppermute | solution.py:85
  4.6 0.7 copy-start.3
  7.5 5.2 %collective-permute-start = (bf16[256,512]{1,0:T(8,128)(2,1)S(1)}, bf16[256,512]{1,0:T(8,128)(2,1)S(1)}, u32[]{:S(2)}, u32[]{:S(2)}) collective-permute-start(bf16[256,512]{1,0:T(8,128)(2,1)S(1)} %get-tuple-element.71.refs_0_), channel_id=1, source_target_pairs={{0,1},{1,0},{2,3},{3,2},{4,5},{5,4},{6,7},{7,6},{8,9},{9,8},{10,11... | collective-permute-start | bytes 786440 | tf_op jit(solution)/shard_map/ppermute | solution.py:85
  10.3 3.7 %collective-permute-start.2 = (bf16[256,512]{1,0:T(8,128)(2,1)S(1)}, bf16[256,512]{1,0:T(8,128)(2,1)S(1)}, u32[]{:S(2)}, u32[]{:S(2)}) collective-permute-start(bf16[256,512]{1,0:T(8,128)(2,1)S(1)} %collective-permute-done.1.refs_2_), channel_id=1, source_target_pairs={{0,1},{1,0},{2,3},{3,2},{4,5},{5,4},{6,7},{7,6},{8,9},{9,8},{10,11... | collective-permute-start | bytes 786440 | tf_op jit(solution)/shard_map/ppermute | solution.py:85
  10.3 2.3 %collective-permute-start.3 = (bf16[144,512]{1,0:T(8,128)(2,1)S(1)}, bf16[144,512]{1,0:T(8,128)(2,1)S(1)}, u32[]{:S(2)}, u32[]{:S(2)}) collective-permute-start(bf16[144,512]{1,0:T(8,128)(2,1)S(1)} %get-tuple-element.72.refs_4_), channel_id=1, source_target_pairs={{0,1},{1,0},{2,3},{3,2},{4,5},{5,4},{6,7},{7,6},{8,9},{9,8},{10,11... | collective-permute-start | bytes 442376 | tf_op jit(solution)/shard_map/ppermute | solution.py:85
  12.6 1.4 %collective-permute-start.5 = (bf16[144,512]{1,0:T(8,128)(2,1)S(1)}, bf16[144,512]{1,0:T(8,128)(2,1)S(1)}, u32[]{:S(2)}, u32[]{:S(2)}) collective-permute-start(bf16[144,512]{1,0:T(8,128)(2,1)S(1)} %collective-permute-done.4.refs_6_), channel_id=1, source_target_pairs={{0,1},{1,0},{2,3},{3,2},{4,5},{5,4},{6,7},{7,6},{8,9},{9,8},{10,11... | collective-permute-start | bytes 442376 | tf_op jit(solution)/shard_map/ppermute | solution.py:85
  16.5 29.2 %copy-start.4 = (bf16[1024,512]{1,0:T(8,128)(2,1)S(1)}, bf16[1024,512]{1,0:T(8,128)(2,1)}, u32[]{:S(2)}) copy-start(bf16[1024,512]{1,0:T(8,128)(2,1)} %es_ref.3) | copy-start | bytes 3145732
  16.5 25.9 %collective-permute-start.13 = (bf16[896,512]{1,0:T(8,128)(2,1)S(1)}, bf16[896,512]{1,0:T(8,128)(2,1)S(1)}, u32[]{:S(2)}, u32[]{:S(2)}) collective-permute-start(bf16[896,512]{1,0:T(8,128)(2,1)S(1)} %get-tuple-element.87.refs_6_), channel_id=1, source_target_pairs={{0,2},{1,3},{2,0},{3,1},{4,6},{5,7},{6,4},{7,5},{8,10},{9,11},{10,... | collective-permute-start | bytes 2752520 | tf_op jit(solution)/shard_map/ppermute | solution.py:85
  18.3 8.2 %collective-permute-start.6 = (bf16[512,128]{1,0:T(8,128)(2,1)S(1)}, bf16[512,128]{1,0:T(8,128)(2,1)S(1)}, u32[]{:S(2)}, u32[]{:S(2)}) collective-permute-start(bf16[512,128]{1,0:T(8,128)(2,1)S(1)} %get-tuple-element.80), channel_id=1, source_target_pairs={{0,12},{4,8},{8,4},{12,0},{1,13},{5,9},{9,5},{13,1},{2,14},{6,10},... | collective-permute-start | bytes 393224 | tf_op jit(solution)/shard_map/ppermute | solution.py:88
  21.9 11.1 %collective-permute-start.7 = (bf16[512,128]{1,0:T(8,128)(2,1)S(1)}, bf16[512,128]{1,0:T(8,128)(2,1)S(1)}, u32[]{:S(2)}, u32[]{:S(2)}) collective-permute-start(bf16[512,128]{1,0:T(8,128)(2,1)S(1)} %get-tuple-element.81), channel_id=1, source_target_pairs={{0,8},{4,12},{8,0},{12,4},{1,9},{5,13},{9,1},{13,5},{2,10},{6,14},... | collective-permute-start | bytes 393224 | tf_op jit(solution)/shard_map/ppermute | solution.py:88
  21.9 11.1 %collective-permute-start.8 = (bf16[512,128]{1,0:T(8,128)(2,1)S(1)}, bf16[512,128]{1,0:T(8,128)(2,1)S(1)}, u32[]{:S(2)}, u32[]{:S(2)}) collective-permute-start(bf16[512,128]{1,0:T(8,128)(2,1)S(1)} %get-tuple-element.82), channel_id=1, source_target_pairs={{0,4},{4,0},{8,12},{12,8},{1,5},{5,1},{9,13},{13,9},{2,6},{6,2},{1... | collective-permute-start | bytes 393224 | tf_op jit(solution)/shard_map/ppermute | solution.py:88
  33.9 8.5 %collective-permute-start.12 = (bf16[512,128]{1,0:T(8,128)(2,1)S(1)}, bf16[512,128]{1,0:T(8,128)(2,1)S(1)}, u32[]{:S(2)}, u32[]{:S(2)}) collective-permute-start(bf16[512,128]{1,0:T(8,128)(2,1)S(1)} %encode.1.state_ref.refs_4_), channel_id=1, source_target_pairs={{0,2},{1,3},{2,0},{3,1},{4,6},{5,7},{6,4},{7,5},{8,10},{9,11},{10,... | collective-permute-start | bytes 393224 | tf_op jit(solution)/shard_map/ppermute | solution.py:85
  35.0 5.9 %collective-permute-start.9 = (bf16[128,128]{1,0:T(8,128)(2,1)S(1)}, bf16[128,128]{1,0:T(8,128)(2,1)S(1)}, u32[]{:S(2)}, u32[]{:S(2)}) collective-permute-start(bf16[128,128]{1,0:T(8,128)(2,1)S(1)} %get-tuple-element.84), channel_id=1, source_target_pairs={{0,12},{4,8},{8,4},{12,0},{1,13},{5,9},{9,5},{13,1},{2,14},{6,10},... | collective-permute-start | bytes 98312 | tf_op jit(solution)/shard_map/ppermute | solution.py:88
  37.6 4.8 %collective-permute-start.10 = (bf16[128,128]{1,0:T(8,128)(2,1)S(1)}, bf16[128,128]{1,0:T(8,128)(2,1)S(1)}, u32[]{:S(2)}, u32[]{:S(2)}) collective-permute-start(bf16[128,128]{1,0:T(8,128)(2,1)S(1)} %get-tuple-element.85), channel_id=1, source_target_pairs={{0,8},{4,12},{8,0},{12,4},{1,9},{5,13},{9,1},{13,5},{2,10},{6,14},... | collective-permute-start | bytes 98312 | tf_op jit(solution)/shard_map/ppermute | solution.py:88
  37.6 4.8 %collective-permute-start.11 = (bf16[128,128]{1,0:T(8,128)(2,1)S(1)}, bf16[128,128]{1,0:T(8,128)(2,1)S(1)}, u32[]{:S(2)}, u32[]{:S(2)}) collective-permute-start(bf16[128,128]{1,0:T(8,128)(2,1)S(1)} %get-tuple-element.86), channel_id=1, source_target_pairs={{0,4},{4,0},{8,12},{12,8},{1,5},{5,1},{9,13},{13,9},{2,6},{6,2},{1... | collective-permute-start | bytes 98312 | tf_op jit(solution)/shard_map/ppermute | solution.py:88
  42.6 3.1 %collective-permute-start.15 = (bf16[2,512,512]{2,1,0:T(8,128)(2,1)S(1)}, bf16[2,512,512]{2,1,0:T(8,128)(2,1)S(1)}, u32[]{:S(2)}, u32[]{:S(2)}) collective-permute-start(bf16[2,512,512]{2,1,0:T(8,128)(2,1)S(1)} %get-tuple-element.89.refs_2_), channel_id=1, source_target_pairs={{0,1},{1,0},{2,3},{3,2},{4,5},{5,4},{6,7},{7,6},{8,9},{9,8},{10,11... | collective-permute-start | bytes 3145736 | tf_op jit(solution)/shard_map/ppermute | solution.py:85
  42.6 3.0 %collective-permute-start.14 = (bf16[2,512,128]{2,1,0:T(8,128)(2,1)S(1)}, bf16[2,512,128]{2,1,0:T(8,128)(2,1)S(1)}, u32[]{:S(2)}, u32[]{:S(2)}) collective-permute-start(bf16[2,512,128]{2,1,0:T(8,128)(2,1)S(1)} %get-tuple-element.88.refs_0_), channel_id=1, source_target_pairs={{0,1},{1,0},{2,3},{3,2},{4,5},{5,4},{6,7},{7,6},{8,9},{9,8},{10,11... | collective-permute-start | bytes 786440 | tf_op jit(solution)/shard_map/ppermute | solution.py:85
  43.1 5.5 %collective-permute-start.16 = (bf16[512,128]{1,0:T(8,128)(2,1)S(1)}, bf16[512,128]{1,0:T(8,128)(2,1)S(1)}, u32[]{:S(2)}, u32[]{:S(2)}) collective-permute-start(bf16[512,128]{1,0:T(8,128)(2,1)S(1)} %get-tuple-element.95.refs_0_), channel_id=1, source_target_pairs={{0,2},{1,3},{2,0},{3,1},{4,6},{5,7},{6,4},{7,5},{8,10},{9,11},{10,... | collective-permute-start | bytes 393224 | tf_op jit(solution)/shard_map/ppermute | solution.py:85
  48.7 1.6 %collective-permute-start.17 = (bf16[2,512,128]{2,1,0:T(8,128)(2,1)S(1)}, bf16[2,512,128]{2,1,0:T(8,128)(2,1)S(1)}, u32[]{:S(2)}, u32[]{:S(2)}) collective-permute-start(bf16[2,512,128]{2,1,0:T(8,128)(2,1)S(1)} %halo_pair.1.refs_0_), channel_id=1, source_target_pairs={{0,1},{1,0},{2,3},{3,2},{4,5},{5,4},{6,7},{7,6},{8,9},{9,8},{10,11... | collective-permute-start | bytes 786440 | tf_op jit(solution)/shard_map/ppermute | solution.py:85
  48.9 7.1 %collective-permute-start.18 = (bf16[2,384,512]{2,1,0:T(8,128)(2,1)S(1)}, bf16[2,384,512]{2,1,0:T(8,128)(2,1)S(1)}, u32[]{:S(2)}, u32[]{:S(2)}) collective-permute-start(bf16[2,384,512]{2,1,0:T(8,128)(2,1)S(1)} %get-tuple-element.99.refs_0_), channel_id=1, source_target_pairs={{0,1},{1,0},{2,3},{3,2},{4,5},{5,4},{6,7},{7,6},{8,9},{9,8},{10,11... | collective-permute-start | bytes 2359304 | tf_op jit(solution)/shard_map/ppermute | solution.py:85
  50.3 5.7 %copy-start = (bf16[512,512]{1,0:T(8,128)(2,1)S(1)}, bf16[512,512]{1,0:T(8,128)(2,1)}, u32[]{:S(2)}) copy-start(bf16[512,512]{1,0:T(8,128)(2,1)} %grad_ref.4) | copy-start | bytes 1572868
  52.8 1.6 %collective-permute-start.19 = (bf16[2,128,512]{2,1,0:T(8,128)(2,1)S(1)}, bf16[2,128,512]{2,1,0:T(8,128)(2,1)S(1)}, u32[]{:S(2)}, u32[]{:S(2)}) collective-permute-start(bf16[2,128,512]{2,1,0:T(8,128)(2,1)S(1)} %get-tuple-element.101), channel_id=1, source_target_pairs={{0,1},{1,0},{2,3},{3,2},{4,5},{5,4},{6,7},{7,6},{8,9},{9,8},{10,11... | collective-permute-start | bytes 786440 | tf_op jit(solution)/shard_map/ppermute | solution.py:85
  54.5 5.6 %collective-permute-start.20 = (bf16[128,512]{1,0:T(8,128)(2,1)S(1)}, bf16[128,512]{1,0:T(8,128)(2,1)S(1)}, u32[]{:S(2)}, u32[]{:S(2)}) collective-permute-start(bf16[128,512]{1,0:T(8,128)(2,1)S(1)} %get-tuple-element.106), channel_id=1, source_target_pairs={{0,2},{1,3},{2,0},{3,1},{4,6},{5,7},{6,4},{7,5},{8,10},{9,11},{10,... | collective-permute-start | bytes 393224 | tf_op jit(solution)/shard_map/ppermute | solution.py:85
  56.0 11.1 %copy-start.1 = (bf16[1024,512]{1,0:T(8,128)(2,1)S(1)}, bf16[1024,512]{1,0:T(8,128)(2,1)}, u32[]{:S(2)}) copy-start(bf16[1024,512]{1,0:T(8,128)(2,1)} %grad_ref.5) | copy-start | bytes 3145732
  60.7 5.0 %collective-permute-start.22 = (bf16[128,512]{1,0:T(8,128)(2,1)S(1)}, bf16[128,512]{1,0:T(8,128)(2,1)S(1)}, u32[]{:S(2)}, u32[]{:S(2)}) collective-permute-start(bf16[128,512]{1,0:T(8,128)(2,1)S(1)} %get-tuple-element.107.refs_0_), channel_id=1, source_target_pairs={{0,2},{1,3},{2,0},{3,1},{4,6},{5,7},{6,4},{7,5},{8,10},{9,11},{10,... | collective-permute-start | bytes 393224 | tf_op jit(solution)/shard_map/ppermute | solution.py:85
  62.3 3.5 %collective-permute-start.21 = (bf16[128,512]{1,0:T(8,128)(2,1)S(1)}, bf16[128,512]{1,0:T(8,128)(2,1)S(1)}, u32[]{:S(2)}, u32[]{:S(2)}) collective-permute-start(bf16[128,512]{1,0:T(8,128)(2,1)S(1)} %get-tuple-element.107.refs_0_), channel_id=1, source_target_pairs={{0,1},{1,0},{2,3},{3,2},{4,5},{5,4},{6,7},{7,6},{8,9},{9,8},{10,11... | collective-permute-start | bytes 393224 | tf_op jit(solution)/shard_map/ppermute | solution.py:85
  65.7 1.3 %collective-permute-start.23 = (bf16[128,512]{1,0:T(8,128)(2,1)S(1)}, bf16[128,512]{1,0:T(8,128)(2,1)S(1)}, u32[]{:S(2)}, u32[]{:S(2)}) collective-permute-start(bf16[128,512]{1,0:T(8,128)(2,1)S(1)} %collective-permute-done.22.refs_2_), channel_id=1, source_target_pairs={{0,1},{1,0},{2,3},{3,2},{4,5},{5,4},{6,7},{7,6},{8,9},{9,8},{10,11... | collective-permute-start | bytes 393224 | tf_op jit(solution)/shard_map/ppermute | solution.py:85
  69.6 2.6 %collective-permute-start.26 = (bf16[2,512,128]{2,1,0:T(8,128)(2,1)S(1)}, bf16[2,512,128]{2,1,0:T(8,128)(2,1)S(1)}, u32[]{:S(2)}, u32[]{:S(2)}) collective-permute-start(bf16[2,512,128]{2,1,0:T(8,128)(2,1)S(1)} %get-tuple-element.116), channel_id=1, source_target_pairs={{0,1},{1,0},{2,3},{3,2},{4,5},{5,4},{6,7},{7,6},{8,9},{9,8},{10,11... | collective-permute-start | bytes 786440 | tf_op jit(solution)/shard_map/ppermute | solution.py:85
  71.7 2.1 %collective-permute-start.24 = (bf16[2,512,128]{2,1,0:T(8,128)(2,1)S(1)}, bf16[2,512,128]{2,1,0:T(8,128)(2,1)S(1)}, u32[]{:S(2)}, u32[]{:S(2)}) collective-permute-start(bf16[2,512,128]{2,1,0:T(8,128)(2,1)S(1)} %get-tuple-element.112), channel_id=1, source_target_pairs={{0,1},{1,0},{2,3},{3,2},{4,5},{5,4},{6,7},{7,6},{8,9},{9,8},{10,11... | collective-permute-start | bytes 786440 | tf_op jit(solution)/shard_map/ppermute | solution.py:85
  72.2 6.4 %collective-permute-start.27 = (bf16[512,128]{1,0:T(8,128)(2,1)S(1)}, bf16[512,128]{1,0:T(8,128)(2,1)S(1)}, u32[]{:S(2)}, u32[]{:S(2)}) collective-permute-start(bf16[512,128]{1,0:T(8,128)(2,1)S(1)} %get-tuple-element.118), channel_id=1, source_target_pairs={{0,2},{1,3},{2,0},{3,1},{4,6},{5,7},{6,4},{7,5},{8,10},{9,11},{10,... | collective-permute-start | bytes 393224 | tf_op jit(solution)/shard_map/ppermute | solution.py:85
  73.9 9.3 %collective-permute-start.25 = (bf16[512,128]{1,0:T(8,128)(2,1)S(1)}, bf16[512,128]{1,0:T(8,128)(2,1)S(1)}, u32[]{:S(2)}, u32[]{:S(2)}) collective-permute-start(bf16[512,128]{1,0:T(8,128)(2,1)S(1)} %get-tuple-element.114), channel_id=1, source_target_pairs={{0,2},{1,3},{2,0},{3,1},{4,6},{5,7},{6,4},{7,5},{8,10},{9,11},{10,... | collective-permute-start | bytes 393224 | tf_op jit(solution)/shard_map/ppermute | solution.py:85
  78.7 5.8 %collective-permute-start.28 = (bf16[128,128]{1,0:T(8,128)(2,1)S(1)}, bf16[128,128]{1,0:T(8,128)(2,1)S(1)}, u32[]{:S(2)}, u32[]{:S(2)}) collective-permute-start(bf16[128,128]{1,0:T(8,128)(2,1)S(1)} %get-tuple-element.120), channel_id=1, source_target_pairs={{0,12},{4,8},{8,4},{12,0},{1,13},{5,9},{9,5},{13,1},{2,14},{6,10},... | collective-permute-start | bytes 98312 | tf_op jit(solution)/shard_map/ppermute | solution.py:88
  82.0 4.8 %collective-permute-start.29 = (bf16[128,128]{1,0:T(8,128)(2,1)S(1)}, bf16[128,128]{1,0:T(8,128)(2,1)S(1)}, u32[]{:S(2)}, u32[]{:S(2)}) collective-permute-start(bf16[128,128]{1,0:T(8,128)(2,1)S(1)} %get-tuple-element.121), channel_id=1, source_target_pairs={{0,8},{4,12},{8,0},{12,4},{1,9},{5,13},{9,1},{13,5},{2,10},{6,14},... | collective-permute-start | bytes 98312 | tf_op jit(solution)/shard_map/ppermute | solution.py:88
  82.0 4.8 %collective-permute-start.30 = (bf16[128,128]{1,0:T(8,128)(2,1)S(1)}, bf16[128,128]{1,0:T(8,128)(2,1)S(1)}, u32[]{:S(2)}, u32[]{:S(2)}) collective-permute-start(bf16[128,128]{1,0:T(8,128)(2,1)S(1)} %get-tuple-element.122), channel_id=1, source_target_pairs={{0,4},{4,0},{8,12},{12,8},{1,5},{5,1},{9,13},{13,9},{2,6},{6,2},{1... | collective-permute-start | bytes 98312 | tf_op jit(solution)/shard_map/ppermute | solution.py:88
  88.0 7.0 %collective-permute-start.31 = (bf16[256,128]{1,0:T(8,128)(2,1)S(1)}, bf16[256,128]{1,0:T(8,128)(2,1)S(1)}, u32[]{:S(2)}, u32[]{:S(2)}) collective-permute-start(bf16[256,128]{1,0:T(8,128)(2,1)S(1)} %get-tuple-element.124), channel_id=1, source_target_pairs={{0,12},{4,8},{8,4},{12,0},{1,13},{5,9},{9,5},{13,1},{2,14},{6,10},... | collective-permute-start | bytes 196616 | tf_op jit(solution)/shard_map/ppermute | solution.py:88
  89.5 8.1 %collective-permute-start.32 = (bf16[256,128]{1,0:T(8,128)(2,1)S(1)}, bf16[256,128]{1,0:T(8,128)(2,1)S(1)}, u32[]{:S(2)}, u32[]{:S(2)}) collective-permute-start(bf16[256,128]{1,0:T(8,128)(2,1)S(1)} %get-tuple-element.125), channel_id=1, source_target_pairs={{0,8},{4,12},{8,0},{12,4},{1,9},{5,13},{9,1},{13,5},{2,10},{6,14},... | collective-permute-start | bytes 196616 | tf_op jit(solution)/shard_map/ppermute | solution.py:88
  90.1 7.5 %collective-permute-start.33 = (bf16[256,128]{1,0:T(8,128)(2,1)S(1)}, bf16[256,128]{1,0:T(8,128)(2,1)S(1)}, u32[]{:S(2)}, u32[]{:S(2)}) collective-permute-start(bf16[256,128]{1,0:T(8,128)(2,1)S(1)} %get-tuple-element.126), channel_id=1, source_target_pairs={{0,4},{4,0},{8,12},{12,8},{1,5},{5,1},{9,13},{13,9},{2,6},{6,2},{1... | collective-permute-start | bytes 196616 | tf_op jit(solution)/shard_map/ppermute | solution.py:88
  92.4 7.0 %collective-permute-start.36 = (bf16[256,128]{1,0:T(8,128)(2,1)S(1)}, bf16[256,128]{1,0:T(8,128)(2,1)S(1)}, u32[]{:S(2)}, u32[]{:S(2)}) collective-permute-start(bf16[256,128]{1,0:T(8,128)(2,1)S(1)} %get-tuple-element.130), channel_id=1, source_target_pairs={{0,12},{4,8},{8,4},{12,0},{1,13},{5,9},{9,5},{13,1},{2,14},{6,10},... | collective-permute-start | bytes 196616 | tf_op jit(solution)/shard_map/ppermute | solution.py:88
  93.9 6.5 %collective-permute-start.37 = (bf16[256,128]{1,0:T(8,128)(2,1)S(1)}, bf16[256,128]{1,0:T(8,128)(2,1)S(1)}, u32[]{:S(2)}, u32[]{:S(2)}) collective-permute-start(bf16[256,128]{1,0:T(8,128)(2,1)S(1)} %get-tuple-element.131), channel_id=1, source_target_pairs={{0,8},{4,12},{8,0},{12,4},{1,9},{5,13},{9,1},{13,5},{2,10},{6,14},... | collective-permute-start | bytes 196616 | tf_op jit(solution)/shard_map/ppermute | solution.py:88
  95.0 5.4 %collective-permute-start.38 = (bf16[256,128]{1,0:T(8,128)(2,1)S(1)}, bf16[256,128]{1,0:T(8,128)(2,1)S(1)}, u32[]{:S(2)}, u32[]{:S(2)}) collective-permute-start(bf16[256,128]{1,0:T(8,128)(2,1)S(1)} %get-tuple-element.132), channel_id=1, source_target_pairs={{0,4},{4,0},{8,12},{12,8},{1,5},{5,1},{9,13},{13,9},{2,6},{6,2},{1... | collective-permute-start | bytes 196616 | tf_op jit(solution)/shard_map/ppermute | solution.py:88
  97.9 4.3 %collective-permute-start.34 = (bf16[256,128]{1,0:T(8,128)(2,1)S(1)}, bf16[256,128]{1,0:T(8,128)(2,1)S(1)}, u32[]{:S(2)}, u32[]{:S(2)}) collective-permute-start(bf16[256,128]{1,0:T(8,128)(2,1)S(1)} %get-tuple-element.127.refs_4_), channel_id=1, source_target_pairs={{0,2},{1,3},{2,0},{3,1},{4,6},{5,7},{6,4},{7,5},{8,10},{9,11},{10,... | collective-permute-start | bytes 196616 | tf_op jit(solution)/shard_map/ppermute | solution.py:85
  99.4 4.2 %collective-permute-start.35 = (bf16[256,128]{1,0:T(8,128)(2,1)S(1)}, bf16[256,128]{1,0:T(8,128)(2,1)S(1)}, u32[]{:S(2)}, u32[]{:S(2)}) collective-permute-start(bf16[256,128]{1,0:T(8,128)(2,1)S(1)} %get-tuple-element.128), channel_id=1, source_target_pairs={{0,3},{1,2},{2,1},{3,0},{4,7},{5,6},{6,5},{7,4},{8,11},{9,10},{10,... | collective-permute-start | bytes 196616 | tf_op jit(solution)/shard_map/ppermute | solution.py:85
  100.7 2.9 %collective-permute-start.39 = (bf16[256,128]{1,0:T(8,128)(2,1)S(1)}, bf16[256,128]{1,0:T(8,128)(2,1)S(1)}, u32[]{:S(2)}, u32[]{:S(2)}) collective-permute-start(bf16[256,128]{1,0:T(8,128)(2,1)S(1)} %get-tuple-element.134), channel_id=1, source_target_pairs={{0,1},{1,0},{2,3},{3,2},{4,5},{5,4},{6,7},{7,6},{8,9},{9,8},{10,11... | collective-permute-start | bytes 196616 | tf_op jit(solution)/shard_map/ppermute | solution.py:85
